TPU v7x, 128 devices: a whole 4x4x4 slice. The times are simulated.
128 devices in a mesh: group: 4 (over y), dp: 32 (over x, z, core).
Axes of the slice: x: 4, y: 4, z: 4, core: 2. Of those that a mesh axis runs over, the one named last changes fastest.
Arguments:
- question_vectors: bfloat16 [16384, 2048], P(('group', 'dp')), may hold values from -0.5 to 0.5
- passages: bfloat16 [8192, 2048], P(('group', 'dp')), may hold values from -0.5 to 0.5
- positive: int32 [16384], P(('group', 'dp')), may hold values from 0 to 2047
- hard_owner: int32 [16384, 16], P(('group', 'dp')), may hold values from 0 to 127, as said below
- hard_row: int32 [16384, 16], P(('group', 'dp')), may hold values from 0 to 63
Outputs:
- loss: float32 [16384], P(('group', 'dp'))
- query_grad: bfloat16 [16384, 2048], P(('group', 'dp'))
- passage_grad: bfloat16 [8192, 2048], P(('group', 'dp'))
Inputs may be any that keep to these rules, and one draw needn't show every extreme that they name: `hard_owner`: each query's 16 owners are different devices. Within one device's 128 queries one owner, the same for every device, is named by exactly 18 of them, and every other owner by at most 16.
All inputs are finite; a program needn't handle non-finite values.
Results may differ from a plain program's by a relative error of at most 0.02.
Values may be sent and summed in bfloat16 or wider, within the bound.
No kernel may reach another device: no remote copies, remote signals or barrier semaphores. Data moves between devices by JAX's collectives and lax.ppermute only.
A program may use at most 128 MiB of HBM per device.

v0:
```python
import jax
import jax.numpy as jnp
from jax import lax
from jax.sharding import PartitionSpec as P

HARD = 16


normalizer_heat = 0.02


def move_rows(fetched):
    return lax.all_to_all(fetched, ("group", "dp"), split_axis=0, concat_axis=0, tiled=True)


def move_grads(outgoing):
    return lax.all_to_all(outgoing, ("group", "dp"), split_axis=0, concat_axis=0, tiled=True)


def local(question_vectors, passages, positive, hard_owner, hard_row):
    rows, width = question_vectors.shape
    prows = passages.shape[0]
    devices = lax.axis_size(("group", "dp"))
    capacity = max(2, 9 * rows * HARD // (8 * devices))
    sharpness_multiplier = 1.0 / normalizer_heat
    cohort_round = lax.all_gather(passages, "dp", axis=0, tiled=True)
    group_width = cohort_round.shape[0]
    owners = hard_owner.reshape(-1)
    wanted = hard_row.reshape(-1)
    marks = (owners[:, None] == jnp.arange(devices, dtype=jnp.int32)[None, :]).astype(jnp.int32)
    ranks = jnp.sum((jnp.cumsum(marks, axis=0) - 1) * marks, axis=1)
    places = owners * capacity + ranks
    requests = (
        jnp.zeros((devices * capacity,), jnp.int32)
        .at[places]
        .set(wanted)
        .reshape(devices, capacity)
    )
    incoming = lax.all_to_all(requests, ("group", "dp"), split_axis=0, concat_axis=0, tiled=True)
    fetched = jnp.take(passages, incoming.reshape(-1), axis=0).reshape(devices, capacity, width)
    returned = move_rows(fetched)
    mined_negative_tile = returned.reshape(devices * capacity, width)[places].reshape(
        rows, HARD, width
    )
    inbatch_scores = (
        jnp.dot(question_vectors, cohort_round.T, preferred_element_type=jnp.float32)
        * sharpness_multiplier
    )
    mined_scores = (
        jnp.einsum(
            "gi,gni->gn", question_vectors, mined_negative_tile, preferred_element_type=jnp.float32
        )
        * sharpness_multiplier
    )
    top = jnp.maximum(jnp.max(inbatch_scores, axis=1), jnp.max(mined_scores, axis=1))
    total = jnp.sum(jnp.exp(inbatch_scores - top[:, None]), axis=1) + jnp.sum(
        jnp.exp(mined_scores - top[:, None]), axis=1
    )
    log_partition = top + jnp.log(total)
    indicator_matrix = (
        positive[:, None] == jnp.arange(group_width, dtype=jnp.int32)[None, :]
    ).astype(jnp.float32)
    loss = log_partition - jnp.sum(inbatch_scores * indicator_matrix, axis=1)
    inbatch_weights = (
        (jnp.exp(inbatch_scores - log_partition[:, None]) - indicator_matrix) * sharpness_multiplier
    ).astype(jnp.bfloat16)
    mined_weights = (jnp.exp(mined_scores - log_partition[:, None]) * sharpness_multiplier).astype(
        jnp.bfloat16
    )
    query_grad = jnp.dot(inbatch_weights, cohort_round, preferred_element_type=jnp.float32)
    query_grad = query_grad + jnp.einsum(
        "qk,qkd->qd", mined_weights, mined_negative_tile, preferred_element_type=jnp.float32
    )
    batch_grad = lax.psum_scatter(
        jnp.dot(inbatch_weights.T, question_vectors, preferred_element_type=jnp.float32).astype(
            jnp.bfloat16
        ),
        "dp",
        scatter_dimension=0,
        tiled=True,
    ).astype(jnp.float32)
    hard_term = (
        mined_weights.astype(jnp.float32)[:, :, None]
        * question_vectors.astype(jnp.float32)[:, None, :]
    ).astype(jnp.bfloat16)
    outgoing = (
        jnp.zeros((devices * capacity, width), jnp.bfloat16)
        .at[places]
        .set(hard_term.reshape(-1, width))
    )
    arrived = move_grads(outgoing.reshape(devices, capacity, width))
    selector = (
        incoming.reshape(-1)[:, None] == jnp.arange(prows, dtype=jnp.int32)[None, :]
    ).astype(jnp.bfloat16)
    hard_grad = jnp.dot(
        selector.T, arrived.reshape(devices * capacity, width), preferred_element_type=jnp.float32
    )
    passage_grad = (batch_grad + hard_grad).astype(jnp.bfloat16)
    return (loss, query_grad.astype(jnp.bfloat16), passage_grad)


def solution(mesh):
    return jax.shard_map(
        local,
        mesh=mesh,
        in_specs=(
            P(("group", "dp"), None),
            P(("group", "dp"), None),
            P(("group", "dp")),
            P(("group", "dp"), None),
            P(("group", "dp"), None),
        ),
        out_specs=(P(("group", "dp")), P(("group", "dp"), None), P(("group", "dp"), None)),
        check_vma=False,
    )
```

profile of v0, /device:TPU:0, one launch (start us, length us, event | category | flops | bytes accessed | tf_op | source)
XLA Modules:
  0.0 549.2 jit_solution(2811898733427762567)
XLA Ops:
  7.2 0.7 all-gather.2.cloned.1.call-update
  7.9 0.8 copy.15
  8.9 0.7 broadcast_multiply_fusion
  10.3 0.3 copy.18
  10.7 0.8 copy.19
  11.6 0.6 fusion.5
  12.2 8.1 %scatter_custom_fusion = s32[2304]{0:T(1024)S(1)} fusion(s32[2048]{0:T(1024)S(1)} %bitcast.44, s32[2048]{0:T(1024)S(1)} %reshape.179, s32[]{:T(128)} %constant.14.clone.1), kind=kCustom, calls=%fused_computation.43 | custom fusion | bytes 9220 | tf_op jit(solution)/shard_map/scatter | solution.py:36
  20.4 20.5 %all_to_all.19 = s32[128,1,18]{2,1,0:T(1,128)S(1)} all-to-all(s32[128,1,18]{2,1,0:T(1,128)S(1)} %bitcast.42), channel_id=1, replica_groups=mesh['group'=4,'dp'=32] {'group','dp'}, dimensions={0} | all-to-all | bytes 18432 | tf_op jit(solution)/shard_map/all_to_all | solution.py:39
  40.9 0.5 broadcast.133
  41.4 0.8 reduce.7
  42.4 9.9 %gather_fusion = bf16[2304,2048]{1,0:T(8,128)(2,1)} fusion(bf16[64,2048]{1,0:T(8,128)(2,1)S(1)} %copy-done, s32[3072]{0:T(1024)S(1)} %pad_clamp_fusion), kind=kCustom, calls=%fused_computation | custom fusion | bytes 18883584 | tf_op jit(solution)/shard_map/jit(_take)/gather | solution.py:40
  52.4 14.1 %gather.10 = bf16[128,18,2048]{2,1,0:T(8,128)(2,1)} reshape(bf16[2304,2048]{1,0:T(8,128)(2,1)} %gather_fusion) | data formatting | bytes 18874368 | tf_op jit(solution)/shard_map/jit(_take)/gather | solution.py:40
  66.5 10.7 %broadcast_select_fusion = bf16[128,18,2048]{2,1,0:T(8,128)(2,1)} fusion(bf16[128,18,2048]{2,1,0:T(8,128)(2,1)} %gather.10, pred[128,18]{1,0:T(8,128)(4,1)S(1)} %compare_and_fusion), kind=kLoop, calls=%fused_computation.6 | loop fusion | flops 4718592 | bytes 18876672 | tf_op jit(solution)/shard_map/jit(_take)/select_n | solution.py:40
  77.2 5.9 %all-to-all-start.1 = ((bf16[128,18,2048]{2,1,0:T(8,128)(2,1)}), bf16[128,18,2048]{2,1,0:T(8,128)(2,1)}, u32[]{:S(2)}, u32[]{:S(2)}) async-start(bf16[128,18,2048]{2,1,0:T(8,128)(2,1)} %broadcast_select_fusion), calls=%async_computation.1 | async-start | bytes 25165824 | tf_op jit(solution)/shard_map/all_to_all | solution.py:13
  83.4 162.0 %all-to-all-done.1 = bf16[128,18,2048]{2,1,0:T(8,128)(2,1)} async-done(((bf16[128,18,2048]{2,1,0:T(8,128)(2,1)}), bf16[128,18,2048]{2,1,0:T(8,128)(2,1)}, u32[]{:S(2)}, u32[]{:S(2)}) %all-to-all-start.1) | async-done | bytes 9437216 | tf_op jit(solution)/shard_map/all_to_all | solution.py:13
  245.4 14.1 %reshape.153 = bf16[2304,2048]{1,0:T(8,128)(2,1)} reshape(bf16[128,18,2048]{2,1,0:T(8,128)(2,1)} %all-to-all-done.1) | data formatting | bytes 18874368 | tf_op jit(solution)/shard_map/reshape | solution.py:42
  259.4 21.3 %gather_fusion.1 = bf16[2048,2048]{1,0:T(8,128)(2,1)} fusion(bf16[2304,2048]{1,0:T(8,128)(2,1)} %reshape.153, s32[2048]{0:T(1024)S(1)} %broadcast_clamp_fusion), kind=kCustom, calls=%fused_computation.1 | custom fusion | bytes 16785408 | tf_op jit(solution)/shard_map/gather | solution.py:42
  280.7 6.4 %fusion.6 = f32[128,1,16]{2,1,0:T(1,128)S(1)} fusion(bf16[128,16,2048]{2,1,0:T(8,128)(2,1)} %bitcast.34, bf16[128,2048,1]{1,0,2:T(8,128)(2,1)S(1)} %bitcast.36), kind=kOutput, calls=%fused_computation.18 | convolution fusion | flops 8388608 | bytes 8921088 | tf_op jit(solution)/shard_map/gi,gni->gn/dot_general | solution.py:50
  287.3 6.4 %fusion.20 = (f32[128]{0:T(128)S(1)}, f32[128,2048]{1,0:T(8,128)S(1)}) fusion(bf16[128,2048]{1,0:T(8,128)(2,1)S(1)} %copy-done.1, bf16[2048,2048]{1,0:T(8,128)(2,1)} %all-gather.2.cloned.1.call-done), kind=kOutput, calls=%fused_computation.51 | convolution fusion | flops 1074265984 | bytes 9961984 | tf_op jit(solution)/shard_map/dot_general | solution.py:46
  293.8 0.4 select_reduce_fusion
  294.2 0.5 fusion.19
  294.8 5.7 %convolution_convert_fusion = bf16[2048,2048]{1,0:T(8,128)(2,1)} fusion(bf16[128,2048]{1,0:T(8,128)(2,1)S(1)} %copy-done.1, f32[128,2048]{1,0:T(8,128)S(1)} %get-tuple-element.10, f32[128]{0:T(128)S(1)} %get-tuple-element.6, s32[128]{0:T(128)S(1)} %copy-done.2), kind=kOutput, calls=%fused_computation.7 | convolution fusion | flops 1079508992 | bytes 9962496 | tf_op jit(solution)/shard_map/dot_general | solution.py:75
  300.8 4.3 fusion
  305.1 18.8 %scatter_custom_fusion.1 = bf16[2304,2048]{1,0:T(8,128)(2,1)} fusion(s32[2048]{0:T(1024)S(1)} %bitcast.46, bf16[2048,2048]{1,0:T(8,128)(2,1)} %fusion, bf16[]{:T(256)} %constant.39.clone.1), kind=kCustom, calls=%fused_computation.8 | custom fusion | bytes 9437696 | tf_op jit(solution)/shard_map/scatter | solution.py:89
  323.8 14.2 %reshape.156 = bf16[128,18,2048]{2,1,0:T(8,128)(2,1)} reshape(bf16[2304,2048]{1,0:T(8,128)(2,1)} %scatter_custom_fusion.1) | data formatting | bytes 18874368 | tf_op jit(solution)/shard_map/reshape | solution.py:91
  338.0 12.2 %all-to-all-start.2 = ((bf16[128,18,2048]{2,1,0:T(8,128)(2,1)}), bf16[128,18,2048]{2,1,0:T(8,128)(2,1)}, u32[]{:S(2)}, u32[]{:S(2)}) async-start(bf16[128,18,2048]{2,1,0:T(8,128)(2,1)} %reshape.156), calls=%async_computation.3 | async-start | bytes 25165824 | tf_op jit(solution)/shard_map/all_to_all | solution.py:17
  350.4 5.0 fusion.12
  355.7 1.3 slice-done.1
  357.0 2.8 fusion.3
  359.8 162.7 %all-to-all-done.2 = bf16[128,18,2048]{2,1,0:T(8,128)(2,1)} async-done(((bf16[128,18,2048]{2,1,0:T(8,128)(2,1)}), bf16[128,18,2048]{2,1,0:T(8,128)(2,1)}, u32[]{:S(2)}, u32[]{:S(2)}) %all-to-all-start.2) | async-done | bytes 9437216 | tf_op jit(solution)/shard_map/all_to_all | solution.py:17
  522.5 14.1 %reshape.157 = bf16[2304,2048]{1,0:T(8,128)(2,1)} reshape(bf16[128,18,2048]{2,1,0:T(8,128)(2,1)} %all-to-all-done.2) | data formatting | bytes 18874368 | tf_op jit(solution)/shard_map/reshape | solution.py:96
  536.6 5.7 %fusion.4 = bf16[64,2048]{1,0:T(8,128)(2,1)} fusion(bf16[2304,2048]{1,0:T(8,128)(2,1)} %reshape.157, s32[2304]{0:T(1024)S(1)} %reshape.155, bf16[64,2048]{1,0:T(8,128)(2,1)} %reduce-scatter.2.cloned.1.call-done), kind=kOutput, calls=%fused_computation.14 | convolution fusion | flops 604520448 | bytes 9970688 | tf_op jit(solution)/shard_map/dot_general | solution.py:95
  (40 shorter events, 2.7 us)
Async XLA Ops:
  7.2 35.3 %copy-start = (bf16[64,2048]{1,0:T(8,128)(2,1)S(1)}, bf16[64,2048]{1,0:T(8,128)(2,1)}, u32[]{:S(2)}) copy-start(bf16[64,2048]{1,0:T(8,128)(2,1)} %param.6) | copy-start | bytes 786436
  7.2 280.1 %all-gather.2.cloned.1.call-start = ((), (), s32[]{:S(2)}) async-start(), calls=%async_computation.4 | async-start | bytes 8650752 | tf_op jit(solution)/shard_map/all_gather | solution.py:26
  77.2 168.2 %all-to-all-start.1 = ((bf16[128,18,2048]{2,1,0:T(8,128)(2,1)}), bf16[128,18,2048]{2,1,0:T(8,128)(2,1)}, u32[]{:S(2)}, u32[]{:S(2)}) async-start(bf16[128,18,2048]{2,1,0:T(8,128)(2,1)} %broadcast_select_fusion), calls=%async_computation.1 | async-start | bytes 25165824 | tf_op jit(solution)/shard_map/all_to_all | solution.py:13
  83.2 453.5 %reduce-scatter.2.cloned.1.call-start = ((), (), s32[]{:S(2)}) async-start(), calls=%async_computation.5 | async-start | bytes 8650752 | tf_op jit(solution)/shard_map/reduce_scatter | solution.py:74
  259.4 21.3 %copy-start.1 = (bf16[128,2048]{1,0:T(8,128)(2,1)S(1)}, bf16[128,2048]{1,0:T(8,128)(2,1)}, u32[]{:S(2)}) copy-start(bf16[128,2048]{1,0:T(8,128)(2,1)} %param.5) | copy-start | bytes 1572868
  280.7 13.1 %copy-start.2 = (s32[128]{0:T(128)S(1)}, s32[128]{0:T(128)}, u32[]{:S(2)}) copy-start(s32[128]{0:T(128)} %param.7) | copy-start | bytes 1540
  338.0 184.5 %all-to-all-start.2 = ((bf16[128,18,2048]{2,1,0:T(8,128)(2,1)}), bf16[128,18,2048]{2,1,0:T(8,128)(2,1)}, u32[]{:S(2)}, u32[]{:S(2)}) async-start(bf16[128,18,2048]{2,1,0:T(8,128)(2,1)} %reshape.156), calls=%async_computation.3 | async-start | bytes 25165824 | tf_op jit(solution)/shard_map/all_to_all | solution.py:17
  350.3 5.4 slice-start
  350.4 6.6 %slice-start.1 = ((s8[8388608]{0:T(1024)(128)(4,1)}), s8[4194304]{0:T(1024)(128)(4,1)S(1)}, s32[]{:S(2)}) async-start(s8[8388608]{0:T(1024)(128)(4,1)} %bitcast.32), calls=%async_computation.7 | async-start | bytes 8388608
Sparse Core Ops, SparseCore 0:
  10.3 55.8 all-gather.1
  300.6 234.8 reduce-scatter.1
where the time goes:
time: 555 us; the launch traced here: 549 us
  waiting for transfers between devices  325 us (59%)
  local copies, waits for them, and re-layouts  120 us (22%)
  matrix products  32 us (6%)
  blocking collectives  20.5 us (4%)
  other arithmetic  19.1 us (3%)
  starting transfers between devices  18.4 us (3%)
  between operations  14.2 us (3%)
    all_to_all x1, waiting for transfers between devices, move_grads(): lax.all_to_all(outgoing, ('group', 'dp'), split_axis=0, concat_axis=0, ti...  163 us
    all_to_all x1, waiting for transfers between devices, move_rows(): lax.all_to_all(fetched, ('group', 'dp'), split_axis=0, concat_axis=0, til...  162 us
    gather x2, local copies, waits for them, and re-layouts, local(): jnp.take(passages, incoming.reshape(-1), axis=0)  24.1 us
    gather x1, local copies, waits for them, and re-layouts, local(): returned.reshape(devices * capacity, width)[places]  21.3 us
    all_to_all x1, blocking collectives, local(): lax.all_to_all(requests, ('group', 'dp'), split_axis=0, concat_axis=0, ti...  20.5 us
    scatter x1, local copies, waits for them, and re-layouts, local(): outgoing = jnp.zeros((devices * capacity, width), jnp.bfloat16).at[places...  18.8 us
    reshape x1, local copies, waits for them, and re-layouts, local(): arrived = move_grads(outgoing.reshape(devices, capacity, width))  14.2 us
    reshape x1, local copies, waits for them, and re-layouts, local(): arrived.reshape(devices * capacity, width)  14.1 us
  transfers between devices with their start and end apart: 4, of which 2 were waited for; matrix products, arithmetic and copies ran while one was open for 27% of the time, Pallas kernels for 0%

commit v1 on v0

v1 whole, which is shorter than its diff:
```python
import jax
import jax.numpy as jnp
from jax import lax
from jax.sharding import PartitionSpec as P

HARD = 16
AXES = ("group", "dp")
SHARP = 1.0 / 0.02
FLOOR = -1e30
BF = jnp.bfloat16
F32 = jnp.float32


def index(y, x, z, c):
    return (((y % 4) * 4 + x % 4) * 4 + z % 4) * 2 + c % 2


def pairs(step):
    found = []
    for y in range(4):
        for x in range(4):
            for z in range(4):
                for c in range(2):
                    found.append((index(y, x, z, c), index(*step(y, x, z, c))))
    return found


def first(d):
    return pairs(lambda y, x, z, c: (y, x, z + d, c) if c else (y, x + d, z, c))


def second(d):
    return pairs(lambda y, x, z, c: (y, x + d, z, c) if c else (y, x, z + d, c))


def along(d):
    return pairs(lambda y, x, z, c: (y - d, x, z, c) if c else (y + d, x, z, c))


CORE = pairs(lambda y, x, z, c: (y, x, z, 1 - c))


def send(v, perm):
    return lax.ppermute(v, AXES, perm)


def join(*v):
    return jnp.concatenate(v, axis=0)


def spread(block, axis):
    h = block.shape[0] // 2
    up = send(block, axis(1))
    down = send(block, axis(-1))
    return block, up, send(up[:h], axis(1)), send(down[h:], axis(-1)), down


def fold(chunks, axis):
    h = chunks[0].shape[0] // 2
    low = [c.astype(BF) for c in chunks]
    up = send(low[2][:h], axis(-1))
    down = send(low[2][h:], axis(1))
    one = join((chunks[1][:h] + up.astype(F32)).astype(BF), low[1][h:])
    three = join(low[3][:h], (chunks[3][h:] + down.astype(F32)).astype(BF))
    return chunks[0] + send(one, axis(-1)).astype(F32) + send(three, axis(1)).astype(F32)


def merge(a, b):
    top = jnp.maximum(a[0], b[0])
    total = a[1] * jnp.exp(a[0] - top) + b[1] * jnp.exp(b[0] - top)
    return top, total, a[2] + b[2]


def local(question_vectors, passages, positive, hard_owner, hard_row):
    width = question_vectors.shape[1]
    group = lax.axis_index("group")
    dp = lax.axis_index("dp")
    core = dp % 2
    z = dp // 2 % 4
    x = dp // 8

    owner_rows = hard_owner.T.astype(BF)
    row_rows = hard_row.T.astype(BF)
    pos_rows = jnp.pad(jnp.stack([positive // 64, positive % 64]), ((0, 14), (0, 0))).astype(BF)
    meta = jnp.concatenate([owner_rows, row_rows, pos_rows], axis=1)
    meta = jnp.pad(meta, ((0, 0), (0, width - meta.shape[1])))
    mine = [join(question_vectors, meta)]
    for _ in range(3):
        mine.append(send(mine[-1], along(1)))
    theirs = [send(v, CORE) for v in mine]
    tiles = mine + theirs
    q = join(*[t[:128] for t in tiles])
    owners = jnp.concatenate([t[128:144, :128] for t in tiles], axis=1).astype(F32)
    rows = jnp.concatenate([t[128:144, 128:256] for t in tiles], axis=1).astype(F32)
    pos = jnp.concatenate([tiles[0][128:130, 256:384], tiles[4][128:130, 256:384]], axis=1).astype(F32)

    keep = lax.dynamic_slice_in_dim(passages, core * 32, 32, 0)
    give = lax.dynamic_slice_in_dim(passages, (1 - core) * 32, 32, 0)
    block = join(keep, send(give, CORE))
    plane = join(*spread(block, first))
    p = join(*spread(plane, second))

    far = jnp.arange(32, dtype=jnp.int32)
    k2, k1, b = far // 8, far // 2 % 4, far % 2
    kx = jnp.where(core == 0, k1, k2)
    kz = jnp.where(core == 0, k2, k1)
    local_id = ((x - kx + 4) % 4 * 4 + (z - kz + 4) % 4) * 2 + (core + b) % 2
    whole_id = group * 32 + local_id
    base = (core * 32 - 1).astype(F32)
    hit = owners[None] == whole_id.astype(F32)[:, None, None]
    hard_place = jnp.sum(jnp.where(hit, rows[None] - base, 0.0), axis=1)
    pos_place = jnp.where(pos[0][None] == local_id.astype(F32)[:, None], pos[1][None] - base, 0.0)
    step = jnp.arange(1, 33, dtype=jnp.int32).astype(F32)
    hard_hit = (hard_place[:, None, :] == step[None, :, None]).reshape(1024, 1024).astype(F32)
    pos_hit = (pos_place[:, None, :] == step[None, :, None]).reshape(1024, 256).astype(F32)

    scores = lax.dot_general(p, q, (((1,), (1,)), ((), ())), preferred_element_type=F32) * SHARP
    column = jnp.arange(1024, dtype=jnp.int32)
    inside = (column % 512 < 128).astype(F32)[None]
    weight = hard_hit + inside
    onehot = jnp.concatenate(
        [jnp.pad(pos_hit[:, :128], ((0, 0), (0, 384))), jnp.pad(pos_hit[:, 128:], ((0, 0), (0, 384)))], axis=1
    )
    masked = jnp.where(weight > 0, scores, FLOOR)
    top = jnp.max(masked, axis=0)
    total = jnp.sum(weight * jnp.exp(masked - top[None]), axis=0)
    chosen = jnp.sum(onehot * scores, axis=0)

    def unpack(v):
        return v[0], v[1], v[2]

    stats = jnp.pad(jnp.stack([top, total, chosen]), ((0, 5), (0, 0)))
    other = jnp.roll(send(stats, CORE), 512, axis=1)
    stats = jnp.pad(jnp.stack(merge(unpack(stats), unpack(other))), ((0, 5), (0, 0)))
    acc = unpack(stats)
    for t in range(1, 4):
        got = send(stats, along(t))
        got = jnp.concatenate(
            [jnp.roll(got[:, :512], 128 * t, axis=1), jnp.roll(got[:, 512:], -128 * t, axis=1)], axis=1
        )
        acc = merge(acc, unpack(got))
    lse = acc[0] + jnp.log(acc[1])
    loss = lse[:128] - acc[2][:128]

    coef = ((weight * jnp.exp(masked - lse[None]) - onehot) * SHARP).astype(BF)
    pg = jnp.dot(coef, q, preferred_element_type=F32)
    parts = fold([pg[256 * k : 256 * k + 256] for k in range(4)], second)
    parts = fold([parts[64 * k : 64 * k + 64] for k in range(4)], first)
    swapped = send(parts[32:].astype(BF), CORE)
    kept = parts[:32].astype(BF)
    passage_grad = jnp.where(core == 0, join(kept, swapped), join(swapped, kept))

    qg = lax.dot_general(coef, p, (((0,), (0,)), ((), ())), preferred_element_type=F32)
    qm = qg[:512] + send(qg[512:].astype(BF), CORE).astype(F32)
    run = qm[384:]
    for k in (2, 1, 0):
        run = qm[128 * k : 128 * k + 128] + send(run.astype(BF), along(-1)).astype(F32)
    return loss, run.astype(BF), passage_grad


def solution(mesh):
    return jax.shard_map(
        local,
        mesh=mesh,
        in_specs=(P(AXES, None), P(AXES, None), P(AXES), P(AXES, None), P(AXES, None)),
        out_specs=(P(AXES), P(AXES, None), P(AXES, None)),
        check_vma=False,
    )
```

time: 555 us -> 148 us (0.27)
  waiting for transfers between devices: 325 us -> 67 us
  local copies, waits for them, and re-layouts: 120 us -> 11.3 us
  starting transfers between devices: 18.4 us -> 41.3 us
  blocking collectives: 20.5 us -> 0 us
  matrix products: 32 us -> 14.1 us
  between operations: 14.2 us -> 1.17 us
  other arithmetic: 19.1 us -> 12.1 us
    all_to_all x2 -> x0, waiting for transfers between devices: 325 us -> none  [the longest x1 163 us: move_grads(): lax.all_to_all(outgoing, ('group', 'dp'), split_axis=0, concat_axis=0, ti...]
    ppermute x0 -> x33, waiting for transfers between devices: none -> 67 us  [send(): return lax.ppermute(v, AXES, perm)]
    gather x3 -> x0, local copies, waits for them, and re-layouts: 45.3 us -> none  [the longest x2 24.1 us: local(): jnp.take(passages, incoming.reshape(-1), axis=0)]
    reshape x6 -> x0, local copies, waits for them, and re-layouts: 42.7 us -> none  [the longest x1 14.2 us: local(): arrived = move_grads(outgoing.reshape(devices, capacity, width))]
    ppermute x0 -> x33, starting transfers between devices: none -> 41.3 us  [send(): return lax.ppermute(v, AXES, perm)]
    scatter x2 -> x0, local copies, waits for them, and re-layouts: 26.8 us -> none  [the longest x1 18.8 us: local(): outgoing = jnp.zeros((devices * capacity, width), jnp.bfloat16).at[places...]
    all_to_all x1 -> x0, blocking collectives: 20.5 us -> none  [local(): lax.all_to_all(requests, ('group', 'dp'), split_axis=0, concat_axis=0, ti...]
    all_to_all x2 -> x0, starting transfers between devices: 18.1 us -> none  [the longest x1 12.2 us: move_grads(): lax.all_to_all(outgoing, ('group', 'dp'), split_axis=0, concat_axis=0, ti...]
  transfers between devices with their start and end apart: 4 -> 33, of which waited for: 2 -> 19; matrix products, arithmetic and copies ran while one was open for 27% -> 13% of each run, Pallas kernels for 0% -> 0%
where the time goes in v1:
time: 148 us; the launch traced here: 147 us
  waiting for transfers between devices  67 us (45%)
  starting transfers between devices  41.3 us (28%)
  matrix products  14.1 us (10%)
  other arithmetic  12.1 us (8%)
  local copies, waits for them, and re-layouts  11.3 us (8%)
    ppermute x33, waiting for transfers between devices, send(): return lax.ppermute(v, AXES, perm)  67 us
    ppermute x33, starting transfers between devices, send(): return lax.ppermute(v, AXES, perm)  41.3 us
    unnamed x26, local copies, waits for them, and re-layouts  9.38 us
    dot_general x1, matrix products, local(): lax.dot_general(p, q, (((1,), (1,)), ((), ())), preferred_element_type=F32)  4.88 us
    dot_general x1, matrix products, local(): lax.dot_general(coef, p, (((0,), (0,)), ((), ())), preferred_element_type...  4.71 us
    dot_general x1, matrix products, local(): pg = jnp.dot(coef, q, preferred_element_type=F32)  4.54 us
  transfers between devices with their start and end apart: 33, of which 19 were waited for; matrix products, arithmetic and copies ran while one was open for 13% of the time, Pallas kernels for 0%

profile of v1, /device:TPU:0, one launch (start us, length us, event | category | flops | bytes accessed | tf_op | source)
XLA Modules:
  0.0 146.9 jit_solution(15466180828785370842)
XLA Ops:
  3.2 1.7 %collective-permute-start = (bf16[144,2048]{1,0:T(8,128)(2,1)S(1)}, bf16[144,2048]{1,0:T(8,128)(2,1)S(1)}, u32[]{:S(2)}, u32[]{:S(2)}) collective-permute-start(bf16[144,2048]{1,0:T(8,128)(2,1)S(1)} %pad_maximum_fusion.2), channel_id=1, source_target_pairs={{0,32},{1,97},{2,34},{3,99},{4,36},{5,101},{6,38},{7,103},{8,40},{... | collective-permute-start | bytes 1769480 | tf_op jit(solution)/shard_map/ppermute | solution.py:44
  4.9 1.7 %constant_dynamic-update-slice_fusion.21 = (bf16[256,2048]{1,0:T(8,128)(2,1)}, bf16[32,2048]{1,0:T(8,128)(2,1)S(1)}, bf16[32,2048]{1,0:T(8,128)(2,1)S(1)}) fusion(bf16[64,2048]{1,0:T(8,128)(2,1)} %param.6, s32[]{:T(128)S(6)} %select_n.207, s32[]{:T(128)S(6)} %select_n.208), kind=kLoop, calls=%fused_computation.74 | loop fusion | bytes 655368
  6.6 1.6 %collective-permute-start.7 = (bf16[32,2048]{1,0:T(8,128)(2,1)S(1)}, bf16[32,2048]{1,0:T(8,128)(2,1)S(1)}, u32[]{:S(2)}, u32[]{:S(2)}) collective-permute-start(bf16[32,2048]{1,0:T(8,128)(2,1)S(1)} %get-tuple-element.58), channel_id=1, source_target_pairs={{0,1},{1,0},{2,3},{3,2},{4,5},{5,4},{6,7},{7,6},{8,9},{9,8},{10,11... | collective-permute-start | bytes 393224 | tf_op jit(solution)/shard_map/ppermute | solution.py:44
  8.2 1.9 %constant_dynamic-update-slice_fusion.32 = bf16[1024,2048]{1,0:T(8,128)(2,1)} fusion(bf16[128,2048]{1,0:T(8,128)(2,1)} %param.5), kind=kLoop, calls=%fused_computation.85 | loop fusion | bytes 1048576
  10.8 2.8 %collective-permute-start.10 = (bf16[64,2048]{1,0:T(8,128)(2,1)S(1)}, bf16[64,2048]{1,0:T(8,128)(2,1)S(1)}, u32[]{:S(2)}, u32[]{:S(2)}) collective-permute-start(bf16[64,2048]{1,0:T(8,128)(2,1)S(1)} %pad_maximum_fusion.3), channel_id=1, source_target_pairs={{0,24},{1,7},{2,26},{3,1},{4,28},{5,3},{6,30},{7,5},{8,0},{9,15},{... | collective-permute-start | bytes 786440 | tf_op jit(solution)/shard_map/ppermute | solution.py:44
  14.5 3.1 %collective-permute-done.10 = bf16[64,2048]{1,0:T(8,128)(2,1)S(1)} collective-permute-done((bf16[64,2048]{1,0:T(8,128)(2,1)S(1)}, bf16[64,2048]{1,0:T(8,128)(2,1)S(1)}, u32[]{:S(2)}, u32[]{:S(2)}) %collective-permute-start.10) | collective-permute-done | bytes 262176 | tf_op jit(solution)/shard_map/ppermute | solution.py:44
  17.6 3.8 %collective-permute-start.11 = (bf16[32,2048]{1,0:T(8,128)(2,1)S(1)}, bf16[32,2048]{1,0:T(8,128)(2,1)S(1)}, u32[]{:S(2)}, u32[]{:S(2)}) collective-permute-start(bf16[32,2048]{1,0:T(8,128)(2,1)S(1)} %slice.418), channel_id=1, source_target_pairs={{0,24},{1,7},{2,26},{3,1},{4,28},{5,3},{6,30},{7,5},{8,0},{9,15},{... | collective-permute-start | bytes 393224 | tf_op jit(solution)/shard_map/ppermute | solution.py:44
  22.3 5.3 %collective-permute-done.9 = bf16[32,2048]{1,0:T(8,128)(2,1)S(1)} collective-permute-done((bf16[32,2048]{1,0:T(8,128)(2,1)S(1)}, bf16[32,2048]{1,0:T(8,128)(2,1)S(1)}, u32[]{:S(2)}, u32[]{:S(2)}) %collective-permute-start.9) | collective-permute-done | bytes 131104 | tf_op jit(solution)/shard_map/ppermute | solution.py:44
  29.9 4.0 %collective-permute-start.14 = (bf16[256,2048]{1,0:T(8,128)(2,1)}, bf16[256,2048]{1,0:T(8,128)(2,1)S(1)}, u32[]{:S(2)}, u32[]{:S(2)}) collective-permute-start(bf16[256,2048]{1,0:T(8,128)(2,1)} %get-tuple-element.54), channel_id=1, source_target_pairs={{0,6},{1,25},{2,0},{3,27},{4,2},{5,29},{6,4},{7,31},{8,14},{9,1},{... | collective-permute-start | bytes 3145736 | tf_op jit(solution)/shard_map/ppermute | solution.py:44
  35.4 9.9 %collective-permute-done.1 = bf16[144,2048]{1,0:T(8,128)(2,1)S(1)} collective-permute-done((bf16[144,2048]{1,0:T(8,128)(2,1)S(1)}, bf16[144,2048]{1,0:T(8,128)(2,1)S(1)}, u32[]{:S(2)}, u32[]{:S(2)}) %collective-permute-start.1) | collective-permute-done | bytes 589856 | tf_op jit(solution)/shard_map/ppermute | solution.py:44
  46.6 3.7 %collective-permute-start.15 = (bf16[128,2048]{1,0:T(8,128)(2,1)S(1)}, bf16[128,2048]{1,0:T(8,128)(2,1)S(1)}, u32[]{:S(2)}, u32[]{:S(2)}) collective-permute-start(bf16[128,2048]{1,0:T(8,128)(2,1)S(1)} %slice.420), channel_id=1, source_target_pairs={{0,6},{1,25},{2,0},{3,27},{4,2},{5,29},{6,4},{7,31},{8,14},{9,1},{... | collective-permute-start | bytes 1572872 | tf_op jit(solution)/shard_map/ppermute | solution.py:44
  50.5 5.9 %collective-permute-done.2 = bf16[144,2048]{1,0:T(8,128)(2,1)S(1)} collective-permute-done((bf16[144,2048]{1,0:T(8,128)(2,1)S(1)}, bf16[144,2048]{1,0:T(8,128)(2,1)S(1)}, u32[]{:S(2)}, u32[]{:S(2)}) %collective-permute-start.2) | collective-permute-done | bytes 589856 | tf_op jit(solution)/shard_map/ppermute | solution.py:44
  56.7 4.2 %collective-permute-done.13 = bf16[128,2048]{1,0:T(8,128)(2,1)S(1)} collective-permute-done((bf16[128,2048]{1,0:T(8,128)(2,1)S(1)}, bf16[128,2048]{1,0:T(8,128)(2,1)S(1)}, u32[]{:S(2)}, u32[]{:S(2)}) %collective-permute-start.13) | collective-permute-done | bytes 524320 | tf_op jit(solution)/shard_map/ppermute | solution.py:44
  61.6 4.9 %fusion.57 = (f32[1024]{0:T(1024)S(1)}, f32[1024,1024]{1,0:T(8,128)S(1)}) fusion(f32[1024]{0:T(1024)S(1)} %fusion.39, f32[1024]{0:T(1024)S(1)} %eq.97, f32[32,1024]{1,0:T(8,128)S(1)} %select_reduce_fusion, bf16[1024,2048]{1,0:T(8,128)(2,1)S(1)} %constant_dynamic-update-slice_fusion.22, bf16[1024,2048]{1,0:T(8,128)(2,1)S(1)} %slice_dynamic-update-slice_fusion), kind=kOutput, calls=%fused_computation.201 | convolution fusion | flops 4302306304 | bytes 12726272 | tf_op jit(solution)/shard_map/dot_general | solution.py:117
  66.5 2.3 %multiply_reduce_fusion.1 = (f32[1024]{0:T(1024)S(1)}, f32[1024]{0:T(1024)S(1)}) fusion(f32[1024]{0:T(1024)S(1)} %get-tuple-element.84, f32[1024]{0:T(1024)S(1)} %fusion.39, f32[1024]{0:T(1024)S(1)} %eq.97, f32[32,1024]{1,0:T(8,128)S(1)} %select_reduce_fusion, f32[1024,1024]{1,0:T(8,128)S(1)} %get-tuple-element.85, f32[1024,128]{1,0:T(8,128)S(1)} %get-tuple-element.37, ...), kind=kLoop, calls=%fused_computation.8 | loop fusion | flops 16775168 | bytes 5394432 | tf_op jit(solution)/shard_map/reduce_sum | solution.py:126
  70.2 3.9 %collective-permute-start.18 = (f32[8,1024]{1,0:T(8,128)S(1)}, f32[8,1024]{1,0:T(8,128)S(1)}, u32[]{:S(2)}, u32[]{:S(2)}) collective-permute-start(f32[8,1024]{1,0:T(8,128)S(1)} %select_maximum_fusion.1), channel_id=1, source_target_pairs={{0,64},{1,65},{2,66},{3,67},{4,68},{5,69},{6,70},{7,71},{8,72},{9,... | collective-permute-start | bytes 98312 | tf_op jit(solution)/shard_map/ppermute | solution.py:44
  75.3 2.6 %collective-permute-done.19 = f32[8,1024]{1,0:T(8,128)S(1)} collective-permute-done((f32[8,1024]{1,0:T(8,128)S(1)}, f32[8,1024]{1,0:T(8,128)S(1)}, u32[]{:S(2)}, u32[]{:S(2)}) %collective-permute-start.19) | collective-permute-done | bytes 32800 | tf_op jit(solution)/shard_map/ppermute | solution.py:44
  78.1 2.1 %multiply_convert_fusion = bf16[1024,1024]{1,0:T(8,128)(2,1)S(1)} fusion(f32[1024,128]{1,0:T(8,128)S(1)} %get-tuple-element.37, f32[1024,128]{1,0:T(8,128)S(1)} %get-tuple-element.36, f32[1024]{0:T(1024)S(1)} %bitcast.60, f32[1024]{0:T(1024)S(1)} %fusion.39, f32[1024]{0:T(1024)S(1)} %eq.97, f32[32,1024]{1,0:T(8,128)S(1)} %select_reduce_fusion, ...), kind=kLoop, calls=%fused_computation.6 | loop fusion | flops 16777216 | bytes 7483392 | tf_op jit(solution)/shard_map/convert_element_type | solution.py:145
  80.1 4.5 %fusion.74 = (bf16[1024,2048]{1,0:T(8,128)(2,1)S(1)}, f32[1024,2048]{1,0:T(8,128)S(1)}) fusion(bf16[1024,1024]{1,0:T(8,128)(2,1)S(1)} %multiply_convert_fusion, bf16[1024,2048]{1,0:T(8,128)(2,1)S(1)} %slice_dynamic-update-slice_fusion), kind=kOutput, calls=%fused_computation.215 | convolution fusion | flops 4297064448 | bytes 18874368 | tf_op jit(solution)/shard_map/dot_general | solution.py:146
  85.2 2.0 %collective-permute-start.26 = (bf16[128,2048]{1,0:T(8,128)(2,1)S(1)}, bf16[128,2048]{1,0:T(8,128)(2,1)S(1)}, u32[]{:S(2)}, u32[]{:S(2)}) collective-permute-start(bf16[128,2048]{1,0:T(8,128)(2,1)S(1)} %get-tuple-element.27), channel_id=1, source_target_pairs={{0,2},{1,9},{2,4},{3,11},{4,6},{5,13},{6,0},{7,15},{8,10},{9,17},{... | collective-permute-start | bytes 1572872 | tf_op jit(solution)/shard_map/ppermute | solution.py:44
  87.2 7.2 %collective-permute-done.24 = bf16[128,2048]{1,0:T(8,128)(2,1)S(1)} collective-permute-done((bf16[128,2048]{1,0:T(8,128)(2,1)S(1)}, bf16[128,2048]{1,0:T(8,128)(2,1)S(1)}, u32[]{:S(2)}, u32[]{:S(2)}) %collective-permute-start.24) | collective-permute-done | bytes 524320 | tf_op jit(solution)/shard_map/ppermute | solution.py:44
  97.0 2.6 %collective-permute-start.25 = (bf16[256,2048]{1,0:T(8,128)(2,1)S(1)}, bf16[256,2048]{1,0:T(8,128)(2,1)S(1)}, u32[]{:S(2)}, u32[]{:S(2)}) collective-permute-start(bf16[256,2048]{1,0:T(8,128)(2,1)S(1)} %pad_maximum_fusion), channel_id=1, source_target_pairs={{0,6},{1,25},{2,0},{3,27},{4,2},{5,29},{6,4},{7,31},{8,14},{9,1},{... | collective-permute-start | bytes 3145736 | tf_op jit(solution)/shard_map/ppermute | solution.py:44
  99.6 4.7 %fusion.75 = f32[1024,2048]{1,0:T(8,128)S(1)} fusion(bf16[1024,1024]{1,0:T(8,128)(2,1)S(1)} %multiply_convert_fusion, bf16[1024,2048]{1,0:T(8,128)(2,1)S(1)} %constant_dynamic-update-slice_fusion.22), kind=kOutput, calls=%fused_computation.216 | convolution fusion | flops 4294967296 | bytes 14680064 | tf_op jit(solution)/shard_map/dot_general | solution.py:153
  104.7 7.5 %collective-permute-done.27 = bf16[256,2048]{1,0:T(8,128)(2,1)S(1)} collective-permute-done((bf16[256,2048]{1,0:T(8,128)(2,1)S(1)}, bf16[256,2048]{1,0:T(8,128)(2,1)S(1)}, u32[]{:S(2)}, u32[]{:S(2)}) %collective-permute-start.27) | collective-permute-done | bytes 1048608 | tf_op jit(solution)/shard_map/ppermute | solution.py:44
  114.0 2.0 %collective-permute-start.30 = (bf16[32,2048]{1,0:T(8,128)(2,1)S(1)}, bf16[32,2048]{1,0:T(8,128)(2,1)S(1)}, u32[]{:S(2)}, u32[]{:S(2)}) collective-permute-start(bf16[32,2048]{1,0:T(8,128)(2,1)S(1)} %get-tuple-element.33), channel_id=1, source_target_pairs={{0,8},{1,3},{2,10},{3,5},{4,12},{5,7},{6,14},{7,1},{8,16},{9,11},{... | collective-permute-start | bytes 393224 | tf_op jit(solution)/shard_map/ppermute | solution.py:44
  116.7 1.5 collective-permute-start.21
  121.2 2.6 %collective-permute-start.29 = (bf16[64,2048]{1,0:T(8,128)(2,1)S(1)}, bf16[64,2048]{1,0:T(8,128)(2,1)S(1)}, u32[]{:S(2)}, u32[]{:S(2)}) collective-permute-start(bf16[64,2048]{1,0:T(8,128)(2,1)S(1)} %pad_maximum_fusion.4), channel_id=1, source_target_pairs={{0,24},{1,7},{2,26},{3,1},{4,28},{5,3},{6,30},{7,5},{8,0},{9,15},{... | collective-permute-start | bytes 786440 | tf_op jit(solution)/shard_map/ppermute | solution.py:44
  123.7 2.2 %collective-permute-done.21 = bf16[128,2048]{1,0:T(8,128)(2,1)S(1)} collective-permute-done((bf16[128,2048]{1,0:T(8,128)(2,1)S(1)}, bf16[128,2048]{1,0:T(8,128)(2,1)S(1)}, u32[]{:S(2)}, u32[]{:S(2)}) %collective-permute-start.21) | collective-permute-done | bytes 524320 | tf_op jit(solution)/shard_map/ppermute | solution.py:44
  126.1 2.7 %collective-permute-start.22 = (bf16[128,2048]{1,0:T(8,128)(2,1)S(1)}, bf16[128,2048]{1,0:T(8,128)(2,1)S(1)}, u32[]{:S(2)}, u32[]{:S(2)}) collective-permute-start(bf16[128,2048]{1,0:T(8,128)(2,1)S(1)} %fusion.5), channel_id=1, source_target_pairs={{0,96},{1,33},{2,98},{3,35},{4,100},{5,37},{6,102},{7,39},{8,104},... | collective-permute-start | bytes 1572872 | tf_op jit(solution)/shard_map/ppermute | solution.py:44
  128.9 6.6 %collective-permute-done.22 = bf16[128,2048]{1,0:T(8,128)(2,1)S(1)} collective-permute-done((bf16[128,2048]{1,0:T(8,128)(2,1)S(1)}, bf16[128,2048]{1,0:T(8,128)(2,1)S(1)}, u32[]{:S(2)}, u32[]{:S(2)}) %collective-permute-start.22) | collective-permute-done | bytes 524320 | tf_op jit(solution)/shard_map/ppermute | solution.py:44
  135.6 3.8 %collective-permute-start.23 = (bf16[128,2048]{1,0:T(8,128)(2,1)S(1)}, bf16[128,2048]{1,0:T(8,128)(2,1)S(1)}, u32[]{:S(2)}, u32[]{:S(2)}) collective-permute-start(bf16[128,2048]{1,0:T(8,128)(2,1)S(1)} %fusion.6), channel_id=1, source_target_pairs={{0,96},{1,33},{2,98},{3,35},{4,100},{5,37},{6,102},{7,39},{8,104},... | collective-permute-start | bytes 1572872 | tf_op jit(solution)/shard_map/ppermute | solution.py:44
  141.5 4.5 %collective-permute-done.23 = bf16[128,2048]{1,0:T(8,128)(2,1)S(1)} collective-permute-done((bf16[128,2048]{1,0:T(8,128)(2,1)S(1)}, bf16[128,2048]{1,0:T(8,128)(2,1)S(1)}, u32[]{:S(2)}, u32[]{:S(2)}) %collective-permute-start.23) | collective-permute-done | bytes 524320 | tf_op jit(solution)/shard_map/ppermute | solution.py:44
  (124 shorter events, 26.5 us)
Async XLA Ops:
  3.1 30.8 %collective-permute-start.3 = (bf16[144,2048]{1,0:T(8,128)(2,1)S(1)}, bf16[144,2048]{1,0:T(8,128)(2,1)S(1)}, u32[]{:S(2)}, u32[]{:S(2)}) collective-permute-start(bf16[144,2048]{1,0:T(8,128)(2,1)S(1)} %pad_maximum_fusion.2), channel_id=1, source_target_pairs={{0,1},{1,0},{2,3},{3,2},{4,5},{5,4},{6,7},{7,6},{8,9},{9,8},{10,11... | collective-permute-start | bytes 1769480 | tf_op jit(solution)/shard_map/ppermute | solution.py:44
  3.2 30.9 %collective-permute-start = (bf16[144,2048]{1,0:T(8,128)(2,1)S(1)}, bf16[144,2048]{1,0:T(8,128)(2,1)S(1)}, u32[]{:S(2)}, u32[]{:S(2)}) collective-permute-start(bf16[144,2048]{1,0:T(8,128)(2,1)S(1)} %pad_maximum_fusion.2), channel_id=1, source_target_pairs={{0,32},{1,97},{2,34},{3,99},{4,36},{5,101},{6,38},{7,103},{8,40},{... | collective-permute-start | bytes 1769480 | tf_op jit(solution)/shard_map/ppermute | solution.py:44
  6.6 4.2 %collective-permute-start.7 = (bf16[32,2048]{1,0:T(8,128)(2,1)S(1)}, bf16[32,2048]{1,0:T(8,128)(2,1)S(1)}, u32[]{:S(2)}, u32[]{:S(2)}) collective-permute-start(bf16[32,2048]{1,0:T(8,128)(2,1)S(1)} %get-tuple-element.58), channel_id=1, source_target_pairs={{0,1},{1,0},{2,3},{3,2},{4,5},{5,4},{6,7},{7,6},{8,9},{9,8},{10,11... | collective-permute-start | bytes 393224 | tf_op jit(solution)/shard_map/ppermute | solution.py:44
  10.8 6.7 %collective-permute-start.10 = (bf16[64,2048]{1,0:T(8,128)(2,1)S(1)}, bf16[64,2048]{1,0:T(8,128)(2,1)S(1)}, u32[]{:S(2)}, u32[]{:S(2)}) collective-permute-start(bf16[64,2048]{1,0:T(8,128)(2,1)S(1)} %pad_maximum_fusion.3), channel_id=1, source_target_pairs={{0,24},{1,7},{2,26},{3,1},{4,28},{5,3},{6,30},{7,5},{8,0},{9,15},{... | collective-permute-start | bytes 786440 | tf_op jit(solution)/shard_map/ppermute | solution.py:44
  13.7 7.7 %collective-permute-start.8 = (bf16[64,2048]{1,0:T(8,128)(2,1)S(1)}, bf16[64,2048]{1,0:T(8,128)(2,1)S(1)}, u32[]{:S(2)}, u32[]{:S(2)}) collective-permute-start(bf16[64,2048]{1,0:T(8,128)(2,1)S(1)} %pad_maximum_fusion.3), channel_id=1, source_target_pairs={{0,8},{1,3},{2,10},{3,5},{4,12},{5,7},{6,14},{7,1},{8,16},{9,11},{... | collective-permute-start | bytes 786440 | tf_op jit(solution)/shard_map/ppermute | solution.py:44
  17.6 10.8 %collective-permute-start.11 = (bf16[32,2048]{1,0:T(8,128)(2,1)S(1)}, bf16[32,2048]{1,0:T(8,128)(2,1)S(1)}, u32[]{:S(2)}, u32[]{:S(2)}) collective-permute-start(bf16[32,2048]{1,0:T(8,128)(2,1)S(1)} %slice.418), channel_id=1, source_target_pairs={{0,24},{1,7},{2,26},{3,1},{4,28},{5,3},{6,30},{7,5},{8,0},{9,15},{... | collective-permute-start | bytes 393224 | tf_op jit(solution)/shard_map/ppermute | solution.py:44
  21.3 6.2 %collective-permute-start.9 = (bf16[32,2048]{1,0:T(8,128)(2,1)S(1)}, bf16[32,2048]{1,0:T(8,128)(2,1)S(1)}, u32[]{:S(2)}, u32[]{:S(2)}) collective-permute-start(bf16[32,2048]{1,0:T(8,128)(2,1)S(1)} %slice.417), channel_id=1, source_target_pairs={{0,8},{1,3},{2,10},{3,5},{4,12},{5,7},{6,14},{7,1},{8,16},{9,11},{... | collective-permute-start | bytes 393224 | tf_op jit(solution)/shard_map/ppermute | solution.py:44
  29.9 16.7 %collective-permute-start.14 = (bf16[256,2048]{1,0:T(8,128)(2,1)}, bf16[256,2048]{1,0:T(8,128)(2,1)S(1)}, u32[]{:S(2)}, u32[]{:S(2)}) collective-permute-start(bf16[256,2048]{1,0:T(8,128)(2,1)} %get-tuple-element.54), channel_id=1, source_target_pairs={{0,6},{1,25},{2,0},{3,27},{4,2},{5,29},{6,4},{7,31},{8,14},{9,1},{... | collective-permute-start | bytes 3145736 | tf_op jit(solution)/shard_map/ppermute | solution.py:44
  34.0 16.3 %collective-permute-start.12 = (bf16[256,2048]{1,0:T(8,128)(2,1)}, bf16[256,2048]{1,0:T(8,128)(2,1)S(1)}, u32[]{:S(2)}, u32[]{:S(2)}) collective-permute-start(bf16[256,2048]{1,0:T(8,128)(2,1)} %get-tuple-element.54), channel_id=1, source_target_pairs={{0,2},{1,9},{2,4},{3,11},{4,6},{5,13},{6,0},{7,15},{8,10},{9,17},{... | collective-permute-start | bytes 3145736 | tf_op jit(solution)/shard_map/ppermute | solution.py:44
  34.1 22.4 %collective-permute-start.4 = (bf16[144,2048]{1,0:T(8,128)(2,1)S(1)}, bf16[144,2048]{1,0:T(8,128)(2,1)S(1)}, u32[]{:S(2)}, u32[]{:S(2)}) collective-permute-start(bf16[144,2048]{1,0:T(8,128)(2,1)S(1)} %collective-permute-done), channel_id=1, source_target_pairs={{0,1},{1,0},{2,3},{3,2},{4,5},{5,4},{6,7},{7,6},{8,9},{9,8},{10,11... | collective-permute-start | bytes 1769480 | tf_op jit(solution)/shard_map/ppermute | solution.py:44
  34.1 11.2 %collective-permute-start.1 = (bf16[144,2048]{1,0:T(8,128)(2,1)S(1)}, bf16[144,2048]{1,0:T(8,128)(2,1)S(1)}, u32[]{:S(2)}, u32[]{:S(2)}) collective-permute-start(bf16[144,2048]{1,0:T(8,128)(2,1)S(1)} %collective-permute-done), channel_id=1, source_target_pairs={{0,32},{1,97},{2,34},{3,99},{4,36},{5,101},{6,38},{7,103},{8,40},{... | collective-permute-start | bytes 1769480 | tf_op jit(solution)/shard_map/ppermute | solution.py:44
  45.3 11.3 %collective-permute-start.5 = (bf16[144,2048]{1,0:T(8,128)(2,1)S(1)}, bf16[144,2048]{1,0:T(8,128)(2,1)S(1)}, u32[]{:S(2)}, u32[]{:S(2)}) collective-permute-start(bf16[144,2048]{1,0:T(8,128)(2,1)S(1)} %collective-permute-done.1), channel_id=1, source_target_pairs={{0,1},{1,0},{2,3},{3,2},{4,5},{5,4},{6,7},{7,6},{8,9},{9,8},{10,11... | collective-permute-start | bytes 1769480 | tf_op jit(solution)/shard_map/ppermute | solution.py:44
  45.3 11.1 %collective-permute-start.2 = (bf16[144,2048]{1,0:T(8,128)(2,1)S(1)}, bf16[144,2048]{1,0:T(8,128)(2,1)S(1)}, u32[]{:S(2)}, u32[]{:S(2)}) collective-permute-start(bf16[144,2048]{1,0:T(8,128)(2,1)S(1)} %collective-permute-done.1), channel_id=1, source_target_pairs={{0,32},{1,97},{2,34},{3,99},{4,36},{5,101},{6,38},{7,103},{8,40},{... | collective-permute-start | bytes 1769480 | tf_op jit(solution)/shard_map/ppermute | solution.py:44
  46.6 14.2 %collective-permute-start.15 = (bf16[128,2048]{1,0:T(8,128)(2,1)S(1)}, bf16[128,2048]{1,0:T(8,128)(2,1)S(1)}, u32[]{:S(2)}, u32[]{:S(2)}) collective-permute-start(bf16[128,2048]{1,0:T(8,128)(2,1)S(1)} %slice.420), channel_id=1, source_target_pairs={{0,6},{1,25},{2,0},{3,27},{4,2},{5,29},{6,4},{7,31},{8,14},{9,1},{... | collective-permute-start | bytes 1572872 | tf_op jit(solution)/shard_map/ppermute | solution.py:44
  50.4 10.5 %collective-permute-start.13 = (bf16[128,2048]{1,0:T(8,128)(2,1)S(1)}, bf16[128,2048]{1,0:T(8,128)(2,1)S(1)}, u32[]{:S(2)}, u32[]{:S(2)}) collective-permute-start(bf16[128,2048]{1,0:T(8,128)(2,1)S(1)} %slice.419), channel_id=1, source_target_pairs={{0,2},{1,9},{2,4},{3,11},{4,6},{5,13},{6,0},{7,15},{8,10},{9,17},{... | collective-permute-start | bytes 1572872 | tf_op jit(solution)/shard_map/ppermute | solution.py:44
  56.4 4.6 %collective-permute-start.6 = (bf16[144,2048]{1,0:T(8,128)(2,1)S(1)}, bf16[144,2048]{1,0:T(8,128)(2,1)S(1)}, u32[]{:S(2)}, u32[]{:S(2)}) collective-permute-start(bf16[144,2048]{1,0:T(8,128)(2,1)S(1)} %collective-permute-done.2), channel_id=1, source_target_pairs={{0,1},{1,0},{2,3},{3,2},{4,5},{5,4},{6,7},{7,6},{8,9},{9,8},{10,11... | collective-permute-start | bytes 1769480 | tf_op jit(solution)/shard_map/ppermute | solution.py:44
  70.1 5.2 %collective-permute-start.17 = (f32[8,1024]{1,0:T(8,128)S(1)}, f32[8,1024]{1,0:T(8,128)S(1)}, u32[]{:S(2)}, u32[]{:S(2)}) collective-permute-start(f32[8,1024]{1,0:T(8,128)S(1)} %select_maximum_fusion.1), channel_id=1, source_target_pairs={{0,32},{1,97},{2,34},{3,99},{4,36},{5,101},{6,38},{7,103},{8,40},{... | collective-permute-start | bytes 98312 | tf_op jit(solution)/shard_map/ppermute | solution.py:44
  70.2 7.8 %collective-permute-start.18 = (f32[8,1024]{1,0:T(8,128)S(1)}, f32[8,1024]{1,0:T(8,128)S(1)}, u32[]{:S(2)}, u32[]{:S(2)}) collective-permute-start(f32[8,1024]{1,0:T(8,128)S(1)} %select_maximum_fusion.1), channel_id=1, source_target_pairs={{0,64},{1,65},{2,66},{3,67},{4,68},{5,69},{6,70},{7,71},{8,72},{9,... | collective-permute-start | bytes 98312 | tf_op jit(solution)/shard_map/ppermute | solution.py:44
  74.1 3.9 %collective-permute-start.19 = (f32[8,1024]{1,0:T(8,128)S(1)}, f32[8,1024]{1,0:T(8,128)S(1)}, u32[]{:S(2)}, u32[]{:S(2)}) collective-permute-start(f32[8,1024]{1,0:T(8,128)S(1)} %select_maximum_fusion.1), channel_id=1, source_target_pairs={{0,96},{1,33},{2,98},{3,35},{4,100},{5,37},{6,102},{7,39},{8,104},... | collective-permute-start | bytes 98312 | tf_op jit(solution)/shard_map/ppermute | solution.py:44
  84.9 9.5 %collective-permute-start.24 = (bf16[128,2048]{1,0:T(8,128)(2,1)S(1)}, bf16[128,2048]{1,0:T(8,128)(2,1)S(1)}, u32[]{:S(2)}, u32[]{:S(2)}) collective-permute-start(bf16[128,2048]{1,0:T(8,128)(2,1)S(1)} %get-tuple-element.26), channel_id=1, source_target_pairs={{0,6},{1,25},{2,0},{3,27},{4,2},{5,29},{6,4},{7,31},{8,14},{9,1},{... | collective-permute-start | bytes 1572872 | tf_op jit(solution)/shard_map/ppermute | solution.py:44
  85.2 10.5 %collective-permute-start.26 = (bf16[128,2048]{1,0:T(8,128)(2,1)S(1)}, bf16[128,2048]{1,0:T(8,128)(2,1)S(1)}, u32[]{:S(2)}, u32[]{:S(2)}) collective-permute-start(bf16[128,2048]{1,0:T(8,128)(2,1)S(1)} %get-tuple-element.27), channel_id=1, source_target_pairs={{0,2},{1,9},{2,4},{3,11},{4,6},{5,13},{6,0},{7,15},{8,10},{9,17},{... | collective-permute-start | bytes 1572872 | tf_op jit(solution)/shard_map/ppermute | solution.py:44
  96.1 16.1 %collective-permute-start.27 = (bf16[256,2048]{1,0:T(8,128)(2,1)S(1)}, bf16[256,2048]{1,0:T(8,128)(2,1)S(1)}, u32[]{:S(2)}, u32[]{:S(2)}) collective-permute-start(bf16[256,2048]{1,0:T(8,128)(2,1)S(1)} %pad_maximum_fusion.1), channel_id=1, source_target_pairs={{0,2},{1,9},{2,4},{3,11},{4,6},{5,13},{6,0},{7,15},{8,10},{9,17},{... | collective-permute-start | bytes 3145736 | tf_op jit(solution)/shard_map/ppermute | solution.py:44
  97.0 16.3 %collective-permute-start.25 = (bf16[256,2048]{1,0:T(8,128)(2,1)S(1)}, bf16[256,2048]{1,0:T(8,128)(2,1)S(1)}, u32[]{:S(2)}, u32[]{:S(2)}) collective-permute-start(bf16[256,2048]{1,0:T(8,128)(2,1)S(1)} %pad_maximum_fusion), channel_id=1, source_target_pairs={{0,6},{1,25},{2,0},{3,27},{4,2},{5,29},{6,4},{7,31},{8,14},{9,1},{... | collective-permute-start | bytes 3145736 | tf_op jit(solution)/shard_map/ppermute | solution.py:44
  104.6 11.4 %collective-permute-start.20 = (bf16[512,2048]{1,0:T(8,128)(2,1)S(1)}, bf16[512,2048]{1,0:T(8,128)(2,1)S(1)}, u32[]{:S(2)}, u32[]{:S(2)}) collective-permute-start(bf16[512,2048]{1,0:T(8,128)(2,1)S(1)} %slice.530), channel_id=1, source_target_pairs={{0,1},{1,0},{2,3},{3,2},{4,5},{5,4},{6,7},{7,6},{8,9},{9,8},{10,11... | collective-permute-start | bytes 6291464 | tf_op jit(solution)/shard_map/ppermute | solution.py:44
  113.9 5.0 %collective-permute-start.28 = (bf16[32,2048]{1,0:T(8,128)(2,1)S(1)}, bf16[32,2048]{1,0:T(8,128)(2,1)S(1)}, u32[]{:S(2)}, u32[]{:S(2)}) collective-permute-start(bf16[32,2048]{1,0:T(8,128)(2,1)S(1)} %get-tuple-element.32), channel_id=1, source_target_pairs={{0,24},{1,7},{2,26},{3,1},{4,28},{5,3},{6,30},{7,5},{8,0},{9,15},{... | collective-permute-start | bytes 393224 | tf_op jit(solution)/shard_map/ppermute | solution.py:44
  114.0 6.2 %collective-permute-start.30 = (bf16[32,2048]{1,0:T(8,128)(2,1)S(1)}, bf16[32,2048]{1,0:T(8,128)(2,1)S(1)}, u32[]{:S(2)}, u32[]{:S(2)}) collective-permute-start(bf16[32,2048]{1,0:T(8,128)(2,1)S(1)} %get-tuple-element.33), channel_id=1, source_target_pairs={{0,8},{1,3},{2,10},{3,5},{4,12},{5,7},{6,14},{7,1},{8,16},{9,11},{... | collective-permute-start | bytes 393224 | tf_op jit(solution)/shard_map/ppermute | solution.py:44
  116.7 9.2 %collective-permute-start.21 = (bf16[128,2048]{1,0:T(8,128)(2,1)S(1)}, bf16[128,2048]{1,0:T(8,128)(2,1)S(1)}, u32[]{:S(2)}, u32[]{:S(2)}) collective-permute-start(bf16[128,2048]{1,0:T(8,128)(2,1)S(1)} %slice.531), channel_id=1, source_target_pairs={{0,96},{1,33},{2,98},{3,35},{4,100},{5,37},{6,102},{7,39},{8,104},... | collective-permute-start | bytes 1572872 | tf_op jit(solution)/shard_map/ppermute | solution.py:44
  120.3 8.4 %collective-permute-start.31 = (bf16[64,2048]{1,0:T(8,128)(2,1)S(1)}, bf16[64,2048]{1,0:T(8,128)(2,1)S(1)}, u32[]{:S(2)}, u32[]{:S(2)}) collective-permute-start(bf16[64,2048]{1,0:T(8,128)(2,1)S(1)} %pad_maximum_fusion.5), channel_id=1, source_target_pairs={{0,8},{1,3},{2,10},{3,5},{4,12},{5,7},{6,14},{7,1},{8,16},{9,11},{... | collective-permute-start | bytes 786440 | tf_op jit(solution)/shard_map/ppermute | solution.py:44
  121.2 7.6 %collective-permute-start.29 = (bf16[64,2048]{1,0:T(8,128)(2,1)S(1)}, bf16[64,2048]{1,0:T(8,128)(2,1)S(1)}, u32[]{:S(2)}, u32[]{:S(2)}) collective-permute-start(bf16[64,2048]{1,0:T(8,128)(2,1)S(1)} %pad_maximum_fusion.4), channel_id=1, source_target_pairs={{0,24},{1,7},{2,26},{3,1},{4,28},{5,3},{6,30},{7,5},{8,0},{9,15},{... | collective-permute-start | bytes 786440 | tf_op jit(solution)/shard_map/ppermute | solution.py:44
  126.1 9.4 %collective-permute-start.22 = (bf16[128,2048]{1,0:T(8,128)(2,1)S(1)}, bf16[128,2048]{1,0:T(8,128)(2,1)S(1)}, u32[]{:S(2)}, u32[]{:S(2)}) collective-permute-start(bf16[128,2048]{1,0:T(8,128)(2,1)S(1)} %fusion.5), channel_id=1, source_target_pairs={{0,96},{1,33},{2,98},{3,35},{4,100},{5,37},{6,102},{7,39},{8,104},... | collective-permute-start | bytes 1572872 | tf_op jit(solution)/shard_map/ppermute | solution.py:44
  135.6 10.5 %collective-permute-start.23 = (bf16[128,2048]{1,0:T(8,128)(2,1)S(1)}, bf16[128,2048]{1,0:T(8,128)(2,1)S(1)}, u32[]{:S(2)}, u32[]{:S(2)}) collective-permute-start(bf16[128,2048]{1,0:T(8,128)(2,1)S(1)} %fusion.6), channel_id=1, source_target_pairs={{0,96},{1,33},{2,98},{3,35},{4,100},{5,37},{6,102},{7,39},{8,104},... | collective-permute-start | bytes 1572872 | tf_op jit(solution)/shard_map/ppermute | solution.py:44
  139.3 1.4 collective-permute-start.32
  (3 other events, 32.1 us)

commit v2 on v1

v2 whole, which is shorter than its diff:
```python
import jax
import jax.numpy as jnp
from jax import lax
from jax.experimental import pallas as pl
from jax.experimental.pallas import tpu as pltpu
from jax.sharding import PartitionSpec as P

AXES = ("group", "dp")
SHARP = 1.0 / 0.02
FLOOR = -1e30
BF = jnp.bfloat16
F32 = jnp.float32
WIDTH = 2048
VMEM = pl.BlockSpec(memory_space=pltpu.VMEM)
SMEM = pl.BlockSpec(memory_space=pltpu.SMEM)


def index(y, x, z, c):
    return (((y % 4) * 4 + x % 4) * 4 + z % 4) * 2 + c % 2


def pairs(step):
    found = []
    for y in range(4):
        for x in range(4):
            for z in range(4):
                for c in range(2):
                    found.append((index(y, x, z, c), index(*step(y, x, z, c))))
    return found


def first(d):
    return pairs(lambda y, x, z, c: (y, x, z + d, c) if c else (y, x + d, z, c))


def second(d):
    return pairs(lambda y, x, z, c: (y, x + d, z, c) if c else (y, x, z + d, c))


def along(d):
    return pairs(lambda y, x, z, c: (y - d, x, z, c) if c else (y + d, x, z, c))


CORE = pairs(lambda y, x, z, c: (y, x, z, 1 - c))


def send(v, perm):
    return lax.ppermute(v, AXES, perm)


def tied(*v):
    return lax.optimization_barrier(v)


def join(*v):
    return jnp.concatenate(v, axis=0)


def call(kernel, outs, specs, flops=0, nbytes=0, scratch=()):
    return pl.pallas_call(
        kernel,
        out_shape=outs,
        in_specs=specs,
        out_specs=jax.tree.map(lambda _: VMEM, outs),
        scratch_shapes=scratch,
        compiler_params=pltpu.CompilerParams(vmem_limit_bytes=32 * 2**20),
        cost_estimate=pl.CostEstimate(flops=flops, bytes_accessed=nbytes, transcendentals=0),
    )


def shape(r, c, t):
    return jax.ShapeDtypeStruct((r, c), t)


def pack_kernel(q_ref, owner_ref, row_ref, pos_ref, out_ref):
    out_ref[0:128, :] = q_ref[...]

    def turned(ref):
        wide = jnp.concatenate([ref[...], jnp.zeros((128, 112), jnp.int32)], axis=1).astype(F32)
        return jnp.transpose(wide)[0:16]

    pos = pos_ref[...]
    high = (pos // 64).astype(F32)
    low = (pos % 64).astype(F32)
    third = jnp.concatenate([high, low, jnp.zeros((14, 128), F32)], axis=0)
    meta = jnp.concatenate([turned(owner_ref), turned(row_ref), third], axis=1)
    out_ref[128:144, 0:384] = meta.astype(BF)
    out_ref[128:144, 384:WIDTH] = jnp.zeros((16, WIDTH - 384), BF)


def owner_id(place, piece, k1):
    x, z, core = place[1], place[2], place[3]
    kx = jnp.where(core == 0, k1, piece)
    kz = jnp.where(core == 0, piece, k1)
    return (lax.rem(x - kx + 4, 4) * 4 + lax.rem(z - kz + 4, 4)) * 2 + core


ORDER = {0: 0, 1: 1, 3: 2}
PIECES = (0, 1, 2, 3)


def steps(n):
    return lax.broadcasted_iota(jnp.int32, (64, n), 0).astype(F32) + 1.0


def score_block(place, piece, pair, a, b, raw, t_ref, write):
    rows = []
    owners = jnp.concatenate([a[128:144, 0:128], b[128:144, 0:128]], axis=1).astype(F32)
    spots = jnp.concatenate([a[128:144, 128:256], b[128:144, 128:256]], axis=1).astype(F32) + 1.0
    step = steps(256)
    hard, where = [], []
    for k1 in range(4):
        whole = (place[0] * 32 + owner_id(place, piece, k1)).astype(F32)
        spot = jnp.sum(jnp.where(owners == whole, spots, 0.0), axis=0, keepdims=True)
        part = raw[64 * k1 : 64 * k1 + 64]
        found = jnp.sum(jnp.where(step == spot, part, 0.0), axis=0, keepdims=True) * SHARP
        hard.append(jnp.where(spot > 0, found, FLOOR))
        where.append(spot)
    top = jnp.maximum(jnp.maximum(hard[0], hard[1]), jnp.maximum(hard[2], hard[3]))
    chosen = jnp.zeros((1, 256), F32)
    marks = [chosen] * 4
    total = chosen
    if pair == 0:
        scores = raw * SHARP
        top = jnp.maximum(top, jnp.max(scores, axis=0, keepdims=True))
        t = jnp.exp(scores - top)
        t_ref[...] = t
        total = jnp.sum(t, axis=0, keepdims=True)
        pos = jnp.concatenate([a[128:144, 256:384], b[128:144, 256:384]], axis=1).astype(F32)
        marks = []
        for k1 in range(4):
            mine = owner_id(place, piece, k1).astype(F32)
            mark = jnp.where(pos[0:1] == mine, pos[1:2] + 1.0, 0.0)
            part = scores[64 * k1 : 64 * k1 + 64]
            chosen = chosen + jnp.sum(jnp.where(step == mark, part, 0.0), axis=0, keepdims=True)
            marks.append(mark)
    for k1 in range(4):
        total = total + jnp.where(where[k1] > 0, jnp.exp(hard[k1] - top), 0.0)
    write(jnp.concatenate([*hard, *where, top, total, chosen, *marks, jnp.zeros((1, 256), F32)], axis=0))


def product(p, a, b):
    q = jnp.concatenate([a[0:128, :], b[0:128, :]], axis=0)
    return lax.dot_general(p, q, (((1,), (1,)), ((), ())), preferred_element_type=F32)


def writer(ref, rows, cols):
    def write(v):
        ref[rows : rows + 16, cols : cols + 256] = v

    return write


def early_kernel(place_ref, *refs):
    p_refs, q_refs, ts, info = refs[0:3], refs[3:9], refs[9:12], refs[12]
    place = [place_ref[i] for i in range(4)]
    p = jnp.concatenate([r[...] for r in p_refs], axis=0)
    for pair in range(3):
        a, b = q_refs[2 * pair], q_refs[2 * pair + 1]
        raw = product(p, a, b)
        for i, piece in enumerate((0, 1, 3)):
            score_block(
                place, piece, pair, a, b, raw[256 * i : 256 * i + 256], ts[i], writer(info, 16 * i, 256 * pair)
            )


class Info:
    def __init__(self, a, b, c):
        self.refs = a, b, c

    def rows(self, piece, pair, first, last):
        a, b, c = self.refs
        cols = slice(256 * pair, 256 * pair + 256)
        if piece == 2:
            return c[first:last, cols]
        i = 16 * ORDER[piece]
        if pair < 3:
            return a[i + first : i + last, cols]
        return b[i + first : i + last, 0:256]


def merge(a, b):
    top = jnp.maximum(a[0], b[0])
    total = a[1] * jnp.exp(a[0] - top) + b[1] * jnp.exp(b[0] - top)
    return top, total, a[2] + b[2]


def unpack(v):
    return v[0:1], v[1:2], v[2:3]


def late_kernel(place_ref, *refs):
    p_refs, low, high, q_refs, info_a = refs[0:3], refs[3], refs[4], refs[5:13], refs[13]
    t_ref, info_b, info_c, stats_ref = refs[14:]
    place = [place_ref[i] for i in range(4)]
    far = jnp.concatenate([low[...], high[...]], axis=0)
    for pair in range(4):
        a, b = q_refs[2 * pair], q_refs[2 * pair + 1]
        raw = product(far, a, b)
        score_block(place, 2, pair, a, b, raw, t_ref, writer(info_c, 0, 256 * pair))
    p = jnp.concatenate([r[...] for r in p_refs], axis=0)
    a, b = q_refs[6], q_refs[7]
    raw = product(p, a, b)
    for i, piece in enumerate((0, 1, 3)):
        score_block(place, piece, 3, a, b, raw[256 * i : 256 * i + 256], None, writer(info_b, 16 * i, 0))
    info = Info(info_a, info_b, info_c)
    for pair in range(4):
        acc = unpack(info.rows(0, pair, 8, 11))
        for piece in (1, 2, 3):
            acc = merge(acc, unpack(info.rows(piece, pair, 8, 11)))
        stats_ref[:, 256 * pair : 256 * pair + 256] = jnp.concatenate([*acc, jnp.zeros((5, 256), F32)], axis=0)


def query_kernel(half, *refs):
    ts, infos, stats, p_refs, out_ref, turned = refs[0:4], refs[4:7], refs[7], refs[8:13], refs[13], refs[14]
    info = Info(*infos)
    step = steps(128)
    side = slice(128 * half, 128 * half + 128)
    for piece in PIECES:
        cols = slice(256 * piece, 256 * piece + 256)
        for pair in range(4):
            top = stats[0:1, 256 * pair + 128 * half : 256 * pair + 128 * half + 128]
            rows = info.rows(piece, pair, 0, 16)[:, side]
            parts = []
            marks = []
            for k1 in range(4):
                part = jnp.where(step == rows[4 + k1 : 5 + k1], jnp.exp(rows[k1 : k1 + 1] - top), 0.0)
                if pair == 0:
                    t = ts[piece][64 * k1 : 64 * k1 + 64, side] * jnp.exp(rows[8:9] - top)
                    mark = step == rows[11 + k1 : 12 + k1]
                    part = part + jnp.where(mark, 0.0, t)
                    marks.append(jnp.where(mark, 1.0, 0.0))
                parts.append(part)
            turned[128 * pair : 128 * pair + 128, cols] = jnp.transpose(jnp.concatenate(parts, axis=0).astype(BF))
            if pair == 0:
                turned[512:640, cols] = jnp.transpose(jnp.concatenate(marks, axis=0).astype(BF))
    for n in range(4):
        cols = slice(512 * n, 512 * n + 512)
        p = jnp.concatenate([r[:, cols] for r in p_refs], axis=0)
        out_ref[:, cols] = jnp.dot(turned[...], p, preferred_element_type=F32).astype(out_ref.dtype)


def swap(v):
    return jnp.concatenate([v[:, 128 * (i ^ 1) : 128 * (i ^ 1) + 128] for i in range(8)], axis=1)


def total_kernel(raw, other, stats, g1, g2, g3, lse_ref, loss_ref, factor_ref):
    acc = unpack(stats[...])
    for t, got in ((1, g1), (2, g2), (3, g3)):
        v = got[...]
        picked = []
        for i in range(4):
            j, k = (i - t) % 4, (i + t) % 4
            picked += [v[:, 256 * j : 256 * j + 128], v[:, 256 * k + 128 : 256 * k + 256]]
        acc = merge(acc, unpack(jnp.concatenate(picked, axis=1)))
    lse = acc[0] + jnp.log(acc[1])
    lse_ref[...] = jnp.broadcast_to(lse, (8, 1024))
    chosen = acc[2][:, 0:128]
    loss_ref[...] = jnp.broadcast_to(lse[:, 0:128] - chosen, (8, 128))
    rows = []
    for top in (raw[0:1, :], swap(other[...])[0:1]):
        f = jnp.exp(top - lse) * SHARP
        rows += [f[:, 256 * j : 256 * j + 128] for j in range(4)]
    pos = ((jnp.exp(chosen - lse[:, 0:128]) - 1.0) * SHARP).astype(BF).astype(F32)
    factor_ref[...] = jnp.transpose(jnp.concatenate([*rows, pos, jnp.zeros((119, 128), F32)], axis=0))


def coefficients(info, piece, t_ref, lse_ref, c_ref, at):
    step = steps(256)
    for pair in range(4):
        cols = slice(256 * pair, 256 * pair + 256)
        lse = lse_ref[0:1, cols]
        rows = info.rows(piece, pair, 0, 16)
        parts = []
        for k1 in range(4):
            part = jnp.where(step == rows[4 + k1 : 5 + k1], jnp.exp(rows[k1 : k1 + 1] - lse) * SHARP, 0.0)
            if pair == 0:
                t = t_ref[64 * k1 : 64 * k1 + 64, :] * jnp.exp(rows[8:9] - lse)
                t = t - jnp.where(step == rows[11 + k1 : 12 + k1], 1.0, 0.0)
                part = part + t * SHARP
            parts.append(part)
        c_ref[at : at + 256, cols] = jnp.concatenate(parts, axis=0).astype(BF)


def far_kernel(t_ref, *refs):
    infos, lse_ref, q_refs = refs[0:3], refs[3], refs[4:12]
    low_ref, high_ref, c = refs[12:]
    coefficients(Info(*infos), 2, t_ref, lse_ref, c, 0)
    for n in range(4):
        cols = slice(512 * n, 512 * n + 512)
        q = jnp.concatenate([r[0:128, cols] for r in q_refs], axis=0)
        g = jnp.dot(c[...], q, preferred_element_type=F32).astype(BF)
        low_ref[:, cols] = g[0:128]
        high_ref[:, cols] = g[128:256]


def near_kernel(*refs):
    ts, infos, lse_ref, q_refs = refs[0:3], refs[3:6], refs[6], refs[7:15]
    zero, one_low, one_high, three_low, three_high, c = refs[15:]
    info = Info(*infos)
    for i, piece in enumerate((0, 1, 3)):
        coefficients(info, piece, ts[i], lse_ref, c, 256 * i)
    for n in range(4):
        cols = slice(512 * n, 512 * n + 512)
        q = jnp.concatenate([r[0:128, cols] for r in q_refs], axis=0)
        g = jnp.dot(c[...], q, preferred_element_type=F32)
        zero[:, cols] = g[0:256]
        one_low[:, cols] = g[256:384]
        one_high[:, cols] = g[384:512].astype(BF)
        three_low[:, cols] = g[512:640].astype(BF)
        three_high[:, cols] = g[640:768]


def local(question_vectors, passages, positive, hard_owner, hard_row):
    group = lax.axis_index("group")
    dp = lax.axis_index("dp")
    place = jnp.stack([group, dp // 8, dp // 2 % 4, dp % 2]).astype(jnp.int32)

    packed = call(pack_kernel, shape(144, WIDTH, BF), [VMEM] * 4)(
        question_vectors, hard_owner, hard_row, positive.reshape(1, 128)
    )

    back = send(passages, first(1))
    ahead = send(passages, first(-1))
    across = send(passages, first(2))
    q1 = send(packed, along(1))
    s0 = send(packed, CORE)
    back, ahead, across, q1 = tied(back, ahead, across, q1)
    plane = join(passages, back, across, ahead)
    up = send(plane, second(1))
    down = send(plane, second(-1))
    q2 = send(q1, along(1))
    s1 = send(q1, CORE)
    up, down, q2 = tied(up, down, q2)
    low = send(up[:128], second(1))
    high = send(down[128:], second(-1))
    q3 = send(q2, along(1))
    s2 = send(q2, CORE)
    low, high, q3 = tied(low, high, q3)
    s3 = send(q3, CORE)
    tiles = (packed, s0, q1, s1, q2, s2, q3, s3)

    t0, t1, t3, info_a = call(
        early_kernel,
        (shape(256, 256, F32), shape(256, 256, F32), shape(256, 256, F32), shape(48, 768, F32)),
        [SMEM] + [VMEM] * 9,
        2 * 768 * 768 * WIDTH,
    )(place, plane, up, down, *tiles[:6])
    t2, info_b, info_c, raw = call(
        late_kernel,
        (shape(256, 256, F32), shape(48, 256, F32), shape(16, 1024, F32), shape(8, 1024, F32)),
        [SMEM] + [VMEM] * 14,
        2 * 448 * 1024 * WIDTH,
    )(place, plane, up, down, low, high, *tiles, info_a)

    other = send(raw, CORE)
    stats = jnp.concatenate([*merge(unpack(raw), unpack(swap(other))), jnp.zeros((5, 1024), F32)], axis=0)
    g1 = send(stats, along(1))
    g2 = send(stats, along(2))
    g3 = send(stats, along(3))
    infos = (info_a, info_b, info_c)
    operands = (t0, t1, t2, t3, *infos, raw, plane, up, low, high, down)

    def query(half, kind):
        return call(
            lambda *r: query_kernel(half, *r),
            shape(640, WIDTH, kind),
            [VMEM] * 13,
            2 * 640 * 1024 * WIDTH,
            scratch=[pltpu.VMEM((640, 1024), BF)],
        )(*operands)

    theirs = send(query(1, BF), CORE)
    mine = query(0, F32)
    lse, loss, factor = call(
        total_kernel, (shape(8, 1024, F32), shape(8, 128, F32), shape(128, 128, F32)), [VMEM] * 6
    )(raw, other, stats, g1, g2, g3)

    two_low, two_high = call(
        far_kernel,
        (shape(128, WIDTH, BF), shape(128, WIDTH, BF)),
        [VMEM] * 13,
        2 * 256 * 1024 * WIDTH,
        scratch=[pltpu.VMEM((256, 1024), BF)],
    )(t2, *infos, lse, *tiles)
    from_high = send(two_low, second(-1))
    from_low = send(two_high, second(1))

    def block(k):
        a = mine[128 * k : 128 * k + 128] * factor[:, k : k + 1]
        return a + theirs[128 * k : 128 * k + 128].astype(F32) * factor[:, 4 + k : 5 + k]

    run = block(3)
    for k in (2, 1, 0):
        run = block(k) + send(run.astype(BF), along(-1)).astype(F32)
    query_grad = run + (mine[512:640] + theirs[512:640].astype(F32)) * factor[:, 8:9]

    zero, one_low, one_high, three_low, three_high = call(
        near_kernel,
        (
            shape(256, WIDTH, F32),
            shape(128, WIDTH, F32),
            shape(128, WIDTH, BF),
            shape(128, WIDTH, BF),
            shape(128, WIDTH, F32),
        ),
        [VMEM] * 15,
        2 * 768 * 1024 * WIDTH,
        scratch=[pltpu.VMEM((768, 1024), BF)],
    )(t0, t1, t3, *infos, lse, *tiles)
    r1b = send(one_high, second(-1))
    r3a = send(three_low, second(1))
    r1a = send((one_low + from_high.astype(F32)).astype(BF), second(-1))
    r3b = send((three_high + from_low.astype(F32)).astype(BF), second(1))
    g = zero + (join(r1a.astype(F32), r1b.astype(F32)) + join(r3a.astype(F32), r3b.astype(F32)))
    passage_grad = g[0:64]
    for k, d in ((2, 2), (1, -1), (3, 1)):
        passage_grad = passage_grad + send(g[64 * k : 64 * k + 64].astype(BF), first(d)).astype(F32)
    return loss[0], query_grad.astype(BF), passage_grad.astype(BF)


def solution(mesh):
    return jax.shard_map(
        local,
        mesh=mesh,
        in_specs=(P(AXES, None), P(AXES, None), P(AXES), P(AXES, None), P(AXES, None)),
        out_specs=(P(AXES), P(AXES, None), P(AXES, None)),
        check_vma=False,
    )
```

time: 148 us -> 130 us (0.88)
  Pallas kernels: 0 us -> 24.1 us
  matrix products: 14.1 us -> 0 us
  waiting for transfers between devices: 67 us -> 56.2 us
  other arithmetic: 12.1 us -> 3.79 us
  starting transfers between devices: 41.3 us -> 35.2 us
  local copies, waits for them, and re-layouts: 11.3 us -> 9.31 us
    pallas_call x0 -> x8, Pallas kernels: none -> 24.1 us  [the longest x2 5.91 us: query(): call(lambda *r: query_kernel(half, *r), shape(640, WIDTH, kind), [VMEM] *...]
    dot_general x3 -> x0, matrix products: 14.1 us -> none  [the longest x1 4.88 us: local(): lax.dot_general(p, q, (((1,), (1,)), ((), ())), preferred_element_type=F32)]
    ppermute x33 -> x31, waiting for transfers between devices: 67 us -> 56.2 us  [send(): return lax.ppermute(v, AXES, perm)]
    ppermute x33 -> x31, starting transfers between devices: 41.3 us -> 35.2 us  [send(): return lax.ppermute(v, AXES, perm)]
    reduce_sum x2 -> x0, other arithmetic: 2.76 us -> none  [the longest x1 2.26 us: local(): total = jnp.sum(weight * jnp.exp(masked - top[None]), axis=0)]
    unnamed x26 -> x28, local copies, waits for them, and re-layouts: 9.38 us -> 8.14 us
    convert_element_type x13 -> x7, other arithmetic: 3.87 us -> 3.06 us  [the longest x2 2.05 us: local(): return (loss[0], query_grad.astype(BF), passage_grad.astype(BF))]
  transfers between devices with their start and end apart: 33 -> 31, of which waited for: 19 -> 15; matrix products, arithmetic and copies ran while one was open for 13% -> 4% of each run, Pallas kernels for 0% -> 15%
where the time goes in v2:
time: 130 us
  waiting for transfers between devices  56.2 us (43%)
  starting transfers between devices  35.2 us (27%)
  Pallas kernels  24.1 us (19%)
  local copies, waits for them, and re-layouts  9.31 us (7%)
  other arithmetic  3.79 us (3%)
    ppermute x31, waiting for transfers between devices, send(): return lax.ppermute(v, AXES, perm)  56.2 us
    ppermute x31, starting transfers between devices, send(): return lax.ppermute(v, AXES, perm)  35.2 us
    unnamed x28, local copies, waits for them, and re-layouts  8.14 us
    pallas_call x2, Pallas kernels, query(): call(lambda *r: query_kernel(half, *r), shape(640, WIDTH, kind), [VMEM] *...  5.91 us
    pallas_call x1, Pallas kernels, local(): call(near_kernel, (shape(256, WIDTH, F32), shape(128, WIDTH, F32), shape(...  5.45 us
    pallas_call x1, Pallas kernels, local(): call(early_kernel, (shape(256, 256, F32), shape(256, 256, F32), shape(256...  4.88 us
    pallas_call x1, Pallas kernels, local(): call(late_kernel, (shape(256, 256, F32), shape(48, 256, F32), shape(16, 1...  4.4 us
    pallas_call x1, Pallas kernels, local(): call(far_kernel, (shape(128, WIDTH, BF), shape(128, WIDTH, BF)), [VMEM] *...  3.24 us
  transfers between devices with their start and end apart: 31, of which 15 were waited for; matrix products, arithmetic and copies ran while one was open for 4% of the time, Pallas kernels for 15%

profile of v2, /device:TPU:0, one launch (start us, length us, event | category | flops | bytes accessed | tf_op | source)
XLA Modules:
  0.0 129.5 jit_solution(326203450887274807)
XLA Ops:
  4.0 1.7 %collective-permute-start.3 = (bf16[144,2048]{1,0:T(8,128)(2,1)S(1)}, bf16[144,2048]{1,0:T(8,128)(2,1)S(1)}, u32[]{:S(2)}, u32[]{:S(2)}) collective-permute-start(bf16[144,2048]{1,0:T(8,128)(2,1)S(1)} %shard_map.76.refs_3_.refs_5_.refs_7_.refs_4_), channel_id=1, source_target_pairs={{0,32},{1,97},{2,34},{3,99},{4,36},{5,101},{6,38},{7,103},{8,40},{... | collective-permute-start | bytes 1769480 | tf_op jit(solution)/shard_map/ppermute | solution.py:48
  5.7 2.8 %collective-permute-start.1 = (bf16[64,2048]{1,0:T(8,128)(2,1)}, bf16[64,2048]{1,0:T(8,128)(2,1)S(1)}, u32[]{:S(2)}, u32[]{:S(2)}) collective-permute-start(bf16[64,2048]{1,0:T(8,128)(2,1)} %param.6), channel_id=1, source_target_pairs={{0,24},{1,7},{2,26},{3,1},{4,28},{5,3},{6,30},{7,5},{8,0},{9,15},{... | collective-permute-start | bytes 786440 | tf_op jit(solution)/shard_map/ppermute | solution.py:48
  8.5 2.3 %collective-permute-start.2 = (bf16[64,2048]{1,0:T(8,128)(2,1)}, bf16[64,2048]{1,0:T(8,128)(2,1)S(1)}, u32[]{:S(2)}, u32[]{:S(2)}) collective-permute-start(bf16[64,2048]{1,0:T(8,128)(2,1)} %param.6), channel_id=1, source_target_pairs={{0,16},{1,5},{2,18},{3,7},{4,20},{5,1},{6,22},{7,3},{8,24},{9,13},... | collective-permute-start | bytes 786440 | tf_op jit(solution)/shard_map/ppermute | solution.py:48
  12.7 6.4 %collective-permute-done = bf16[64,2048]{1,0:T(8,128)(2,1)S(1)} collective-permute-done((bf16[64,2048]{1,0:T(8,128)(2,1)}, bf16[64,2048]{1,0:T(8,128)(2,1)S(1)}, u32[]{:S(2)}, u32[]{:S(2)}) %collective-permute-start) | collective-permute-done | bytes 262176 | tf_op jit(solution)/shard_map/ppermute | solution.py:48
  19.1 4.1 %collective-permute-start.5 = (bf16[256,2048]{1,0:T(8,128)(2,1)S(1)}, bf16[256,2048]{1,0:T(8,128)(2,1)S(1)}, u32[]{:S(2)}, u32[]{:S(2)}) collective-permute-start(bf16[256,2048]{1,0:T(8,128)(2,1)S(1)} %constant_dynamic-update-slice_fusion.refs_0_.r_8_), channel_id=1, source_target_pairs={{0,6},{1,25},{2,0},{3,27},{4,2},{5,29},{6,4},{7,31},{8,14},{9,1},{... | collective-permute-start | bytes 3145736 | tf_op jit(solution)/shard_map/ppermute | solution.py:48
  24.2 1.6 %collective-permute-start.6 = (bf16[144,2048]{1,0:T(8,128)(2,1)S(1)}, bf16[144,2048]{1,0:T(8,128)(2,1)}, u32[]{:S(2)}, u32[]{:S(2)}) collective-permute-start(bf16[144,2048]{1,0:T(8,128)(2,1)S(1)} %collective-permute-done.3.refs_5_.refs_7_.refs_9_.refs_6_), channel_id=1, source_target_pairs={{0,32},{1,97},{2,34},{3,99},{4,36},{5,101},{6,38},{7,103},{8,40},{... | collective-permute-start | bytes 1769480 | tf_op jit(solution)/shard_map/ppermute | solution.py:48
  25.8 9.6 %collective-permute-done.6.refs_7_.refs_9_.refs_11_.refs_8_ = bf16[144,2048]{1,0:T(8,128)(2,1)} collective-permute-done((bf16[144,2048]{1,0:T(8,128)(2,1)S(1)}, bf16[144,2048]{1,0:T(8,128)(2,1)}, u32[]{:S(2)}, u32[]{:S(2)}) %collective-permute-start.6) | collective-permute-done | bytes 589856 | tf_op jit(solution)/shard_map/ppermute | solution.py:48
  35.6 3.7 %collective-permute-done.4.refs_1_.r_9_ = bf16[256,2048]{1,0:T(8,128)(2,1)S(1)} collective-permute-done((bf16[256,2048]{1,0:T(8,128)(2,1)S(1)}, bf16[256,2048]{1,0:T(8,128)(2,1)S(1)}, u32[]{:S(2)}, u32[]{:S(2)}) %collective-permute-start.4) | collective-permute-done | bytes 1048608 | tf_op jit(solution)/shard_map/ppermute | solution.py:48
  39.4 1.6 %collective-permute-start.9 = (bf16[144,2048]{1,0:T(8,128)(2,1)}, bf16[144,2048]{1,0:T(8,128)(2,1)}, u32[]{:S(2)}, u32[]{:S(2)}) collective-permute-start(bf16[144,2048]{1,0:T(8,128)(2,1)} %collective-permute-done.6.refs_7_.refs_9_.refs_11_.refs_8_), channel_id=1, source_target_pairs={{0,32},{1,97},{2,34},{3,99},{4,36},{5,101},{6,38},{7,103},{8,40},{... | collective-permute-start | bytes 1769480 | tf_op jit(solution)/shard_map/ppermute | solution.py:48
  41.1 2.0 %collective-permute-start.7 = (bf16[128,2048]{1,0:T(8,128)(2,1)S(1)}, bf16[128,2048]{1,0:T(8,128)(2,1)S(1)}, u32[]{:S(2)}, u32[]{:S(2)}) collective-permute-start(bf16[128,2048]{1,0:T(8,128)(2,1)S(1)} %slice.123), channel_id=1, source_target_pairs={{0,2},{1,9},{2,4},{3,11},{4,6},{5,13},{6,0},{7,15},{8,10},{9,17},{... | collective-permute-start | bytes 1572872 | tf_op jit(solution)/shard_map/ppermute | solution.py:48
  43.6 5.0 %collective-permute-done.8.refs_4_.r_11_ = bf16[128,2048]{1,0:T(8,128)(2,1)S(1)} collective-permute-done((bf16[128,2048]{1,0:T(8,128)(2,1)S(1)}, bf16[128,2048]{1,0:T(8,128)(2,1)S(1)}, u32[]{:S(2)}, u32[]{:S(2)}) %collective-permute-start.8) | collective-permute-done | bytes 524320 | tf_op jit(solution)/shard_map/ppermute | solution.py:48
  49.4 2.2 %collective-permute-done.7.refs_3_.r_10_ = bf16[128,2048]{1,0:T(8,128)(2,1)S(1)} collective-permute-done((bf16[128,2048]{1,0:T(8,128)(2,1)S(1)}, bf16[128,2048]{1,0:T(8,128)(2,1)S(1)}, u32[]{:S(2)}, u32[]{:S(2)}) %collective-permute-start.7) | collective-permute-done | bytes 524320 | tf_op jit(solution)/shard_map/ppermute | solution.py:48
  53.8 4.9 %shard_map.77 = (f32[256,256]{1,0:T(8,128)S(1)}, f32[256,256]{1,0:T(8,128)S(1)}, f32[256,256]{1,0:T(8,128)S(1)}, f32[48,768]{1,0:T(8,128)S(1)}) custom-call(s32[4]{0:T(128)S(1)} %pad_add_fusion.place_ref, bf16[256,2048]{1,0:T(8,128)(2,1)S(1)} %copy-done.1, bf16[256,2048]{1,0:T(8,128)(2,1)S(1)} %collective-permute-done.4.refs_1_.r_9_, ...), custom_call_target="tpu_custom_call" | custom-call | flops 2415919104 | tf_op jit(solution)/shard_map/pallas_call | solution.py:343
  58.7 4.4 %shard_map.78 = (f32[256,256]{1,0:T(8,128)S(1)}, f32[48,256]{1,0:T(8,128)S(1)}, f32[16,1024]{1,0:T(8,128)S(1)}, f32[8,1024]{1,0:T(8,128)S(1)}) custom-call(s32[4]{0:T(128)S(1)} %pad_add_fusion.place_ref, bf16[256,2048]{1,0:T(8,128)(2,1)S(1)} %copy-done.1, bf16[256,2048]{1,0:T(8,128)(2,1)S(1)} %collective-permute-done.4.refs_1_.r_9_, ...), custom_call_target="tpu_custom_call" | custom-call | flops 1879048192 | tf_op jit(solution)/shard_map/pallas_call | solution.py:349
  63.8 3.0 %shard_map.81 = bf16[640,2048]{1,0:T(8,128)(2,1)S(1)} custom-call(f32[256,256]{1,0:T(8,128)S(1)} %get-tuple-element.44.r_0_.refs_0_, f32[256,256]{1,0:T(8,128)S(1)} %get-tuple-element.45.r_1_.refs_1_, f32[256,256]{1,0:T(8,128)S(1)} %get-tuple-element.46.r_2_.t_ref, f32[256,256]{1,0:T(8,128)S(1)} %get-tuple-element.47.r_3_.refs_2_, ...), custom_call_target="tpu_custom_call" | custom-call | flops 2684354560 | tf_op jit(solution)/shard_map/pallas_call | solution.py:365
  67.1 1.7 %collective-permute-start.17 = (f32[8,1024]{1,0:T(8,128)S(1)}, f32[8,1024]{1,0:T(8,128)S(1)}, u32[]{:S(2)}, u32[]{:S(2)}) collective-permute-start(f32[8,1024]{1,0:T(8,128)S(1)} %maximum_maximum_fusion.stats), channel_id=1, source_target_pairs={{0,96},{1,33},{2,98},{3,35},{4,100},{5,37},{6,102},{7,39},{8,104},... | collective-permute-start | bytes 98312 | tf_op jit(solution)/shard_map/ppermute | solution.py:48
  68.8 1.7 %collective-permute-start.16 = (f32[8,1024]{1,0:T(8,128)S(1)}, f32[8,1024]{1,0:T(8,128)S(1)}, u32[]{:S(2)}, u32[]{:S(2)}) collective-permute-start(f32[8,1024]{1,0:T(8,128)S(1)} %maximum_maximum_fusion.stats), channel_id=1, source_target_pairs={{0,64},{1,65},{2,66},{3,67},{4,68},{5,69},{6,70},{7,71},{8,72},{9,... | collective-permute-start | bytes 98312 | tf_op jit(solution)/shard_map/ppermute | solution.py:48
  70.6 3.0 %shard_map.80 = f32[640,2048]{1,0:T(8,128)S(1)} custom-call(f32[256,256]{1,0:T(8,128)S(1)} %get-tuple-element.44.r_0_.refs_0_, f32[256,256]{1,0:T(8,128)S(1)} %get-tuple-element.45.r_1_.refs_1_, f32[256,256]{1,0:T(8,128)S(1)} %get-tuple-element.46.r_2_.t_ref, f32[256,256]{1,0:T(8,128)S(1)} %get-tuple-element.47.r_3_.refs_2_, ...), custom_call_target="tpu_custom_call" | custom-call | flops 2684354560 | tf_op jit(solution)/shard_map/pallas_call | solution.py:365
  74.2 1.4 %collective-permute-done.15.g1 = f32[8,1024]{1,0:T(8,128)S(1)} collective-permute-done((f32[8,1024]{1,0:T(8,128)S(1)}, f32[8,1024]{1,0:T(8,128)S(1)}, u32[]{:S(2)}, u32[]{:S(2)}) %collective-permute-start.15) | collective-permute-done | bytes 32800 | tf_op jit(solution)/shard_map/ppermute | solution.py:48
  75.8 3.2 %shard_map.83 = (bf16[128,2048]{1,0:T(8,128)(2,1)S(1)}, bf16[128,2048]{1,0:T(8,128)(2,1)S(1)}) custom-call(f32[256,256]{1,0:T(8,128)S(1)} %get-tuple-element.46.r_2_.t_ref, f32[48,768]{1,0:T(8,128)S(1)} %get-tuple-element.41.refs_13_.r_4_.refs_3_.refs_0_, f32[48,256]{1,0:T(8,128)S(1)} %get-tuple-element.48.r_5_.refs_4_.refs_1_, ...), custom_call_target="tpu_custom_call" | custom-call | flops 1073741824 | tf_op jit(solution)/shard_map/pallas_call | solution.py:379
  79.7 5.5 %shard_map.82 = (f32[256,2048]{1,0:T(8,128)S(1)}, f32[128,2048]{1,0:T(8,128)S(1)}, bf16[128,2048]{1,0:T(8,128)(2,1)S(1)}, bf16[128,2048]{1,0:T(8,128)(2,1)S(1)}, f32[128,2048]{1,0:T(8,128)S(1)}) custom-call(f32[256,256]{1,0:T(8,128)S(1)} %get-tuple-element.44.r_0_.refs_0_, f32[256,256]{1,0:T(8,128)S(1)} %get-tuple-element.45.r_1_.refs_1_, ...), custom_call_target="tpu_custom_call" | custom-call | flops 3221225472 | tf_op jit(solution)/shard_map/pallas_call | solution.py:398
  86.4 1.3 %collective-permute-start.25 = (bf16[128,2048]{1,0:T(8,128)(2,1)S(1)}, bf16[128,2048]{1,0:T(8,128)(2,1)S(1)}, u32[]{:S(2)}, u32[]{:S(2)}) collective-permute-start(bf16[128,2048]{1,0:T(8,128)(2,1)S(1)} %get-tuple-element.56), channel_id=1, source_target_pairs={{0,2},{1,9},{2,4},{3,11},{4,6},{5,13},{6,0},{7,15},{8,10},{9,17},{... | collective-permute-start | bytes 1572872 | tf_op jit(solution)/shard_map/ppermute | solution.py:48
  87.7 1.4 %collective-permute-start.26 = (bf16[128,2048]{1,0:T(8,128)(2,1)S(1)}, bf16[128,2048]{1,0:T(8,128)(2,1)S(1)}, u32[]{:S(2)}, u32[]{:S(2)}) collective-permute-start(bf16[128,2048]{1,0:T(8,128)(2,1)S(1)} %get-tuple-element.58), channel_id=1, source_target_pairs={{0,2},{1,9},{2,4},{3,11},{4,6},{5,13},{6,0},{7,15},{8,10},{9,17},{... | collective-permute-start | bytes 1572872 | tf_op jit(solution)/shard_map/ppermute | solution.py:48
  90.6 2.2 %collective-permute-start.23 = (bf16[128,2048]{1,0:T(8,128)(2,1)S(1)}, bf16[128,2048]{1,0:T(8,128)(2,1)S(1)}, u32[]{:S(2)}, u32[]{:S(2)}) collective-permute-start(bf16[128,2048]{1,0:T(8,128)(2,1)S(1)} %add_convert_fusion.1), channel_id=1, source_target_pairs={{0,6},{1,25},{2,0},{3,27},{4,2},{5,29},{6,4},{7,31},{8,14},{9,1},{... | collective-permute-start | bytes 1572872 | tf_op jit(solution)/shard_map/ppermute | solution.py:48
  92.7 9.6 %collective-permute-done.26 = bf16[128,2048]{1,0:T(8,128)(2,1)S(1)} collective-permute-done((bf16[128,2048]{1,0:T(8,128)(2,1)S(1)}, bf16[128,2048]{1,0:T(8,128)(2,1)S(1)}, u32[]{:S(2)}, u32[]{:S(2)}) %collective-permute-start.26) | collective-permute-done | bytes 524320 | tf_op jit(solution)/shard_map/ppermute | solution.py:48
  104.2 8.8 %collective-permute-done.27 = bf16[128,2048]{1,0:T(8,128)(2,1)S(1)} collective-permute-done((bf16[128,2048]{1,0:T(8,128)(2,1)S(1)}, bf16[128,2048]{1,0:T(8,128)(2,1)S(1)}, u32[]{:S(2)}, u32[]{:S(2)}) %collective-permute-start.27) | collective-permute-done | bytes 524320 | tf_op jit(solution)/shard_map/ppermute | solution.py:48
  114.0 4.8 %collective-permute-start.30 = (bf16[64,2048]{1,0:T(8,128)(2,1)S(1)}, bf16[64,2048]{1,0:T(8,128)(2,1)S(1)}, u32[]{:S(2)}, u32[]{:S(2)}) collective-permute-start(bf16[64,2048]{1,0:T(8,128)(2,1)S(1)} %get-tuple-element.73), channel_id=1, source_target_pairs={{0,8},{1,3},{2,10},{3,5},{4,12},{5,7},{6,14},{7,1},{8,16},{9,11},{... | collective-permute-start | bytes 786440 | tf_op jit(solution)/shard_map/ppermute | solution.py:48
  119.7 2.0 %collective-permute-done.28 = bf16[64,2048]{1,0:T(8,128)(2,1)S(1)} collective-permute-done((bf16[64,2048]{1,0:T(8,128)(2,1)S(1)}, bf16[64,2048]{1,0:T(8,128)(2,1)S(1)}, u32[]{:S(2)}, u32[]{:S(2)}) %collective-permute-start.28) | collective-permute-done | bytes 262176 | tf_op jit(solution)/shard_map/ppermute | solution.py:48
  121.6 2.7 %collective-permute-done.30 = bf16[64,2048]{1,0:T(8,128)(2,1)S(1)} collective-permute-done((bf16[64,2048]{1,0:T(8,128)(2,1)S(1)}, bf16[64,2048]{1,0:T(8,128)(2,1)S(1)}, u32[]{:S(2)}, u32[]{:S(2)}) %collective-permute-start.30) | collective-permute-done | bytes 262176 | tf_op jit(solution)/shard_map/ppermute | solution.py:48
  124.3 1.6 %collective-permute-done.29 = bf16[64,2048]{1,0:T(8,128)(2,1)S(1)} collective-permute-done((bf16[64,2048]{1,0:T(8,128)(2,1)S(1)}, bf16[64,2048]{1,0:T(8,128)(2,1)S(1)}, u32[]{:S(2)}, u32[]{:S(2)}) %collective-permute-start.29) | collective-permute-done | bytes 262176 | tf_op jit(solution)/shard_map/ppermute | solution.py:48
  126.8 1.5 %collective-permute-done.21 = bf16[128,2048]{1,0:T(8,128)(2,1)S(1)} collective-permute-done((bf16[128,2048]{1,0:T(8,128)(2,1)S(1)}, bf16[128,2048]{1,0:T(8,128)(2,1)S(1)}, u32[]{:S(2)}, u32[]{:S(2)}) %collective-permute-start.21) | collective-permute-done | bytes 524320 | tf_op jit(solution)/shard_map/ppermute | solution.py:48
  128.3 1.2 fusion.2
  (86 shorter events, 19.9 us)
Async XLA Ops:
  4.0 15.1 %collective-permute-start.3 = (bf16[144,2048]{1,0:T(8,128)(2,1)S(1)}, bf16[144,2048]{1,0:T(8,128)(2,1)S(1)}, u32[]{:S(2)}, u32[]{:S(2)}) collective-permute-start(bf16[144,2048]{1,0:T(8,128)(2,1)S(1)} %shard_map.76.refs_3_.refs_5_.refs_7_.refs_4_), channel_id=1, source_target_pairs={{0,32},{1,97},{2,34},{3,99},{4,36},{5,101},{6,38},{7,103},{8,40},{... | collective-permute-start | bytes 1769480 | tf_op jit(solution)/shard_map/ppermute | solution.py:48
  5.7 7.0 %collective-permute-start.1 = (bf16[64,2048]{1,0:T(8,128)(2,1)}, bf16[64,2048]{1,0:T(8,128)(2,1)S(1)}, u32[]{:S(2)}, u32[]{:S(2)}) collective-permute-start(bf16[64,2048]{1,0:T(8,128)(2,1)} %param.6), channel_id=1, source_target_pairs={{0,24},{1,7},{2,26},{3,1},{4,28},{5,3},{6,30},{7,5},{8,0},{9,15},{... | collective-permute-start | bytes 786440 | tf_op jit(solution)/shard_map/ppermute | solution.py:48
  8.5 10.6 %collective-permute-start = (bf16[64,2048]{1,0:T(8,128)(2,1)}, bf16[64,2048]{1,0:T(8,128)(2,1)S(1)}, u32[]{:S(2)}, u32[]{:S(2)}) collective-permute-start(bf16[64,2048]{1,0:T(8,128)(2,1)} %param.6), channel_id=1, source_target_pairs={{0,8},{1,3},{2,10},{3,5},{4,12},{5,7},{6,14},{7,1},{8,16},{9,11},{... | collective-permute-start | bytes 786440 | tf_op jit(solution)/shard_map/ppermute | solution.py:48
  8.5 10.6 %collective-permute-start.2 = (bf16[64,2048]{1,0:T(8,128)(2,1)}, bf16[64,2048]{1,0:T(8,128)(2,1)S(1)}, u32[]{:S(2)}, u32[]{:S(2)}) collective-permute-start(bf16[64,2048]{1,0:T(8,128)(2,1)} %param.6), channel_id=1, source_target_pairs={{0,16},{1,5},{2,18},{3,7},{4,20},{5,1},{6,22},{7,3},{8,24},{9,13},... | collective-permute-start | bytes 786440 | tf_op jit(solution)/shard_map/ppermute | solution.py:48
  19.1 16.4 %collective-permute-start.5 = (bf16[256,2048]{1,0:T(8,128)(2,1)S(1)}, bf16[256,2048]{1,0:T(8,128)(2,1)S(1)}, u32[]{:S(2)}, u32[]{:S(2)}) collective-permute-start(bf16[256,2048]{1,0:T(8,128)(2,1)S(1)} %constant_dynamic-update-slice_fusion.refs_0_.r_8_), channel_id=1, source_target_pairs={{0,6},{1,25},{2,0},{3,27},{4,2},{5,29},{6,4},{7,31},{8,14},{9,1},{... | collective-permute-start | bytes 3145736 | tf_op jit(solution)/shard_map/ppermute | solution.py:48
  23.3 16.0 %collective-permute-start.4 = (bf16[256,2048]{1,0:T(8,128)(2,1)S(1)}, bf16[256,2048]{1,0:T(8,128)(2,1)S(1)}, u32[]{:S(2)}, u32[]{:S(2)}) collective-permute-start(bf16[256,2048]{1,0:T(8,128)(2,1)S(1)} %constant_dynamic-update-slice_fusion.refs_0_.r_8_), channel_id=1, source_target_pairs={{0,2},{1,9},{2,4},{3,11},{4,6},{5,13},{6,0},{7,15},{8,10},{9,17},{... | collective-permute-start | bytes 3145736 | tf_op jit(solution)/shard_map/ppermute | solution.py:48
  24.2 11.2 %collective-permute-start.6 = (bf16[144,2048]{1,0:T(8,128)(2,1)S(1)}, bf16[144,2048]{1,0:T(8,128)(2,1)}, u32[]{:S(2)}, u32[]{:S(2)}) collective-permute-start(bf16[144,2048]{1,0:T(8,128)(2,1)S(1)} %collective-permute-done.3.refs_5_.refs_7_.refs_9_.refs_6_), channel_id=1, source_target_pairs={{0,32},{1,97},{2,34},{3,99},{4,36},{5,101},{6,38},{7,103},{8,40},{... | collective-permute-start | bytes 1769480 | tf_op jit(solution)/shard_map/ppermute | solution.py:48
  39.3 9.3 %collective-permute-start.8 = (bf16[128,2048]{1,0:T(8,128)(2,1)S(1)}, bf16[128,2048]{1,0:T(8,128)(2,1)S(1)}, u32[]{:S(2)}, u32[]{:S(2)}) collective-permute-start(bf16[128,2048]{1,0:T(8,128)(2,1)S(1)} %slice.124), channel_id=1, source_target_pairs={{0,6},{1,25},{2,0},{3,27},{4,2},{5,29},{6,4},{7,31},{8,14},{9,1},{... | collective-permute-start | bytes 1572872 | tf_op jit(solution)/shard_map/ppermute | solution.py:48
  39.4 13.0 %collective-permute-start.9 = (bf16[144,2048]{1,0:T(8,128)(2,1)}, bf16[144,2048]{1,0:T(8,128)(2,1)}, u32[]{:S(2)}, u32[]{:S(2)}) collective-permute-start(bf16[144,2048]{1,0:T(8,128)(2,1)} %collective-permute-done.6.refs_7_.refs_9_.refs_11_.refs_8_), channel_id=1, source_target_pairs={{0,32},{1,97},{2,34},{3,99},{4,36},{5,101},{6,38},{7,103},{8,40},{... | collective-permute-start | bytes 1769480 | tf_op jit(solution)/shard_map/ppermute | solution.py:48
  41.1 10.5 %collective-permute-start.7 = (bf16[128,2048]{1,0:T(8,128)(2,1)S(1)}, bf16[128,2048]{1,0:T(8,128)(2,1)S(1)}, u32[]{:S(2)}, u32[]{:S(2)}) collective-permute-start(bf16[128,2048]{1,0:T(8,128)(2,1)S(1)} %slice.123), channel_id=1, source_target_pairs={{0,2},{1,9},{2,4},{3,11},{4,6},{5,13},{6,0},{7,15},{8,10},{9,17},{... | collective-permute-start | bytes 1572872 | tf_op jit(solution)/shard_map/ppermute | solution.py:48
  43.1 9.4 %collective-permute-start.10 = (bf16[144,2048]{1,0:T(8,128)(2,1)S(1)}, bf16[144,2048]{1,0:T(8,128)(2,1)}, u32[]{:S(2)}, u32[]{:S(2)}) collective-permute-start(bf16[144,2048]{1,0:T(8,128)(2,1)S(1)} %shard_map.76.refs_3_.refs_5_.refs_7_.refs_4_), channel_id=1, source_target_pairs={{0,1},{1,0},{2,3},{3,2},{4,5},{5,4},{6,7},{7,6},{8,9},{9,8},{10,11... | collective-permute-start | bytes 1769480 | tf_op jit(solution)/shard_map/ppermute | solution.py:48
  43.1 9.4 %collective-permute-start.11 = (bf16[144,2048]{1,0:T(8,128)(2,1)S(1)}, bf16[144,2048]{1,0:T(8,128)(2,1)}, u32[]{:S(2)}, u32[]{:S(2)}) collective-permute-start(bf16[144,2048]{1,0:T(8,128)(2,1)S(1)} %collective-permute-done.3.refs_5_.refs_7_.refs_9_.refs_6_), channel_id=1, source_target_pairs={{0,1},{1,0},{2,3},{3,2},{4,5},{5,4},{6,7},{7,6},{8,9},{9,8},{10,11... | collective-permute-start | bytes 1769480 | tf_op jit(solution)/shard_map/ppermute | solution.py:48
  49.4 3.2 %collective-permute-start.12 = (bf16[144,2048]{1,0:T(8,128)(2,1)}, bf16[144,2048]{1,0:T(8,128)(2,1)}, u32[]{:S(2)}, u32[]{:S(2)}) collective-permute-start(bf16[144,2048]{1,0:T(8,128)(2,1)} %collective-permute-done.6.refs_7_.refs_9_.refs_11_.refs_8_), channel_id=1, source_target_pairs={{0,1},{1,0},{2,3},{3,2},{4,5},{5,4},{6,7},{7,6},{8,9},{9,8},{10,11... | collective-permute-start | bytes 1769480 | tf_op jit(solution)/shard_map/ppermute | solution.py:48
  52.3 6.3 %collective-permute-start.13 = (bf16[144,2048]{1,0:T(8,128)(2,1)}, bf16[144,2048]{1,0:T(8,128)(2,1)}, u32[]{:S(2)}, u32[]{:S(2)}) collective-permute-start(bf16[144,2048]{1,0:T(8,128)(2,1)} %collective-permute-done.9.refs_11_.refs_13_.refs_10_), channel_id=1, source_target_pairs={{0,1},{1,0},{2,3},{3,2},{4,5},{5,4},{6,7},{7,6},{8,9},{9,8},{10,11... | collective-permute-start | bytes 1769480 | tf_op jit(solution)/shard_map/ppermute | solution.py:48
  53.7 4.9 %copy-start.5 = (bf16[128,2048]{1,0:T(8,128)(2,1)S(1)}, bf16[128,2048]{1,0:T(8,128)(2,1)}, u32[]{:S(2)}) copy-start(bf16[128,2048]{1,0:T(8,128)(2,1)} %copy-done.4) | copy-start | bytes 1572868
  63.1 3.8 %collective-permute-start.14 = (f32[8,1024]{1,0:T(8,128)S(1)}, f32[8,1024]{1,0:T(8,128)S(1)}, u32[]{:S(2)}, u32[]{:S(2)}) collective-permute-start(f32[8,1024]{1,0:T(8,128)S(1)} %get-tuple-element.42.raw.r_7_), channel_id=1, source_target_pairs={{0,1},{1,0},{2,3},{3,2},{4,5},{5,4},{6,7},{7,6},{8,9},{9,8},{10,11... | collective-permute-start | bytes 98312 | tf_op jit(solution)/shard_map/ppermute | solution.py:48
  66.8 22.3 %collective-permute-start.18 = (bf16[640,2048]{1,0:T(8,128)(2,1)S(1)}, bf16[640,2048]{1,0:T(8,128)(2,1)S(1)}, u32[]{:S(2)}, u32[]{:S(2)}) collective-permute-start(bf16[640,2048]{1,0:T(8,128)(2,1)S(1)} %shard_map.81), channel_id=1, source_target_pairs={{0,1},{1,0},{2,3},{3,2},{4,5},{5,4},{6,7},{7,6},{8,9},{9,8},{10,11... | collective-permute-start | bytes 7864328 | tf_op jit(solution)/shard_map/ppermute | solution.py:48
  67.1 6.5 %collective-permute-start.17 = (f32[8,1024]{1,0:T(8,128)S(1)}, f32[8,1024]{1,0:T(8,128)S(1)}, u32[]{:S(2)}, u32[]{:S(2)}) collective-permute-start(f32[8,1024]{1,0:T(8,128)S(1)} %maximum_maximum_fusion.stats), channel_id=1, source_target_pairs={{0,96},{1,33},{2,98},{3,35},{4,100},{5,37},{6,102},{7,39},{8,104},... | collective-permute-start | bytes 98312 | tf_op jit(solution)/shard_map/ppermute | solution.py:48
  68.8 5.4 %collective-permute-start.16 = (f32[8,1024]{1,0:T(8,128)S(1)}, f32[8,1024]{1,0:T(8,128)S(1)}, u32[]{:S(2)}, u32[]{:S(2)}) collective-permute-start(f32[8,1024]{1,0:T(8,128)S(1)} %maximum_maximum_fusion.stats), channel_id=1, source_target_pairs={{0,64},{1,65},{2,66},{3,67},{4,68},{5,69},{6,70},{7,71},{8,72},{9,... | collective-permute-start | bytes 98312 | tf_op jit(solution)/shard_map/ppermute | solution.py:48
  70.5 5.1 %collective-permute-start.15 = (f32[8,1024]{1,0:T(8,128)S(1)}, f32[8,1024]{1,0:T(8,128)S(1)}, u32[]{:S(2)}, u32[]{:S(2)}) collective-permute-start(f32[8,1024]{1,0:T(8,128)S(1)} %maximum_maximum_fusion.stats), channel_id=1, source_target_pairs={{0,32},{1,97},{2,34},{3,99},{4,36},{5,101},{6,38},{7,103},{8,40},{... | collective-permute-start | bytes 98312 | tf_op jit(solution)/shard_map/ppermute | solution.py:48
  79.0 11.5 %collective-permute-start.22 = (bf16[128,2048]{1,0:T(8,128)(2,1)S(1)}, bf16[128,2048]{1,0:T(8,128)(2,1)S(1)}, u32[]{:S(2)}, u32[]{:S(2)}) collective-permute-start(bf16[128,2048]{1,0:T(8,128)(2,1)S(1)} %get-tuple-element.54), channel_id=1, source_target_pairs={{0,6},{1,25},{2,0},{3,27},{4,2},{5,29},{6,4},{7,31},{8,14},{9,1},{... | collective-permute-start | bytes 1572872 | tf_op jit(solution)/shard_map/ppermute | solution.py:48
  85.6 18.5 %collective-permute-start.24 = (bf16[128,2048]{1,0:T(8,128)(2,1)S(1)}, bf16[128,2048]{1,0:T(8,128)(2,1)S(1)}, u32[]{:S(2)}, u32[]{:S(2)}) collective-permute-start(bf16[128,2048]{1,0:T(8,128)(2,1)S(1)} %get-tuple-element.55), channel_id=1, source_target_pairs={{0,6},{1,25},{2,0},{3,27},{4,2},{5,29},{6,4},{7,31},{8,14},{9,1},{... | collective-permute-start | bytes 1572872 | tf_op jit(solution)/shard_map/ppermute | solution.py:48
  86.4 17.8 %collective-permute-start.25 = (bf16[128,2048]{1,0:T(8,128)(2,1)S(1)}, bf16[128,2048]{1,0:T(8,128)(2,1)S(1)}, u32[]{:S(2)}, u32[]{:S(2)}) collective-permute-start(bf16[128,2048]{1,0:T(8,128)(2,1)S(1)} %get-tuple-element.56), channel_id=1, source_target_pairs={{0,2},{1,9},{2,4},{3,11},{4,6},{5,13},{6,0},{7,15},{8,10},{9,17},{... | collective-permute-start | bytes 1572872 | tf_op jit(solution)/shard_map/ppermute | solution.py:48
  87.7 14.7 %collective-permute-start.26 = (bf16[128,2048]{1,0:T(8,128)(2,1)S(1)}, bf16[128,2048]{1,0:T(8,128)(2,1)S(1)}, u32[]{:S(2)}, u32[]{:S(2)}) collective-permute-start(bf16[128,2048]{1,0:T(8,128)(2,1)S(1)} %get-tuple-element.58), channel_id=1, source_target_pairs={{0,2},{1,9},{2,4},{3,11},{4,6},{5,13},{6,0},{7,15},{8,10},{9,17},{... | collective-permute-start | bytes 1572872 | tf_op jit(solution)/shard_map/ppermute | solution.py:48
  89.3 13.4 %collective-permute-start.19 = (bf16[128,2048]{1,0:T(8,128)(2,1)S(1)}, bf16[128,2048]{1,0:T(8,128)(2,1)S(1)}, u32[]{:S(2)}, u32[]{:S(2)}) collective-permute-start(bf16[128,2048]{1,0:T(8,128)(2,1)S(1)} %fusion.4), channel_id=1, source_target_pairs={{0,96},{1,33},{2,98},{3,35},{4,100},{5,37},{6,102},{7,39},{8,104},... | collective-permute-start | bytes 1572872 | tf_op jit(solution)/shard_map/ppermute | solution.py:48
  90.6 13.6 %collective-permute-start.23 = (bf16[128,2048]{1,0:T(8,128)(2,1)S(1)}, bf16[128,2048]{1,0:T(8,128)(2,1)S(1)}, u32[]{:S(2)}, u32[]{:S(2)}) collective-permute-start(bf16[128,2048]{1,0:T(8,128)(2,1)S(1)} %add_convert_fusion.1), channel_id=1, source_target_pairs={{0,6},{1,25},{2,0},{3,27},{4,2},{5,29},{6,4},{7,31},{8,14},{9,1},{... | collective-permute-start | bytes 1572872 | tf_op jit(solution)/shard_map/ppermute | solution.py:48
  102.5 10.5 %collective-permute-start.27 = (bf16[128,2048]{1,0:T(8,128)(2,1)S(1)}, bf16[128,2048]{1,0:T(8,128)(2,1)S(1)}, u32[]{:S(2)}, u32[]{:S(2)}) collective-permute-start(bf16[128,2048]{1,0:T(8,128)(2,1)S(1)} %add_convert_fusion), channel_id=1, source_target_pairs={{0,2},{1,9},{2,4},{3,11},{4,6},{5,13},{6,0},{7,15},{8,10},{9,17},{... | collective-permute-start | bytes 1572872 | tf_op jit(solution)/shard_map/ppermute | solution.py:48
  103.0 15.8 %collective-permute-start.20 = (bf16[128,2048]{1,0:T(8,128)(2,1)S(1)}, bf16[128,2048]{1,0:T(8,128)(2,1)S(1)}, u32[]{:S(2)}, u32[]{:S(2)}) collective-permute-start(bf16[128,2048]{1,0:T(8,128)(2,1)S(1)} %fusion.7), channel_id=1, source_target_pairs={{0,96},{1,33},{2,98},{3,35},{4,100},{5,37},{6,102},{7,39},{8,104},... | collective-permute-start | bytes 1572872 | tf_op jit(solution)/shard_map/ppermute | solution.py:48
  113.6 8.1 %collective-permute-start.28 = (bf16[64,2048]{1,0:T(8,128)(2,1)S(1)}, bf16[64,2048]{1,0:T(8,128)(2,1)S(1)}, u32[]{:S(2)}, u32[]{:S(2)}) collective-permute-start(bf16[64,2048]{1,0:T(8,128)(2,1)S(1)} %get-tuple-element.72), channel_id=1, source_target_pairs={{0,16},{1,5},{2,18},{3,7},{4,20},{5,1},{6,22},{7,3},{8,24},{9,13},... | collective-permute-start | bytes 786440 | tf_op jit(solution)/shard_map/ppermute | solution.py:48
  114.0 10.4 %collective-permute-start.30 = (bf16[64,2048]{1,0:T(8,128)(2,1)S(1)}, bf16[64,2048]{1,0:T(8,128)(2,1)S(1)}, u32[]{:S(2)}, u32[]{:S(2)}) collective-permute-start(bf16[64,2048]{1,0:T(8,128)(2,1)S(1)} %get-tuple-element.73), channel_id=1, source_target_pairs={{0,8},{1,3},{2,10},{3,5},{4,12},{5,7},{6,14},{7,1},{8,16},{9,11},{... | collective-permute-start | bytes 786440 | tf_op jit(solution)/shard_map/ppermute | solution.py:48
  118.8 7.2 %collective-permute-start.29 = (bf16[64,2048]{1,0:T(8,128)(2,1)S(1)}, bf16[64,2048]{1,0:T(8,128)(2,1)S(1)}, u32[]{:S(2)}, u32[]{:S(2)}) collective-permute-start(bf16[64,2048]{1,0:T(8,128)(2,1)S(1)} %get-tuple-element.74), channel_id=1, source_target_pairs={{0,24},{1,7},{2,26},{3,1},{4,28},{5,3},{6,30},{7,5},{8,0},{9,15},{... | collective-permute-start | bytes 786440 | tf_op jit(solution)/shard_map/ppermute | solution.py:48
  119.1 9.2 %collective-permute-start.21 = (bf16[128,2048]{1,0:T(8,128)(2,1)S(1)}, bf16[128,2048]{1,0:T(8,128)(2,1)S(1)}, u32[]{:S(2)}, u32[]{:S(2)}) collective-permute-start(bf16[128,2048]{1,0:T(8,128)(2,1)S(1)} %fusion.10), channel_id=1, source_target_pairs={{0,96},{1,33},{2,98},{3,35},{4,100},{5,37},{6,102},{7,39},{8,104},... | collective-permute-start | bytes 1572872 | tf_op jit(solution)/shard_map/ppermute | solution.py:48
  (7 other events, 10.4 us)

commit v3 on v2

--- a/solution.py
+++ b/solution.py
@@ -12,7 +12,7 @@
 F32 = jnp.float32
 WIDTH = 2048
 VMEM = pl.BlockSpec(memory_space=pltpu.VMEM)
-SMEM = pl.BlockSpec(memory_space=pltpu.SMEM)
+ANY = pl.BlockSpec(memory_space=pl.ANY)
 
 
 def index(y, x, z, c):
@@ -56,14 +56,14 @@
     return jnp.concatenate(v, axis=0)
 
 
-def call(kernel, outs, specs, flops=0, nbytes=0, scratch=()):
+def call(kernel, outs, specs, flops=0, nbytes=0, scratch=(), limit=16):
     return pl.pallas_call(
         kernel,
         out_shape=outs,
         in_specs=specs,
         out_specs=jax.tree.map(lambda _: VMEM, outs),
         scratch_shapes=scratch,
-        compiler_params=pltpu.CompilerParams(vmem_limit_bytes=32 * 2**20),
+        compiler_params=pltpu.CompilerParams(vmem_limit_bytes=limit * 2**20),
         cost_estimate=pl.CostEstimate(flops=flops, bytes_accessed=nbytes, transcendentals=0),
     )
 
@@ -72,20 +72,33 @@
     return jax.ShapeDtypeStruct((r, c), t)
 
 
-def pack_kernel(q_ref, owner_ref, row_ref, pos_ref, out_ref):
-    out_ref[0:128, :] = q_ref[...]
-
-    def turned(ref):
-        wide = jnp.concatenate([ref[...], jnp.zeros((128, 112), jnp.int32)], axis=1).astype(F32)
-        return jnp.transpose(wide)[0:16]
-
-    pos = pos_ref[...]
-    high = (pos // 64).astype(F32)
-    low = (pos % 64).astype(F32)
+def pack_kernel(q_ref, owner_ref, row_ref, pos_ref, p_ref, out_ref, kept_ref, owner, row, pos, sems):
+    copies = []
+    for i, (src, dst) in enumerate(
+        ((owner_ref, owner), (row_ref, row), (pos_ref, pos), (q_ref, out_ref.at[0:128, :]), (p_ref, kept_ref))
+    ):
+        copies.append(pltpu.make_async_copy(src, dst, sems.at[i]))
+        copies[-1].start()
+    out_ref[128:144, 384:WIDTH] = jnp.zeros((16, WIDTH - 384), BF)
+    for c in copies[:3]:
+        c.wait()
+    high = (pos[...] // 64).astype(F32)
+    low = (pos[...] % 64).astype(F32)
     third = jnp.concatenate([high, low, jnp.zeros((14, 128), F32)], axis=0)
-    meta = jnp.concatenate([turned(owner_ref), turned(row_ref), third], axis=1)
+    meta = jnp.concatenate([owner[...].astype(F32), row[...].astype(F32), third], axis=1)
     out_ref[128:144, 0:384] = meta.astype(BF)
-    out_ref[128:144, 384:WIDTH] = jnp.zeros((16, WIDTH - 384), BF)
+    copies[3].wait()
+    copies[4].wait()
+
+
+def join_kernel(*refs):
+    for i, r in enumerate(refs[:4]):
+        refs[4][64 * i : 64 * i + 64, :] = r[...]
+
+
+def whereabouts():
+    dp = lax.axis_index("dp")
+    return lax.axis_index("group"), dp // 8, lax.rem(dp // 2, 4), lax.rem(dp, 2)
 
 
 def owner_id(place, piece, k1):
@@ -95,7 +108,6 @@
     return (lax.rem(x - kx + 4, 4) * 4 + lax.rem(z - kz + 4, 4)) * 2 + core
 
 
-ORDER = {0: 0, 1: 1, 3: 2}
 PIECES = (0, 1, 2, 3)
 
 
@@ -151,31 +163,27 @@
     return write
 
 
-def early_kernel(place_ref, *refs):
-    p_refs, q_refs, ts, info = refs[0:3], refs[3:9], refs[9:12], refs[12]
-    place = [place_ref[i] for i in range(4)]
+def early_kernel(*refs):
+    p_refs, q_refs, ts, info = refs[0:4], refs[4:10], refs[10:14], refs[14]
+    place = whereabouts()
     p = jnp.concatenate([r[...] for r in p_refs], axis=0)
     for pair in range(3):
         a, b = q_refs[2 * pair], q_refs[2 * pair + 1]
         raw = product(p, a, b)
-        for i, piece in enumerate((0, 1, 3)):
-            score_block(
-                place, piece, pair, a, b, raw[256 * i : 256 * i + 256], ts[i], writer(info, 16 * i, 256 * pair)
-            )
+        for i in PIECES:
+            part = raw[256 * i : 256 * i + 256]
+            score_block(place, i, pair, a, b, part, ts[i], writer(info, 16 * i, 256 * pair))
 
 
 class Info:
-    def __init__(self, a, b, c):
-        self.refs = a, b, c
+    def __init__(self, a, b):
+        self.refs = a, b
 
     def rows(self, piece, pair, first, last):
-        a, b, c = self.refs
-        cols = slice(256 * pair, 256 * pair + 256)
-        if piece == 2:
-            return c[first:last, cols]
-        i = 16 * ORDER[piece]
+        a, b = self.refs
+        i = 16 * piece
         if pair < 3:
-            return a[i + first : i + last, cols]
+            return a[i + first : i + last, 256 * pair : 256 * pair + 256]
         return b[i + first : i + last, 0:256]
 
 
@@ -189,21 +197,15 @@
     return v[0:1], v[1:2], v[2:3]
 
 
-def late_kernel(place_ref, *refs):
-    p_refs, low, high, q_refs, info_a = refs[0:3], refs[3], refs[4], refs[5:13], refs[13]
-    t_ref, info_b, info_c, stats_ref = refs[14:]
-    place = [place_ref[i] for i in range(4)]
-    far = jnp.concatenate([low[...], high[...]], axis=0)
-    for pair in range(4):
-        a, b = q_refs[2 * pair], q_refs[2 * pair + 1]
-        raw = product(far, a, b)
-        score_block(place, 2, pair, a, b, raw, t_ref, writer(info_c, 0, 256 * pair))
+def late_kernel(*refs):
+    p_refs, q_refs, info_a, info_b, stats_ref = refs[0:4], refs[4:6], refs[6], refs[7], refs[8]
+    place = whereabouts()
     p = jnp.concatenate([r[...] for r in p_refs], axis=0)
-    a, b = q_refs[6], q_refs[7]
-    raw = product(p, a, b)
-    for i, piece in enumerate((0, 1, 3)):
-        score_block(place, piece, 3, a, b, raw[256 * i : 256 * i + 256], None, writer(info_b, 16 * i, 0))
-    info = Info(info_a, info_b, info_c)
+    raw = product(p, q_refs[0], q_refs[1])
+    for i in PIECES:
+        part = raw[256 * i : 256 * i + 256]
+        score_block(place, i, 3, q_refs[0], q_refs[1], part, None, writer(info_b, 16 * i, 0))
+    info = Info(info_a, info_b)
     for pair in range(4):
         acc = unpack(info.rows(0, pair, 8, 11))
         for piece in (1, 2, 3):
@@ -212,7 +214,7 @@
 
 
 def query_kernel(half, *refs):
-    ts, infos, stats, p_refs, out_ref, turned = refs[0:4], refs[4:7], refs[7], refs[8:13], refs[13], refs[14]
+    ts, infos, stats, p_refs, out_ref, turned = refs[0:4], refs[4:6], refs[6], refs[7:11], refs[12], refs[13]
     info = Info(*infos)
     step = steps(128)
     side = slice(128 * half, 128 * half + 128)
@@ -244,6 +246,37 @@
     return jnp.concatenate([v[:, 128 * (i ^ 1) : 128 * (i ^ 1) + 128] for i in range(8)], axis=1)
 
 
+def merge_kernel(raw, other, out_ref):
+    both = merge(unpack(raw[...]), unpack(swap(other[...])))
+    out_ref[...] = jnp.concatenate([*both, jnp.zeros((5, 1024), F32)], axis=0)
+
+
+def block_kernel(k, mine, theirs, factor, *refs):
+    out_ref = refs[-1]
+    rows = slice(128 * k, 128 * k + 128)
+    f = factor[...]
+    for n in range(4):
+        cols = slice(512 * n, 512 * n + 512)
+        v = mine[rows, cols] * f[:, k : k + 1] + theirs[rows, cols].astype(F32) * f[:, 4 + k : 5 + k]
+        if k == 0:
+            v = v + (mine[512:640, cols] + theirs[512:640, cols].astype(F32)) * f[:, 8:9]
+        if k < 3:
+            v = v + refs[0][:, cols].astype(F32)
+        out_ref[:, cols] = v.astype(BF)
+
+
+def gather_kernel(zero, one, two, three, *outs):
+    for k in range(4):
+        rows = slice(64 * k, 64 * k + 64)
+        v = zero[rows] + two[rows].astype(F32) + (one[rows].astype(F32) + three[rows].astype(F32))
+        outs[k][...] = v.astype(outs[k].dtype)
+
+
+def last_kernel(a, b, c, d, _, out_ref):
+    v = a[...] + c[...].astype(F32) + (b[...].astype(F32) + d[...].astype(F32))
+    out_ref[...] = v.astype(BF)
+
+
 def total_kernel(raw, other, stats, g1, g2, g3, lse_ref, loss_ref, factor_ref):
     acc = unpack(stats[...])
     for t, got in ((1, g1), (2, g2), (3, g3)):
@@ -283,20 +316,18 @@
 
 
 def far_kernel(t_ref, *refs):
-    infos, lse_ref, q_refs = refs[0:3], refs[3], refs[4:12]
-    low_ref, high_ref, c = refs[12:]
+    infos, lse_ref, q_refs = refs[0:2], refs[2], refs[3:11]
+    out_ref, c = refs[11:]
     coefficients(Info(*infos), 2, t_ref, lse_ref, c, 0)
     for n in range(4):
         cols = slice(512 * n, 512 * n + 512)
         q = jnp.concatenate([r[0:128, cols] for r in q_refs], axis=0)
-        g = jnp.dot(c[...], q, preferred_element_type=F32).astype(BF)
-        low_ref[:, cols] = g[0:128]
-        high_ref[:, cols] = g[128:256]
+        out_ref[:, cols] = jnp.dot(c[...], q, preferred_element_type=F32).astype(BF)
 
 
 def near_kernel(*refs):
-    ts, infos, lse_ref, q_refs = refs[0:3], refs[3:6], refs[6], refs[7:15]
-    zero, one_low, one_high, three_low, three_high, c = refs[15:]
+    ts, infos, lse_ref, q_refs = refs[0:3], refs[3:5], refs[5], refs[6:14]
+    zero, one, three, c = refs[15:]
     info = Info(*infos)
     for i, piece in enumerate((0, 1, 3)):
         coefficients(info, piece, ts[i], lse_ref, c, 256 * i)
@@ -305,67 +336,63 @@
         q = jnp.concatenate([r[0:128, cols] for r in q_refs], axis=0)
         g = jnp.dot(c[...], q, preferred_element_type=F32)
         zero[:, cols] = g[0:256]
-        one_low[:, cols] = g[256:384]
-        one_high[:, cols] = g[384:512].astype(BF)
-        three_low[:, cols] = g[512:640].astype(BF)
-        three_high[:, cols] = g[640:768]
+        one[:, cols] = g[256:512].astype(BF)
+        three[:, cols] = g[512:768].astype(BF)
 
 
 def local(question_vectors, passages, positive, hard_owner, hard_row):
-    group = lax.axis_index("group")
-    dp = lax.axis_index("dp")
-    place = jnp.stack([group, dp // 8, dp // 2 % 4, dp % 2]).astype(jnp.int32)
-
-    packed = call(pack_kernel, shape(144, WIDTH, BF), [VMEM] * 4)(
-        question_vectors, hard_owner, hard_row, positive.reshape(1, 128)
-    )
+    packed, kept = call(
+        pack_kernel,
+        (shape(144, WIDTH, BF), shape(64, WIDTH, BF)),
+        [ANY] * 5,
+        scratch=[
+            pltpu.VMEM((16, 128), jnp.int32),
+            pltpu.VMEM((16, 128), jnp.int32),
+            pltpu.VMEM((1, 128), jnp.int32),
+            pltpu.SemaphoreType.DMA((5,)),
+        ],
+        limit=56,
+    )(question_vectors, hard_owner.T, hard_row.T, positive.reshape(1, 128), passages)
 
     back = send(passages, first(1))
     ahead = send(passages, first(-1))
     across = send(passages, first(2))
     q1 = send(packed, along(1))
     s0 = send(packed, CORE)
-    back, ahead, across, q1 = tied(back, ahead, across, q1)
-    plane = join(passages, back, across, ahead)
+    back, ahead, across, q1, s0 = tied(back, ahead, across, q1, s0)
+    plane = call(join_kernel, shape(256, WIDTH, BF), [VMEM] * 4)(kept, back, across, ahead)
     up = send(plane, second(1))
     down = send(plane, second(-1))
+    over = send(plane, second(2))
     q2 = send(q1, along(1))
     s1 = send(q1, CORE)
-    up, down, q2 = tied(up, down, q2)
-    low = send(up[:128], second(1))
-    high = send(down[128:], second(-1))
     q3 = send(q2, along(1))
     s2 = send(q2, CORE)
-    low, high, q3 = tied(low, high, q3)
     s3 = send(q3, CORE)
     tiles = (packed, s0, q1, s1, q2, s2, q3, s3)
 
-    t0, t1, t3, info_a = call(
-        early_kernel,
-        (shape(256, 256, F32), shape(256, 256, F32), shape(256, 256, F32), shape(48, 768, F32)),
-        [SMEM] + [VMEM] * 9,
-        2 * 768 * 768 * WIDTH,
-    )(place, plane, up, down, *tiles[:6])
-    t2, info_b, info_c, raw = call(
-        late_kernel,
-        (shape(256, 256, F32), shape(48, 256, F32), shape(16, 1024, F32), shape(8, 1024, F32)),
-        [SMEM] + [VMEM] * 14,
-        2 * 448 * 1024 * WIDTH,
-    )(place, plane, up, down, low, high, *tiles, info_a)
+    pieces = (plane, up, over, down)
+    tile = shape(256, 256, F32)
+    t0, t1, t2, t3, info_a = call(
+        early_kernel, (tile, tile, tile, tile, shape(64, 768, F32)), [VMEM] * 10, 2 * 1024 * 768 * WIDTH
+    )(*pieces, *tiles[:6])
+    info_b, raw = call(
+        late_kernel, (shape(64, 256, F32), shape(8, 1024, F32)), [VMEM] * 7, 2 * 1024 * 256 * WIDTH
+    )(*pieces, *tiles[6:], info_a)
 
     other = send(raw, CORE)
-    stats = jnp.concatenate([*merge(unpack(raw), unpack(swap(other))), jnp.zeros((5, 1024), F32)], axis=0)
+    stats = call(merge_kernel, shape(8, 1024, F32), [VMEM] * 2)(raw, other)
     g1 = send(stats, along(1))
     g2 = send(stats, along(2))
     g3 = send(stats, along(3))
-    infos = (info_a, info_b, info_c)
-    operands = (t0, t1, t2, t3, *infos, raw, plane, up, low, high, down)
+    infos = (info_a, info_b)
+    operands = (t0, t1, t2, t3, *infos, raw, *pieces, stats)
 
     def query(half, kind):
         return call(
             lambda *r: query_kernel(half, *r),
             shape(640, WIDTH, kind),
-            [VMEM] * 13,
+            [VMEM] * 12,
             2 * 640 * 1024 * WIDTH,
             scratch=[pltpu.VMEM((640, 1024), BF)],
         )(*operands)
@@ -376,47 +403,35 @@
         total_kernel, (shape(8, 1024, F32), shape(8, 128, F32), shape(128, 128, F32)), [VMEM] * 6
     )(raw, other, stats, g1, g2, g3)
 
-    two_low, two_high = call(
-        far_kernel,
-        (shape(128, WIDTH, BF), shape(128, WIDTH, BF)),
-        [VMEM] * 13,
-        2 * 256 * 1024 * WIDTH,
-        scratch=[pltpu.VMEM((256, 1024), BF)],
-    )(t2, *infos, lse, *tiles)
-    from_high = send(two_low, second(-1))
-    from_low = send(two_high, second(1))
-
-    def block(k):
-        a = mine[128 * k : 128 * k + 128] * factor[:, k : k + 1]
-        return a + theirs[128 * k : 128 * k + 128].astype(F32) * factor[:, 4 + k : 5 + k]
+    far = call(far_kernel, shape(256, WIDTH, BF), [VMEM] * 12, 2 * 256 * 1024 * WIDTH, scratch=[pltpu.VMEM((256, 1024), BF)])(
+        t2, *infos, lse, *tiles
+    )
+    two = send(far, second(2))
+
+    def block(k, *got):
+        kernel = lambda *r: block_kernel(k, *r)
+        return call(kernel, shape(128, WIDTH, BF), [VMEM] * (3 + len(got)))(mine, theirs, factor, *got)
 
     run = block(3)
     for k in (2, 1, 0):
-        run = block(k) + send(run.astype(BF), along(-1)).astype(F32)
-    query_grad = run + (mine[512:640] + theirs[512:640].astype(F32)) * factor[:, 8:9]
-
-    zero, one_low, one_high, three_low, three_high = call(
+        run = block(k, send(run, along(-1)))
+
+    zero, one, three = call(
         near_kernel,
-        (
-            shape(256, WIDTH, F32),
-            shape(128, WIDTH, F32),
-            shape(128, WIDTH, BF),
-            shape(128, WIDTH, BF),
-            shape(128, WIDTH, F32),
-        ),
+        (shape(256, WIDTH, F32), shape(256, WIDTH, BF), shape(256, WIDTH, BF)),
         [VMEM] * 15,
         2 * 768 * 1024 * WIDTH,
         scratch=[pltpu.VMEM((768, 1024), BF)],
-    )(t0, t1, t3, *infos, lse, *tiles)
-    r1b = send(one_high, second(-1))
-    r3a = send(three_low, second(1))
-    r1a = send((one_low + from_high.astype(F32)).astype(BF), second(-1))
-    r3b = send((three_high + from_low.astype(F32)).astype(BF), second(1))
-    g = zero + (join(r1a.astype(F32), r1b.astype(F32)) + join(r3a.astype(F32), r3b.astype(F32)))
-    passage_grad = g[0:64]
-    for k, d in ((2, 2), (1, -1), (3, 1)):
-        passage_grad = passage_grad + send(g[64 * k : 64 * k + 64].astype(BF), first(d)).astype(F32)
-    return loss[0], query_grad.astype(BF), passage_grad.astype(BF)
+    )(t0, t1, t3, *infos, lse, *tiles, far)
+    one = send(one, second(-1))
+    three = send(three, second(1))
+    half = shape(64, WIDTH, BF)
+    g0, g1, g2, g3 = call(gather_kernel, (shape(64, WIDTH, F32), half, half, half), [VMEM] * 4)(zero, one, two, three)
+    g2 = send(g2, first(2))
+    g1 = send(g1, first(-1))
+    g3 = send(g3, first(1))
+    passage_grad = call(last_kernel, half, [VMEM] * 5)(g0, g1, g2, g3, run)
+    return loss[0], run, passage_grad
 
 
 def solution(mesh):

time: 130 us -> 120 us (0.923)
  local copies, waits for them, and re-layouts: 9.31 us -> 3.57 us
  waiting for transfers between devices: 56.2 us -> 60.1 us
  other arithmetic: 3.79 us -> 0 us
  Pallas kernels: 24.1 us -> 21.9 us
  starting transfers between devices: 35.2 us -> 33.6 us
    unnamed x28 -> x8, local copies, waits for them, and re-layouts: 8.14 us -> 3.06 us
    ppermute x31 -> x27, waiting for transfers between devices: 56.2 us -> 60.1 us  [send(): return lax.ppermute(v, AXES, perm)]
    convert_element_type x7 -> x0, other arithmetic: 3.06 us -> none  [the longest x2 2.05 us: local(): return (loss[0], query_grad.astype(BF), passage_grad.astype(BF))]
    pallas_call x5 -> x13, Pallas kernels: 18 us -> 15.9 us  [the longest x1 4.1 us: local(): call(early_kernel, (tile, tile, tile, tile, shape(64, 768, F32)), [VMEM]...]
    ppermute x31 -> x27, starting transfers between devices: 35.2 us -> 33.6 us  [send(): return lax.ppermute(v, AXES, perm)]
  transfers between devices with their start and end apart: 31 -> 27, of which waited for: 15 -> 15; matrix products, arithmetic and copies ran while one was open for 4% -> 0% of each run, Pallas kernels for 15% -> 12%
where the time goes in v3:
time: 120 us
  waiting for transfers between devices  60.1 us (50%)
  starting transfers between devices  33.6 us (28%)
  Pallas kernels  21.9 us (18%)
  local copies, waits for them, and re-layouts  3.57 us (3%)
    ppermute x27, waiting for transfers between devices, send(): return lax.ppermute(v, AXES, perm)  60.1 us
    ppermute x27, starting transfers between devices, send(): return lax.ppermute(v, AXES, perm)  33.6 us
    pallas_call x2, Pallas kernels, query(): call(lambda *r: query_kernel(half, *r), shape(640, WIDTH, kind), [VMEM] *...  5.9 us
    pallas_call x1, Pallas kernels, local(): call(early_kernel, (tile, tile, tile, tile, shape(64, 768, F32)), [VMEM]...  4.1 us
    pallas_call x1, Pallas kernels, local(): call(near_kernel, (shape(256, WIDTH, F32), shape(256, WIDTH, BF), shape(2...  3.51 us
    unnamed x8, local copies, waits for them, and re-layouts  3.06 us
  transfers between devices with their start and end apart: 27, of which 15 were waited for; matrix products, arithmetic and copies ran while one was open for 0% of the time, Pallas kernels for 12%

profile of v3, /device:TPU:0, one launch (start us, length us, event | category | flops | bytes accessed | tf_op | source)
XLA Modules:
  0.0 120.0 jit_solution(10853174412672605159)
XLA Ops:
  0.6 2.1 %shard_map.76 = (bf16[144,2048]{1,0:T(8,128)(2,1)}, bf16[64,2048]{1,0:T(8,128)(2,1)}) custom-call(bf16[128,2048]{1,0:T(8,128)(2,1)} %q_ref.1, s32[16,128]{1,0:T(8,128)} %bitcast.5, s32[16,128]{1,0:T(8,128)} %bitcast.6, s32[1,128]{1,0:T(1,128)} %bitcast.7, bf16[64,2048]{1,0:T(8,128)(2,1)} %p_ref.1), custom_call_target="tpu_custom_call" | custom-call | tf_op jit(solution)/shard_map/pallas_call | solution.py:344
  2.8 1.7 %collective-permute-start.3 = (bf16[144,2048]{1,0:T(8,128)(2,1)}, bf16[144,2048]{1,0:T(8,128)(2,1)S(1)}, u32[]{:S(2)}, u32[]{:S(2)}) collective-permute-start(bf16[144,2048]{1,0:T(8,128)(2,1)} %get-tuple-element.28.refs_4_.refs_3_.refs_6_), channel_id=1, source_target_pairs={{0,32},{1,97},{2,34},{3,99},{4,36},{5,101},{6,38},{7,103},{8,40},{... | collective-permute-start | bytes 1769480 | tf_op jit(solution)/shard_map/ppermute | solution.py:48
  4.6 1.5 %collective-permute-start = (bf16[64,2048]{1,0:T(8,128)(2,1)}, bf16[64,2048]{1,0:T(8,128)(2,1)S(1)}, u32[]{:S(2)}, u32[]{:S(2)}) collective-permute-start(bf16[64,2048]{1,0:T(8,128)(2,1)} %p_ref.1), channel_id=1, source_target_pairs={{0,8},{1,3},{2,10},{3,5},{4,12},{5,7},{6,14},{7,1},{8,16},{9,11},{... | collective-permute-start | bytes 786440 | tf_op jit(solution)/shard_map/ppermute | solution.py:48
  6.0 2.7 %collective-permute-start.2 = (bf16[64,2048]{1,0:T(8,128)(2,1)}, bf16[64,2048]{1,0:T(8,128)(2,1)S(1)}, u32[]{:S(2)}, u32[]{:S(2)}) collective-permute-start(bf16[64,2048]{1,0:T(8,128)(2,1)} %p_ref.1), channel_id=1, source_target_pairs={{0,16},{1,5},{2,18},{3,7},{4,20},{5,1},{6,22},{7,3},{8,24},{9,13},... | collective-permute-start | bytes 786440 | tf_op jit(solution)/shard_map/ppermute | solution.py:48
  8.8 1.4 %collective-permute-start.1 = (bf16[64,2048]{1,0:T(8,128)(2,1)}, bf16[64,2048]{1,0:T(8,128)(2,1)S(1)}, u32[]{:S(2)}, u32[]{:S(2)}) collective-permute-start(bf16[64,2048]{1,0:T(8,128)(2,1)} %p_ref.1), channel_id=1, source_target_pairs={{0,24},{1,7},{2,26},{3,1},{4,28},{5,3},{6,30},{7,5},{8,0},{9,15},{... | collective-permute-start | bytes 786440 | tf_op jit(solution)/shard_map/ppermute | solution.py:48
  10.2 2.1 %collective-permute-done.refs_1_ = bf16[64,2048]{1,0:T(8,128)(2,1)S(1)} collective-permute-done((bf16[64,2048]{1,0:T(8,128)(2,1)}, bf16[64,2048]{1,0:T(8,128)(2,1)S(1)}, u32[]{:S(2)}, u32[]{:S(2)}) %collective-permute-start) | collective-permute-done | bytes 262176 | tf_op jit(solution)/shard_map/ppermute | solution.py:48
  12.4 3.8 %collective-permute-done.2.refs_2_ = bf16[64,2048]{1,0:T(8,128)(2,1)S(1)} collective-permute-done((bf16[64,2048]{1,0:T(8,128)(2,1)}, bf16[64,2048]{1,0:T(8,128)(2,1)S(1)}, u32[]{:S(2)}, u32[]{:S(2)}) %collective-permute-start.2) | collective-permute-done | bytes 262176 | tf_op jit(solution)/shard_map/ppermute | solution.py:48
  16.2 1.6 %collective-permute-start.8 = (bf16[144,2048]{1,0:T(8,128)(2,1)S(1)}, bf16[144,2048]{1,0:T(8,128)(2,1)S(1)}, u32[]{:S(2)}, u32[]{:S(2)}) collective-permute-start(bf16[144,2048]{1,0:T(8,128)(2,1)S(1)} %collective-permute-done.3.refs_6_.refs_5_.refs_8_), channel_id=1, source_target_pairs={{0,32},{1,97},{2,34},{3,99},{4,36},{5,101},{6,38},{7,103},{8,40},{... | collective-permute-start | bytes 1769480 | tf_op jit(solution)/shard_map/ppermute | solution.py:48
  19.4 3.5 %collective-permute-start.7 = (bf16[256,2048]{1,0:T(8,128)(2,1)S(1)}, bf16[256,2048]{1,0:T(8,128)(2,1)S(1)}, u32[]{:S(2)}, u32[]{:S(2)}) collective-permute-start(bf16[256,2048]{1,0:T(8,128)(2,1)S(1)} %shard_map.77.refs_0_.r_7_), channel_id=1, source_target_pairs={{0,6},{1,25},{2,0},{3,27},{4,2},{5,29},{6,4},{7,31},{8,14},{9,1},{... | collective-permute-start | bytes 3145736 | tf_op jit(solution)/shard_map/ppermute | solution.py:48
  24.2 3.1 %collective-permute-done.8.refs_8_.refs_7_.refs_10_ = bf16[144,2048]{1,0:T(8,128)(2,1)S(1)} collective-permute-done((bf16[144,2048]{1,0:T(8,128)(2,1)S(1)}, bf16[144,2048]{1,0:T(8,128)(2,1)S(1)}, u32[]{:S(2)}, u32[]{:S(2)}) %collective-permute-start.8) | collective-permute-done | bytes 589856 | tf_op jit(solution)/shard_map/ppermute | solution.py:48
  28.4 10.1 %collective-permute-done.9.refs_4_.refs_9_.refs_12_ = bf16[144,2048]{1,0:T(8,128)(2,1)S(1)} collective-permute-done((bf16[144,2048]{1,0:T(8,128)(2,1)S(1)}, bf16[144,2048]{1,0:T(8,128)(2,1)S(1)}, u32[]{:S(2)}, u32[]{:S(2)}) %collective-permute-start.9) | collective-permute-done | bytes 589856 | tf_op jit(solution)/shard_map/ppermute | solution.py:48
  38.4 8.1 %collective-permute-done.7.refs_3_.r_10_ = bf16[256,2048]{1,0:T(8,128)(2,1)S(1)} collective-permute-done((bf16[256,2048]{1,0:T(8,128)(2,1)S(1)}, bf16[256,2048]{1,0:T(8,128)(2,1)S(1)}, u32[]{:S(2)}, u32[]{:S(2)}) %collective-permute-start.7) | collective-permute-done | bytes 1048608 | tf_op jit(solution)/shard_map/ppermute | solution.py:48
  46.5 3.7 %collective-permute-done.5.refs_1_.r_8_ = bf16[256,2048]{1,0:T(8,128)(2,1)S(1)} collective-permute-done((bf16[256,2048]{1,0:T(8,128)(2,1)S(1)}, bf16[256,2048]{1,0:T(8,128)(2,1)S(1)}, u32[]{:S(2)}, u32[]{:S(2)}) %collective-permute-start.5) | collective-permute-done | bytes 1048608 | tf_op jit(solution)/shard_map/ppermute | solution.py:48
  51.3 4.1 %shard_map.78 = (f32[256,256]{1,0:T(8,128)S(1)}, f32[256,256]{1,0:T(8,128)S(1)}, f32[256,256]{1,0:T(8,128)S(1)}, f32[256,256]{1,0:T(8,128)S(1)}, f32[64,768]{1,0:T(8,128)S(1)}) custom-call(bf16[256,2048]{1,0:T(8,128)(2,1)S(1)} %shard_map.77.refs_0_.r_7_, bf16[256,2048]{1,0:T(8,128)(2,1)S(1)} %collective-permute-done.5.refs_1_.r_8_, ...), custom_call_target="tpu_custom_call" | custom-call | flops 3221225472 | tf_op jit(solution)/shard_map/pallas_call | solution.py:376
  55.4 1.4 %shard_map.79 = (f32[64,256]{1,0:T(8,128)S(1)}, f32[8,1024]{1,0:T(8,128)S(1)}) custom-call(bf16[256,2048]{1,0:T(8,128)(2,1)S(1)} %shard_map.77.refs_0_.r_7_, bf16[256,2048]{1,0:T(8,128)(2,1)S(1)} %collective-permute-done.5.refs_1_.r_8_, bf16[256,2048]{1,0:T(8,128)(2,1)S(1)} %collective-permute-done.6.refs_2_.r_9_, ...), custom_call_target="tpu_custom_call" | custom-call | flops 1073741824 | tf_op jit(solution)/shard_map/pallas_call | solution.py:379
  58.1 3.0 %shard_map.83 = bf16[640,2048]{1,0:T(8,128)(2,1)S(1)} custom-call(f32[256,256]{1,0:T(8,128)S(1)} %get-tuple-element.37.r_0_.refs_0_, f32[256,256]{1,0:T(8,128)S(1)} %get-tuple-element.38.r_1_.refs_1_, f32[256,256]{1,0:T(8,128)S(1)} %get-tuple-element.39.r_2_.t_ref, f32[256,256]{1,0:T(8,128)S(1)} %get-tuple-element.40.r_3_.refs_2_, ...), custom_call_target="tpu_custom_call" | custom-call | flops 2684354560 | tf_op jit(solution)/shard_map/pallas_call | solution.py:392
  61.3 1.8 %collective-permute-start.16 = (f32[8,1024]{1,0:T(8,128)S(1)}, f32[8,1024]{1,0:T(8,128)S(1)}, u32[]{:S(2)}, u32[]{:S(2)}) collective-permute-start(f32[8,1024]{1,0:T(8,128)S(1)} %shard_map.80.stats.r_11_), channel_id=1, source_target_pairs={{0,96},{1,33},{2,98},{3,35},{4,100},{5,37},{6,102},{7,39},{8,104},... | collective-permute-start | bytes 98312 | tf_op jit(solution)/shard_map/ppermute | solution.py:48
  63.1 1.7 %collective-permute-start.15 = (f32[8,1024]{1,0:T(8,128)S(1)}, f32[8,1024]{1,0:T(8,128)S(1)}, u32[]{:S(2)}, u32[]{:S(2)}) collective-permute-start(f32[8,1024]{1,0:T(8,128)S(1)} %shard_map.80.stats.r_11_), channel_id=1, source_target_pairs={{0,64},{1,65},{2,66},{3,67},{4,68},{5,69},{6,70},{7,71},{8,72},{9,... | collective-permute-start | bytes 98312 | tf_op jit(solution)/shard_map/ppermute | solution.py:48
  64.7 2.9 %shard_map.82.r_0_ = f32[640,2048]{1,0:T(8,128)S(1)} custom-call(f32[256,256]{1,0:T(8,128)S(1)} %get-tuple-element.37.r_0_.refs_0_, f32[256,256]{1,0:T(8,128)S(1)} %get-tuple-element.38.r_1_.refs_1_, f32[256,256]{1,0:T(8,128)S(1)} %get-tuple-element.39.r_2_.t_ref, f32[256,256]{1,0:T(8,128)S(1)} %get-tuple-element.40.r_3_.refs_2_, ...), custom_call_target="tpu_custom_call" | custom-call | flops 2684354560 | tf_op jit(solution)/shard_map/pallas_call | solution.py:392
  68.5 1.4 %collective-permute-done.14.g1 = f32[8,1024]{1,0:T(8,128)S(1)} collective-permute-done((f32[8,1024]{1,0:T(8,128)S(1)}, f32[8,1024]{1,0:T(8,128)S(1)}, u32[]{:S(2)}, u32[]{:S(2)}) %collective-permute-start.14) | collective-permute-done | bytes 32800 | tf_op jit(solution)/shard_map/ppermute | solution.py:48
  70.0 1.3 %shard_map.88.refs_14_ = bf16[256,2048]{1,0:T(8,128)(2,1)S(1)} custom-call(f32[256,256]{1,0:T(8,128)S(1)} %get-tuple-element.39.r_2_.t_ref, f32[64,768]{1,0:T(8,128)S(1)} %get-tuple-element.34.refs_6_.r_4_.refs_0_.refs_3_, f32[64,256]{1,0:T(8,128)S(1)} %get-tuple-element.41.r_5_.refs_1_.refs_4_, f32[8,1024]{1,0:T(8,128)S(1)} %get-tuple-element.43.refs_2_.refs_5_, ...), custom_call_target="tpu_custom_call" | custom-call | flops 1073741824 | tf_op jit(solution)/shard_map/pallas_call | solution.py:406
  72.8 3.5 %shard_map.89 = (f32[256,2048]{1,0:T(8,128)S(1)}, bf16[256,2048]{1,0:T(8,128)(2,1)S(1)}, bf16[256,2048]{1,0:T(8,128)(2,1)S(1)}) custom-call(f32[256,256]{1,0:T(8,128)S(1)} %get-tuple-element.37.r_0_.refs_0_, f32[256,256]{1,0:T(8,128)S(1)} %get-tuple-element.38.r_1_.refs_1_, f32[256,256]{1,0:T(8,128)S(1)} %get-tuple-element.40.r_3_.refs_2_, ...), custom_call_target="tpu_custom_call" | custom-call | flops 3221225472 | tf_op jit(solution)/shard_map/pallas_call | solution.py:419
  76.3 1.6 %collective-permute-start.21 = (bf16[256,2048]{1,0:T(8,128)(2,1)S(1)}, bf16[256,2048]{1,0:T(8,128)(2,1)S(1)}, u32[]{:S(2)}, u32[]{:S(2)}) collective-permute-start(bf16[256,2048]{1,0:T(8,128)(2,1)S(1)} %get-tuple-element.45), channel_id=1, source_target_pairs={{0,6},{1,25},{2,0},{3,27},{4,2},{5,29},{6,4},{7,31},{8,14},{9,1},{... | collective-permute-start | bytes 3145736 | tf_op jit(solution)/shard_map/ppermute | solution.py:48
  78.4 1.4 %collective-permute-start.22 = (bf16[256,2048]{1,0:T(8,128)(2,1)S(1)}, bf16[256,2048]{1,0:T(8,128)(2,1)S(1)}, u32[]{:S(2)}, u32[]{:S(2)}) collective-permute-start(bf16[256,2048]{1,0:T(8,128)(2,1)S(1)} %shard_map.88.refs_14_), channel_id=1, source_target_pairs={{0,4},{1,17},{2,6},{3,19},{4,0},{5,21},{6,2},{7,23},{8,12},{9,25},... | collective-permute-start | bytes 3145736 | tf_op jit(solution)/shard_map/ppermute | solution.py:48
  81.2 2.4 %collective-permute-start.19 = (bf16[128,2048]{1,0:T(8,128)(2,1)S(1)}, bf16[128,2048]{1,0:T(8,128)(2,1)S(1)}, u32[]{:S(2)}, u32[]{:S(2)}) collective-permute-start(bf16[128,2048]{1,0:T(8,128)(2,1)S(1)} %shard_map.85), channel_id=1, source_target_pairs={{0,96},{1,33},{2,98},{3,35},{4,100},{5,37},{6,102},{7,39},{8,104},... | collective-permute-start | bytes 1572872 | tf_op jit(solution)/shard_map/ppermute | solution.py:48
  83.6 6.9 %collective-permute-done.19.r_3_ = bf16[128,2048]{1,0:T(8,128)(2,1)S(1)} collective-permute-done((bf16[128,2048]{1,0:T(8,128)(2,1)S(1)}, bf16[128,2048]{1,0:T(8,128)(2,1)S(1)}, u32[]{:S(2)}, u32[]{:S(2)}) %collective-permute-start.19) | collective-permute-done | bytes 524320 | tf_op jit(solution)/shard_map/ppermute | solution.py:48
  90.8 3.6 %collective-permute-start.20 = (bf16[128,2048]{1,0:T(8,128)(2,1)S(1)}, bf16[128,2048]{1,0:T(8,128)(2,1)S(1)}, u32[]{:S(2)}, u32[]{:S(2)}) collective-permute-start(bf16[128,2048]{1,0:T(8,128)(2,1)S(1)} %shard_map.86), channel_id=1, source_target_pairs={{0,96},{1,33},{2,98},{3,35},{4,100},{5,37},{6,102},{7,39},{8,104},... | collective-permute-start | bytes 1572872 | tf_op jit(solution)/shard_map/ppermute | solution.py:48
  94.3 10.9 %collective-permute-done.23.three = bf16[256,2048]{1,0:T(8,128)(2,1)S(1)} collective-permute-done((bf16[256,2048]{1,0:T(8,128)(2,1)S(1)}, bf16[256,2048]{1,0:T(8,128)(2,1)S(1)}, u32[]{:S(2)}, u32[]{:S(2)}) %collective-permute-start.23) | collective-permute-done | bytes 1048608 | tf_op jit(solution)/shard_map/ppermute | solution.py:48
  105.6 1.9 %collective-permute-start.24 = (bf16[64,2048]{1,0:T(8,128)(2,1)S(1)}, bf16[64,2048]{1,0:T(8,128)(2,1)S(1)}, u32[]{:S(2)}, u32[]{:S(2)}) collective-permute-start(bf16[64,2048]{1,0:T(8,128)(2,1)S(1)} %get-tuple-element.48), channel_id=1, source_target_pairs={{0,24},{1,7},{2,26},{3,1},{4,28},{5,3},{6,30},{7,5},{8,0},{9,15},{... | collective-permute-start | bytes 786440 | tf_op jit(solution)/shard_map/ppermute | solution.py:48
  107.5 1.4 %collective-permute-start.25 = (bf16[64,2048]{1,0:T(8,128)(2,1)S(1)}, bf16[64,2048]{1,0:T(8,128)(2,1)S(1)}, u32[]{:S(2)}, u32[]{:S(2)}) collective-permute-start(bf16[64,2048]{1,0:T(8,128)(2,1)S(1)} %get-tuple-element.49), channel_id=1, source_target_pairs={{0,16},{1,5},{2,18},{3,7},{4,20},{5,1},{6,22},{7,3},{8,24},{9,13},... | collective-permute-start | bytes 786440 | tf_op jit(solution)/shard_map/ppermute | solution.py:48
  111.1 3.1 %collective-permute-done.24.b = bf16[64,2048]{1,0:T(8,128)(2,1)S(1)} collective-permute-done((bf16[64,2048]{1,0:T(8,128)(2,1)S(1)}, bf16[64,2048]{1,0:T(8,128)(2,1)S(1)}, u32[]{:S(2)}, u32[]{:S(2)}) %collective-permute-start.24) | collective-permute-done | bytes 262176 | tf_op jit(solution)/shard_map/ppermute | solution.py:48
  115.5 2.7 %collective-permute-done.26.d = bf16[64,2048]{1,0:T(8,128)(2,1)S(1)} collective-permute-done((bf16[64,2048]{1,0:T(8,128)(2,1)S(1)}, bf16[64,2048]{1,0:T(8,128)(2,1)S(1)}, u32[]{:S(2)}, u32[]{:S(2)}) %collective-permute-start.26) | collective-permute-done | bytes 262176 | tf_op jit(solution)/shard_map/ppermute | solution.py:48
  (47 shorter events, 16.8 us)
Async XLA Ops:
  2.7 13.4 %collective-permute-start.4 = (bf16[144,2048]{1,0:T(8,128)(2,1)}, bf16[144,2048]{1,0:T(8,128)(2,1)S(1)}, u32[]{:S(2)}, u32[]{:S(2)}) collective-permute-start(bf16[144,2048]{1,0:T(8,128)(2,1)} %get-tuple-element.28.refs_4_.refs_3_.refs_6_), channel_id=1, source_target_pairs={{0,1},{1,0},{2,3},{3,2},{4,5},{5,4},{6,7},{7,6},{8,9},{9,8},{10,11... | collective-permute-start | bytes 1769480 | tf_op jit(solution)/shard_map/ppermute | solution.py:48
  2.8 13.3 %collective-permute-start.3 = (bf16[144,2048]{1,0:T(8,128)(2,1)}, bf16[144,2048]{1,0:T(8,128)(2,1)S(1)}, u32[]{:S(2)}, u32[]{:S(2)}) collective-permute-start(bf16[144,2048]{1,0:T(8,128)(2,1)} %get-tuple-element.28.refs_4_.refs_3_.refs_6_), channel_id=1, source_target_pairs={{0,32},{1,97},{2,34},{3,99},{4,36},{5,101},{6,38},{7,103},{8,40},{... | collective-permute-start | bytes 1769480 | tf_op jit(solution)/shard_map/ppermute | solution.py:48
  4.6 7.8 %collective-permute-start = (bf16[64,2048]{1,0:T(8,128)(2,1)}, bf16[64,2048]{1,0:T(8,128)(2,1)S(1)}, u32[]{:S(2)}, u32[]{:S(2)}) collective-permute-start(bf16[64,2048]{1,0:T(8,128)(2,1)} %p_ref.1), channel_id=1, source_target_pairs={{0,8},{1,3},{2,10},{3,5},{4,12},{5,7},{6,14},{7,1},{8,16},{9,11},{... | collective-permute-start | bytes 786440 | tf_op jit(solution)/shard_map/ppermute | solution.py:48
  6.0 10.1 %collective-permute-start.2 = (bf16[64,2048]{1,0:T(8,128)(2,1)}, bf16[64,2048]{1,0:T(8,128)(2,1)S(1)}, u32[]{:S(2)}, u32[]{:S(2)}) collective-permute-start(bf16[64,2048]{1,0:T(8,128)(2,1)} %p_ref.1), channel_id=1, source_target_pairs={{0,16},{1,5},{2,18},{3,7},{4,20},{5,1},{6,22},{7,3},{8,24},{9,13},... | collective-permute-start | bytes 786440 | tf_op jit(solution)/shard_map/ppermute | solution.py:48
  8.8 7.4 %collective-permute-start.1 = (bf16[64,2048]{1,0:T(8,128)(2,1)}, bf16[64,2048]{1,0:T(8,128)(2,1)S(1)}, u32[]{:S(2)}, u32[]{:S(2)}) collective-permute-start(bf16[64,2048]{1,0:T(8,128)(2,1)} %p_ref.1), channel_id=1, source_target_pairs={{0,24},{1,7},{2,26},{3,1},{4,28},{5,3},{6,30},{7,5},{8,0},{9,15},{... | collective-permute-start | bytes 786440 | tf_op jit(solution)/shard_map/ppermute | solution.py:48
  16.2 11.2 %collective-permute-start.8 = (bf16[144,2048]{1,0:T(8,128)(2,1)S(1)}, bf16[144,2048]{1,0:T(8,128)(2,1)S(1)}, u32[]{:S(2)}, u32[]{:S(2)}) collective-permute-start(bf16[144,2048]{1,0:T(8,128)(2,1)S(1)} %collective-permute-done.3.refs_6_.refs_5_.refs_8_), channel_id=1, source_target_pairs={{0,32},{1,97},{2,34},{3,99},{4,36},{5,101},{6,38},{7,103},{8,40},{... | collective-permute-start | bytes 1769480 | tf_op jit(solution)/shard_map/ppermute | solution.py:48
  17.8 9.9 %collective-permute-start.11 = (bf16[144,2048]{1,0:T(8,128)(2,1)S(1)}, bf16[144,2048]{1,0:T(8,128)(2,1)S(1)}, u32[]{:S(2)}, u32[]{:S(2)}) collective-permute-start(bf16[144,2048]{1,0:T(8,128)(2,1)S(1)} %collective-permute-done.3.refs_6_.refs_5_.refs_8_), channel_id=1, source_target_pairs={{0,1},{1,0},{2,3},{3,2},{4,5},{5,4},{6,7},{7,6},{8,9},{9,8},{10,11... | collective-permute-start | bytes 1769480 | tf_op jit(solution)/shard_map/ppermute | solution.py:48
  18.4 0.9 copy-start.3
  19.4 27.1 %collective-permute-start.7 = (bf16[256,2048]{1,0:T(8,128)(2,1)S(1)}, bf16[256,2048]{1,0:T(8,128)(2,1)S(1)}, u32[]{:S(2)}, u32[]{:S(2)}) collective-permute-start(bf16[256,2048]{1,0:T(8,128)(2,1)S(1)} %shard_map.77.refs_0_.r_7_), channel_id=1, source_target_pairs={{0,6},{1,25},{2,0},{3,27},{4,2},{5,29},{6,4},{7,31},{8,14},{9,1},{... | collective-permute-start | bytes 3145736 | tf_op jit(solution)/shard_map/ppermute | solution.py:48
  22.9 23.6 %collective-permute-start.6 = (bf16[256,2048]{1,0:T(8,128)(2,1)S(1)}, bf16[256,2048]{1,0:T(8,128)(2,1)S(1)}, u32[]{:S(2)}, u32[]{:S(2)}) collective-permute-start(bf16[256,2048]{1,0:T(8,128)(2,1)S(1)} %shard_map.77.refs_0_.r_7_), channel_id=1, source_target_pairs={{0,4},{1,17},{2,6},{3,19},{4,0},{5,21},{6,2},{7,23},{8,12},{9,25},... | collective-permute-start | bytes 3145736 | tf_op jit(solution)/shard_map/ppermute | solution.py:48
  22.9 27.2 %collective-permute-start.5 = (bf16[256,2048]{1,0:T(8,128)(2,1)S(1)}, bf16[256,2048]{1,0:T(8,128)(2,1)S(1)}, u32[]{:S(2)}, u32[]{:S(2)}) collective-permute-start(bf16[256,2048]{1,0:T(8,128)(2,1)S(1)} %shard_map.77.refs_0_.r_7_), channel_id=1, source_target_pairs={{0,2},{1,9},{2,4},{3,11},{4,6},{5,13},{6,0},{7,15},{8,10},{9,17},{... | collective-permute-start | bytes 3145736 | tf_op jit(solution)/shard_map/ppermute | solution.py:48
  27.3 11.1 %collective-permute-start.9 = (bf16[144,2048]{1,0:T(8,128)(2,1)S(1)}, bf16[144,2048]{1,0:T(8,128)(2,1)S(1)}, u32[]{:S(2)}, u32[]{:S(2)}) collective-permute-start(bf16[144,2048]{1,0:T(8,128)(2,1)S(1)} %collective-permute-done.8.refs_8_.refs_7_.refs_10_), channel_id=1, source_target_pairs={{0,32},{1,97},{2,34},{3,99},{4,36},{5,101},{6,38},{7,103},{8,40},{... | collective-permute-start | bytes 1769480 | tf_op jit(solution)/shard_map/ppermute | solution.py:48
  27.7 22.5 %collective-permute-start.12 = (bf16[144,2048]{1,0:T(8,128)(2,1)S(1)}, bf16[144,2048]{1,0:T(8,128)(2,1)S(1)}, u32[]{:S(2)}, u32[]{:S(2)}) collective-permute-start(bf16[144,2048]{1,0:T(8,128)(2,1)S(1)} %collective-permute-done.8.refs_8_.refs_7_.refs_10_), channel_id=1, source_target_pairs={{0,1},{1,0},{2,3},{3,2},{4,5},{5,4},{6,7},{7,6},{8,9},{9,8},{10,11... | collective-permute-start | bytes 1769480 | tf_op jit(solution)/shard_map/ppermute | solution.py:48
  38.4 17.0 %collective-permute-start.10 = (bf16[144,2048]{1,0:T(8,128)(2,1)S(1)}, bf16[144,2048]{1,0:T(8,128)(2,1)S(1)}, u32[]{:S(2)}, u32[]{:S(2)}) collective-permute-start(bf16[144,2048]{1,0:T(8,128)(2,1)S(1)} %collective-permute-done.9.refs_4_.refs_9_.refs_12_), channel_id=1, source_target_pairs={{0,1},{1,0},{2,3},{3,2},{4,5},{5,4},{6,7},{7,6},{8,9},{9,8},{10,11... | collective-permute-start | bytes 1769480 | tf_op jit(solution)/shard_map/ppermute | solution.py:48
  50.2 1.1 copy-start.1
  56.8 1.3 %collective-permute-start.13 = (f32[8,1024]{1,0:T(8,128)S(1)}, f32[8,1024]{1,0:T(8,128)S(1)}, u32[]{:S(2)}, u32[]{:S(2)}) collective-permute-start(f32[8,1024]{1,0:T(8,128)S(1)} %get-tuple-element.35.raw.r_6_), channel_id=1, source_target_pairs={{0,1},{1,0},{2,3},{3,2},{4,5},{5,4},{6,7},{7,6},{8,9},{9,8},{10,11... | collective-permute-start | bytes 98312 | tf_op jit(solution)/shard_map/ppermute | solution.py:48
  61.0 9.0 %copy-start.2 = (bf16[144,2048]{1,0:T(8,128)(2,1)S(1)}, bf16[144,2048]{1,0:T(8,128)(2,1)}, u32[]{:S(2)}) copy-start(bf16[144,2048]{1,0:T(8,128)(2,1)} %get-tuple-element.28.refs_4_.refs_3_.refs_6_) | copy-start | bytes 1769476
  61.1 10.3 %collective-permute-start.17 = (bf16[640,2048]{1,0:T(8,128)(2,1)S(1)}, bf16[640,2048]{1,0:T(8,128)(2,1)S(1)}, u32[]{:S(2)}, u32[]{:S(2)}) collective-permute-start(bf16[640,2048]{1,0:T(8,128)(2,1)S(1)} %shard_map.83), channel_id=1, source_target_pairs={{0,1},{1,0},{2,3},{3,2},{4,5},{5,4},{6,7},{7,6},{8,9},{9,8},{10,11... | collective-permute-start | bytes 7864328 | tf_op jit(solution)/shard_map/ppermute | solution.py:48
  61.3 6.4 %collective-permute-start.16 = (f32[8,1024]{1,0:T(8,128)S(1)}, f32[8,1024]{1,0:T(8,128)S(1)}, u32[]{:S(2)}, u32[]{:S(2)}) collective-permute-start(f32[8,1024]{1,0:T(8,128)S(1)} %shard_map.80.stats.r_11_), channel_id=1, source_target_pairs={{0,96},{1,33},{2,98},{3,35},{4,100},{5,37},{6,102},{7,39},{8,104},... | collective-permute-start | bytes 98312 | tf_op jit(solution)/shard_map/ppermute | solution.py:48
  63.1 5.4 %collective-permute-start.15 = (f32[8,1024]{1,0:T(8,128)S(1)}, f32[8,1024]{1,0:T(8,128)S(1)}, u32[]{:S(2)}, u32[]{:S(2)}) collective-permute-start(f32[8,1024]{1,0:T(8,128)S(1)} %shard_map.80.stats.r_11_), channel_id=1, source_target_pairs={{0,64},{1,65},{2,66},{3,67},{4,68},{5,69},{6,70},{7,71},{8,72},{9,... | collective-permute-start | bytes 98312 | tf_op jit(solution)/shard_map/ppermute | solution.py:48
  64.7 5.1 %collective-permute-start.14 = (f32[8,1024]{1,0:T(8,128)S(1)}, f32[8,1024]{1,0:T(8,128)S(1)}, u32[]{:S(2)}, u32[]{:S(2)}) collective-permute-start(f32[8,1024]{1,0:T(8,128)S(1)} %shard_map.80.stats.r_11_), channel_id=1, source_target_pairs={{0,32},{1,97},{2,34},{3,99},{4,36},{5,101},{6,38},{7,103},{8,40},{... | collective-permute-start | bytes 98312 | tf_op jit(solution)/shard_map/ppermute | solution.py:48
  71.6 9.2 %collective-permute-start.18 = (bf16[128,2048]{1,0:T(8,128)(2,1)S(1)}, bf16[128,2048]{1,0:T(8,128)(2,1)S(1)}, u32[]{:S(2)}, u32[]{:S(2)}) collective-permute-start(bf16[128,2048]{1,0:T(8,128)(2,1)S(1)} %shard_map.84), channel_id=1, source_target_pairs={{0,96},{1,33},{2,98},{3,35},{4,100},{5,37},{6,102},{7,39},{8,104},... | collective-permute-start | bytes 1572872 | tf_op jit(solution)/shard_map/ppermute | solution.py:48
  76.3 18.0 %collective-permute-start.21 = (bf16[256,2048]{1,0:T(8,128)(2,1)S(1)}, bf16[256,2048]{1,0:T(8,128)(2,1)S(1)}, u32[]{:S(2)}, u32[]{:S(2)}) collective-permute-start(bf16[256,2048]{1,0:T(8,128)(2,1)S(1)} %get-tuple-element.45), channel_id=1, source_target_pairs={{0,6},{1,25},{2,0},{3,27},{4,2},{5,29},{6,4},{7,31},{8,14},{9,1},{... | collective-permute-start | bytes 3145736 | tf_op jit(solution)/shard_map/ppermute | solution.py:48
  77.9 27.2 %collective-permute-start.23 = (bf16[256,2048]{1,0:T(8,128)(2,1)S(1)}, bf16[256,2048]{1,0:T(8,128)(2,1)S(1)}, u32[]{:S(2)}, u32[]{:S(2)}) collective-permute-start(bf16[256,2048]{1,0:T(8,128)(2,1)S(1)} %get-tuple-element.46), channel_id=1, source_target_pairs={{0,2},{1,9},{2,4},{3,11},{4,6},{5,13},{6,0},{7,15},{8,10},{9,17},{... | collective-permute-start | bytes 3145736 | tf_op jit(solution)/shard_map/ppermute | solution.py:48
  78.4 26.8 %collective-permute-start.22 = (bf16[256,2048]{1,0:T(8,128)(2,1)S(1)}, bf16[256,2048]{1,0:T(8,128)(2,1)S(1)}, u32[]{:S(2)}, u32[]{:S(2)}) collective-permute-start(bf16[256,2048]{1,0:T(8,128)(2,1)S(1)} %shard_map.88.refs_14_), channel_id=1, source_target_pairs={{0,4},{1,17},{2,6},{3,19},{4,0},{5,21},{6,2},{7,23},{8,12},{9,25},... | collective-permute-start | bytes 3145736 | tf_op jit(solution)/shard_map/ppermute | solution.py:48
  81.2 9.2 %collective-permute-start.19 = (bf16[128,2048]{1,0:T(8,128)(2,1)S(1)}, bf16[128,2048]{1,0:T(8,128)(2,1)S(1)}, u32[]{:S(2)}, u32[]{:S(2)}) collective-permute-start(bf16[128,2048]{1,0:T(8,128)(2,1)S(1)} %shard_map.85), channel_id=1, source_target_pairs={{0,96},{1,33},{2,98},{3,35},{4,100},{5,37},{6,102},{7,39},{8,104},... | collective-permute-start | bytes 1572872 | tf_op jit(solution)/shard_map/ppermute | solution.py:48
  90.8 19.1 %collective-permute-start.20 = (bf16[128,2048]{1,0:T(8,128)(2,1)S(1)}, bf16[128,2048]{1,0:T(8,128)(2,1)S(1)}, u32[]{:S(2)}, u32[]{:S(2)}) collective-permute-start(bf16[128,2048]{1,0:T(8,128)(2,1)S(1)} %shard_map.86), channel_id=1, source_target_pairs={{0,96},{1,33},{2,98},{3,35},{4,100},{5,37},{6,102},{7,39},{8,104},... | collective-permute-start | bytes 1572872 | tf_op jit(solution)/shard_map/ppermute | solution.py:48
  105.6 8.6 %collective-permute-start.24 = (bf16[64,2048]{1,0:T(8,128)(2,1)S(1)}, bf16[64,2048]{1,0:T(8,128)(2,1)S(1)}, u32[]{:S(2)}, u32[]{:S(2)}) collective-permute-start(bf16[64,2048]{1,0:T(8,128)(2,1)S(1)} %get-tuple-element.48), channel_id=1, source_target_pairs={{0,24},{1,7},{2,26},{3,1},{4,28},{5,3},{6,30},{7,5},{8,0},{9,15},{... | collective-permute-start | bytes 786440 | tf_op jit(solution)/shard_map/ppermute | solution.py:48
  107.5 8.0 %collective-permute-start.25 = (bf16[64,2048]{1,0:T(8,128)(2,1)S(1)}, bf16[64,2048]{1,0:T(8,128)(2,1)S(1)}, u32[]{:S(2)}, u32[]{:S(2)}) collective-permute-start(bf16[64,2048]{1,0:T(8,128)(2,1)S(1)} %get-tuple-element.49), channel_id=1, source_target_pairs={{0,16},{1,5},{2,18},{3,7},{4,20},{5,1},{6,22},{7,3},{8,24},{9,13},... | collective-permute-start | bytes 786440 | tf_op jit(solution)/shard_map/ppermute | solution.py:48
  108.9 9.3 %collective-permute-start.26 = (bf16[64,2048]{1,0:T(8,128)(2,1)S(1)}, bf16[64,2048]{1,0:T(8,128)(2,1)S(1)}, u32[]{:S(2)}, u32[]{:S(2)}) collective-permute-start(bf16[64,2048]{1,0:T(8,128)(2,1)S(1)} %get-tuple-element.50), channel_id=1, source_target_pairs={{0,8},{1,3},{2,10},{3,5},{4,12},{5,7},{6,14},{7,1},{8,16},{9,11},{... | collective-permute-start | bytes 786440 | tf_op jit(solution)/shard_map/ppermute | solution.py:48
  118.2 1.0 copy-start

commit v4 on v3

--- a/solution.py
+++ b/solution.py
@@ -72,10 +72,10 @@
     return jax.ShapeDtypeStruct((r, c), t)
 
 
-def pack_kernel(q_ref, owner_ref, row_ref, pos_ref, p_ref, out_ref, kept_ref, owner, row, pos, sems):
+def pack_kernel(q_ref, owner_ref, row_ref, pos_ref, out_ref, owner, row, pos, sems):
     copies = []
     for i, (src, dst) in enumerate(
-        ((owner_ref, owner), (row_ref, row), (pos_ref, pos), (q_ref, out_ref.at[0:128, :]), (p_ref, kept_ref))
+        ((owner_ref, owner), (row_ref, row), (pos_ref, pos), (q_ref, out_ref.at[0:128, :]))
     ):
         copies.append(pltpu.make_async_copy(src, dst, sems.at[i]))
         copies[-1].start()
@@ -88,7 +88,15 @@
     meta = jnp.concatenate([owner[...].astype(F32), row[...].astype(F32), third], axis=1)
     out_ref[128:144, 0:384] = meta.astype(BF)
     copies[3].wait()
-    copies[4].wait()
+
+
+def stage_kernel(a_ref, b_ref, a_out, b_out, sems):
+    one = pltpu.make_async_copy(a_ref, a_out, sems.at[0])
+    two = pltpu.make_async_copy(b_ref, b_out, sems.at[1])
+    one.start()
+    two.start()
+    one.wait()
+    two.wait()
 
 
 def join_kernel(*refs):
@@ -163,28 +171,32 @@
     return write
 
 
-def early_kernel(*refs):
-    p_refs, q_refs, ts, info = refs[0:4], refs[4:10], refs[10:14], refs[14]
+def early_kernel(pieces, *refs):
+    p_refs, q_refs, ts, info = refs[0:2], refs[2:8], refs[8:10], refs[10]
     place = whereabouts()
     p = jnp.concatenate([r[...] for r in p_refs], axis=0)
     for pair in range(3):
         a, b = q_refs[2 * pair], q_refs[2 * pair + 1]
         raw = product(p, a, b)
-        for i in PIECES:
+        for i, piece in enumerate(pieces):
             part = raw[256 * i : 256 * i + 256]
-            score_block(place, i, pair, a, b, part, ts[i], writer(info, 16 * i, 256 * pair))
+            score_block(place, piece, pair, a, b, part, ts[i], writer(info, 16 * i, 256 * pair))
+
+
+SOON, LATER = (0, 3), (1, 2)
 
 
 class Info:
-    def __init__(self, a, b):
-        self.refs = a, b
+    def __init__(self, *refs):
+        self.refs = refs
 
     def rows(self, piece, pair, first, last):
-        a, b = self.refs
+        if pair < 3:
+            ref = self.refs[0 if piece in SOON else 1]
+            i = 16 * (SOON if piece in SOON else LATER).index(piece)
+            return ref[i + first : i + last, 256 * pair : 256 * pair + 256]
         i = 16 * piece
-        if pair < 3:
-            return a[i + first : i + last, 256 * pair : 256 * pair + 256]
-        return b[i + first : i + last, 0:256]
+        return self.refs[2][i + first : i + last, 0:256]
 
 
 def merge(a, b):
@@ -198,14 +210,14 @@
 
 
 def late_kernel(*refs):
-    p_refs, q_refs, info_a, info_b, stats_ref = refs[0:4], refs[4:6], refs[6], refs[7], refs[8]
+    p_refs, q_refs, soon, later, info_b, stats_ref = refs[0:4], refs[4:6], *refs[6:10]
     place = whereabouts()
     p = jnp.concatenate([r[...] for r in p_refs], axis=0)
     raw = product(p, q_refs[0], q_refs[1])
     for i in PIECES:
         part = raw[256 * i : 256 * i + 256]
         score_block(place, i, 3, q_refs[0], q_refs[1], part, None, writer(info_b, 16 * i, 0))
-    info = Info(info_a, info_b)
+    info = Info(soon, later, info_b)
     for pair in range(4):
         acc = unpack(info.rows(0, pair, 8, 11))
         for piece in (1, 2, 3):
@@ -214,7 +226,7 @@
 
 
 def query_kernel(half, *refs):
-    ts, infos, stats, p_refs, out_ref, turned = refs[0:4], refs[4:6], refs[6], refs[7:11], refs[12], refs[13]
+    ts, infos, stats, p_refs, out_ref, turned = refs[0:4], refs[4:7], refs[7], refs[8:12], refs[13], refs[14]
     info = Info(*infos)
     step = steps(128)
     side = slice(128 * half, 128 * half + 128)
@@ -246,13 +258,24 @@
     return jnp.concatenate([v[:, 128 * (i ^ 1) : 128 * (i ^ 1) + 128] for i in range(8)], axis=1)
 
 
-def merge_kernel(raw, other, out_ref):
-    both = merge(unpack(raw[...]), unpack(swap(other[...])))
-    out_ref[...] = jnp.concatenate([*both, jnp.zeros((5, 1024), F32)], axis=0)
+def aligned(v, t):
+    picked = []
+    for i in range(4):
+        j, k = (i - t) % 4, (i + t) % 4
+        picked += [v[:, 256 * j : 256 * j + 128], v[:, 256 * k + 128 : 256 * k + 256]]
+    return jnp.concatenate(picked, axis=1)
+
+
+def merge_kernel(t, raw, other, *refs):
+    got = aligned(other[...], t) if t else swap(other[...])
+    both = merge(unpack(raw[...]), unpack(got))
+    refs[-1][...] = jnp.concatenate([*both, jnp.zeros((5, 1024), F32)], axis=0)
 
 
 def block_kernel(k, mine, theirs, factor, *refs):
-    out_ref = refs[-1]
+    got, out_ref = refs[0], refs[1 if k < 3 else 0]
+    if k == 0:
+        refs[2][...] = jnp.zeros((8, 128), F32)
     rows = slice(128 * k, 128 * k + 128)
     f = factor[...]
     for n in range(4):
@@ -261,7 +284,7 @@
         if k == 0:
             v = v + (mine[512:640, cols] + theirs[512:640, cols].astype(F32)) * f[:, 8:9]
         if k < 3:
-            v = v + refs[0][:, cols].astype(F32)
+            v = v + got[:, cols].astype(F32)
         out_ref[:, cols] = v.astype(BF)
 
 
@@ -277,19 +300,12 @@
     out_ref[...] = v.astype(BF)
 
 
-def total_kernel(raw, other, stats, g1, g2, g3, lse_ref, loss_ref, factor_ref):
-    acc = unpack(stats[...])
-    for t, got in ((1, g1), (2, g2), (3, g3)):
-        v = got[...]
-        picked = []
-        for i in range(4):
-            j, k = (i - t) % 4, (i + t) % 4
-            picked += [v[:, 256 * j : 256 * j + 128], v[:, 256 * k + 128 : 256 * k + 256]]
-        acc = merge(acc, unpack(jnp.concatenate(picked, axis=1)))
+def total_kernel(raw, other, stats, got, _, lse_ref, loss_ref, factor_ref):
+    acc = merge(unpack(stats[...]), unpack(aligned(got[...], 2)))
     lse = acc[0] + jnp.log(acc[1])
     lse_ref[...] = jnp.broadcast_to(lse, (8, 1024))
     chosen = acc[2][:, 0:128]
-    loss_ref[...] = jnp.broadcast_to(lse[:, 0:128] - chosen, (8, 128))
+    loss_ref[...] = lse[:, 0:128] - chosen
     rows = []
     for top in (raw[0:1, :], swap(other[...])[0:1]):
         f = jnp.exp(top - lse) * SHARP
@@ -316,8 +332,8 @@
 
 
 def far_kernel(t_ref, *refs):
-    infos, lse_ref, q_refs = refs[0:2], refs[2], refs[3:11]
-    out_ref, c = refs[11:]
+    infos, lse_ref, q_refs = refs[0:3], refs[3], refs[4:12]
+    out_ref, c = refs[12:]
     coefficients(Info(*infos), 2, t_ref, lse_ref, c, 0)
     for n in range(4):
         cols = slice(512 * n, 512 * n + 512)
@@ -326,8 +342,8 @@
 
 
 def near_kernel(*refs):
-    ts, infos, lse_ref, q_refs = refs[0:3], refs[3:5], refs[5], refs[6:14]
-    zero, one, three, c = refs[15:]
+    ts, infos, lse_ref, q_refs = refs[0:3], refs[3:6], refs[6], refs[7:15]
+    zero, one, three, c = refs[16:]
     info = Info(*infos)
     for i, piece in enumerate((0, 1, 3)):
         coefficients(info, piece, ts[i], lse_ref, c, 256 * i)
@@ -341,23 +357,29 @@
 
 
 def local(question_vectors, passages, positive, hard_owner, hard_row):
-    packed, kept = call(
+    packed = call(
         pack_kernel,
-        (shape(144, WIDTH, BF), shape(64, WIDTH, BF)),
-        [ANY] * 5,
+        shape(144, WIDTH, BF),
+        [ANY] * 4,
         scratch=[
             pltpu.VMEM((16, 128), jnp.int32),
             pltpu.VMEM((16, 128), jnp.int32),
             pltpu.VMEM((1, 128), jnp.int32),
-            pltpu.SemaphoreType.DMA((5,)),
+            pltpu.SemaphoreType.DMA((4,)),
         ],
         limit=56,
-    )(question_vectors, hard_owner.T, hard_row.T, positive.reshape(1, 128), passages)
+    )(question_vectors, hard_owner.T, hard_row.T, positive.reshape(1, 128))
 
     back = send(passages, first(1))
     ahead = send(passages, first(-1))
     across = send(passages, first(2))
     q1 = send(packed, along(1))
+    mine0, kept = call(
+        stage_kernel,
+        (shape(144, WIDTH, BF), shape(64, WIDTH, BF)),
+        [ANY, ANY],
+        scratch=[pltpu.SemaphoreType.DMA((2,))],
+    )(packed, passages)
     s0 = send(packed, CORE)
     back, ahead, across, q1, s0 = tied(back, ahead, across, q1, s0)
     plane = call(join_kernel, shape(256, WIDTH, BF), [VMEM] * 4)(kept, back, across, ahead)
@@ -365,64 +387,76 @@
     down = send(plane, second(-1))
     over = send(plane, second(2))
     q2 = send(q1, along(1))
+    q2, q1 = tied(q2, q1)
     s1 = send(q1, CORE)
     q3 = send(q2, along(1))
     s2 = send(q2, CORE)
     s3 = send(q3, CORE)
-    tiles = (packed, s0, q1, s1, q2, s2, q3, s3)
+    tiles = (mine0, s0, q1, s1, q2, s2, q3, s3)
 
     pieces = (plane, up, over, down)
     tile = shape(256, 256, F32)
-    t0, t1, t2, t3, info_a = call(
-        early_kernel, (tile, tile, tile, tile, shape(64, 768, F32)), [VMEM] * 10, 2 * 1024 * 768 * WIDTH
-    )(*pieces, *tiles[:6])
+
+    def early(which):
+        return call(
+            lambda *r: early_kernel(which, *r),
+            (tile, tile, shape(32, 768, F32)),
+            [VMEM] * 8,
+            2 * 512 * 768 * WIDTH,
+        )(*[pieces[i] for i in which], *tiles[:6])
+
+    t0, t3, soon = early(SOON)
+    t1, t2, later = early(LATER)
     info_b, raw = call(
-        late_kernel, (shape(64, 256, F32), shape(8, 1024, F32)), [VMEM] * 7, 2 * 1024 * 256 * WIDTH
-    )(*pieces, *tiles[6:], info_a)
+        late_kernel, (shape(64, 256, F32), shape(8, 1024, F32)), [VMEM] * 8, 2 * 1024 * 256 * WIDTH
+    )(*pieces, *tiles[6:], soon, later)
 
     other = send(raw, CORE)
-    stats = call(merge_kernel, shape(8, 1024, F32), [VMEM] * 2)(raw, other)
-    g1 = send(stats, along(1))
-    g2 = send(stats, along(2))
-    g3 = send(stats, along(3))
-    infos = (info_a, info_b)
-    operands = (t0, t1, t2, t3, *infos, raw, *pieces, stats)
-
-    def query(half, kind):
+    stats = call(lambda *r: merge_kernel(0, *r), shape(8, 1024, F32), [VMEM] * 2)(raw, other)
+    infos = (soon, later, info_b)
+    operands = (t0, t1, t2, t3, *infos, raw, *pieces)
+
+    def query(half, kind, after):
         return call(
             lambda *r: query_kernel(half, *r),
             shape(640, WIDTH, kind),
-            [VMEM] * 12,
+            [VMEM] * 13,
             2 * 640 * 1024 * WIDTH,
             scratch=[pltpu.VMEM((640, 1024), BF)],
-        )(*operands)
-
-    theirs = send(query(1, BF), CORE)
-    mine = query(0, F32)
+        )(*operands, after)
+
+    mine = query(0, F32, stats)
+    both = call(lambda *r: merge_kernel(1, *r), shape(8, 1024, F32), [VMEM] * 3)(stats, send(stats, along(1)), mine)
+    four = send(both, along(2))
+    theirs = query(1, BF, both)
     lse, loss, factor = call(
-        total_kernel, (shape(8, 1024, F32), shape(8, 128, F32), shape(128, 128, F32)), [VMEM] * 6
-    )(raw, other, stats, g1, g2, g3)
-
-    far = call(far_kernel, shape(256, WIDTH, BF), [VMEM] * 12, 2 * 256 * 1024 * WIDTH, scratch=[pltpu.VMEM((256, 1024), BF)])(
+        total_kernel, (shape(8, 1024, F32), shape(1, 128, F32), shape(128, 128, F32)), [VMEM] * 5
+    )(raw, other, both, four, theirs)
+    theirs, lse = tied(theirs, lse)
+    theirs = send(theirs, CORE)
+
+    far = call(far_kernel, shape(256, WIDTH, BF), [VMEM] * 13, 2 * 256 * 1024 * WIDTH, scratch=[pltpu.VMEM((256, 1024), BF)])(
         t2, *infos, lse, *tiles
     )
     two = send(far, second(2))
 
+    zero, one, three = call(
+        near_kernel,
+        (shape(256, WIDTH, F32), shape(256, WIDTH, BF), shape(256, WIDTH, BF)),
+        [VMEM] * 16,
+        2 * 768 * 1024 * WIDTH,
+        scratch=[pltpu.VMEM((768, 1024), BF)],
+    )(t0, t1, t3, *infos, lse, *tiles, far)
     def block(k, *got):
         kernel = lambda *r: block_kernel(k, *r)
-        return call(kernel, shape(128, WIDTH, BF), [VMEM] * (3 + len(got)))(mine, theirs, factor, *got)
+        outs = (shape(128, WIDTH, BF), shape(8, 128, F32)) if k == 0 else shape(128, WIDTH, BF)
+        return call(kernel, outs, [VMEM] * (3 + len(got)))(mine, theirs, factor, *got)
 
     run = block(3)
     for k in (2, 1, 0):
         run = block(k, send(run, along(-1)))
-
-    zero, one, three = call(
-        near_kernel,
-        (shape(256, WIDTH, F32), shape(256, WIDTH, BF), shape(256, WIDTH, BF)),
-        [VMEM] * 15,
-        2 * 768 * 1024 * WIDTH,
-        scratch=[pltpu.VMEM((768, 1024), BF)],
-    )(t0, t1, t3, *infos, lse, *tiles, far)
+    run, token = run
+
     one = send(one, second(-1))
     three = send(three, second(1))
     half = shape(64, WIDTH, BF)
@@ -430,8 +464,8 @@
     g2 = send(g2, first(2))
     g1 = send(g1, first(-1))
     g3 = send(g3, first(1))
-    passage_grad = call(last_kernel, half, [VMEM] * 5)(g0, g1, g2, g3, run)
-    return loss[0], run, passage_grad
+    passage_grad = call(last_kernel, half, [VMEM] * 5)(g0, g1, g2, g3, token)
+    return loss.reshape(128), run, passage_grad
 
 
 def solution(mesh):

time: 120 us -> 110 us (0.917)
  waiting for transfers between devices: 60.1 us -> 50.4 us
  local copies, waits for them, and re-layouts: 3.57 us -> 2.01 us
    ppermute x27 -> x26, waiting for transfers between devices: 60.1 us -> 50.4 us  [send(): return lax.ppermute(v, AXES, perm)]
    unnamed x8 -> x4, local copies, waits for them, and re-layouts: 3.06 us -> 2.01 us
    pallas_call x11 -> x14, Pallas kernels: 12 us -> 12.6 us  [the longest x2 4.28 us: early(): call(lambda *r: early_kernel(which, *r), (tile, tile, shape(32, 768, F32)...]
    ppermute x27 -> x26, starting transfers between devices: 33.6 us -> 33.7 us  [send(): return lax.ppermute(v, AXES, perm)]
  transfers between devices with their start and end apart: 27 -> 26, of which waited for: 15 -> 18; matrix products, arithmetic and copies ran while one was open for 0% -> 0% of each run, Pallas kernels for 12% -> 16%
where the time goes in v4:
time: 110 us; the launch traced here: 109 us
  waiting for transfers between devices  50.4 us (46%)
  starting transfers between devices  33.7 us (31%)
  Pallas kernels  22.5 us (20%)
  local copies, waits for them, and re-layouts  2.01 us (2%)
    ppermute x26, waiting for transfers between devices, send(): return lax.ppermute(v, AXES, perm)  50.4 us
    ppermute x26, starting transfers between devices, send(): return lax.ppermute(v, AXES, perm)  33.7 us
    pallas_call x2, Pallas kernels, query(): call(lambda *r: query_kernel(half, *r), shape(640, WIDTH, kind), [VMEM] *...  5.9 us
    pallas_call x2, Pallas kernels, early(): call(lambda *r: early_kernel(which, *r), (tile, tile, shape(32, 768, F32)...  4.28 us
    pallas_call x1, Pallas kernels, local(): call(near_kernel, (shape(256, WIDTH, F32), shape(256, WIDTH, BF), shape(2...  3.5 us
  transfers between devices with their start and end apart: 26, of which 18 were waited for; matrix products, arithmetic and copies ran while one was open for 0% of the time, Pallas kernels for 16%

profile of v4, /device:TPU:0, one launch (start us, length us, event | category | flops | bytes accessed | tf_op | source)
XLA Modules:
  0.0 109.4 jit_solution(8675487445391128324)
XLA Ops:
  0.6 1.9 %shard_map.76.a_ref = bf16[144,2048]{1,0:T(8,128)(2,1)} custom-call(bf16[128,2048]{1,0:T(8,128)(2,1)} %q_ref.1, s32[16,128]{1,0:T(8,128)} %bitcast.4, s32[16,128]{1,0:T(8,128)} %bitcast.5, s32[1,128]{1,0:T(1,128)} %bitcast.6), custom_call_target="tpu_custom_call" | custom-call | tf_op jit(solution)/shard_map/pallas_call | solution.py:360
  2.6 1.7 %collective-permute-start.3 = (bf16[144,2048]{1,0:T(8,128)(2,1)}, bf16[144,2048]{1,0:T(8,128)(2,1)S(1)}, u32[]{:S(2)}, u32[]{:S(2)}) collective-permute-start(bf16[144,2048]{1,0:T(8,128)(2,1)} %shard_map.76.a_ref), channel_id=1, source_target_pairs={{0,32},{1,97},{2,34},{3,99},{4,36},{5,101},{6,38},{7,103},{8,40},{... | collective-permute-start | bytes 1769480 | tf_op jit(solution)/shard_map/ppermute | solution.py:48
  5.3 1.5 %collective-permute-start = (bf16[64,2048]{1,0:T(8,128)(2,1)}, bf16[64,2048]{1,0:T(8,128)(2,1)S(1)}, u32[]{:S(2)}, u32[]{:S(2)}) collective-permute-start(bf16[64,2048]{1,0:T(8,128)(2,1)} %b_ref.1), channel_id=1, source_target_pairs={{0,8},{1,3},{2,10},{3,5},{4,12},{5,7},{6,14},{7,1},{8,16},{9,11},{... | collective-permute-start | bytes 786440 | tf_op jit(solution)/shard_map/ppermute | solution.py:48
  6.8 1.7 %collective-permute-start.1 = (bf16[64,2048]{1,0:T(8,128)(2,1)}, bf16[64,2048]{1,0:T(8,128)(2,1)S(1)}, u32[]{:S(2)}, u32[]{:S(2)}) collective-permute-start(bf16[64,2048]{1,0:T(8,128)(2,1)} %b_ref.1), channel_id=1, source_target_pairs={{0,24},{1,7},{2,26},{3,1},{4,28},{5,3},{6,30},{7,5},{8,0},{9,15},{... | collective-permute-start | bytes 786440 | tf_op jit(solution)/shard_map/ppermute | solution.py:48
  8.5 1.8 %collective-permute-start.2 = (bf16[64,2048]{1,0:T(8,128)(2,1)}, bf16[64,2048]{1,0:T(8,128)(2,1)S(1)}, u32[]{:S(2)}, u32[]{:S(2)}) collective-permute-start(bf16[64,2048]{1,0:T(8,128)(2,1)} %b_ref.1), channel_id=1, source_target_pairs={{0,16},{1,5},{2,18},{3,7},{4,20},{5,1},{6,22},{7,3},{8,24},{9,13},... | collective-permute-start | bytes 786440 | tf_op jit(solution)/shard_map/ppermute | solution.py:48
  13.1 2.5 %collective-permute-done.1.refs_3_ = bf16[64,2048]{1,0:T(8,128)(2,1)S(1)} collective-permute-done((bf16[64,2048]{1,0:T(8,128)(2,1)}, bf16[64,2048]{1,0:T(8,128)(2,1)S(1)}, u32[]{:S(2)}, u32[]{:S(2)}) %collective-permute-start.1) | collective-permute-done | bytes 262176 | tf_op jit(solution)/shard_map/ppermute | solution.py:48
  15.6 1.3 %collective-permute-done.2.refs_2_ = bf16[64,2048]{1,0:T(8,128)(2,1)S(1)} collective-permute-done((bf16[64,2048]{1,0:T(8,128)(2,1)}, bf16[64,2048]{1,0:T(8,128)(2,1)S(1)}, u32[]{:S(2)}, u32[]{:S(2)}) %collective-permute-start.2) | collective-permute-done | bytes 262176 | tf_op jit(solution)/shard_map/ppermute | solution.py:48
  17.0 4.1 %collective-permute-start.7 = (bf16[256,2048]{1,0:T(8,128)(2,1)S(1)}, bf16[256,2048]{1,0:T(8,128)(2,1)S(1)}, u32[]{:S(2)}, u32[]{:S(2)}) collective-permute-start(bf16[256,2048]{1,0:T(8,128)(2,1)S(1)} %shard_map.78.r_0_.refs_0_.r_8_), channel_id=1, source_target_pairs={{0,6},{1,25},{2,0},{3,27},{4,2},{5,29},{6,4},{7,31},{8,14},{9,1},{... | collective-permute-start | bytes 3145736 | tf_op jit(solution)/shard_map/ppermute | solution.py:48
  21.7 1.9 %collective-permute-start.6 = (bf16[256,2048]{1,0:T(8,128)(2,1)S(1)}, bf16[256,2048]{1,0:T(8,128)(2,1)S(1)}, u32[]{:S(2)}, u32[]{:S(2)}) collective-permute-start(bf16[256,2048]{1,0:T(8,128)(2,1)S(1)} %shard_map.78.r_0_.refs_0_.r_8_), channel_id=1, source_target_pairs={{0,4},{1,17},{2,6},{3,19},{4,0},{5,21},{6,2},{7,23},{8,12},{9,25},... | collective-permute-start | bytes 3145736 | tf_op jit(solution)/shard_map/ppermute | solution.py:48
  23.5 8.6 %collective-permute-done.8.r_6_.refs_8_.refs_11_ = bf16[144,2048]{1,0:T(8,128)(2,1)S(1)} collective-permute-done((bf16[144,2048]{1,0:T(8,128)(2,1)S(1)}, bf16[144,2048]{1,0:T(8,128)(2,1)S(1)}, u32[]{:S(2)}, u32[]{:S(2)}) %collective-permute-start.8) | collective-permute-done | bytes 589856 | tf_op jit(solution)/shard_map/ppermute | solution.py:48
  32.2 12.5 %collective-permute-done.7.r_1_.refs_3_.r_11_ = bf16[256,2048]{1,0:T(8,128)(2,1)S(1)} collective-permute-done((bf16[256,2048]{1,0:T(8,128)(2,1)S(1)}, bf16[256,2048]{1,0:T(8,128)(2,1)S(1)}, u32[]{:S(2)}, u32[]{:S(2)}) %collective-permute-start.7) | collective-permute-done | bytes 1048608 | tf_op jit(solution)/shard_map/ppermute | solution.py:48
  45.1 1.5 %collective-permute-done.12.r_7_.refs_9_.refs_12_ = bf16[144,2048]{1,0:T(8,128)(2,1)S(1)} collective-permute-done((bf16[144,2048]{1,0:T(8,128)(2,1)S(1)}, bf16[144,2048]{1,0:T(8,128)(2,1)S(1)}, u32[]{:S(2)}, u32[]{:S(2)}) %collective-permute-start.12) | collective-permute-done | bytes 589856 | tf_op jit(solution)/shard_map/ppermute | solution.py:48
  46.6 2.1 %shard_map.79 = (f32[256,256]{1,0:T(8,128)S(1)}, f32[256,256]{1,0:T(8,128)S(1)}, f32[32,768]{1,0:T(8,128)S(1)}) custom-call(bf16[256,2048]{1,0:T(8,128)(2,1)S(1)} %shard_map.78.r_0_.refs_0_.r_8_, bf16[256,2048]{1,0:T(8,128)(2,1)S(1)} %collective-permute-done.7.r_1_.refs_3_.r_11_, bf16[144,2048]{1,0:T(8,128)(2,1)S(1)} %get-tuple-element.40.r_2_.refs_4_.refs_7_, ...), custom_call_target="tpu_custom_call" | custom-call | flops 1610612736 | tf_op jit(solution)/shard_map/pallas_call | solution.py:401
  48.9 2.1 %shard_map.80 = (f32[256,256]{1,0:T(8,128)S(1)}, f32[256,256]{1,0:T(8,128)S(1)}, f32[32,768]{1,0:T(8,128)S(1)}) custom-call(bf16[256,2048]{1,0:T(8,128)(2,1)S(1)} %collective-permute-done.5.r_0_.refs_1_.r_9_, bf16[256,2048]{1,0:T(8,128)(2,1)S(1)} %collective-permute-done.6.r_1_.refs_2_.r_10_, bf16[144,2048]{1,0:T(8,128)(2,1)S(1)} %get-tuple-element.40.r_2_.refs_4_.refs_7_, ...), custom_call_target="tpu_custom_call" | custom-call | flops 1610612736 | tf_op jit(solution)/shard_map/pallas_call | solution.py:401
  51.1 1.4 %shard_map.81 = (f32[64,256]{1,0:T(8,128)S(1)}, f32[8,1024]{1,0:T(8,128)S(1)}) custom-call(bf16[256,2048]{1,0:T(8,128)(2,1)S(1)} %shard_map.78.r_0_.refs_0_.r_8_, bf16[256,2048]{1,0:T(8,128)(2,1)S(1)} %collective-permute-done.5.r_0_.refs_1_.r_9_, bf16[256,2048]{1,0:T(8,128)(2,1)S(1)} %collective-permute-done.6.r_1_.refs_2_.r_10_, ...), custom_call_target="tpu_custom_call" | custom-call | flops 1073741824 | tf_op jit(solution)/shard_map/pallas_call | solution.py:410
  53.8 1.5 %collective-permute-start.14 = (f32[8,1024]{1,0:T(8,128)S(1)}, f32[8,1024]{1,0:T(8,128)S(1)}, u32[]{:S(2)}, u32[]{:S(2)}) collective-permute-start(f32[8,1024]{1,0:T(8,128)S(1)} %shard_map.82.r_12_.r_0_), channel_id=1, source_target_pairs={{0,32},{1,97},{2,34},{3,99},{4,36},{5,101},{6,38},{7,103},{8,40},{... | collective-permute-start | bytes 98312 | tf_op jit(solution)/shard_map/ppermute | solution.py:48
  55.3 2.9 %shard_map.83.r_2_.r_0_ = f32[640,2048]{1,0:T(8,128)S(1)} custom-call(f32[256,256]{1,0:T(8,128)S(1)} %get-tuple-element.46.r_0_.refs_0_, f32[256,256]{1,0:T(8,128)S(1)} %get-tuple-element.47.r_1_.refs_1_, f32[256,256]{1,0:T(8,128)S(1)} %get-tuple-element.48.r_2_.t_ref, f32[256,256]{1,0:T(8,128)S(1)} %get-tuple-element.49.r_3_.refs_2_, ...), custom_call_target="tpu_custom_call" | custom-call | flops 2684354560 | tf_op jit(solution)/shard_map/pallas_call | solution.py:420
  59.2 2.0 %collective-permute-start.15 = (f32[8,1024]{1,0:T(8,128)S(1)}, f32[8,1024]{1,0:T(8,128)S(1)}, u32[]{:S(2)}, u32[]{:S(2)}) collective-permute-start(f32[8,1024]{1,0:T(8,128)S(1)} %shard_map.84.r_12_.stats), channel_id=1, source_target_pairs={{0,64},{1,65},{2,66},{3,67},{4,68},{5,69},{6,70},{7,71},{8,72},{9,... | collective-permute-start | bytes 98312 | tf_op jit(solution)/shard_map/ppermute | solution.py:48
  61.2 3.0 %shard_map.85._ = bf16[640,2048]{1,0:T(8,128)(2,1)S(1)} custom-call(f32[256,256]{1,0:T(8,128)S(1)} %get-tuple-element.46.r_0_.refs_0_, f32[256,256]{1,0:T(8,128)S(1)} %get-tuple-element.47.r_1_.refs_1_, f32[256,256]{1,0:T(8,128)S(1)} %get-tuple-element.48.r_2_.t_ref, f32[256,256]{1,0:T(8,128)S(1)} %get-tuple-element.49.r_3_.refs_2_, ...), custom_call_target="tpu_custom_call" | custom-call | flops 2684354560 | tf_op jit(solution)/shard_map/pallas_call | solution.py:420
  65.2 1.3 %shard_map.91.refs_15_ = bf16[256,2048]{1,0:T(8,128)(2,1)S(1)} custom-call(f32[256,256]{1,0:T(8,128)S(1)} %get-tuple-element.48.r_2_.t_ref, f32[32,768]{1,0:T(8,128)S(1)} %get-tuple-element.43.refs_6_.r_4_.refs_0_.refs_3_, f32[32,768]{1,0:T(8,128)S(1)} %get-tuple-element.44.refs_7_.r_5_.refs_1_.refs_4_, ...), custom_call_target="tpu_custom_call" | custom-call | flops 1073741824 | tf_op jit(solution)/shard_map/pallas_call | solution.py:438
  66.9 3.2 %collective-permute-done.16.r_1_ = bf16[640,2048]{1,0:T(8,128)(2,1)S(1)} collective-permute-done((bf16[640,2048]{1,0:T(8,128)(2,1)S(1)}, bf16[640,2048]{1,0:T(8,128)(2,1)S(1)}, u32[]{:S(2)}, u32[]{:S(2)}) %collective-permute-start.16) | collective-permute-done | bytes 2621472 | tf_op jit(solution)/shard_map/ppermute | solution.py:48
  70.4 1.5 %collective-permute-start.17 = (bf16[128,2048]{1,0:T(8,128)(2,1)S(1)}, bf16[128,2048]{1,0:T(8,128)(2,1)S(1)}, u32[]{:S(2)}, u32[]{:S(2)}) collective-permute-start(bf16[128,2048]{1,0:T(8,128)(2,1)S(1)} %shard_map.87), channel_id=1, source_target_pairs={{0,96},{1,33},{2,98},{3,35},{4,100},{5,37},{6,102},{7,39},{8,104},... | collective-permute-start | bytes 1572872 | tf_op jit(solution)/shard_map/ppermute | solution.py:48
  71.9 3.5 %shard_map.92 = (f32[256,2048]{1,0:T(8,128)S(1)}, bf16[256,2048]{1,0:T(8,128)(2,1)S(1)}, bf16[256,2048]{1,0:T(8,128)(2,1)S(1)}) custom-call(f32[256,256]{1,0:T(8,128)S(1)} %get-tuple-element.46.r_0_.refs_0_, f32[256,256]{1,0:T(8,128)S(1)} %get-tuple-element.47.r_1_.refs_1_, f32[256,256]{1,0:T(8,128)S(1)} %get-tuple-element.49.r_3_.refs_2_, ...), custom_call_target="tpu_custom_call" | custom-call | flops 3221225472 | tf_op jit(solution)/shard_map/pallas_call | solution.py:443
  75.4 3.3 %collective-permute-start.20 = (bf16[256,2048]{1,0:T(8,128)(2,1)S(1)}, bf16[256,2048]{1,0:T(8,128)(2,1)S(1)}, u32[]{:S(2)}, u32[]{:S(2)}) collective-permute-start(bf16[256,2048]{1,0:T(8,128)(2,1)S(1)} %get-tuple-element.58), channel_id=1, source_target_pairs={{0,6},{1,25},{2,0},{3,27},{4,2},{5,29},{6,4},{7,31},{8,14},{9,1},{... | collective-permute-start | bytes 3145736 | tf_op jit(solution)/shard_map/ppermute | solution.py:48
  80.0 2.7 %collective-permute-start.18 = (bf16[128,2048]{1,0:T(8,128)(2,1)S(1)}, bf16[128,2048]{1,0:T(8,128)(2,1)S(1)}, u32[]{:S(2)}, u32[]{:S(2)}) collective-permute-start(bf16[128,2048]{1,0:T(8,128)(2,1)S(1)} %shard_map.88), channel_id=1, source_target_pairs={{0,96},{1,33},{2,98},{3,35},{4,100},{5,37},{6,102},{7,39},{8,104},... | collective-permute-start | bytes 1572872 | tf_op jit(solution)/shard_map/ppermute | solution.py:48
  82.7 6.7 %collective-permute-done.18.r_3_ = bf16[128,2048]{1,0:T(8,128)(2,1)S(1)} collective-permute-done((bf16[128,2048]{1,0:T(8,128)(2,1)S(1)}, bf16[128,2048]{1,0:T(8,128)(2,1)S(1)}, u32[]{:S(2)}, u32[]{:S(2)}) %collective-permute-start.18) | collective-permute-done | bytes 524320 | tf_op jit(solution)/shard_map/ppermute | solution.py:48
  89.7 3.8 %collective-permute-start.19 = (bf16[128,2048]{1,0:T(8,128)(2,1)S(1)}, bf16[128,2048]{1,0:T(8,128)(2,1)S(1)}, u32[]{:S(2)}, u32[]{:S(2)}) collective-permute-start(bf16[128,2048]{1,0:T(8,128)(2,1)S(1)} %shard_map.89), channel_id=1, source_target_pairs={{0,96},{1,33},{2,98},{3,35},{4,100},{5,37},{6,102},{7,39},{8,104},... | collective-permute-start | bytes 1572872 | tf_op jit(solution)/shard_map/ppermute | solution.py:48
  93.4 1.7 %collective-permute-done.20.one = bf16[256,2048]{1,0:T(8,128)(2,1)S(1)} collective-permute-done((bf16[256,2048]{1,0:T(8,128)(2,1)S(1)}, bf16[256,2048]{1,0:T(8,128)(2,1)S(1)}, u32[]{:S(2)}, u32[]{:S(2)}) %collective-permute-start.20) | collective-permute-done | bytes 1048608 | tf_op jit(solution)/shard_map/ppermute | solution.py:48
  95.5 2.3 %collective-permute-start.23 = (bf16[64,2048]{1,0:T(8,128)(2,1)S(1)}, bf16[64,2048]{1,0:T(8,128)(2,1)S(1)}, u32[]{:S(2)}, u32[]{:S(2)}) collective-permute-start(bf16[64,2048]{1,0:T(8,128)(2,1)S(1)} %get-tuple-element.61), channel_id=1, source_target_pairs={{0,24},{1,7},{2,26},{3,1},{4,28},{5,3},{6,30},{7,5},{8,0},{9,15},{... | collective-permute-start | bytes 786440 | tf_op jit(solution)/shard_map/ppermute | solution.py:48
  100.1 1.3 %shard_map.90 = (bf16[128,2048]{1,0:T(8,128)(2,1)}, f32[8,128]{1,0:T(8,128)S(1)}) custom-call(f32[640,2048]{1,0:T(8,128)S(1)} %shard_map.83.r_2_.r_0_, bf16[640,2048]{1,0:T(8,128)(2,1)S(1)} %collective-permute-done.16.r_1_, f32[128,128]{1,0:T(8,128)S(1)} %get-tuple-element.54.r_2_, bf16[128,2048]{1,0:T(8,128)(2,1)S(1)} %collective-permute-done.19.r_3_), custom_call_target="tpu_custom_call" | custom-call | tf_op jit(solution)/shard_map/pallas_call | solution.py:453
  101.4 3.2 %collective-permute-done.23.b = bf16[64,2048]{1,0:T(8,128)(2,1)S(1)} collective-permute-done((bf16[64,2048]{1,0:T(8,128)(2,1)S(1)}, bf16[64,2048]{1,0:T(8,128)(2,1)S(1)}, u32[]{:S(2)}, u32[]{:S(2)}) %collective-permute-start.23) | collective-permute-done | bytes 262176 | tf_op jit(solution)/shard_map/ppermute | solution.py:48
  105.8 2.7 %collective-permute-done.25.d = bf16[64,2048]{1,0:T(8,128)(2,1)S(1)} collective-permute-done((bf16[64,2048]{1,0:T(8,128)(2,1)S(1)}, bf16[64,2048]{1,0:T(8,128)(2,1)S(1)}, u32[]{:S(2)}, u32[]{:S(2)}) %collective-permute-start.25) | collective-permute-done | bytes 262176 | tf_op jit(solution)/shard_map/ppermute | solution.py:48
  (43 shorter events, 15.3 us)
Async XLA Ops:
  2.6 14.3 %collective-permute-start.3 = (bf16[144,2048]{1,0:T(8,128)(2,1)}, bf16[144,2048]{1,0:T(8,128)(2,1)S(1)}, u32[]{:S(2)}, u32[]{:S(2)}) collective-permute-start(bf16[144,2048]{1,0:T(8,128)(2,1)} %shard_map.76.a_ref), channel_id=1, source_target_pairs={{0,32},{1,97},{2,34},{3,99},{4,36},{5,101},{6,38},{7,103},{8,40},{... | collective-permute-start | bytes 1769480 | tf_op jit(solution)/shard_map/ppermute | solution.py:48
  4.3 12.6 %collective-permute-start.4 = (bf16[144,2048]{1,0:T(8,128)(2,1)}, bf16[144,2048]{1,0:T(8,128)(2,1)S(1)}, u32[]{:S(2)}, u32[]{:S(2)}) collective-permute-start(bf16[144,2048]{1,0:T(8,128)(2,1)} %shard_map.76.a_ref), channel_id=1, source_target_pairs={{0,1},{1,0},{2,3},{3,2},{4,5},{5,4},{6,7},{7,6},{8,9},{9,8},{10,11... | collective-permute-start | bytes 1769480 | tf_op jit(solution)/shard_map/ppermute | solution.py:48
  5.3 7.8 %collective-permute-start = (bf16[64,2048]{1,0:T(8,128)(2,1)}, bf16[64,2048]{1,0:T(8,128)(2,1)S(1)}, u32[]{:S(2)}, u32[]{:S(2)}) collective-permute-start(bf16[64,2048]{1,0:T(8,128)(2,1)} %b_ref.1), channel_id=1, source_target_pairs={{0,8},{1,3},{2,10},{3,5},{4,12},{5,7},{6,14},{7,1},{8,16},{9,11},{... | collective-permute-start | bytes 786440 | tf_op jit(solution)/shard_map/ppermute | solution.py:48
  6.8 8.8 %collective-permute-start.1 = (bf16[64,2048]{1,0:T(8,128)(2,1)}, bf16[64,2048]{1,0:T(8,128)(2,1)S(1)}, u32[]{:S(2)}, u32[]{:S(2)}) collective-permute-start(bf16[64,2048]{1,0:T(8,128)(2,1)} %b_ref.1), channel_id=1, source_target_pairs={{0,24},{1,7},{2,26},{3,1},{4,28},{5,3},{6,30},{7,5},{8,0},{9,15},{... | collective-permute-start | bytes 786440 | tf_op jit(solution)/shard_map/ppermute | solution.py:48
  8.5 8.3 %collective-permute-start.2 = (bf16[64,2048]{1,0:T(8,128)(2,1)}, bf16[64,2048]{1,0:T(8,128)(2,1)S(1)}, u32[]{:S(2)}, u32[]{:S(2)}) collective-permute-start(bf16[64,2048]{1,0:T(8,128)(2,1)} %b_ref.1), channel_id=1, source_target_pairs={{0,16},{1,5},{2,18},{3,7},{4,20},{5,1},{6,22},{7,3},{8,24},{9,13},... | collective-permute-start | bytes 786440 | tf_op jit(solution)/shard_map/ppermute | solution.py:48
  10.3 1.1 copy-start
  11.4 0.9 copy-start.1
  17.0 27.7 %collective-permute-start.7 = (bf16[256,2048]{1,0:T(8,128)(2,1)S(1)}, bf16[256,2048]{1,0:T(8,128)(2,1)S(1)}, u32[]{:S(2)}, u32[]{:S(2)}) collective-permute-start(bf16[256,2048]{1,0:T(8,128)(2,1)S(1)} %shard_map.78.r_0_.refs_0_.r_8_), channel_id=1, source_target_pairs={{0,6},{1,25},{2,0},{3,27},{4,2},{5,29},{6,4},{7,31},{8,14},{9,1},{... | collective-permute-start | bytes 3145736 | tf_op jit(solution)/shard_map/ppermute | solution.py:48
  21.1 11.1 %collective-permute-start.8 = (bf16[144,2048]{1,0:T(8,128)(2,1)S(1)}, bf16[144,2048]{1,0:T(8,128)(2,1)S(1)}, u32[]{:S(2)}, u32[]{:S(2)}) collective-permute-start(bf16[144,2048]{1,0:T(8,128)(2,1)S(1)} %collective-permute-done.3.r_4_.refs_6_.refs_9_), channel_id=1, source_target_pairs={{0,32},{1,97},{2,34},{3,99},{4,36},{5,101},{6,38},{7,103},{8,40},{... | collective-permute-start | bytes 1769480 | tf_op jit(solution)/shard_map/ppermute | solution.py:48
  21.7 27.2 %collective-permute-start.5 = (bf16[256,2048]{1,0:T(8,128)(2,1)S(1)}, bf16[256,2048]{1,0:T(8,128)(2,1)S(1)}, u32[]{:S(2)}, u32[]{:S(2)}) collective-permute-start(bf16[256,2048]{1,0:T(8,128)(2,1)S(1)} %shard_map.78.r_0_.refs_0_.r_8_), channel_id=1, source_target_pairs={{0,2},{1,9},{2,4},{3,11},{4,6},{5,13},{6,0},{7,15},{8,10},{9,17},{... | collective-permute-start | bytes 3145736 | tf_op jit(solution)/shard_map/ppermute | solution.py:48
  21.7 27.2 %collective-permute-start.6 = (bf16[256,2048]{1,0:T(8,128)(2,1)S(1)}, bf16[256,2048]{1,0:T(8,128)(2,1)S(1)}, u32[]{:S(2)}, u32[]{:S(2)}) collective-permute-start(bf16[256,2048]{1,0:T(8,128)(2,1)S(1)} %shard_map.78.r_0_.refs_0_.r_8_), channel_id=1, source_target_pairs={{0,4},{1,17},{2,6},{3,19},{4,0},{5,21},{6,2},{7,23},{8,12},{9,25},... | collective-permute-start | bytes 3145736 | tf_op jit(solution)/shard_map/ppermute | solution.py:48
  32.2 12.5 %collective-permute-start.9 = (bf16[144,2048]{1,0:T(8,128)(2,1)S(1)}, bf16[144,2048]{1,0:T(8,128)(2,1)S(1)}, u32[]{:S(2)}, u32[]{:S(2)}) collective-permute-start(bf16[144,2048]{1,0:T(8,128)(2,1)S(1)} %collective-permute-done.8.r_6_.refs_8_.refs_11_), channel_id=1, source_target_pairs={{0,32},{1,97},{2,34},{3,99},{4,36},{5,101},{6,38},{7,103},{8,40},{... | collective-permute-start | bytes 1769480 | tf_op jit(solution)/shard_map/ppermute | solution.py:48
  32.2 13.0 %collective-permute-start.11 = (bf16[144,2048]{1,0:T(8,128)(2,1)S(1)}, bf16[144,2048]{1,0:T(8,128)(2,1)S(1)}, u32[]{:S(2)}, u32[]{:S(2)}) collective-permute-start(bf16[144,2048]{1,0:T(8,128)(2,1)S(1)} %collective-permute-done.3.r_4_.refs_6_.refs_9_), channel_id=1, source_target_pairs={{0,1},{1,0},{2,3},{3,2},{4,5},{5,4},{6,7},{7,6},{8,9},{9,8},{10,11... | collective-permute-start | bytes 1769480 | tf_op jit(solution)/shard_map/ppermute | solution.py:48
  44.6 2.0 %collective-permute-start.12 = (bf16[144,2048]{1,0:T(8,128)(2,1)S(1)}, bf16[144,2048]{1,0:T(8,128)(2,1)S(1)}, u32[]{:S(2)}, u32[]{:S(2)}) collective-permute-start(bf16[144,2048]{1,0:T(8,128)(2,1)S(1)} %collective-permute-done.8.r_6_.refs_8_.refs_11_), channel_id=1, source_target_pairs={{0,1},{1,0},{2,3},{3,2},{4,5},{5,4},{6,7},{7,6},{8,9},{9,8},{10,11... | collective-permute-start | bytes 1769480 | tf_op jit(solution)/shard_map/ppermute | solution.py:48
  44.6 6.4 %collective-permute-start.10 = (bf16[144,2048]{1,0:T(8,128)(2,1)S(1)}, bf16[144,2048]{1,0:T(8,128)(2,1)S(1)}, u32[]{:S(2)}, u32[]{:S(2)}) collective-permute-start(bf16[144,2048]{1,0:T(8,128)(2,1)S(1)} %collective-permute-done.9.refs_4_.refs_10_.refs_13_), channel_id=1, source_target_pairs={{0,1},{1,0},{2,3},{3,2},{4,5},{5,4},{6,7},{7,6},{8,9},{9,8},{10,11... | collective-permute-start | bytes 1769480 | tf_op jit(solution)/shard_map/ppermute | solution.py:48
  52.5 1.3 %collective-permute-start.13 = (f32[8,1024]{1,0:T(8,128)S(1)}, f32[8,1024]{1,0:T(8,128)S(1)}, u32[]{:S(2)}, u32[]{:S(2)}) collective-permute-start(f32[8,1024]{1,0:T(8,128)S(1)} %get-tuple-element.45.r_0_.r_7_.raw), channel_id=1, source_target_pairs={{0,1},{1,0},{2,3},{3,2},{4,5},{5,4},{6,7},{7,6},{8,9},{9,8},{10,11... | collective-permute-start | bytes 98312 | tf_op jit(solution)/shard_map/ppermute | solution.py:48
  53.8 5.4 %collective-permute-start.14 = (f32[8,1024]{1,0:T(8,128)S(1)}, f32[8,1024]{1,0:T(8,128)S(1)}, u32[]{:S(2)}, u32[]{:S(2)}) collective-permute-start(f32[8,1024]{1,0:T(8,128)S(1)} %shard_map.82.r_12_.r_0_), channel_id=1, source_target_pairs={{0,32},{1,97},{2,34},{3,99},{4,36},{5,101},{6,38},{7,103},{8,40},{... | collective-permute-start | bytes 98312 | tf_op jit(solution)/shard_map/ppermute | solution.py:48
  59.2 5.5 %collective-permute-start.15 = (f32[8,1024]{1,0:T(8,128)S(1)}, f32[8,1024]{1,0:T(8,128)S(1)}, u32[]{:S(2)}, u32[]{:S(2)}) collective-permute-start(f32[8,1024]{1,0:T(8,128)S(1)} %shard_map.84.r_12_.stats), channel_id=1, source_target_pairs={{0,64},{1,65},{2,66},{3,67},{4,68},{5,69},{6,70},{7,71},{8,72},{9,... | collective-permute-start | bytes 98312 | tf_op jit(solution)/shard_map/ppermute | solution.py:48
  65.2 4.9 %collective-permute-start.16 = (bf16[640,2048]{1,0:T(8,128)(2,1)S(1)}, bf16[640,2048]{1,0:T(8,128)(2,1)S(1)}, u32[]{:S(2)}, u32[]{:S(2)}) collective-permute-start(bf16[640,2048]{1,0:T(8,128)(2,1)S(1)} %shard_map.85._), channel_id=1, source_target_pairs={{0,1},{1,0},{2,3},{3,2},{4,5},{5,4},{6,7},{7,6},{8,9},{9,8},{10,11... | collective-permute-start | bytes 7864328 | tf_op jit(solution)/shard_map/ppermute | solution.py:48
  66.5 28.6 %collective-permute-start.21 = (bf16[256,2048]{1,0:T(8,128)(2,1)S(1)}, bf16[256,2048]{1,0:T(8,128)(2,1)S(1)}, u32[]{:S(2)}, u32[]{:S(2)}) collective-permute-start(bf16[256,2048]{1,0:T(8,128)(2,1)S(1)} %shard_map.91.refs_15_), channel_id=1, source_target_pairs={{0,4},{1,17},{2,6},{3,19},{4,0},{5,21},{6,2},{7,23},{8,12},{9,25},... | collective-permute-start | bytes 3145736 | tf_op jit(solution)/shard_map/ppermute | solution.py:48
  70.4 9.2 %collective-permute-start.17 = (bf16[128,2048]{1,0:T(8,128)(2,1)S(1)}, bf16[128,2048]{1,0:T(8,128)(2,1)S(1)}, u32[]{:S(2)}, u32[]{:S(2)}) collective-permute-start(bf16[128,2048]{1,0:T(8,128)(2,1)S(1)} %shard_map.87), channel_id=1, source_target_pairs={{0,96},{1,33},{2,98},{3,35},{4,100},{5,37},{6,102},{7,39},{8,104},... | collective-permute-start | bytes 1572872 | tf_op jit(solution)/shard_map/ppermute | solution.py:48
  75.4 19.7 %collective-permute-start.20 = (bf16[256,2048]{1,0:T(8,128)(2,1)S(1)}, bf16[256,2048]{1,0:T(8,128)(2,1)S(1)}, u32[]{:S(2)}, u32[]{:S(2)}) collective-permute-start(bf16[256,2048]{1,0:T(8,128)(2,1)S(1)} %get-tuple-element.58), channel_id=1, source_target_pairs={{0,6},{1,25},{2,0},{3,27},{4,2},{5,29},{6,4},{7,31},{8,14},{9,1},{... | collective-permute-start | bytes 3145736 | tf_op jit(solution)/shard_map/ppermute | solution.py:48
  78.7 16.4 %collective-permute-start.22 = (bf16[256,2048]{1,0:T(8,128)(2,1)S(1)}, bf16[256,2048]{1,0:T(8,128)(2,1)S(1)}, u32[]{:S(2)}, u32[]{:S(2)}) collective-permute-start(bf16[256,2048]{1,0:T(8,128)(2,1)S(1)} %get-tuple-element.59), channel_id=1, source_target_pairs={{0,2},{1,9},{2,4},{3,11},{4,6},{5,13},{6,0},{7,15},{8,10},{9,17},{... | collective-permute-start | bytes 3145736 | tf_op jit(solution)/shard_map/ppermute | solution.py:48
  80.0 9.4 %collective-permute-start.18 = (bf16[128,2048]{1,0:T(8,128)(2,1)S(1)}, bf16[128,2048]{1,0:T(8,128)(2,1)S(1)}, u32[]{:S(2)}, u32[]{:S(2)}) collective-permute-start(bf16[128,2048]{1,0:T(8,128)(2,1)S(1)} %shard_map.88), channel_id=1, source_target_pairs={{0,96},{1,33},{2,98},{3,35},{4,100},{5,37},{6,102},{7,39},{8,104},... | collective-permute-start | bytes 1572872 | tf_op jit(solution)/shard_map/ppermute | solution.py:48
  89.7 10.5 %collective-permute-start.19 = (bf16[128,2048]{1,0:T(8,128)(2,1)S(1)}, bf16[128,2048]{1,0:T(8,128)(2,1)S(1)}, u32[]{:S(2)}, u32[]{:S(2)}) collective-permute-start(bf16[128,2048]{1,0:T(8,128)(2,1)S(1)} %shard_map.89), channel_id=1, source_target_pairs={{0,96},{1,33},{2,98},{3,35},{4,100},{5,37},{6,102},{7,39},{8,104},... | collective-permute-start | bytes 1572872 | tf_op jit(solution)/shard_map/ppermute | solution.py:48
  95.5 9.1 %collective-permute-start.23 = (bf16[64,2048]{1,0:T(8,128)(2,1)S(1)}, bf16[64,2048]{1,0:T(8,128)(2,1)S(1)}, u32[]{:S(2)}, u32[]{:S(2)}) collective-permute-start(bf16[64,2048]{1,0:T(8,128)(2,1)S(1)} %get-tuple-element.61), channel_id=1, source_target_pairs={{0,24},{1,7},{2,26},{3,1},{4,28},{5,3},{6,30},{7,5},{8,0},{9,15},{... | collective-permute-start | bytes 786440 | tf_op jit(solution)/shard_map/ppermute | solution.py:48
  97.9 8.0 %collective-permute-start.24 = (bf16[64,2048]{1,0:T(8,128)(2,1)S(1)}, bf16[64,2048]{1,0:T(8,128)(2,1)S(1)}, u32[]{:S(2)}, u32[]{:S(2)}) collective-permute-start(bf16[64,2048]{1,0:T(8,128)(2,1)S(1)} %get-tuple-element.62), channel_id=1, source_target_pairs={{0,16},{1,5},{2,18},{3,7},{4,20},{5,1},{6,22},{7,3},{8,24},{9,13},... | collective-permute-start | bytes 786440 | tf_op jit(solution)/shard_map/ppermute | solution.py:48
  99.1 9.5 %collective-permute-start.25 = (bf16[64,2048]{1,0:T(8,128)(2,1)S(1)}, bf16[64,2048]{1,0:T(8,128)(2,1)S(1)}, u32[]{:S(2)}, u32[]{:S(2)}) collective-permute-start(bf16[64,2048]{1,0:T(8,128)(2,1)S(1)} %get-tuple-element.63), channel_id=1, source_target_pairs={{0,8},{1,3},{2,10},{3,5},{4,12},{5,7},{6,14},{7,1},{8,16},{9,11},{... | collective-permute-start | bytes 786440 | tf_op jit(solution)/shard_map/ppermute | solution.py:48

commit v5 on v4

--- a/solution.py
+++ b/solution.py
@@ -183,7 +183,7 @@
             score_block(place, piece, pair, a, b, part, ts[i], writer(info, 16 * i, 256 * pair))
 
 
-SOON, LATER = (0, 3), (1, 2)
+SOON, LATER = (0, 2), (1, 3)
 
 
 class Info:
@@ -272,10 +272,11 @@
     refs[-1][...] = jnp.concatenate([*both, jnp.zeros((5, 1024), F32)], axis=0)
 
 
-def block_kernel(k, mine, theirs, factor, *refs):
+def block_kernel(k, mine, theirs, factor, extra, *refs):
     got, out_ref = refs[0], refs[1 if k < 3 else 0]
     if k == 0:
         refs[2][...] = jnp.zeros((8, 128), F32)
+        refs[3][...] = extra[1:2, 0:128]
     rows = slice(128 * k, 128 * k + 128)
     f = factor[...]
     for n in range(4):
@@ -300,12 +301,12 @@
     out_ref[...] = v.astype(BF)
 
 
-def total_kernel(raw, other, stats, got, _, lse_ref, loss_ref, factor_ref):
+def total_kernel(raw, other, stats, got, _, lse_ref, factor_ref):
     acc = merge(unpack(stats[...]), unpack(aligned(got[...], 2)))
     lse = acc[0] + jnp.log(acc[1])
-    lse_ref[...] = jnp.broadcast_to(lse, (8, 1024))
     chosen = acc[2][:, 0:128]
-    loss_ref[...] = lse[:, 0:128] - chosen
+    loss = jnp.concatenate([lse[:, 0:128] - chosen, jnp.zeros((1, 896), F32)], axis=1)
+    lse_ref[...] = jnp.concatenate([lse, loss, jnp.zeros((6, 1024), F32)], axis=0)
     rows = []
     for top in (raw[0:1, :], swap(other[...])[0:1]):
         f = jnp.exp(top - lse) * SHARP
@@ -405,8 +406,8 @@
             2 * 512 * 768 * WIDTH,
         )(*[pieces[i] for i in which], *tiles[:6])
 
-    t0, t3, soon = early(SOON)
-    t1, t2, later = early(LATER)
+    t0, t2, soon = early(SOON)
+    t1, t3, later = early(LATER)
     info_b, raw = call(
         late_kernel, (shape(64, 256, F32), shape(8, 1024, F32)), [VMEM] * 8, 2 * 1024 * 256 * WIDTH
     )(*pieces, *tiles[6:], soon, later)
@@ -429,8 +430,8 @@
     both = call(lambda *r: merge_kernel(1, *r), shape(8, 1024, F32), [VMEM] * 3)(stats, send(stats, along(1)), mine)
     four = send(both, along(2))
     theirs = query(1, BF, both)
-    lse, loss, factor = call(
-        total_kernel, (shape(8, 1024, F32), shape(1, 128, F32), shape(128, 128, F32)), [VMEM] * 5
+    lse, factor = call(
+        total_kernel, (shape(8, 1024, F32), shape(128, 128, F32)), [VMEM] * 5
     )(raw, other, both, four, theirs)
     theirs, lse = tied(theirs, lse)
     theirs = send(theirs, CORE)
@@ -446,16 +447,16 @@
         [VMEM] * 16,
         2 * 768 * 1024 * WIDTH,
         scratch=[pltpu.VMEM((768, 1024), BF)],
-    )(t0, t1, t3, *infos, lse, *tiles, far)
+    )(t0, t1, t3, *infos, lse, *tiles, theirs)
     def block(k, *got):
         kernel = lambda *r: block_kernel(k, *r)
-        outs = (shape(128, WIDTH, BF), shape(8, 128, F32)) if k == 0 else shape(128, WIDTH, BF)
-        return call(kernel, outs, [VMEM] * (3 + len(got)))(mine, theirs, factor, *got)
+        outs = (shape(128, WIDTH, BF), shape(8, 128, F32), shape(1, 128, F32)) if k == 0 else shape(128, WIDTH, BF)
+        return call(kernel, outs, [VMEM] * (4 + len(got)))(mine, theirs, factor, lse, *got)
 
     run = block(3)
     for k in (2, 1, 0):
         run = block(k, send(run, along(-1)))
-    run, token = run
+    run, token, loss = run
 
     one = send(one, second(-1))
     three = send(three, second(1))

time: 110 us -> 105 us (0.955)
  waiting for transfers between devices: 50.4 us -> 47 us
    ppermute x26, waiting for transfers between devices: 50.4 us -> 47 us  [send(): return lax.ppermute(v, AXES, perm)]
  transfers between devices with their start and end apart: 26 -> 26, of which waited for: 18 -> 18; matrix products, arithmetic and copies ran while one was open for 0% -> 0% of each run, Pallas kernels for 16% -> 17%
where the time goes in v5:
time: 105 us
  waiting for transfers between devices  47 us (45%)
  starting transfers between devices  33.3 us (32%)
  Pallas kernels  22.1 us (21%)
  local copies, waits for them, and re-layouts  2.01 us (2%)
    ppermute x26, waiting for transfers between devices, send(): return lax.ppermute(v, AXES, perm)  47 us
    ppermute x26, starting transfers between devices, send(): return lax.ppermute(v, AXES, perm)  33.3 us
    pallas_call x2, Pallas kernels, query(): call(lambda *r: query_kernel(half, *r), shape(640, WIDTH, kind), [VMEM] *...  5.9 us
    pallas_call x2, Pallas kernels, early(): call(lambda *r: early_kernel(which, *r), (tile, tile, shape(32, 768, F32)...  4.26 us
    pallas_call x1, Pallas kernels, local(): call(near_kernel, (shape(256, WIDTH, F32), shape(256, WIDTH, BF), shape(2...  3.5 us
    pallas_call x4, Pallas kernels, block(): call(kernel, outs, [VMEM] * (4 + len(got)))(mine, theirs, factor, lse, *got)  2.14 us
  transfers between devices with their start and end apart: 26, of which 18 were waited for; matrix products, arithmetic and copies ran while one was open for 0% of the time, Pallas kernels for 17%

profile of v5, /device:TPU:0, one launch (start us, length us, event | category | flops | bytes accessed | tf_op | source)
XLA Modules:
  0.0 105.2 jit_solution(6713478775553162987)
XLA Ops:
  0.6 1.9 %shard_map.76.a_ref = bf16[144,2048]{1,0:T(8,128)(2,1)} custom-call(bf16[128,2048]{1,0:T(8,128)(2,1)} %q_ref.1, s32[16,128]{1,0:T(8,128)} %bitcast.4, s32[16,128]{1,0:T(8,128)} %bitcast.5, s32[1,128]{1,0:T(1,128)} %bitcast.6), custom_call_target="tpu_custom_call" | custom-call | tf_op jit(solution)/shard_map/pallas_call | solution.py:361
  2.6 1.7 %collective-permute-start.3 = (bf16[144,2048]{1,0:T(8,128)(2,1)}, bf16[144,2048]{1,0:T(8,128)(2,1)S(1)}, u32[]{:S(2)}, u32[]{:S(2)}) collective-permute-start(bf16[144,2048]{1,0:T(8,128)(2,1)} %shard_map.76.a_ref), channel_id=1, source_target_pairs={{0,32},{1,97},{2,34},{3,99},{4,36},{5,101},{6,38},{7,103},{8,40},{... | collective-permute-start | bytes 1769480 | tf_op jit(solution)/shard_map/ppermute | solution.py:48
  5.3 1.5 %collective-permute-start = (bf16[64,2048]{1,0:T(8,128)(2,1)}, bf16[64,2048]{1,0:T(8,128)(2,1)S(1)}, u32[]{:S(2)}, u32[]{:S(2)}) collective-permute-start(bf16[64,2048]{1,0:T(8,128)(2,1)} %b_ref.1), channel_id=1, source_target_pairs={{0,8},{1,3},{2,10},{3,5},{4,12},{5,7},{6,14},{7,1},{8,16},{9,11},{... | collective-permute-start | bytes 786440 | tf_op jit(solution)/shard_map/ppermute | solution.py:48
  6.8 1.7 %collective-permute-start.1 = (bf16[64,2048]{1,0:T(8,128)(2,1)}, bf16[64,2048]{1,0:T(8,128)(2,1)S(1)}, u32[]{:S(2)}, u32[]{:S(2)}) collective-permute-start(bf16[64,2048]{1,0:T(8,128)(2,1)} %b_ref.1), channel_id=1, source_target_pairs={{0,24},{1,7},{2,26},{3,1},{4,28},{5,3},{6,30},{7,5},{8,0},{9,15},{... | collective-permute-start | bytes 786440 | tf_op jit(solution)/shard_map/ppermute | solution.py:48
  8.5 1.8 %collective-permute-start.2 = (bf16[64,2048]{1,0:T(8,128)(2,1)}, bf16[64,2048]{1,0:T(8,128)(2,1)S(1)}, u32[]{:S(2)}, u32[]{:S(2)}) collective-permute-start(bf16[64,2048]{1,0:T(8,128)(2,1)} %b_ref.1), channel_id=1, source_target_pairs={{0,16},{1,5},{2,18},{3,7},{4,20},{5,1},{6,22},{7,3},{8,24},{9,13},... | collective-permute-start | bytes 786440 | tf_op jit(solution)/shard_map/ppermute | solution.py:48
  13.1 2.5 %collective-permute-done.1.refs_3_ = bf16[64,2048]{1,0:T(8,128)(2,1)S(1)} collective-permute-done((bf16[64,2048]{1,0:T(8,128)(2,1)}, bf16[64,2048]{1,0:T(8,128)(2,1)S(1)}, u32[]{:S(2)}, u32[]{:S(2)}) %collective-permute-start.1) | collective-permute-done | bytes 262176 | tf_op jit(solution)/shard_map/ppermute | solution.py:48
  15.6 1.3 %collective-permute-done.2.refs_2_ = bf16[64,2048]{1,0:T(8,128)(2,1)S(1)} collective-permute-done((bf16[64,2048]{1,0:T(8,128)(2,1)}, bf16[64,2048]{1,0:T(8,128)(2,1)S(1)}, u32[]{:S(2)}, u32[]{:S(2)}) %collective-permute-start.2) | collective-permute-done | bytes 262176 | tf_op jit(solution)/shard_map/ppermute | solution.py:48
  17.0 4.0 %collective-permute-start.5 = (bf16[256,2048]{1,0:T(8,128)(2,1)S(1)}, bf16[256,2048]{1,0:T(8,128)(2,1)S(1)}, u32[]{:S(2)}, u32[]{:S(2)}) collective-permute-start(bf16[256,2048]{1,0:T(8,128)(2,1)S(1)} %shard_map.78.r_0_.refs_0_.r_8_), channel_id=1, source_target_pairs={{0,4},{1,17},{2,6},{3,19},{4,0},{5,21},{6,2},{7,23},{8,12},{9,25},... | collective-permute-start | bytes 3145736 | tf_op jit(solution)/shard_map/ppermute | solution.py:48
  22.5 2.2 %collective-permute-start.10 = (bf16[256,2048]{1,0:T(8,128)(2,1)S(1)}, bf16[256,2048]{1,0:T(8,128)(2,1)S(1)}, u32[]{:S(2)}, u32[]{:S(2)}) collective-permute-start(bf16[256,2048]{1,0:T(8,128)(2,1)S(1)} %shard_map.78.r_0_.refs_0_.r_8_), channel_id=1, source_target_pairs={{0,6},{1,25},{2,0},{3,27},{4,2},{5,29},{6,4},{7,31},{8,14},{9,1},{... | collective-permute-start | bytes 3145736 | tf_op jit(solution)/shard_map/ppermute | solution.py:48
  24.7 7.3 %collective-permute-done.6.r_6_.refs_11_.refs_8_ = bf16[144,2048]{1,0:T(8,128)(2,1)S(1)} collective-permute-done((bf16[144,2048]{1,0:T(8,128)(2,1)S(1)}, bf16[144,2048]{1,0:T(8,128)(2,1)S(1)}, u32[]{:S(2)}, u32[]{:S(2)}) %collective-permute-start.6) | collective-permute-done | bytes 589856 | tf_op jit(solution)/shard_map/ppermute | solution.py:48
  32.0 1.8 %collective-permute-done.5.r_1_.refs_2_.r_10_ = bf16[256,2048]{1,0:T(8,128)(2,1)S(1)} collective-permute-done((bf16[256,2048]{1,0:T(8,128)(2,1)S(1)}, bf16[256,2048]{1,0:T(8,128)(2,1)S(1)}, u32[]{:S(2)}, u32[]{:S(2)}) %collective-permute-start.5) | collective-permute-done | bytes 1048608 | tf_op jit(solution)/shard_map/ppermute | solution.py:48
  33.8 9.3 %collective-permute-done.11.refs_4_.refs_13_.refs_10_ = bf16[144,2048]{1,0:T(8,128)(2,1)S(1)} collective-permute-done((bf16[144,2048]{1,0:T(8,128)(2,1)S(1)}, bf16[144,2048]{1,0:T(8,128)(2,1)S(1)}, u32[]{:S(2)}, u32[]{:S(2)}) %collective-permute-start.11) | collective-permute-done | bytes 589856 | tf_op jit(solution)/shard_map/ppermute | solution.py:48
  43.1 2.1 %shard_map.79 = (f32[256,256]{1,0:T(8,128)S(1)}, f32[256,256]{1,0:T(8,128)S(1)}, f32[32,768]{1,0:T(8,128)S(1)}) custom-call(bf16[256,2048]{1,0:T(8,128)(2,1)S(1)} %shard_map.78.r_0_.refs_0_.r_8_, bf16[256,2048]{1,0:T(8,128)(2,1)S(1)} %collective-permute-done.5.r_1_.refs_2_.r_10_, bf16[144,2048]{1,0:T(8,128)(2,1)S(1)} %get-tuple-element.38.r_2_.refs_7_.refs_4_, ...), custom_call_target="tpu_custom_call" | custom-call | flops 1610612736 | tf_op jit(solution)/shard_map/pallas_call | solution.py:402
  46.0 2.1 %shard_map.80 = (f32[256,256]{1,0:T(8,128)S(1)}, f32[256,256]{1,0:T(8,128)S(1)}, f32[32,768]{1,0:T(8,128)S(1)}) custom-call(bf16[256,2048]{1,0:T(8,128)(2,1)S(1)} %collective-permute-done.9.r_0_.refs_1_.r_9_, bf16[256,2048]{1,0:T(8,128)(2,1)S(1)} %collective-permute-done.10.r_1_.refs_3_.r_11_, bf16[144,2048]{1,0:T(8,128)(2,1)S(1)} %get-tuple-element.38.r_2_.refs_7_.refs_4_, ...), custom_call_target="tpu_custom_call" | custom-call | flops 1610612736 | tf_op jit(solution)/shard_map/pallas_call | solution.py:402
  48.1 1.4 %shard_map.81 = (f32[64,256]{1,0:T(8,128)S(1)}, f32[8,1024]{1,0:T(8,128)S(1)}) custom-call(bf16[256,2048]{1,0:T(8,128)(2,1)S(1)} %shard_map.78.r_0_.refs_0_.r_8_, bf16[256,2048]{1,0:T(8,128)(2,1)S(1)} %collective-permute-done.9.r_0_.refs_1_.r_9_, bf16[256,2048]{1,0:T(8,128)(2,1)S(1)} %collective-permute-done.5.r_1_.refs_2_.r_10_, ...), custom_call_target="tpu_custom_call" | custom-call | flops 1073741824 | tf_op jit(solution)/shard_map/pallas_call | solution.py:411
  51.7 2.9 %shard_map.83.r_2_.r_0_ = f32[640,2048]{1,0:T(8,128)S(1)} custom-call(f32[256,256]{1,0:T(8,128)S(1)} %get-tuple-element.43.r_0_.refs_0_, f32[256,256]{1,0:T(8,128)S(1)} %get-tuple-element.44.r_1_.refs_1_, f32[256,256]{1,0:T(8,128)S(1)} %get-tuple-element.45.r_2_.t_ref, f32[256,256]{1,0:T(8,128)S(1)} %get-tuple-element.46.r_3_.refs_2_, ...), custom_call_target="tpu_custom_call" | custom-call | flops 2684354560 | tf_op jit(solution)/shard_map/pallas_call | solution.py:421
  54.6 1.6 %collective-permute-done.14.r_1_ = f32[8,1024]{1,0:T(8,128)S(1)} collective-permute-done((f32[8,1024]{1,0:T(8,128)S(1)}, f32[8,1024]{1,0:T(8,128)S(1)}, u32[]{:S(2)}, u32[]{:S(2)}) %collective-permute-start.14) | collective-permute-done | bytes 32800 | tf_op jit(solution)/shard_map/ppermute | solution.py:48
  57.0 3.0 %shard_map.85._ = bf16[640,2048]{1,0:T(8,128)(2,1)S(1)} custom-call(f32[256,256]{1,0:T(8,128)S(1)} %get-tuple-element.43.r_0_.refs_0_, f32[256,256]{1,0:T(8,128)S(1)} %get-tuple-element.44.r_1_.refs_1_, f32[256,256]{1,0:T(8,128)S(1)} %get-tuple-element.45.r_2_.t_ref, f32[256,256]{1,0:T(8,128)S(1)} %get-tuple-element.46.r_3_.refs_2_, ...), custom_call_target="tpu_custom_call" | custom-call | flops 2684354560 | tf_op jit(solution)/shard_map/pallas_call | solution.py:421
  60.0 1.8 %collective-permute-done.15.got = f32[8,1024]{1,0:T(8,128)S(1)} collective-permute-done((f32[8,1024]{1,0:T(8,128)S(1)}, f32[8,1024]{1,0:T(8,128)S(1)}, u32[]{:S(2)}, u32[]{:S(2)}) %collective-permute-start.15) | collective-permute-done | bytes 32800 | tf_op jit(solution)/shard_map/ppermute | solution.py:48
  62.0 1.3 %shard_map.92 = bf16[256,2048]{1,0:T(8,128)(2,1)S(1)} custom-call(f32[256,256]{1,0:T(8,128)S(1)} %get-tuple-element.45.r_2_.t_ref, f32[32,768]{1,0:T(8,128)S(1)} %get-tuple-element.47.refs_6_.r_4_.refs_3_.refs_0_, f32[32,768]{1,0:T(8,128)S(1)} %get-tuple-element.48.refs_7_.r_5_.refs_4_.refs_1_, f32[64,256]{1,0:T(8,128)S(1)} %get-tuple-element.49.r_6_.refs_5_.refs_2_, ...), custom_call_target="tpu_custom_call" | custom-call | flops 1073741824 | tf_op jit(solution)/shard_map/pallas_call | solution.py:439
  63.3 2.6 %collective-permute-start.21 = (bf16[256,2048]{1,0:T(8,128)(2,1)S(1)}, bf16[256,2048]{1,0:T(8,128)(2,1)S(1)}, u32[]{:S(2)}, u32[]{:S(2)}) collective-permute-start(bf16[256,2048]{1,0:T(8,128)(2,1)S(1)} %shard_map.92), channel_id=1, source_target_pairs={{0,4},{1,17},{2,6},{3,19},{4,0},{5,21},{6,2},{7,23},{8,12},{9,25},... | collective-permute-start | bytes 3145736 | tf_op jit(solution)/shard_map/ppermute | solution.py:48
  68.3 3.5 %shard_map.91 = (f32[256,2048]{1,0:T(8,128)S(1)}, bf16[256,2048]{1,0:T(8,128)(2,1)S(1)}, bf16[256,2048]{1,0:T(8,128)(2,1)S(1)}) custom-call(f32[256,256]{1,0:T(8,128)S(1)} %get-tuple-element.43.r_0_.refs_0_, f32[256,256]{1,0:T(8,128)S(1)} %get-tuple-element.44.r_1_.refs_1_, f32[256,256]{1,0:T(8,128)S(1)} %get-tuple-element.46.r_3_.refs_2_, ...), custom_call_target="tpu_custom_call" | custom-call | flops 3221225472 | tf_op jit(solution)/shard_map/pallas_call | solution.py:444
  71.8 2.7 %collective-permute-start.20 = (bf16[256,2048]{1,0:T(8,128)(2,1)S(1)}, bf16[256,2048]{1,0:T(8,128)(2,1)S(1)}, u32[]{:S(2)}, u32[]{:S(2)}) collective-permute-start(bf16[256,2048]{1,0:T(8,128)(2,1)S(1)} %get-tuple-element.58), channel_id=1, source_target_pairs={{0,6},{1,25},{2,0},{3,27},{4,2},{5,29},{6,4},{7,31},{8,14},{9,1},{... | collective-permute-start | bytes 3145736 | tf_op jit(solution)/shard_map/ppermute | solution.py:48
  74.5 1.9 %collective-permute-done.17.r_4_ = bf16[128,2048]{1,0:T(8,128)(2,1)S(1)} collective-permute-done((bf16[128,2048]{1,0:T(8,128)(2,1)S(1)}, bf16[128,2048]{1,0:T(8,128)(2,1)S(1)}, u32[]{:S(2)}, u32[]{:S(2)}) %collective-permute-start.17) | collective-permute-done | bytes 524320 | tf_op jit(solution)/shard_map/ppermute | solution.py:48
  76.7 2.4 %collective-permute-start.18 = (bf16[128,2048]{1,0:T(8,128)(2,1)S(1)}, bf16[128,2048]{1,0:T(8,128)(2,1)S(1)}, u32[]{:S(2)}, u32[]{:S(2)}) collective-permute-start(bf16[128,2048]{1,0:T(8,128)(2,1)S(1)} %shard_map.88), channel_id=1, source_target_pairs={{0,96},{1,33},{2,98},{3,35},{4,100},{5,37},{6,102},{7,39},{8,104},... | collective-permute-start | bytes 1572872 | tf_op jit(solution)/shard_map/ppermute | solution.py:48
  79.1 6.9 %collective-permute-done.18.r_4_ = bf16[128,2048]{1,0:T(8,128)(2,1)S(1)} collective-permute-done((bf16[128,2048]{1,0:T(8,128)(2,1)S(1)}, bf16[128,2048]{1,0:T(8,128)(2,1)S(1)}, u32[]{:S(2)}, u32[]{:S(2)}) %collective-permute-start.18) | collective-permute-done | bytes 524320 | tf_op jit(solution)/shard_map/ppermute | solution.py:48
  86.3 3.6 %collective-permute-start.19 = (bf16[128,2048]{1,0:T(8,128)(2,1)S(1)}, bf16[128,2048]{1,0:T(8,128)(2,1)S(1)}, u32[]{:S(2)}, u32[]{:S(2)}) collective-permute-start(bf16[128,2048]{1,0:T(8,128)(2,1)S(1)} %shard_map.89), channel_id=1, source_target_pairs={{0,96},{1,33},{2,98},{3,35},{4,100},{5,37},{6,102},{7,39},{8,104},... | collective-permute-start | bytes 1572872 | tf_op jit(solution)/shard_map/ppermute | solution.py:48
  91.3 2.3 %collective-permute-start.23 = (bf16[64,2048]{1,0:T(8,128)(2,1)S(1)}, bf16[64,2048]{1,0:T(8,128)(2,1)S(1)}, u32[]{:S(2)}, u32[]{:S(2)}) collective-permute-start(bf16[64,2048]{1,0:T(8,128)(2,1)S(1)} %get-tuple-element.61), channel_id=1, source_target_pairs={{0,24},{1,7},{2,26},{3,1},{4,28},{5,3},{6,30},{7,5},{8,0},{9,15},{... | collective-permute-start | bytes 786440 | tf_op jit(solution)/shard_map/ppermute | solution.py:48
  94.9 1.6 %collective-permute-done.19.r_4_ = bf16[128,2048]{1,0:T(8,128)(2,1)S(1)} collective-permute-done((bf16[128,2048]{1,0:T(8,128)(2,1)S(1)}, bf16[128,2048]{1,0:T(8,128)(2,1)S(1)}, u32[]{:S(2)}, u32[]{:S(2)}) %collective-permute-start.19) | collective-permute-done | bytes 524320 | tf_op jit(solution)/shard_map/ppermute | solution.py:48
  96.5 1.3 %shard_map.90 = (bf16[128,2048]{1,0:T(8,128)(2,1)}, f32[8,128]{1,0:T(8,128)S(1)}, f32[1,128]{1,0:T(1,128)}) custom-call(f32[640,2048]{1,0:T(8,128)S(1)} %shard_map.83.r_2_.r_0_, bf16[640,2048]{1,0:T(8,128)(2,1)S(1)} %collective-permute-done.16.r_1_.refs_15_, f32[128,128]{1,0:T(8,128)S(1)} %get-tuple-element.53.r_2_, ...), custom_call_target="tpu_custom_call" | custom-call | tf_op jit(solution)/shard_map/pallas_call | solution.py:454
  97.8 2.6 %collective-permute-done.23.b = bf16[64,2048]{1,0:T(8,128)(2,1)S(1)} collective-permute-done((bf16[64,2048]{1,0:T(8,128)(2,1)S(1)}, bf16[64,2048]{1,0:T(8,128)(2,1)S(1)}, u32[]{:S(2)}, u32[]{:S(2)}) %collective-permute-start.23) | collective-permute-done | bytes 262176 | tf_op jit(solution)/shard_map/ppermute | solution.py:48
  101.6 2.7 %collective-permute-done.25.d = bf16[64,2048]{1,0:T(8,128)(2,1)S(1)} collective-permute-done((bf16[64,2048]{1,0:T(8,128)(2,1)S(1)}, bf16[64,2048]{1,0:T(8,128)(2,1)S(1)}, u32[]{:S(2)}, u32[]{:S(2)}) %collective-permute-start.25) | collective-permute-done | bytes 262176 | tf_op jit(solution)/shard_map/ppermute | solution.py:48
  (43 shorter events, 17.2 us)
Async XLA Ops:
  2.6 14.3 %collective-permute-start.3 = (bf16[144,2048]{1,0:T(8,128)(2,1)}, bf16[144,2048]{1,0:T(8,128)(2,1)S(1)}, u32[]{:S(2)}, u32[]{:S(2)}) collective-permute-start(bf16[144,2048]{1,0:T(8,128)(2,1)} %shard_map.76.a_ref), channel_id=1, source_target_pairs={{0,32},{1,97},{2,34},{3,99},{4,36},{5,101},{6,38},{7,103},{8,40},{... | collective-permute-start | bytes 1769480 | tf_op jit(solution)/shard_map/ppermute | solution.py:48
  4.3 12.6 %collective-permute-start.4 = (bf16[144,2048]{1,0:T(8,128)(2,1)}, bf16[144,2048]{1,0:T(8,128)(2,1)S(1)}, u32[]{:S(2)}, u32[]{:S(2)}) collective-permute-start(bf16[144,2048]{1,0:T(8,128)(2,1)} %shard_map.76.a_ref), channel_id=1, source_target_pairs={{0,1},{1,0},{2,3},{3,2},{4,5},{5,4},{6,7},{7,6},{8,9},{9,8},{10,11... | collective-permute-start | bytes 1769480 | tf_op jit(solution)/shard_map/ppermute | solution.py:48
  5.3 7.8 %collective-permute-start = (bf16[64,2048]{1,0:T(8,128)(2,1)}, bf16[64,2048]{1,0:T(8,128)(2,1)S(1)}, u32[]{:S(2)}, u32[]{:S(2)}) collective-permute-start(bf16[64,2048]{1,0:T(8,128)(2,1)} %b_ref.1), channel_id=1, source_target_pairs={{0,8},{1,3},{2,10},{3,5},{4,12},{5,7},{6,14},{7,1},{8,16},{9,11},{... | collective-permute-start | bytes 786440 | tf_op jit(solution)/shard_map/ppermute | solution.py:48
  6.8 8.8 %collective-permute-start.1 = (bf16[64,2048]{1,0:T(8,128)(2,1)}, bf16[64,2048]{1,0:T(8,128)(2,1)S(1)}, u32[]{:S(2)}, u32[]{:S(2)}) collective-permute-start(bf16[64,2048]{1,0:T(8,128)(2,1)} %b_ref.1), channel_id=1, source_target_pairs={{0,24},{1,7},{2,26},{3,1},{4,28},{5,3},{6,30},{7,5},{8,0},{9,15},{... | collective-permute-start | bytes 786440 | tf_op jit(solution)/shard_map/ppermute | solution.py:48
  8.5 8.3 %collective-permute-start.2 = (bf16[64,2048]{1,0:T(8,128)(2,1)}, bf16[64,2048]{1,0:T(8,128)(2,1)S(1)}, u32[]{:S(2)}, u32[]{:S(2)}) collective-permute-start(bf16[64,2048]{1,0:T(8,128)(2,1)} %b_ref.1), channel_id=1, source_target_pairs={{0,16},{1,5},{2,18},{3,7},{4,20},{5,1},{6,22},{7,3},{8,24},{9,13},... | collective-permute-start | bytes 786440 | tf_op jit(solution)/shard_map/ppermute | solution.py:48
  10.3 1.1 %copy-start = (bf16[144,2048]{1,0:T(8,128)(2,1)S(1)}, bf16[144,2048]{1,0:T(8,128)(2,1)}, u32[]{:S(2)}) copy-start(bf16[144,2048]{1,0:T(8,128)(2,1)} %shard_map.76.a_ref) | copy-start | bytes 1769476
  11.4 0.9 copy-start.1
  17.0 16.8 %collective-permute-start.5 = (bf16[256,2048]{1,0:T(8,128)(2,1)S(1)}, bf16[256,2048]{1,0:T(8,128)(2,1)S(1)}, u32[]{:S(2)}, u32[]{:S(2)}) collective-permute-start(bf16[256,2048]{1,0:T(8,128)(2,1)S(1)} %shard_map.78.r_0_.refs_0_.r_8_), channel_id=1, source_target_pairs={{0,4},{1,17},{2,6},{3,19},{4,0},{5,21},{6,2},{7,23},{8,12},{9,25},... | collective-permute-start | bytes 3145736 | tf_op jit(solution)/shard_map/ppermute | solution.py:48
  20.9 11.1 %collective-permute-start.6 = (bf16[144,2048]{1,0:T(8,128)(2,1)S(1)}, bf16[144,2048]{1,0:T(8,128)(2,1)S(1)}, u32[]{:S(2)}, u32[]{:S(2)}) collective-permute-start(bf16[144,2048]{1,0:T(8,128)(2,1)S(1)} %collective-permute-done.3.r_4_.refs_9_.refs_6_), channel_id=1, source_target_pairs={{0,32},{1,97},{2,34},{3,99},{4,36},{5,101},{6,38},{7,103},{8,40},{... | collective-permute-start | bytes 1769480 | tf_op jit(solution)/shard_map/ppermute | solution.py:48
  21.5 23.8 %collective-permute-start.9 = (bf16[256,2048]{1,0:T(8,128)(2,1)S(1)}, bf16[256,2048]{1,0:T(8,128)(2,1)S(1)}, u32[]{:S(2)}, u32[]{:S(2)}) collective-permute-start(bf16[256,2048]{1,0:T(8,128)(2,1)S(1)} %shard_map.78.r_0_.refs_0_.r_8_), channel_id=1, source_target_pairs={{0,2},{1,9},{2,4},{3,11},{4,6},{5,13},{6,0},{7,15},{8,10},{9,17},{... | collective-permute-start | bytes 3145736 | tf_op jit(solution)/shard_map/ppermute | solution.py:48
  22.5 23.5 %collective-permute-start.10 = (bf16[256,2048]{1,0:T(8,128)(2,1)S(1)}, bf16[256,2048]{1,0:T(8,128)(2,1)S(1)}, u32[]{:S(2)}, u32[]{:S(2)}) collective-permute-start(bf16[256,2048]{1,0:T(8,128)(2,1)S(1)} %shard_map.78.r_0_.refs_0_.r_8_), channel_id=1, source_target_pairs={{0,6},{1,25},{2,0},{3,27},{4,2},{5,29},{6,4},{7,31},{8,14},{9,1},{... | collective-permute-start | bytes 3145736 | tf_op jit(solution)/shard_map/ppermute | solution.py:48
  32.0 11.1 %collective-permute-start.11 = (bf16[144,2048]{1,0:T(8,128)(2,1)S(1)}, bf16[144,2048]{1,0:T(8,128)(2,1)S(1)}, u32[]{:S(2)}, u32[]{:S(2)}) collective-permute-start(bf16[144,2048]{1,0:T(8,128)(2,1)S(1)} %collective-permute-done.6.r_6_.refs_11_.refs_8_), channel_id=1, source_target_pairs={{0,32},{1,97},{2,34},{3,99},{4,36},{5,101},{6,38},{7,103},{8,40},{... | collective-permute-start | bytes 1769480 | tf_op jit(solution)/shard_map/ppermute | solution.py:48
  32.0 11.1 %collective-permute-start.7 = (bf16[144,2048]{1,0:T(8,128)(2,1)S(1)}, bf16[144,2048]{1,0:T(8,128)(2,1)S(1)}, u32[]{:S(2)}, u32[]{:S(2)}) collective-permute-start(bf16[144,2048]{1,0:T(8,128)(2,1)S(1)} %collective-permute-done.3.r_4_.refs_9_.refs_6_), channel_id=1, source_target_pairs={{0,1},{1,0},{2,3},{3,2},{4,5},{5,4},{6,7},{7,6},{8,9},{9,8},{10,11... | collective-permute-start | bytes 1769480 | tf_op jit(solution)/shard_map/ppermute | solution.py:48
  33.8 9.3 %collective-permute-start.8 = (bf16[144,2048]{1,0:T(8,128)(2,1)S(1)}, bf16[144,2048]{1,0:T(8,128)(2,1)S(1)}, u32[]{:S(2)}, u32[]{:S(2)}) collective-permute-start(bf16[144,2048]{1,0:T(8,128)(2,1)S(1)} %collective-permute-done.6.r_6_.refs_11_.refs_8_), channel_id=1, source_target_pairs={{0,1},{1,0},{2,3},{3,2},{4,5},{5,4},{6,7},{7,6},{8,9},{9,8},{10,11... | collective-permute-start | bytes 1769480 | tf_op jit(solution)/shard_map/ppermute | solution.py:48
  43.1 5.0 %collective-permute-start.12 = (bf16[144,2048]{1,0:T(8,128)(2,1)S(1)}, bf16[144,2048]{1,0:T(8,128)(2,1)S(1)}, u32[]{:S(2)}, u32[]{:S(2)}) collective-permute-start(bf16[144,2048]{1,0:T(8,128)(2,1)S(1)} %collective-permute-done.11.refs_4_.refs_13_.refs_10_), channel_id=1, source_target_pairs={{0,1},{1,0},{2,3},{3,2},{4,5},{5,4},{6,7},{7,6},{8,9},{9,8},{10,11... | collective-permute-start | bytes 1769480 | tf_op jit(solution)/shard_map/ppermute | solution.py:48
  49.5 1.3 %collective-permute-start.13 = (f32[8,1024]{1,0:T(8,128)S(1)}, f32[8,1024]{1,0:T(8,128)S(1)}, u32[]{:S(2)}, u32[]{:S(2)}) collective-permute-start(f32[8,1024]{1,0:T(8,128)S(1)} %get-tuple-element.50.r_0_.r_7_.raw), channel_id=1, source_target_pairs={{0,1},{1,0},{2,3},{3,2},{4,5},{5,4},{6,7},{7,6},{8,9},{9,8},{10,11... | collective-permute-start | bytes 98312 | tf_op jit(solution)/shard_map/ppermute | solution.py:48
  50.8 5.4 %collective-permute-start.14 = (f32[8,1024]{1,0:T(8,128)S(1)}, f32[8,1024]{1,0:T(8,128)S(1)}, u32[]{:S(2)}, u32[]{:S(2)}) collective-permute-start(f32[8,1024]{1,0:T(8,128)S(1)} %shard_map.82.r_12_.r_0_), channel_id=1, source_target_pairs={{0,32},{1,97},{2,34},{3,99},{4,36},{5,101},{6,38},{7,103},{8,40},{... | collective-permute-start | bytes 98312 | tf_op jit(solution)/shard_map/ppermute | solution.py:48
  56.2 5.5 %collective-permute-start.15 = (f32[8,1024]{1,0:T(8,128)S(1)}, f32[8,1024]{1,0:T(8,128)S(1)}, u32[]{:S(2)}, u32[]{:S(2)}) collective-permute-start(f32[8,1024]{1,0:T(8,128)S(1)} %shard_map.84.r_12_.stats), channel_id=1, source_target_pairs={{0,64},{1,65},{2,66},{3,67},{4,68},{5,69},{6,70},{7,71},{8,72},{9,... | collective-permute-start | bytes 98312 | tf_op jit(solution)/shard_map/ppermute | solution.py:48
  61.9 5.0 %collective-permute-start.16 = (bf16[640,2048]{1,0:T(8,128)(2,1)S(1)}, bf16[640,2048]{1,0:T(8,128)(2,1)S(1)}, u32[]{:S(2)}, u32[]{:S(2)}) collective-permute-start(bf16[640,2048]{1,0:T(8,128)(2,1)S(1)} %shard_map.85._), channel_id=1, source_target_pairs={{0,1},{1,0},{2,3},{3,2},{4,5},{5,4},{6,7},{7,6},{8,9},{9,8},{10,11... | collective-permute-start | bytes 7864328 | tf_op jit(solution)/shard_map/ppermute | solution.py:48
  63.3 26.6 %collective-permute-start.21 = (bf16[256,2048]{1,0:T(8,128)(2,1)S(1)}, bf16[256,2048]{1,0:T(8,128)(2,1)S(1)}, u32[]{:S(2)}, u32[]{:S(2)}) collective-permute-start(bf16[256,2048]{1,0:T(8,128)(2,1)S(1)} %shard_map.92), channel_id=1, source_target_pairs={{0,4},{1,17},{2,6},{3,19},{4,0},{5,21},{6,2},{7,23},{8,12},{9,25},... | collective-permute-start | bytes 3145736 | tf_op jit(solution)/shard_map/ppermute | solution.py:48
  67.1 9.2 %collective-permute-start.17 = (bf16[128,2048]{1,0:T(8,128)(2,1)S(1)}, bf16[128,2048]{1,0:T(8,128)(2,1)S(1)}, u32[]{:S(2)}, u32[]{:S(2)}) collective-permute-start(bf16[128,2048]{1,0:T(8,128)(2,1)S(1)} %shard_map.87), channel_id=1, source_target_pairs={{0,96},{1,33},{2,98},{3,35},{4,100},{5,37},{6,102},{7,39},{8,104},... | collective-permute-start | bytes 1572872 | tf_op jit(solution)/shard_map/ppermute | solution.py:48
  71.8 19.1 %collective-permute-start.20 = (bf16[256,2048]{1,0:T(8,128)(2,1)S(1)}, bf16[256,2048]{1,0:T(8,128)(2,1)S(1)}, u32[]{:S(2)}, u32[]{:S(2)}) collective-permute-start(bf16[256,2048]{1,0:T(8,128)(2,1)S(1)} %get-tuple-element.58), channel_id=1, source_target_pairs={{0,6},{1,25},{2,0},{3,27},{4,2},{5,29},{6,4},{7,31},{8,14},{9,1},{... | collective-permute-start | bytes 3145736 | tf_op jit(solution)/shard_map/ppermute | solution.py:48
  74.5 16.4 %collective-permute-start.22 = (bf16[256,2048]{1,0:T(8,128)(2,1)S(1)}, bf16[256,2048]{1,0:T(8,128)(2,1)S(1)}, u32[]{:S(2)}, u32[]{:S(2)}) collective-permute-start(bf16[256,2048]{1,0:T(8,128)(2,1)S(1)} %get-tuple-element.59), channel_id=1, source_target_pairs={{0,2},{1,9},{2,4},{3,11},{4,6},{5,13},{6,0},{7,15},{8,10},{9,17},{... | collective-permute-start | bytes 3145736 | tf_op jit(solution)/shard_map/ppermute | solution.py:48
  76.7 9.2 %collective-permute-start.18 = (bf16[128,2048]{1,0:T(8,128)(2,1)S(1)}, bf16[128,2048]{1,0:T(8,128)(2,1)S(1)}, u32[]{:S(2)}, u32[]{:S(2)}) collective-permute-start(bf16[128,2048]{1,0:T(8,128)(2,1)S(1)} %shard_map.88), channel_id=1, source_target_pairs={{0,96},{1,33},{2,98},{3,35},{4,100},{5,37},{6,102},{7,39},{8,104},... | collective-permute-start | bytes 1572872 | tf_op jit(solution)/shard_map/ppermute | solution.py:48
  86.3 10.3 %collective-permute-start.19 = (bf16[128,2048]{1,0:T(8,128)(2,1)S(1)}, bf16[128,2048]{1,0:T(8,128)(2,1)S(1)}, u32[]{:S(2)}, u32[]{:S(2)}) collective-permute-start(bf16[128,2048]{1,0:T(8,128)(2,1)S(1)} %shard_map.89), channel_id=1, source_target_pairs={{0,96},{1,33},{2,98},{3,35},{4,100},{5,37},{6,102},{7,39},{8,104},... | collective-permute-start | bytes 1572872 | tf_op jit(solution)/shard_map/ppermute | solution.py:48
  91.3 9.1 %collective-permute-start.23 = (bf16[64,2048]{1,0:T(8,128)(2,1)S(1)}, bf16[64,2048]{1,0:T(8,128)(2,1)S(1)}, u32[]{:S(2)}, u32[]{:S(2)}) collective-permute-start(bf16[64,2048]{1,0:T(8,128)(2,1)S(1)} %get-tuple-element.61), channel_id=1, source_target_pairs={{0,24},{1,7},{2,26},{3,1},{4,28},{5,3},{6,30},{7,5},{8,0},{9,15},{... | collective-permute-start | bytes 786440 | tf_op jit(solution)/shard_map/ppermute | solution.py:48
  93.7 8.0 %collective-permute-start.24 = (bf16[64,2048]{1,0:T(8,128)(2,1)S(1)}, bf16[64,2048]{1,0:T(8,128)(2,1)S(1)}, u32[]{:S(2)}, u32[]{:S(2)}) collective-permute-start(bf16[64,2048]{1,0:T(8,128)(2,1)S(1)} %get-tuple-element.62), channel_id=1, source_target_pairs={{0,16},{1,5},{2,18},{3,7},{4,20},{5,1},{6,22},{7,3},{8,24},{9,13},... | collective-permute-start | bytes 786440 | tf_op jit(solution)/shard_map/ppermute | solution.py:48
  94.9 9.5 %collective-permute-start.25 = (bf16[64,2048]{1,0:T(8,128)(2,1)S(1)}, bf16[64,2048]{1,0:T(8,128)(2,1)S(1)}, u32[]{:S(2)}, u32[]{:S(2)}) collective-permute-start(bf16[64,2048]{1,0:T(8,128)(2,1)S(1)} %get-tuple-element.63), channel_id=1, source_target_pairs={{0,8},{1,3},{2,10},{3,5},{4,12},{5,7},{6,14},{7,1},{8,16},{9,11},{... | collective-permute-start | bytes 786440 | tf_op jit(solution)/shard_map/ppermute | solution.py:48

commit v6 on v5

--- a/solution.py
+++ b/solution.py
@@ -297,7 +297,7 @@
 
 
 def last_kernel(a, b, c, d, _, out_ref):
-    v = a[...] + c[...].astype(F32) + (b[...].astype(F32) + d[...].astype(F32))
+    v = a[...] + b[...].astype(F32) + (c[...].astype(F32) + d[...].astype(F32))
     out_ref[...] = v.astype(BF)
 
 
@@ -382,7 +382,7 @@
         scratch=[pltpu.SemaphoreType.DMA((2,))],
     )(packed, passages)
     s0 = send(packed, CORE)
-    back, ahead, across, q1, s0 = tied(back, ahead, across, q1, s0)
+    across, back, ahead, q1, s0 = tied(across, back, ahead, q1, s0)
     plane = call(join_kernel, shape(256, WIDTH, BF), [VMEM] * 4)(kept, back, across, ahead)
     up = send(plane, second(1))
     down = send(plane, second(-1))
@@ -465,7 +465,7 @@
     g2 = send(g2, first(2))
     g1 = send(g1, first(-1))
     g3 = send(g3, first(1))
-    passage_grad = call(last_kernel, half, [VMEM] * 5)(g0, g1, g2, g3, token)
+    passage_grad = call(last_kernel, half, [VMEM] * 5)(g0, g2, g1, g3, token)
     return loss.reshape(128), run, passage_grad
 
 

time: 105 us -> 104 us (level)
  waiting for transfers between devices: 47 us -> 43.3 us
  starting transfers between devices: 33.3 us -> 35.1 us
    ppermute x26, waiting for transfers between devices: 47 us -> 43.3 us  [send(): return lax.ppermute(v, AXES, perm)]
    ppermute x26, starting transfers between devices: 33.3 us -> 35.1 us  [send(): return lax.ppermute(v, AXES, perm)]
  transfers between devices with their start and end apart: 26 -> 26, of which waited for: 18 -> 17; matrix products, arithmetic and copies ran while one was open for 0% -> 0% of each run, Pallas kernels for 17% -> 17%
where the time goes in v6:
time: 104 us; the launch traced here: 103 us
  waiting for transfers between devices  43.3 us (42%)
  starting transfers between devices  35.1 us (34%)
  Pallas kernels  22.1 us (21%)
  local copies, waits for them, and re-layouts  2.01 us (2%)
    ppermute x26, waiting for transfers between devices, send(): return lax.ppermute(v, AXES, perm)  43.3 us
    ppermute x26, starting transfers between devices, send(): return lax.ppermute(v, AXES, perm)  35.1 us
    pallas_call x2, Pallas kernels, query(): call(lambda *r: query_kernel(half, *r), shape(640, WIDTH, kind), [VMEM] *...  5.9 us
    pallas_call x2, Pallas kernels, early(): call(lambda *r: early_kernel(which, *r), (tile, tile, shape(32, 768, F32)...  4.26 us
    pallas_call x1, Pallas kernels, local(): call(near_kernel, (shape(256, WIDTH, F32), shape(256, WIDTH, BF), shape(2...  3.5 us
    pallas_call x4, Pallas kernels, block(): call(kernel, outs, [VMEM] * (4 + len(got)))(mine, theirs, factor, lse, *got)  2.14 us
  transfers between devices with their start and end apart: 26, of which 17 were waited for; matrix products, arithmetic and copies ran while one was open for 0% of the time, Pallas kernels for 17%

profile of v6, /device:TPU:0, one launch (start us, length us, event | category | flops | bytes accessed | tf_op | source)
XLA Modules:
  0.0 103.4 jit_solution(11717989986427997336)
XLA Ops:
  0.6 1.9 %shard_map.76.a_ref = bf16[144,2048]{1,0:T(8,128)(2,1)} custom-call(bf16[128,2048]{1,0:T(8,128)(2,1)} %q_ref.1, s32[16,128]{1,0:T(8,128)} %bitcast.4, s32[16,128]{1,0:T(8,128)} %bitcast.5, s32[1,128]{1,0:T(1,128)} %bitcast.6), custom_call_target="tpu_custom_call" | custom-call | tf_op jit(solution)/shard_map/pallas_call | solution.py:361
  2.6 1.7 %collective-permute-start.3 = (bf16[144,2048]{1,0:T(8,128)(2,1)}, bf16[144,2048]{1,0:T(8,128)(2,1)S(1)}, u32[]{:S(2)}, u32[]{:S(2)}) collective-permute-start(bf16[144,2048]{1,0:T(8,128)(2,1)} %shard_map.76.a_ref), channel_id=1, source_target_pairs={{0,32},{1,97},{2,34},{3,99},{4,36},{5,101},{6,38},{7,103},{8,40},{... | collective-permute-start | bytes 1769480 | tf_op jit(solution)/shard_map/ppermute | solution.py:48
  5.3 3.0 %collective-permute-start = (bf16[64,2048]{1,0:T(8,128)(2,1)}, bf16[64,2048]{1,0:T(8,128)(2,1)S(1)}, u32[]{:S(2)}, u32[]{:S(2)}) collective-permute-start(bf16[64,2048]{1,0:T(8,128)(2,1)} %b_ref.1), channel_id=1, source_target_pairs={{0,16},{1,5},{2,18},{3,7},{4,20},{5,1},{6,22},{7,3},{8,24},{9,13},... | collective-permute-start | bytes 786440 | tf_op jit(solution)/shard_map/ppermute | solution.py:48
  8.9 2.6 %collective-permute-start.2 = (bf16[64,2048]{1,0:T(8,128)(2,1)}, bf16[64,2048]{1,0:T(8,128)(2,1)S(1)}, u32[]{:S(2)}, u32[]{:S(2)}) collective-permute-start(bf16[64,2048]{1,0:T(8,128)(2,1)} %b_ref.1), channel_id=1, source_target_pairs={{0,24},{1,7},{2,26},{3,1},{4,28},{5,3},{6,30},{7,5},{8,0},{9,15},{... | collective-permute-start | bytes 786440 | tf_op jit(solution)/shard_map/ppermute | solution.py:48
  13.7 2.4 %collective-permute-done.1.refs_1_ = bf16[64,2048]{1,0:T(8,128)(2,1)S(1)} collective-permute-done((bf16[64,2048]{1,0:T(8,128)(2,1)}, bf16[64,2048]{1,0:T(8,128)(2,1)S(1)}, u32[]{:S(2)}, u32[]{:S(2)}) %collective-permute-start.1) | collective-permute-done | bytes 262176 | tf_op jit(solution)/shard_map/ppermute | solution.py:48
  16.4 4.0 %collective-permute-start.5 = (bf16[256,2048]{1,0:T(8,128)(2,1)S(1)}, bf16[256,2048]{1,0:T(8,128)(2,1)S(1)}, u32[]{:S(2)}, u32[]{:S(2)}) collective-permute-start(bf16[256,2048]{1,0:T(8,128)(2,1)S(1)} %shard_map.78.r_0_.refs_0_.r_8_), channel_id=1, source_target_pairs={{0,4},{1,17},{2,6},{3,19},{4,0},{5,21},{6,2},{7,23},{8,12},{9,25},... | collective-permute-start | bytes 3145736 | tf_op jit(solution)/shard_map/ppermute | solution.py:48
  21.9 2.2 %collective-permute-start.10 = (bf16[256,2048]{1,0:T(8,128)(2,1)S(1)}, bf16[256,2048]{1,0:T(8,128)(2,1)S(1)}, u32[]{:S(2)}, u32[]{:S(2)}) collective-permute-start(bf16[256,2048]{1,0:T(8,128)(2,1)S(1)} %shard_map.78.r_0_.refs_0_.r_8_), channel_id=1, source_target_pairs={{0,6},{1,25},{2,0},{3,27},{4,2},{5,29},{6,4},{7,31},{8,14},{9,1},{... | collective-permute-start | bytes 3145736 | tf_op jit(solution)/shard_map/ppermute | solution.py:48
  24.1 7.3 %collective-permute-done.6.r_6_.refs_11_.refs_8_ = bf16[144,2048]{1,0:T(8,128)(2,1)S(1)} collective-permute-done((bf16[144,2048]{1,0:T(8,128)(2,1)S(1)}, bf16[144,2048]{1,0:T(8,128)(2,1)S(1)}, u32[]{:S(2)}, u32[]{:S(2)}) %collective-permute-start.6) | collective-permute-done | bytes 589856 | tf_op jit(solution)/shard_map/ppermute | solution.py:48
  31.4 1.8 %collective-permute-done.5.r_1_.refs_2_.r_10_ = bf16[256,2048]{1,0:T(8,128)(2,1)S(1)} collective-permute-done((bf16[256,2048]{1,0:T(8,128)(2,1)S(1)}, bf16[256,2048]{1,0:T(8,128)(2,1)S(1)}, u32[]{:S(2)}, u32[]{:S(2)}) %collective-permute-start.5) | collective-permute-done | bytes 1048608 | tf_op jit(solution)/shard_map/ppermute | solution.py:48
  33.2 9.3 %collective-permute-done.11.refs_4_.refs_13_.refs_10_ = bf16[144,2048]{1,0:T(8,128)(2,1)S(1)} collective-permute-done((bf16[144,2048]{1,0:T(8,128)(2,1)S(1)}, bf16[144,2048]{1,0:T(8,128)(2,1)S(1)}, u32[]{:S(2)}, u32[]{:S(2)}) %collective-permute-start.11) | collective-permute-done | bytes 589856 | tf_op jit(solution)/shard_map/ppermute | solution.py:48
  42.5 2.1 %shard_map.79 = (f32[256,256]{1,0:T(8,128)S(1)}, f32[256,256]{1,0:T(8,128)S(1)}, f32[32,768]{1,0:T(8,128)S(1)}) custom-call(bf16[256,2048]{1,0:T(8,128)(2,1)S(1)} %shard_map.78.r_0_.refs_0_.r_8_, bf16[256,2048]{1,0:T(8,128)(2,1)S(1)} %collective-permute-done.5.r_1_.refs_2_.r_10_, bf16[144,2048]{1,0:T(8,128)(2,1)S(1)} %get-tuple-element.38.r_2_.refs_7_.refs_4_, ...), custom_call_target="tpu_custom_call" | custom-call | flops 1610612736 | tf_op jit(solution)/shard_map/pallas_call | solution.py:402
  45.4 2.1 %shard_map.80 = (f32[256,256]{1,0:T(8,128)S(1)}, f32[256,256]{1,0:T(8,128)S(1)}, f32[32,768]{1,0:T(8,128)S(1)}) custom-call(bf16[256,2048]{1,0:T(8,128)(2,1)S(1)} %collective-permute-done.9.r_0_.refs_1_.r_9_, bf16[256,2048]{1,0:T(8,128)(2,1)S(1)} %collective-permute-done.10.r_1_.refs_3_.r_11_, bf16[144,2048]{1,0:T(8,128)(2,1)S(1)} %get-tuple-element.38.r_2_.refs_7_.refs_4_, ...), custom_call_target="tpu_custom_call" | custom-call | flops 1610612736 | tf_op jit(solution)/shard_map/pallas_call | solution.py:402
  47.5 1.4 %shard_map.81 = (f32[64,256]{1,0:T(8,128)S(1)}, f32[8,1024]{1,0:T(8,128)S(1)}) custom-call(bf16[256,2048]{1,0:T(8,128)(2,1)S(1)} %shard_map.78.r_0_.refs_0_.r_8_, bf16[256,2048]{1,0:T(8,128)(2,1)S(1)} %collective-permute-done.9.r_0_.refs_1_.r_9_, bf16[256,2048]{1,0:T(8,128)(2,1)S(1)} %collective-permute-done.5.r_1_.refs_2_.r_10_, ...), custom_call_target="tpu_custom_call" | custom-call | flops 1073741824 | tf_op jit(solution)/shard_map/pallas_call | solution.py:411
  49.0 1.2 %collective-permute-done.13.r_1_.other = f32[8,1024]{1,0:T(8,128)S(1)} collective-permute-done((f32[8,1024]{1,0:T(8,128)S(1)}, f32[8,1024]{1,0:T(8,128)S(1)}, u32[]{:S(2)}, u32[]{:S(2)}) %collective-permute-start.13) | collective-permute-done | bytes 32800 | tf_op jit(solution)/shard_map/ppermute | solution.py:48
  51.1 2.9 %shard_map.83.r_2_.r_0_ = f32[640,2048]{1,0:T(8,128)S(1)} custom-call(f32[256,256]{1,0:T(8,128)S(1)} %get-tuple-element.43.r_0_.refs_0_, f32[256,256]{1,0:T(8,128)S(1)} %get-tuple-element.44.r_1_.refs_1_, f32[256,256]{1,0:T(8,128)S(1)} %get-tuple-element.45.r_2_.t_ref, f32[256,256]{1,0:T(8,128)S(1)} %get-tuple-element.46.r_3_.refs_2_, ...), custom_call_target="tpu_custom_call" | custom-call | flops 2684354560 | tf_op jit(solution)/shard_map/pallas_call | solution.py:421
  54.0 1.6 %collective-permute-done.14.r_1_ = f32[8,1024]{1,0:T(8,128)S(1)} collective-permute-done((f32[8,1024]{1,0:T(8,128)S(1)}, f32[8,1024]{1,0:T(8,128)S(1)}, u32[]{:S(2)}, u32[]{:S(2)}) %collective-permute-start.14) | collective-permute-done | bytes 32800 | tf_op jit(solution)/shard_map/ppermute | solution.py:48
  56.4 3.0 %shard_map.85._ = bf16[640,2048]{1,0:T(8,128)(2,1)S(1)} custom-call(f32[256,256]{1,0:T(8,128)S(1)} %get-tuple-element.43.r_0_.refs_0_, f32[256,256]{1,0:T(8,128)S(1)} %get-tuple-element.44.r_1_.refs_1_, f32[256,256]{1,0:T(8,128)S(1)} %get-tuple-element.45.r_2_.t_ref, f32[256,256]{1,0:T(8,128)S(1)} %get-tuple-element.46.r_3_.refs_2_, ...), custom_call_target="tpu_custom_call" | custom-call | flops 2684354560 | tf_op jit(solution)/shard_map/pallas_call | solution.py:421
  59.4 1.8 %collective-permute-done.15.got = f32[8,1024]{1,0:T(8,128)S(1)} collective-permute-done((f32[8,1024]{1,0:T(8,128)S(1)}, f32[8,1024]{1,0:T(8,128)S(1)}, u32[]{:S(2)}, u32[]{:S(2)}) %collective-permute-start.15) | collective-permute-done | bytes 32800 | tf_op jit(solution)/shard_map/ppermute | solution.py:48
  61.4 1.3 %shard_map.92 = bf16[256,2048]{1,0:T(8,128)(2,1)S(1)} custom-call(f32[256,256]{1,0:T(8,128)S(1)} %get-tuple-element.45.r_2_.t_ref, f32[32,768]{1,0:T(8,128)S(1)} %get-tuple-element.47.refs_6_.r_4_.refs_3_.refs_0_, f32[32,768]{1,0:T(8,128)S(1)} %get-tuple-element.48.refs_7_.r_5_.refs_4_.refs_1_, f32[64,256]{1,0:T(8,128)S(1)} %get-tuple-element.49.r_6_.refs_5_.refs_2_, ...), custom_call_target="tpu_custom_call" | custom-call | flops 1073741824 | tf_op jit(solution)/shard_map/pallas_call | solution.py:439
  62.7 2.6 %collective-permute-start.21 = (bf16[256,2048]{1,0:T(8,128)(2,1)S(1)}, bf16[256,2048]{1,0:T(8,128)(2,1)S(1)}, u32[]{:S(2)}, u32[]{:S(2)}) collective-permute-start(bf16[256,2048]{1,0:T(8,128)(2,1)S(1)} %shard_map.92), channel_id=1, source_target_pairs={{0,4},{1,17},{2,6},{3,19},{4,0},{5,21},{6,2},{7,23},{8,12},{9,25},... | collective-permute-start | bytes 3145736 | tf_op jit(solution)/shard_map/ppermute | solution.py:48
  66.5 1.1 %collective-permute-start.17 = (bf16[128,2048]{1,0:T(8,128)(2,1)S(1)}, bf16[128,2048]{1,0:T(8,128)(2,1)S(1)}, u32[]{:S(2)}, u32[]{:S(2)}) collective-permute-start(bf16[128,2048]{1,0:T(8,128)(2,1)S(1)} %shard_map.87), channel_id=1, source_target_pairs={{0,96},{1,33},{2,98},{3,35},{4,100},{5,37},{6,102},{7,39},{8,104},... | collective-permute-start | bytes 1572872 | tf_op jit(solution)/shard_map/ppermute | solution.py:48
  67.7 3.5 %shard_map.91 = (f32[256,2048]{1,0:T(8,128)S(1)}, bf16[256,2048]{1,0:T(8,128)(2,1)S(1)}, bf16[256,2048]{1,0:T(8,128)(2,1)S(1)}) custom-call(f32[256,256]{1,0:T(8,128)S(1)} %get-tuple-element.43.r_0_.refs_0_, f32[256,256]{1,0:T(8,128)S(1)} %get-tuple-element.44.r_1_.refs_1_, f32[256,256]{1,0:T(8,128)S(1)} %get-tuple-element.46.r_3_.refs_2_, ...), custom_call_target="tpu_custom_call" | custom-call | flops 3221225472 | tf_op jit(solution)/shard_map/pallas_call | solution.py:444
  71.2 2.7 %collective-permute-start.20 = (bf16[256,2048]{1,0:T(8,128)(2,1)S(1)}, bf16[256,2048]{1,0:T(8,128)(2,1)S(1)}, u32[]{:S(2)}, u32[]{:S(2)}) collective-permute-start(bf16[256,2048]{1,0:T(8,128)(2,1)S(1)} %get-tuple-element.58), channel_id=1, source_target_pairs={{0,6},{1,25},{2,0},{3,27},{4,2},{5,29},{6,4},{7,31},{8,14},{9,1},{... | collective-permute-start | bytes 3145736 | tf_op jit(solution)/shard_map/ppermute | solution.py:48
  73.9 1.9 %collective-permute-done.17.r_4_ = bf16[128,2048]{1,0:T(8,128)(2,1)S(1)} collective-permute-done((bf16[128,2048]{1,0:T(8,128)(2,1)S(1)}, bf16[128,2048]{1,0:T(8,128)(2,1)S(1)}, u32[]{:S(2)}, u32[]{:S(2)}) %collective-permute-start.17) | collective-permute-done | bytes 524320 | tf_op jit(solution)/shard_map/ppermute | solution.py:48
  76.1 2.4 %collective-permute-start.18 = (bf16[128,2048]{1,0:T(8,128)(2,1)S(1)}, bf16[128,2048]{1,0:T(8,128)(2,1)S(1)}, u32[]{:S(2)}, u32[]{:S(2)}) collective-permute-start(bf16[128,2048]{1,0:T(8,128)(2,1)S(1)} %shard_map.88), channel_id=1, source_target_pairs={{0,96},{1,33},{2,98},{3,35},{4,100},{5,37},{6,102},{7,39},{8,104},... | collective-permute-start | bytes 1572872 | tf_op jit(solution)/shard_map/ppermute | solution.py:48
  78.5 6.9 %collective-permute-done.18.r_4_ = bf16[128,2048]{1,0:T(8,128)(2,1)S(1)} collective-permute-done((bf16[128,2048]{1,0:T(8,128)(2,1)S(1)}, bf16[128,2048]{1,0:T(8,128)(2,1)S(1)}, u32[]{:S(2)}, u32[]{:S(2)}) %collective-permute-start.18) | collective-permute-done | bytes 524320 | tf_op jit(solution)/shard_map/ppermute | solution.py:48
  85.7 3.6 %collective-permute-start.19 = (bf16[128,2048]{1,0:T(8,128)(2,1)S(1)}, bf16[128,2048]{1,0:T(8,128)(2,1)S(1)}, u32[]{:S(2)}, u32[]{:S(2)}) collective-permute-start(bf16[128,2048]{1,0:T(8,128)(2,1)S(1)} %shard_map.89), channel_id=1, source_target_pairs={{0,96},{1,33},{2,98},{3,35},{4,100},{5,37},{6,102},{7,39},{8,104},... | collective-permute-start | bytes 1572872 | tf_op jit(solution)/shard_map/ppermute | solution.py:48
  90.7 2.2 %collective-permute-start.23 = (bf16[64,2048]{1,0:T(8,128)(2,1)S(1)}, bf16[64,2048]{1,0:T(8,128)(2,1)S(1)}, u32[]{:S(2)}, u32[]{:S(2)}) collective-permute-start(bf16[64,2048]{1,0:T(8,128)(2,1)S(1)} %get-tuple-element.61), channel_id=1, source_target_pairs={{0,16},{1,5},{2,18},{3,7},{4,20},{5,1},{6,22},{7,3},{8,24},{9,13},... | collective-permute-start | bytes 786440 | tf_op jit(solution)/shard_map/ppermute | solution.py:48
  92.9 2.0 %collective-permute-start.24 = (bf16[64,2048]{1,0:T(8,128)(2,1)S(1)}, bf16[64,2048]{1,0:T(8,128)(2,1)S(1)}, u32[]{:S(2)}, u32[]{:S(2)}) collective-permute-start(bf16[64,2048]{1,0:T(8,128)(2,1)S(1)} %get-tuple-element.62), channel_id=1, source_target_pairs={{0,24},{1,7},{2,26},{3,1},{4,28},{5,3},{6,30},{7,5},{8,0},{9,15},{... | collective-permute-start | bytes 786440 | tf_op jit(solution)/shard_map/ppermute | solution.py:48
  95.9 1.3 %shard_map.90 = (bf16[128,2048]{1,0:T(8,128)(2,1)}, f32[8,128]{1,0:T(8,128)S(1)}, f32[1,128]{1,0:T(1,128)}) custom-call(f32[640,2048]{1,0:T(8,128)S(1)} %shard_map.83.r_2_.r_0_, bf16[640,2048]{1,0:T(8,128)(2,1)S(1)} %collective-permute-done.16.r_1_.refs_15_, f32[128,128]{1,0:T(8,128)S(1)} %get-tuple-element.53.r_2_, ...), custom_call_target="tpu_custom_call" | custom-call | tf_op jit(solution)/shard_map/pallas_call | solution.py:454
  97.2 1.5 %collective-permute-done.23.b = bf16[64,2048]{1,0:T(8,128)(2,1)S(1)} collective-permute-done((bf16[64,2048]{1,0:T(8,128)(2,1)S(1)}, bf16[64,2048]{1,0:T(8,128)(2,1)S(1)}, u32[]{:S(2)}, u32[]{:S(2)}) %collective-permute-start.23) | collective-permute-done | bytes 262176 | tf_op jit(solution)/shard_map/ppermute | solution.py:48
  98.7 3.3 %collective-permute-done.24.c = bf16[64,2048]{1,0:T(8,128)(2,1)S(1)} collective-permute-done((bf16[64,2048]{1,0:T(8,128)(2,1)S(1)}, bf16[64,2048]{1,0:T(8,128)(2,1)S(1)}, u32[]{:S(2)}, u32[]{:S(2)}) %collective-permute-start.24) | collective-permute-done | bytes 262176 | tf_op jit(solution)/shard_map/ppermute | solution.py:48
  (43 shorter events, 14.0 us)
Async XLA Ops:
  2.6 13.7 %collective-permute-start.3 = (bf16[144,2048]{1,0:T(8,128)(2,1)}, bf16[144,2048]{1,0:T(8,128)(2,1)S(1)}, u32[]{:S(2)}, u32[]{:S(2)}) collective-permute-start(bf16[144,2048]{1,0:T(8,128)(2,1)} %shard_map.76.a_ref), channel_id=1, source_target_pairs={{0,32},{1,97},{2,34},{3,99},{4,36},{5,101},{6,38},{7,103},{8,40},{... | collective-permute-start | bytes 1769480 | tf_op jit(solution)/shard_map/ppermute | solution.py:48
  4.3 12.0 %collective-permute-start.4 = (bf16[144,2048]{1,0:T(8,128)(2,1)}, bf16[144,2048]{1,0:T(8,128)(2,1)S(1)}, u32[]{:S(2)}, u32[]{:S(2)}) collective-permute-start(bf16[144,2048]{1,0:T(8,128)(2,1)} %shard_map.76.a_ref), channel_id=1, source_target_pairs={{0,1},{1,0},{2,3},{3,2},{4,5},{5,4},{6,7},{7,6},{8,9},{9,8},{10,11... | collective-permute-start | bytes 1769480 | tf_op jit(solution)/shard_map/ppermute | solution.py:48
  5.3 8.4 %collective-permute-start = (bf16[64,2048]{1,0:T(8,128)(2,1)}, bf16[64,2048]{1,0:T(8,128)(2,1)S(1)}, u32[]{:S(2)}, u32[]{:S(2)}) collective-permute-start(bf16[64,2048]{1,0:T(8,128)(2,1)} %b_ref.1), channel_id=1, source_target_pairs={{0,16},{1,5},{2,18},{3,7},{4,20},{5,1},{6,22},{7,3},{8,24},{9,13},... | collective-permute-start | bytes 786440 | tf_op jit(solution)/shard_map/ppermute | solution.py:48
  8.3 7.9 %collective-permute-start.1 = (bf16[64,2048]{1,0:T(8,128)(2,1)}, bf16[64,2048]{1,0:T(8,128)(2,1)S(1)}, u32[]{:S(2)}, u32[]{:S(2)}) collective-permute-start(bf16[64,2048]{1,0:T(8,128)(2,1)} %b_ref.1), channel_id=1, source_target_pairs={{0,8},{1,3},{2,10},{3,5},{4,12},{5,7},{6,14},{7,1},{8,16},{9,11},{... | collective-permute-start | bytes 786440 | tf_op jit(solution)/shard_map/ppermute | solution.py:48
  8.9 7.4 %collective-permute-start.2 = (bf16[64,2048]{1,0:T(8,128)(2,1)}, bf16[64,2048]{1,0:T(8,128)(2,1)S(1)}, u32[]{:S(2)}, u32[]{:S(2)}) collective-permute-start(bf16[64,2048]{1,0:T(8,128)(2,1)} %b_ref.1), channel_id=1, source_target_pairs={{0,24},{1,7},{2,26},{3,1},{4,28},{5,3},{6,30},{7,5},{8,0},{9,15},{... | collective-permute-start | bytes 786440 | tf_op jit(solution)/shard_map/ppermute | solution.py:48
  11.6 1.1 %copy-start = (bf16[144,2048]{1,0:T(8,128)(2,1)S(1)}, bf16[144,2048]{1,0:T(8,128)(2,1)}, u32[]{:S(2)}) copy-start(bf16[144,2048]{1,0:T(8,128)(2,1)} %shard_map.76.a_ref) | copy-start | bytes 1769476
  12.6 0.9 copy-start.1
  16.4 16.8 %collective-permute-start.5 = (bf16[256,2048]{1,0:T(8,128)(2,1)S(1)}, bf16[256,2048]{1,0:T(8,128)(2,1)S(1)}, u32[]{:S(2)}, u32[]{:S(2)}) collective-permute-start(bf16[256,2048]{1,0:T(8,128)(2,1)S(1)} %shard_map.78.r_0_.refs_0_.r_8_), channel_id=1, source_target_pairs={{0,4},{1,17},{2,6},{3,19},{4,0},{5,21},{6,2},{7,23},{8,12},{9,25},... | collective-permute-start | bytes 3145736 | tf_op jit(solution)/shard_map/ppermute | solution.py:48
  20.3 11.1 %collective-permute-start.6 = (bf16[144,2048]{1,0:T(8,128)(2,1)S(1)}, bf16[144,2048]{1,0:T(8,128)(2,1)S(1)}, u32[]{:S(2)}, u32[]{:S(2)}) collective-permute-start(bf16[144,2048]{1,0:T(8,128)(2,1)S(1)} %collective-permute-done.3.r_4_.refs_9_.refs_6_), channel_id=1, source_target_pairs={{0,32},{1,97},{2,34},{3,99},{4,36},{5,101},{6,38},{7,103},{8,40},{... | collective-permute-start | bytes 1769480 | tf_op jit(solution)/shard_map/ppermute | solution.py:48
  20.9 23.8 %collective-permute-start.9 = (bf16[256,2048]{1,0:T(8,128)(2,1)S(1)}, bf16[256,2048]{1,0:T(8,128)(2,1)S(1)}, u32[]{:S(2)}, u32[]{:S(2)}) collective-permute-start(bf16[256,2048]{1,0:T(8,128)(2,1)S(1)} %shard_map.78.r_0_.refs_0_.r_8_), channel_id=1, source_target_pairs={{0,2},{1,9},{2,4},{3,11},{4,6},{5,13},{6,0},{7,15},{8,10},{9,17},{... | collective-permute-start | bytes 3145736 | tf_op jit(solution)/shard_map/ppermute | solution.py:48
  21.9 23.5 %collective-permute-start.10 = (bf16[256,2048]{1,0:T(8,128)(2,1)S(1)}, bf16[256,2048]{1,0:T(8,128)(2,1)S(1)}, u32[]{:S(2)}, u32[]{:S(2)}) collective-permute-start(bf16[256,2048]{1,0:T(8,128)(2,1)S(1)} %shard_map.78.r_0_.refs_0_.r_8_), channel_id=1, source_target_pairs={{0,6},{1,25},{2,0},{3,27},{4,2},{5,29},{6,4},{7,31},{8,14},{9,1},{... | collective-permute-start | bytes 3145736 | tf_op jit(solution)/shard_map/ppermute | solution.py:48
  31.4 11.1 %collective-permute-start.11 = (bf16[144,2048]{1,0:T(8,128)(2,1)S(1)}, bf16[144,2048]{1,0:T(8,128)(2,1)S(1)}, u32[]{:S(2)}, u32[]{:S(2)}) collective-permute-start(bf16[144,2048]{1,0:T(8,128)(2,1)S(1)} %collective-permute-done.6.r_6_.refs_11_.refs_8_), channel_id=1, source_target_pairs={{0,32},{1,97},{2,34},{3,99},{4,36},{5,101},{6,38},{7,103},{8,40},{... | collective-permute-start | bytes 1769480 | tf_op jit(solution)/shard_map/ppermute | solution.py:48
  31.4 11.1 %collective-permute-start.7 = (bf16[144,2048]{1,0:T(8,128)(2,1)S(1)}, bf16[144,2048]{1,0:T(8,128)(2,1)S(1)}, u32[]{:S(2)}, u32[]{:S(2)}) collective-permute-start(bf16[144,2048]{1,0:T(8,128)(2,1)S(1)} %collective-permute-done.3.r_4_.refs_9_.refs_6_), channel_id=1, source_target_pairs={{0,1},{1,0},{2,3},{3,2},{4,5},{5,4},{6,7},{7,6},{8,9},{9,8},{10,11... | collective-permute-start | bytes 1769480 | tf_op jit(solution)/shard_map/ppermute | solution.py:48
  33.2 9.3 %collective-permute-start.8 = (bf16[144,2048]{1,0:T(8,128)(2,1)S(1)}, bf16[144,2048]{1,0:T(8,128)(2,1)S(1)}, u32[]{:S(2)}, u32[]{:S(2)}) collective-permute-start(bf16[144,2048]{1,0:T(8,128)(2,1)S(1)} %collective-permute-done.6.r_6_.refs_11_.refs_8_), channel_id=1, source_target_pairs={{0,1},{1,0},{2,3},{3,2},{4,5},{5,4},{6,7},{7,6},{8,9},{9,8},{10,11... | collective-permute-start | bytes 1769480 | tf_op jit(solution)/shard_map/ppermute | solution.py:48
  42.5 5.0 %collective-permute-start.12 = (bf16[144,2048]{1,0:T(8,128)(2,1)S(1)}, bf16[144,2048]{1,0:T(8,128)(2,1)S(1)}, u32[]{:S(2)}, u32[]{:S(2)}) collective-permute-start(bf16[144,2048]{1,0:T(8,128)(2,1)S(1)} %collective-permute-done.11.refs_4_.refs_13_.refs_10_), channel_id=1, source_target_pairs={{0,1},{1,0},{2,3},{3,2},{4,5},{5,4},{6,7},{7,6},{8,9},{9,8},{10,11... | collective-permute-start | bytes 1769480 | tf_op jit(solution)/shard_map/ppermute | solution.py:48
  48.9 1.3 %collective-permute-start.13 = (f32[8,1024]{1,0:T(8,128)S(1)}, f32[8,1024]{1,0:T(8,128)S(1)}, u32[]{:S(2)}, u32[]{:S(2)}) collective-permute-start(f32[8,1024]{1,0:T(8,128)S(1)} %get-tuple-element.50.r_0_.r_7_.raw), channel_id=1, source_target_pairs={{0,1},{1,0},{2,3},{3,2},{4,5},{5,4},{6,7},{7,6},{8,9},{9,8},{10,11... | collective-permute-start | bytes 98312 | tf_op jit(solution)/shard_map/ppermute | solution.py:48
  50.2 5.4 %collective-permute-start.14 = (f32[8,1024]{1,0:T(8,128)S(1)}, f32[8,1024]{1,0:T(8,128)S(1)}, u32[]{:S(2)}, u32[]{:S(2)}) collective-permute-start(f32[8,1024]{1,0:T(8,128)S(1)} %shard_map.82.r_12_.r_0_), channel_id=1, source_target_pairs={{0,32},{1,97},{2,34},{3,99},{4,36},{5,101},{6,38},{7,103},{8,40},{... | collective-permute-start | bytes 98312 | tf_op jit(solution)/shard_map/ppermute | solution.py:48
  55.6 5.5 %collective-permute-start.15 = (f32[8,1024]{1,0:T(8,128)S(1)}, f32[8,1024]{1,0:T(8,128)S(1)}, u32[]{:S(2)}, u32[]{:S(2)}) collective-permute-start(f32[8,1024]{1,0:T(8,128)S(1)} %shard_map.84.r_12_.stats), channel_id=1, source_target_pairs={{0,64},{1,65},{2,66},{3,67},{4,68},{5,69},{6,70},{7,71},{8,72},{9,... | collective-permute-start | bytes 98312 | tf_op jit(solution)/shard_map/ppermute | solution.py:48
  61.3 5.0 %collective-permute-start.16 = (bf16[640,2048]{1,0:T(8,128)(2,1)S(1)}, bf16[640,2048]{1,0:T(8,128)(2,1)S(1)}, u32[]{:S(2)}, u32[]{:S(2)}) collective-permute-start(bf16[640,2048]{1,0:T(8,128)(2,1)S(1)} %shard_map.85._), channel_id=1, source_target_pairs={{0,1},{1,0},{2,3},{3,2},{4,5},{5,4},{6,7},{7,6},{8,9},{9,8},{10,11... | collective-permute-start | bytes 7864328 | tf_op jit(solution)/shard_map/ppermute | solution.py:48
  62.7 26.6 %collective-permute-start.21 = (bf16[256,2048]{1,0:T(8,128)(2,1)S(1)}, bf16[256,2048]{1,0:T(8,128)(2,1)S(1)}, u32[]{:S(2)}, u32[]{:S(2)}) collective-permute-start(bf16[256,2048]{1,0:T(8,128)(2,1)S(1)} %shard_map.92), channel_id=1, source_target_pairs={{0,4},{1,17},{2,6},{3,19},{4,0},{5,21},{6,2},{7,23},{8,12},{9,25},... | collective-permute-start | bytes 3145736 | tf_op jit(solution)/shard_map/ppermute | solution.py:48
  66.5 9.2 %collective-permute-start.17 = (bf16[128,2048]{1,0:T(8,128)(2,1)S(1)}, bf16[128,2048]{1,0:T(8,128)(2,1)S(1)}, u32[]{:S(2)}, u32[]{:S(2)}) collective-permute-start(bf16[128,2048]{1,0:T(8,128)(2,1)S(1)} %shard_map.87), channel_id=1, source_target_pairs={{0,96},{1,33},{2,98},{3,35},{4,100},{5,37},{6,102},{7,39},{8,104},... | collective-permute-start | bytes 1572872 | tf_op jit(solution)/shard_map/ppermute | solution.py:48
  71.2 19.1 %collective-permute-start.20 = (bf16[256,2048]{1,0:T(8,128)(2,1)S(1)}, bf16[256,2048]{1,0:T(8,128)(2,1)S(1)}, u32[]{:S(2)}, u32[]{:S(2)}) collective-permute-start(bf16[256,2048]{1,0:T(8,128)(2,1)S(1)} %get-tuple-element.58), channel_id=1, source_target_pairs={{0,6},{1,25},{2,0},{3,27},{4,2},{5,29},{6,4},{7,31},{8,14},{9,1},{... | collective-permute-start | bytes 3145736 | tf_op jit(solution)/shard_map/ppermute | solution.py:48
  73.9 16.4 %collective-permute-start.22 = (bf16[256,2048]{1,0:T(8,128)(2,1)S(1)}, bf16[256,2048]{1,0:T(8,128)(2,1)S(1)}, u32[]{:S(2)}, u32[]{:S(2)}) collective-permute-start(bf16[256,2048]{1,0:T(8,128)(2,1)S(1)} %get-tuple-element.59), channel_id=1, source_target_pairs={{0,2},{1,9},{2,4},{3,11},{4,6},{5,13},{6,0},{7,15},{8,10},{9,17},{... | collective-permute-start | bytes 3145736 | tf_op jit(solution)/shard_map/ppermute | solution.py:48
  76.1 9.2 %collective-permute-start.18 = (bf16[128,2048]{1,0:T(8,128)(2,1)S(1)}, bf16[128,2048]{1,0:T(8,128)(2,1)S(1)}, u32[]{:S(2)}, u32[]{:S(2)}) collective-permute-start(bf16[128,2048]{1,0:T(8,128)(2,1)S(1)} %shard_map.88), channel_id=1, source_target_pairs={{0,96},{1,33},{2,98},{3,35},{4,100},{5,37},{6,102},{7,39},{8,104},... | collective-permute-start | bytes 1572872 | tf_op jit(solution)/shard_map/ppermute | solution.py:48
  85.7 10.3 %collective-permute-start.19 = (bf16[128,2048]{1,0:T(8,128)(2,1)S(1)}, bf16[128,2048]{1,0:T(8,128)(2,1)S(1)}, u32[]{:S(2)}, u32[]{:S(2)}) collective-permute-start(bf16[128,2048]{1,0:T(8,128)(2,1)S(1)} %shard_map.89), channel_id=1, source_target_pairs={{0,96},{1,33},{2,98},{3,35},{4,100},{5,37},{6,102},{7,39},{8,104},... | collective-permute-start | bytes 1572872 | tf_op jit(solution)/shard_map/ppermute | solution.py:48
  90.7 8.0 %collective-permute-start.23 = (bf16[64,2048]{1,0:T(8,128)(2,1)S(1)}, bf16[64,2048]{1,0:T(8,128)(2,1)S(1)}, u32[]{:S(2)}, u32[]{:S(2)}) collective-permute-start(bf16[64,2048]{1,0:T(8,128)(2,1)S(1)} %get-tuple-element.61), channel_id=1, source_target_pairs={{0,16},{1,5},{2,18},{3,7},{4,20},{5,1},{6,22},{7,3},{8,24},{9,13},... | collective-permute-start | bytes 786440 | tf_op jit(solution)/shard_map/ppermute | solution.py:48
  92.9 9.0 %collective-permute-start.24 = (bf16[64,2048]{1,0:T(8,128)(2,1)S(1)}, bf16[64,2048]{1,0:T(8,128)(2,1)S(1)}, u32[]{:S(2)}, u32[]{:S(2)}) collective-permute-start(bf16[64,2048]{1,0:T(8,128)(2,1)S(1)} %get-tuple-element.62), channel_id=1, source_target_pairs={{0,24},{1,7},{2,26},{3,1},{4,28},{5,3},{6,30},{7,5},{8,0},{9,15},{... | collective-permute-start | bytes 786440 | tf_op jit(solution)/shard_map/ppermute | solution.py:48
  95.0 7.6 %collective-permute-start.25 = (bf16[64,2048]{1,0:T(8,128)(2,1)S(1)}, bf16[64,2048]{1,0:T(8,128)(2,1)S(1)}, u32[]{:S(2)}, u32[]{:S(2)}) collective-permute-start(bf16[64,2048]{1,0:T(8,128)(2,1)S(1)} %get-tuple-element.63), channel_id=1, source_target_pairs={{0,8},{1,3},{2,10},{3,5},{4,12},{5,7},{6,14},{7,1},{8,16},{9,11},{... | collective-permute-start | bytes 786440 | tf_op jit(solution)/shard_map/ppermute | solution.py:48

commit v7 on v6

--- a/solution.py
+++ b/solution.py
@@ -382,7 +382,7 @@
         scratch=[pltpu.SemaphoreType.DMA((2,))],
     )(packed, passages)
     s0 = send(packed, CORE)
-    across, back, ahead, q1, s0 = tied(across, back, ahead, q1, s0)
+    across, back, ahead, s0 = tied(across, back, ahead, s0)
     plane = call(join_kernel, shape(256, WIDTH, BF), [VMEM] * 4)(kept, back, across, ahead)
     up = send(plane, second(1))
     down = send(plane, second(-1))

time: 104 us -> 103 us (level)
  waiting for transfers between devices: 43.3 us -> 39.8 us
  starting transfers between devices: 35.1 us -> 37.8 us
    ppermute x26, waiting for transfers between devices: 43.3 us -> 39.8 us  [send(): return lax.ppermute(v, AXES, perm)]
    ppermute x26, starting transfers between devices: 35.1 us -> 37.8 us  [send(): return lax.ppermute(v, AXES, perm)]
where the time goes in v7:
time: 103 us; the launch traced here: 102 us
  waiting for transfers between devices  39.8 us (39%)
  starting transfers between devices  37.8 us (37%)
  Pallas kernels  22.1 us (21%)
  local copies, waits for them, and re-layouts  2.01 us (2%)
    ppermute x26, waiting for transfers between devices, send(): return lax.ppermute(v, AXES, perm)  39.8 us
    ppermute x26, starting transfers between devices, send(): return lax.ppermute(v, AXES, perm)  37.8 us
    pallas_call x2, Pallas kernels, query(): call(lambda *r: query_kernel(half, *r), shape(640, WIDTH, kind), [VMEM] *...  5.9 us
    pallas_call x2, Pallas kernels, early(): call(lambda *r: early_kernel(which, *r), (tile, tile, shape(32, 768, F32)...  4.28 us
    pallas_call x1, Pallas kernels, local(): call(near_kernel, (shape(256, WIDTH, F32), shape(256, WIDTH, BF), shape(2...  3.5 us
    pallas_call x4, Pallas kernels, block(): call(kernel, outs, [VMEM] * (4 + len(got)))(mine, theirs, factor, lse, *got)  2.11 us
  transfers between devices with their start and end apart: 26, of which 17 were waited for; matrix products, arithmetic and copies ran while one was open for 0% of the time, Pallas kernels for 17%

profile of v7, /device:TPU:0, one launch (start us, length us, event | category | flops | bytes accessed | tf_op | source)
XLA Modules:
  0.0 102.5 jit_solution(551683811593951018)
XLA Ops:
  0.6 1.9 %shard_map.76.a_ref = bf16[144,2048]{1,0:T(8,128)(2,1)} custom-call(bf16[128,2048]{1,0:T(8,128)(2,1)} %q_ref.1, s32[16,128]{1,0:T(8,128)} %bitcast.4, s32[16,128]{1,0:T(8,128)} %bitcast.5, s32[1,128]{1,0:T(1,128)} %bitcast.6), custom_call_target="tpu_custom_call" | custom-call | tf_op jit(solution)/shard_map/pallas_call | solution.py:361
  2.7 1.7 %collective-permute-start.5 = (bf16[144,2048]{1,0:T(8,128)(2,1)}, bf16[144,2048]{1,0:T(8,128)(2,1)S(1)}, u32[]{:S(2)}, u32[]{:S(2)}) collective-permute-start(bf16[144,2048]{1,0:T(8,128)(2,1)} %shard_map.76.a_ref), channel_id=1, source_target_pairs={{0,32},{1,97},{2,34},{3,99},{4,36},{5,101},{6,38},{7,103},{8,40},{... | collective-permute-start | bytes 1769480 | tf_op jit(solution)/shard_map/ppermute | solution.py:48
  4.4 3.0 %collective-permute-start = (bf16[64,2048]{1,0:T(8,128)(2,1)}, bf16[64,2048]{1,0:T(8,128)(2,1)S(1)}, u32[]{:S(2)}, u32[]{:S(2)}) collective-permute-start(bf16[64,2048]{1,0:T(8,128)(2,1)} %b_ref.1), channel_id=1, source_target_pairs={{0,16},{1,5},{2,18},{3,7},{4,20},{5,1},{6,22},{7,3},{8,24},{9,13},... | collective-permute-start | bytes 786440 | tf_op jit(solution)/shard_map/ppermute | solution.py:48
  8.0 2.6 %collective-permute-start.2 = (bf16[64,2048]{1,0:T(8,128)(2,1)}, bf16[64,2048]{1,0:T(8,128)(2,1)S(1)}, u32[]{:S(2)}, u32[]{:S(2)}) collective-permute-start(bf16[64,2048]{1,0:T(8,128)(2,1)} %b_ref.1), channel_id=1, source_target_pairs={{0,24},{1,7},{2,26},{3,1},{4,28},{5,3},{6,30},{7,5},{8,0},{9,15},{... | collective-permute-start | bytes 786440 | tf_op jit(solution)/shard_map/ppermute | solution.py:48
  12.8 2.4 %collective-permute-done.1.refs_1_ = bf16[64,2048]{1,0:T(8,128)(2,1)S(1)} collective-permute-done((bf16[64,2048]{1,0:T(8,128)(2,1)}, bf16[64,2048]{1,0:T(8,128)(2,1)S(1)}, u32[]{:S(2)}, u32[]{:S(2)}) %collective-permute-start.1) | collective-permute-done | bytes 262176 | tf_op jit(solution)/shard_map/ppermute | solution.py:48
  15.5 4.0 %collective-permute-start.4 = (bf16[256,2048]{1,0:T(8,128)(2,1)S(1)}, bf16[256,2048]{1,0:T(8,128)(2,1)S(1)}, u32[]{:S(2)}, u32[]{:S(2)}) collective-permute-start(bf16[256,2048]{1,0:T(8,128)(2,1)S(1)} %shard_map.78.r_0_.refs_0_.r_8_), channel_id=1, source_target_pairs={{0,4},{1,17},{2,6},{3,19},{4,0},{5,21},{6,2},{7,23},{8,12},{9,25},... | collective-permute-start | bytes 3145736 | tf_op jit(solution)/shard_map/ppermute | solution.py:48
  19.4 1.6 %collective-permute-start.6 = (bf16[144,2048]{1,0:T(8,128)(2,1)S(1)}, bf16[144,2048]{1,0:T(8,128)(2,1)S(1)}, u32[]{:S(2)}, u32[]{:S(2)}) collective-permute-start(bf16[144,2048]{1,0:T(8,128)(2,1)S(1)} %collective-permute-done.5.r_4_.refs_9_.refs_6_), channel_id=1, source_target_pairs={{0,32},{1,97},{2,34},{3,99},{4,36},{5,101},{6,38},{7,103},{8,40},{... | collective-permute-start | bytes 1769480 | tf_op jit(solution)/shard_map/ppermute | solution.py:48
  22.0 2.2 %collective-permute-start.10 = (bf16[256,2048]{1,0:T(8,128)(2,1)S(1)}, bf16[256,2048]{1,0:T(8,128)(2,1)S(1)}, u32[]{:S(2)}, u32[]{:S(2)}) collective-permute-start(bf16[256,2048]{1,0:T(8,128)(2,1)S(1)} %shard_map.78.r_0_.refs_0_.r_8_), channel_id=1, source_target_pairs={{0,6},{1,25},{2,0},{3,27},{4,2},{5,29},{6,4},{7,31},{8,14},{9,1},{... | collective-permute-start | bytes 3145736 | tf_op jit(solution)/shard_map/ppermute | solution.py:48
  24.2 6.3 %collective-permute-done.6.r_6_.refs_11_.refs_8_ = bf16[144,2048]{1,0:T(8,128)(2,1)S(1)} collective-permute-done((bf16[144,2048]{1,0:T(8,128)(2,1)S(1)}, bf16[144,2048]{1,0:T(8,128)(2,1)S(1)}, u32[]{:S(2)}, u32[]{:S(2)}) %collective-permute-start.6) | collective-permute-done | bytes 589856 | tf_op jit(solution)/shard_map/ppermute | solution.py:48
  30.9 1.4 %collective-permute-done.4.r_1_.refs_2_.r_10_ = bf16[256,2048]{1,0:T(8,128)(2,1)S(1)} collective-permute-done((bf16[256,2048]{1,0:T(8,128)(2,1)S(1)}, bf16[256,2048]{1,0:T(8,128)(2,1)S(1)}, u32[]{:S(2)}, u32[]{:S(2)}) %collective-permute-start.4) | collective-permute-done | bytes 1048608 | tf_op jit(solution)/shard_map/ppermute | solution.py:48
  32.5 9.1 %collective-permute-done.11.refs_4_.refs_13_.refs_10_ = bf16[144,2048]{1,0:T(8,128)(2,1)S(1)} collective-permute-done((bf16[144,2048]{1,0:T(8,128)(2,1)S(1)}, bf16[144,2048]{1,0:T(8,128)(2,1)S(1)}, u32[]{:S(2)}, u32[]{:S(2)}) %collective-permute-start.11) | collective-permute-done | bytes 589856 | tf_op jit(solution)/shard_map/ppermute | solution.py:48
  41.6 2.1 %shard_map.79 = (f32[256,256]{1,0:T(8,128)S(1)}, f32[256,256]{1,0:T(8,128)S(1)}, f32[32,768]{1,0:T(8,128)S(1)}) custom-call(bf16[256,2048]{1,0:T(8,128)(2,1)S(1)} %shard_map.78.r_0_.refs_0_.r_8_, bf16[256,2048]{1,0:T(8,128)(2,1)S(1)} %collective-permute-done.4.r_1_.refs_2_.r_10_, bf16[144,2048]{1,0:T(8,128)(2,1)S(1)} %get-tuple-element.37.r_2_.refs_7_.refs_4_, ...), custom_call_target="tpu_custom_call" | custom-call | flops 1610612736 | tf_op jit(solution)/shard_map/pallas_call | solution.py:402
  44.5 2.1 %shard_map.80 = (f32[256,256]{1,0:T(8,128)S(1)}, f32[256,256]{1,0:T(8,128)S(1)}, f32[32,768]{1,0:T(8,128)S(1)}) custom-call(bf16[256,2048]{1,0:T(8,128)(2,1)S(1)} %collective-permute-done.9.r_0_.refs_1_.r_9_, bf16[256,2048]{1,0:T(8,128)(2,1)S(1)} %collective-permute-done.10.r_1_.refs_3_.r_11_, bf16[144,2048]{1,0:T(8,128)(2,1)S(1)} %get-tuple-element.37.r_2_.refs_7_.refs_4_, ...), custom_call_target="tpu_custom_call" | custom-call | flops 1610612736 | tf_op jit(solution)/shard_map/pallas_call | solution.py:402
  46.6 1.4 %shard_map.81 = (f32[64,256]{1,0:T(8,128)S(1)}, f32[8,1024]{1,0:T(8,128)S(1)}) custom-call(bf16[256,2048]{1,0:T(8,128)(2,1)S(1)} %shard_map.78.r_0_.refs_0_.r_8_, bf16[256,2048]{1,0:T(8,128)(2,1)S(1)} %collective-permute-done.9.r_0_.refs_1_.r_9_, bf16[256,2048]{1,0:T(8,128)(2,1)S(1)} %collective-permute-done.4.r_1_.refs_2_.r_10_, ...), custom_call_target="tpu_custom_call" | custom-call | flops 1073741824 | tf_op jit(solution)/shard_map/pallas_call | solution.py:411
  48.1 1.2 %collective-permute-done.13.r_1_.other = f32[8,1024]{1,0:T(8,128)S(1)} collective-permute-done((f32[8,1024]{1,0:T(8,128)S(1)}, f32[8,1024]{1,0:T(8,128)S(1)}, u32[]{:S(2)}, u32[]{:S(2)}) %collective-permute-start.13) | collective-permute-done | bytes 32800 | tf_op jit(solution)/shard_map/ppermute | solution.py:48
  49.3 1.8 %collective-permute-start.14 = (f32[8,1024]{1,0:T(8,128)S(1)}, f32[8,1024]{1,0:T(8,128)S(1)}, u32[]{:S(2)}, u32[]{:S(2)}) collective-permute-start(f32[8,1024]{1,0:T(8,128)S(1)} %shard_map.82.r_12_.r_0_), channel_id=1, source_target_pairs={{0,32},{1,97},{2,34},{3,99},{4,36},{5,101},{6,38},{7,103},{8,40},{... | collective-permute-start | bytes 98312 | tf_op jit(solution)/shard_map/ppermute | solution.py:48
  51.2 2.9 %shard_map.83.r_2_.r_0_ = f32[640,2048]{1,0:T(8,128)S(1)} custom-call(f32[256,256]{1,0:T(8,128)S(1)} %get-tuple-element.41.r_0_.refs_0_, f32[256,256]{1,0:T(8,128)S(1)} %get-tuple-element.42.r_1_.refs_1_, f32[256,256]{1,0:T(8,128)S(1)} %get-tuple-element.43.r_2_.t_ref, f32[256,256]{1,0:T(8,128)S(1)} %get-tuple-element.44.r_3_.refs_2_, ...), custom_call_target="tpu_custom_call" | custom-call | flops 2684354560 | tf_op jit(solution)/shard_map/pallas_call | solution.py:421
  54.7 1.8 %collective-permute-start.15 = (f32[8,1024]{1,0:T(8,128)S(1)}, f32[8,1024]{1,0:T(8,128)S(1)}, u32[]{:S(2)}, u32[]{:S(2)}) collective-permute-start(f32[8,1024]{1,0:T(8,128)S(1)} %shard_map.84.r_12_.stats), channel_id=1, source_target_pairs={{0,64},{1,65},{2,66},{3,67},{4,68},{5,69},{6,70},{7,71},{8,72},{9,... | collective-permute-start | bytes 98312 | tf_op jit(solution)/shard_map/ppermute | solution.py:48
  56.5 3.0 %shard_map.85._ = bf16[640,2048]{1,0:T(8,128)(2,1)S(1)} custom-call(f32[256,256]{1,0:T(8,128)S(1)} %get-tuple-element.41.r_0_.refs_0_, f32[256,256]{1,0:T(8,128)S(1)} %get-tuple-element.42.r_1_.refs_1_, f32[256,256]{1,0:T(8,128)S(1)} %get-tuple-element.43.r_2_.t_ref, f32[256,256]{1,0:T(8,128)S(1)} %get-tuple-element.44.r_3_.refs_2_, ...), custom_call_target="tpu_custom_call" | custom-call | flops 2684354560 | tf_op jit(solution)/shard_map/pallas_call | solution.py:421
  60.5 1.3 %shard_map.92 = bf16[256,2048]{1,0:T(8,128)(2,1)S(1)} custom-call(f32[256,256]{1,0:T(8,128)S(1)} %get-tuple-element.43.r_2_.t_ref, f32[32,768]{1,0:T(8,128)S(1)} %get-tuple-element.45.refs_6_.r_4_.refs_3_.refs_0_, f32[32,768]{1,0:T(8,128)S(1)} %get-tuple-element.46.refs_7_.r_5_.refs_4_.refs_1_, f32[64,256]{1,0:T(8,128)S(1)} %get-tuple-element.47.r_6_.refs_5_.refs_2_, ...), custom_call_target="tpu_custom_call" | custom-call | flops 1073741824 | tf_op jit(solution)/shard_map/pallas_call | solution.py:439
  61.8 2.6 %collective-permute-start.21 = (bf16[256,2048]{1,0:T(8,128)(2,1)S(1)}, bf16[256,2048]{1,0:T(8,128)(2,1)S(1)}, u32[]{:S(2)}, u32[]{:S(2)}) collective-permute-start(bf16[256,2048]{1,0:T(8,128)(2,1)S(1)} %shard_map.92), channel_id=1, source_target_pairs={{0,4},{1,17},{2,6},{3,19},{4,0},{5,21},{6,2},{7,23},{8,12},{9,25},... | collective-permute-start | bytes 3145736 | tf_op jit(solution)/shard_map/ppermute | solution.py:48
  66.8 3.5 %shard_map.91 = (f32[256,2048]{1,0:T(8,128)S(1)}, bf16[256,2048]{1,0:T(8,128)(2,1)S(1)}, bf16[256,2048]{1,0:T(8,128)(2,1)S(1)}) custom-call(f32[256,256]{1,0:T(8,128)S(1)} %get-tuple-element.41.r_0_.refs_0_, f32[256,256]{1,0:T(8,128)S(1)} %get-tuple-element.42.r_1_.refs_1_, f32[256,256]{1,0:T(8,128)S(1)} %get-tuple-element.44.r_3_.refs_2_, ...), custom_call_target="tpu_custom_call" | custom-call | flops 3221225472 | tf_op jit(solution)/shard_map/pallas_call | solution.py:444
  70.3 2.7 %collective-permute-start.20 = (bf16[256,2048]{1,0:T(8,128)(2,1)S(1)}, bf16[256,2048]{1,0:T(8,128)(2,1)S(1)}, u32[]{:S(2)}, u32[]{:S(2)}) collective-permute-start(bf16[256,2048]{1,0:T(8,128)(2,1)S(1)} %get-tuple-element.56), channel_id=1, source_target_pairs={{0,6},{1,25},{2,0},{3,27},{4,2},{5,29},{6,4},{7,31},{8,14},{9,1},{... | collective-permute-start | bytes 3145736 | tf_op jit(solution)/shard_map/ppermute | solution.py:48
  73.0 1.9 %collective-permute-done.17.r_4_ = bf16[128,2048]{1,0:T(8,128)(2,1)S(1)} collective-permute-done((bf16[128,2048]{1,0:T(8,128)(2,1)S(1)}, bf16[128,2048]{1,0:T(8,128)(2,1)S(1)}, u32[]{:S(2)}, u32[]{:S(2)}) %collective-permute-start.17) | collective-permute-done | bytes 524320 | tf_op jit(solution)/shard_map/ppermute | solution.py:48
  75.2 2.4 %collective-permute-start.18 = (bf16[128,2048]{1,0:T(8,128)(2,1)S(1)}, bf16[128,2048]{1,0:T(8,128)(2,1)S(1)}, u32[]{:S(2)}, u32[]{:S(2)}) collective-permute-start(bf16[128,2048]{1,0:T(8,128)(2,1)S(1)} %shard_map.88), channel_id=1, source_target_pairs={{0,96},{1,33},{2,98},{3,35},{4,100},{5,37},{6,102},{7,39},{8,104},... | collective-permute-start | bytes 1572872 | tf_op jit(solution)/shard_map/ppermute | solution.py:48
  77.6 6.9 %collective-permute-done.18.r_4_ = bf16[128,2048]{1,0:T(8,128)(2,1)S(1)} collective-permute-done((bf16[128,2048]{1,0:T(8,128)(2,1)S(1)}, bf16[128,2048]{1,0:T(8,128)(2,1)S(1)}, u32[]{:S(2)}, u32[]{:S(2)}) %collective-permute-start.18) | collective-permute-done | bytes 524320 | tf_op jit(solution)/shard_map/ppermute | solution.py:48
  84.8 3.6 %collective-permute-start.19 = (bf16[128,2048]{1,0:T(8,128)(2,1)S(1)}, bf16[128,2048]{1,0:T(8,128)(2,1)S(1)}, u32[]{:S(2)}, u32[]{:S(2)}) collective-permute-start(bf16[128,2048]{1,0:T(8,128)(2,1)S(1)} %shard_map.89), channel_id=1, source_target_pairs={{0,96},{1,33},{2,98},{3,35},{4,100},{5,37},{6,102},{7,39},{8,104},... | collective-permute-start | bytes 1572872 | tf_op jit(solution)/shard_map/ppermute | solution.py:48
  89.8 2.2 %collective-permute-start.23 = (bf16[64,2048]{1,0:T(8,128)(2,1)S(1)}, bf16[64,2048]{1,0:T(8,128)(2,1)S(1)}, u32[]{:S(2)}, u32[]{:S(2)}) collective-permute-start(bf16[64,2048]{1,0:T(8,128)(2,1)S(1)} %get-tuple-element.59), channel_id=1, source_target_pairs={{0,16},{1,5},{2,18},{3,7},{4,20},{5,1},{6,22},{7,3},{8,24},{9,13},... | collective-permute-start | bytes 786440 | tf_op jit(solution)/shard_map/ppermute | solution.py:48
  92.0 2.1 %collective-permute-start.24 = (bf16[64,2048]{1,0:T(8,128)(2,1)S(1)}, bf16[64,2048]{1,0:T(8,128)(2,1)S(1)}, u32[]{:S(2)}, u32[]{:S(2)}) collective-permute-start(bf16[64,2048]{1,0:T(8,128)(2,1)S(1)} %get-tuple-element.60), channel_id=1, source_target_pairs={{0,24},{1,7},{2,26},{3,1},{4,28},{5,3},{6,30},{7,5},{8,0},{9,15},{... | collective-permute-start | bytes 786440 | tf_op jit(solution)/shard_map/ppermute | solution.py:48
  95.0 1.2 %shard_map.90 = (bf16[128,2048]{1,0:T(8,128)(2,1)}, f32[8,128]{1,0:T(8,128)S(1)}, f32[1,128]{1,0:T(1,128)}) custom-call(f32[640,2048]{1,0:T(8,128)S(1)} %shard_map.83.r_2_.r_0_, bf16[640,2048]{1,0:T(8,128)(2,1)S(1)} %collective-permute-done.16.r_1_.refs_15_, f32[128,128]{1,0:T(8,128)S(1)} %get-tuple-element.51.r_2_, ...), custom_call_target="tpu_custom_call" | custom-call | tf_op jit(solution)/shard_map/pallas_call | solution.py:454
  96.3 1.5 %collective-permute-done.23.b = bf16[64,2048]{1,0:T(8,128)(2,1)S(1)} collective-permute-done((bf16[64,2048]{1,0:T(8,128)(2,1)S(1)}, bf16[64,2048]{1,0:T(8,128)(2,1)S(1)}, u32[]{:S(2)}, u32[]{:S(2)}) %collective-permute-start.23) | collective-permute-done | bytes 262176 | tf_op jit(solution)/shard_map/ppermute | solution.py:48
  97.8 3.2 %collective-permute-done.24.c = bf16[64,2048]{1,0:T(8,128)(2,1)S(1)} collective-permute-done((bf16[64,2048]{1,0:T(8,128)(2,1)S(1)}, bf16[64,2048]{1,0:T(8,128)(2,1)S(1)}, u32[]{:S(2)}, u32[]{:S(2)}) %collective-permute-start.24) | collective-permute-done | bytes 262176 | tf_op jit(solution)/shard_map/ppermute | solution.py:48
  (43 shorter events, 14.0 us)
Async XLA Ops:
  2.6 12.8 %collective-permute-start.3 = (bf16[144,2048]{1,0:T(8,128)(2,1)}, bf16[144,2048]{1,0:T(8,128)(2,1)S(1)}, u32[]{:S(2)}, u32[]{:S(2)}) collective-permute-start(bf16[144,2048]{1,0:T(8,128)(2,1)} %shard_map.76.a_ref), channel_id=1, source_target_pairs={{0,1},{1,0},{2,3},{3,2},{4,5},{5,4},{6,7},{7,6},{8,9},{9,8},{10,11... | collective-permute-start | bytes 1769480 | tf_op jit(solution)/shard_map/ppermute | solution.py:48
  2.7 16.7 %collective-permute-start.5 = (bf16[144,2048]{1,0:T(8,128)(2,1)}, bf16[144,2048]{1,0:T(8,128)(2,1)S(1)}, u32[]{:S(2)}, u32[]{:S(2)}) collective-permute-start(bf16[144,2048]{1,0:T(8,128)(2,1)} %shard_map.76.a_ref), channel_id=1, source_target_pairs={{0,32},{1,97},{2,34},{3,99},{4,36},{5,101},{6,38},{7,103},{8,40},{... | collective-permute-start | bytes 1769480 | tf_op jit(solution)/shard_map/ppermute | solution.py:48
  4.4 8.4 %collective-permute-start = (bf16[64,2048]{1,0:T(8,128)(2,1)}, bf16[64,2048]{1,0:T(8,128)(2,1)S(1)}, u32[]{:S(2)}, u32[]{:S(2)}) collective-permute-start(bf16[64,2048]{1,0:T(8,128)(2,1)} %b_ref.1), channel_id=1, source_target_pairs={{0,16},{1,5},{2,18},{3,7},{4,20},{5,1},{6,22},{7,3},{8,24},{9,13},... | collective-permute-start | bytes 786440 | tf_op jit(solution)/shard_map/ppermute | solution.py:48
  7.4 7.9 %collective-permute-start.1 = (bf16[64,2048]{1,0:T(8,128)(2,1)}, bf16[64,2048]{1,0:T(8,128)(2,1)S(1)}, u32[]{:S(2)}, u32[]{:S(2)}) collective-permute-start(bf16[64,2048]{1,0:T(8,128)(2,1)} %b_ref.1), channel_id=1, source_target_pairs={{0,8},{1,3},{2,10},{3,5},{4,12},{5,7},{6,14},{7,1},{8,16},{9,11},{... | collective-permute-start | bytes 786440 | tf_op jit(solution)/shard_map/ppermute | solution.py:48
  8.0 7.4 %collective-permute-start.2 = (bf16[64,2048]{1,0:T(8,128)(2,1)}, bf16[64,2048]{1,0:T(8,128)(2,1)S(1)}, u32[]{:S(2)}, u32[]{:S(2)}) collective-permute-start(bf16[64,2048]{1,0:T(8,128)(2,1)} %b_ref.1), channel_id=1, source_target_pairs={{0,24},{1,7},{2,26},{3,1},{4,28},{5,3},{6,30},{7,5},{8,0},{9,15},{... | collective-permute-start | bytes 786440 | tf_op jit(solution)/shard_map/ppermute | solution.py:48
  10.7 1.1 %copy-start = (bf16[144,2048]{1,0:T(8,128)(2,1)S(1)}, bf16[144,2048]{1,0:T(8,128)(2,1)}, u32[]{:S(2)}) copy-start(bf16[144,2048]{1,0:T(8,128)(2,1)} %shard_map.76.a_ref) | copy-start | bytes 1769476
  11.7 0.9 copy-start.1
  15.5 16.8 %collective-permute-start.4 = (bf16[256,2048]{1,0:T(8,128)(2,1)S(1)}, bf16[256,2048]{1,0:T(8,128)(2,1)S(1)}, u32[]{:S(2)}, u32[]{:S(2)}) collective-permute-start(bf16[256,2048]{1,0:T(8,128)(2,1)S(1)} %shard_map.78.r_0_.refs_0_.r_8_), channel_id=1, source_target_pairs={{0,4},{1,17},{2,6},{3,19},{4,0},{5,21},{6,2},{7,23},{8,12},{9,25},... | collective-permute-start | bytes 3145736 | tf_op jit(solution)/shard_map/ppermute | solution.py:48
  19.4 11.1 %collective-permute-start.6 = (bf16[144,2048]{1,0:T(8,128)(2,1)S(1)}, bf16[144,2048]{1,0:T(8,128)(2,1)S(1)}, u32[]{:S(2)}, u32[]{:S(2)}) collective-permute-start(bf16[144,2048]{1,0:T(8,128)(2,1)S(1)} %collective-permute-done.5.r_4_.refs_9_.refs_6_), channel_id=1, source_target_pairs={{0,32},{1,97},{2,34},{3,99},{4,36},{5,101},{6,38},{7,103},{8,40},{... | collective-permute-start | bytes 1769480 | tf_op jit(solution)/shard_map/ppermute | solution.py:48
  21.0 22.8 %collective-permute-start.9 = (bf16[256,2048]{1,0:T(8,128)(2,1)S(1)}, bf16[256,2048]{1,0:T(8,128)(2,1)S(1)}, u32[]{:S(2)}, u32[]{:S(2)}) collective-permute-start(bf16[256,2048]{1,0:T(8,128)(2,1)S(1)} %shard_map.78.r_0_.refs_0_.r_8_), channel_id=1, source_target_pairs={{0,2},{1,9},{2,4},{3,11},{4,6},{5,13},{6,0},{7,15},{8,10},{9,17},{... | collective-permute-start | bytes 3145736 | tf_op jit(solution)/shard_map/ppermute | solution.py:48
  22.0 22.5 %collective-permute-start.10 = (bf16[256,2048]{1,0:T(8,128)(2,1)S(1)}, bf16[256,2048]{1,0:T(8,128)(2,1)S(1)}, u32[]{:S(2)}, u32[]{:S(2)}) collective-permute-start(bf16[256,2048]{1,0:T(8,128)(2,1)S(1)} %shard_map.78.r_0_.refs_0_.r_8_), channel_id=1, source_target_pairs={{0,6},{1,25},{2,0},{3,27},{4,2},{5,29},{6,4},{7,31},{8,14},{9,1},{... | collective-permute-start | bytes 3145736 | tf_op jit(solution)/shard_map/ppermute | solution.py:48
  30.5 11.1 %collective-permute-start.11 = (bf16[144,2048]{1,0:T(8,128)(2,1)S(1)}, bf16[144,2048]{1,0:T(8,128)(2,1)S(1)}, u32[]{:S(2)}, u32[]{:S(2)}) collective-permute-start(bf16[144,2048]{1,0:T(8,128)(2,1)S(1)} %collective-permute-done.6.r_6_.refs_11_.refs_8_), channel_id=1, source_target_pairs={{0,32},{1,97},{2,34},{3,99},{4,36},{5,101},{6,38},{7,103},{8,40},{... | collective-permute-start | bytes 1769480 | tf_op jit(solution)/shard_map/ppermute | solution.py:48
  30.9 10.7 %collective-permute-start.7 = (bf16[144,2048]{1,0:T(8,128)(2,1)S(1)}, bf16[144,2048]{1,0:T(8,128)(2,1)S(1)}, u32[]{:S(2)}, u32[]{:S(2)}) collective-permute-start(bf16[144,2048]{1,0:T(8,128)(2,1)S(1)} %collective-permute-done.5.r_4_.refs_9_.refs_6_), channel_id=1, source_target_pairs={{0,1},{1,0},{2,3},{3,2},{4,5},{5,4},{6,7},{7,6},{8,9},{9,8},{10,11... | collective-permute-start | bytes 1769480 | tf_op jit(solution)/shard_map/ppermute | solution.py:48
  32.3 9.3 %collective-permute-start.8 = (bf16[144,2048]{1,0:T(8,128)(2,1)S(1)}, bf16[144,2048]{1,0:T(8,128)(2,1)S(1)}, u32[]{:S(2)}, u32[]{:S(2)}) collective-permute-start(bf16[144,2048]{1,0:T(8,128)(2,1)S(1)} %collective-permute-done.6.r_6_.refs_11_.refs_8_), channel_id=1, source_target_pairs={{0,1},{1,0},{2,3},{3,2},{4,5},{5,4},{6,7},{7,6},{8,9},{9,8},{10,11... | collective-permute-start | bytes 1769480 | tf_op jit(solution)/shard_map/ppermute | solution.py:48
  41.6 5.0 %collective-permute-start.12 = (bf16[144,2048]{1,0:T(8,128)(2,1)S(1)}, bf16[144,2048]{1,0:T(8,128)(2,1)S(1)}, u32[]{:S(2)}, u32[]{:S(2)}) collective-permute-start(bf16[144,2048]{1,0:T(8,128)(2,1)S(1)} %collective-permute-done.11.refs_4_.refs_13_.refs_10_), channel_id=1, source_target_pairs={{0,1},{1,0},{2,3},{3,2},{4,5},{5,4},{6,7},{7,6},{8,9},{9,8},{10,11... | collective-permute-start | bytes 1769480 | tf_op jit(solution)/shard_map/ppermute | solution.py:48
  48.0 1.3 %collective-permute-start.13 = (f32[8,1024]{1,0:T(8,128)S(1)}, f32[8,1024]{1,0:T(8,128)S(1)}, u32[]{:S(2)}, u32[]{:S(2)}) collective-permute-start(f32[8,1024]{1,0:T(8,128)S(1)} %get-tuple-element.48.r_0_.r_7_.raw), channel_id=1, source_target_pairs={{0,1},{1,0},{2,3},{3,2},{4,5},{5,4},{6,7},{7,6},{8,9},{9,8},{10,11... | collective-permute-start | bytes 98312 | tf_op jit(solution)/shard_map/ppermute | solution.py:48
  49.3 5.4 %collective-permute-start.14 = (f32[8,1024]{1,0:T(8,128)S(1)}, f32[8,1024]{1,0:T(8,128)S(1)}, u32[]{:S(2)}, u32[]{:S(2)}) collective-permute-start(f32[8,1024]{1,0:T(8,128)S(1)} %shard_map.82.r_12_.r_0_), channel_id=1, source_target_pairs={{0,32},{1,97},{2,34},{3,99},{4,36},{5,101},{6,38},{7,103},{8,40},{... | collective-permute-start | bytes 98312 | tf_op jit(solution)/shard_map/ppermute | solution.py:48
  54.7 5.5 %collective-permute-start.15 = (f32[8,1024]{1,0:T(8,128)S(1)}, f32[8,1024]{1,0:T(8,128)S(1)}, u32[]{:S(2)}, u32[]{:S(2)}) collective-permute-start(f32[8,1024]{1,0:T(8,128)S(1)} %shard_map.84.r_12_.stats), channel_id=1, source_target_pairs={{0,64},{1,65},{2,66},{3,67},{4,68},{5,69},{6,70},{7,71},{8,72},{9,... | collective-permute-start | bytes 98312 | tf_op jit(solution)/shard_map/ppermute | solution.py:48
  60.4 5.0 %collective-permute-start.16 = (bf16[640,2048]{1,0:T(8,128)(2,1)S(1)}, bf16[640,2048]{1,0:T(8,128)(2,1)S(1)}, u32[]{:S(2)}, u32[]{:S(2)}) collective-permute-start(bf16[640,2048]{1,0:T(8,128)(2,1)S(1)} %shard_map.85._), channel_id=1, source_target_pairs={{0,1},{1,0},{2,3},{3,2},{4,5},{5,4},{6,7},{7,6},{8,9},{9,8},{10,11... | collective-permute-start | bytes 7864328 | tf_op jit(solution)/shard_map/ppermute | solution.py:48
  61.8 26.5 %collective-permute-start.21 = (bf16[256,2048]{1,0:T(8,128)(2,1)S(1)}, bf16[256,2048]{1,0:T(8,128)(2,1)S(1)}, u32[]{:S(2)}, u32[]{:S(2)}) collective-permute-start(bf16[256,2048]{1,0:T(8,128)(2,1)S(1)} %shard_map.92), channel_id=1, source_target_pairs={{0,4},{1,17},{2,6},{3,19},{4,0},{5,21},{6,2},{7,23},{8,12},{9,25},... | collective-permute-start | bytes 3145736 | tf_op jit(solution)/shard_map/ppermute | solution.py:48
  65.6 9.2 %collective-permute-start.17 = (bf16[128,2048]{1,0:T(8,128)(2,1)S(1)}, bf16[128,2048]{1,0:T(8,128)(2,1)S(1)}, u32[]{:S(2)}, u32[]{:S(2)}) collective-permute-start(bf16[128,2048]{1,0:T(8,128)(2,1)S(1)} %shard_map.87), channel_id=1, source_target_pairs={{0,96},{1,33},{2,98},{3,35},{4,100},{5,37},{6,102},{7,39},{8,104},... | collective-permute-start | bytes 1572872 | tf_op jit(solution)/shard_map/ppermute | solution.py:48
  70.3 19.1 %collective-permute-start.20 = (bf16[256,2048]{1,0:T(8,128)(2,1)S(1)}, bf16[256,2048]{1,0:T(8,128)(2,1)S(1)}, u32[]{:S(2)}, u32[]{:S(2)}) collective-permute-start(bf16[256,2048]{1,0:T(8,128)(2,1)S(1)} %get-tuple-element.56), channel_id=1, source_target_pairs={{0,6},{1,25},{2,0},{3,27},{4,2},{5,29},{6,4},{7,31},{8,14},{9,1},{... | collective-permute-start | bytes 3145736 | tf_op jit(solution)/shard_map/ppermute | solution.py:48
  73.0 16.4 %collective-permute-start.22 = (bf16[256,2048]{1,0:T(8,128)(2,1)S(1)}, bf16[256,2048]{1,0:T(8,128)(2,1)S(1)}, u32[]{:S(2)}, u32[]{:S(2)}) collective-permute-start(bf16[256,2048]{1,0:T(8,128)(2,1)S(1)} %get-tuple-element.57), channel_id=1, source_target_pairs={{0,2},{1,9},{2,4},{3,11},{4,6},{5,13},{6,0},{7,15},{8,10},{9,17},{... | collective-permute-start | bytes 3145736 | tf_op jit(solution)/shard_map/ppermute | solution.py:48
  75.2 9.2 %collective-permute-start.18 = (bf16[128,2048]{1,0:T(8,128)(2,1)S(1)}, bf16[128,2048]{1,0:T(8,128)(2,1)S(1)}, u32[]{:S(2)}, u32[]{:S(2)}) collective-permute-start(bf16[128,2048]{1,0:T(8,128)(2,1)S(1)} %shard_map.88), channel_id=1, source_target_pairs={{0,96},{1,33},{2,98},{3,35},{4,100},{5,37},{6,102},{7,39},{8,104},... | collective-permute-start | bytes 1572872 | tf_op jit(solution)/shard_map/ppermute | solution.py:48
  84.8 10.3 %collective-permute-start.19 = (bf16[128,2048]{1,0:T(8,128)(2,1)S(1)}, bf16[128,2048]{1,0:T(8,128)(2,1)S(1)}, u32[]{:S(2)}, u32[]{:S(2)}) collective-permute-start(bf16[128,2048]{1,0:T(8,128)(2,1)S(1)} %shard_map.89), channel_id=1, source_target_pairs={{0,96},{1,33},{2,98},{3,35},{4,100},{5,37},{6,102},{7,39},{8,104},... | collective-permute-start | bytes 1572872 | tf_op jit(solution)/shard_map/ppermute | solution.py:48
  89.8 8.0 %collective-permute-start.23 = (bf16[64,2048]{1,0:T(8,128)(2,1)S(1)}, bf16[64,2048]{1,0:T(8,128)(2,1)S(1)}, u32[]{:S(2)}, u32[]{:S(2)}) collective-permute-start(bf16[64,2048]{1,0:T(8,128)(2,1)S(1)} %get-tuple-element.59), channel_id=1, source_target_pairs={{0,16},{1,5},{2,18},{3,7},{4,20},{5,1},{6,22},{7,3},{8,24},{9,13},... | collective-permute-start | bytes 786440 | tf_op jit(solution)/shard_map/ppermute | solution.py:48
  92.0 9.0 %collective-permute-start.24 = (bf16[64,2048]{1,0:T(8,128)(2,1)S(1)}, bf16[64,2048]{1,0:T(8,128)(2,1)S(1)}, u32[]{:S(2)}, u32[]{:S(2)}) collective-permute-start(bf16[64,2048]{1,0:T(8,128)(2,1)S(1)} %get-tuple-element.60), channel_id=1, source_target_pairs={{0,24},{1,7},{2,26},{3,1},{4,28},{5,3},{6,30},{7,5},{8,0},{9,15},{... | collective-permute-start | bytes 786440 | tf_op jit(solution)/shard_map/ppermute | solution.py:48
  94.1 7.6 %collective-permute-start.25 = (bf16[64,2048]{1,0:T(8,128)(2,1)S(1)}, bf16[64,2048]{1,0:T(8,128)(2,1)S(1)}, u32[]{:S(2)}, u32[]{:S(2)}) collective-permute-start(bf16[64,2048]{1,0:T(8,128)(2,1)S(1)} %get-tuple-element.61), channel_id=1, source_target_pairs={{0,8},{1,3},{2,10},{3,5},{4,12},{5,7},{6,14},{7,1},{8,16},{9,11},{... | collective-permute-start | bytes 786440 | tf_op jit(solution)/shard_map/ppermute | solution.py:48

commit v8 on v7

--- a/solution.py
+++ b/solution.py
@@ -382,7 +382,7 @@
         scratch=[pltpu.SemaphoreType.DMA((2,))],
     )(packed, passages)
     s0 = send(packed, CORE)
-    across, back, ahead, s0 = tied(across, back, ahead, s0)
+    across, ahead, back, s0 = tied(across, ahead, back, s0)
     plane = call(join_kernel, shape(256, WIDTH, BF), [VMEM] * 4)(kept, back, across, ahead)
     up = send(plane, second(1))
     down = send(plane, second(-1))
@@ -465,7 +465,7 @@
     g2 = send(g2, first(2))
     g1 = send(g1, first(-1))
     g3 = send(g3, first(1))
-    passage_grad = call(last_kernel, half, [VMEM] * 5)(g0, g2, g1, g3, token)
+    passage_grad = call(last_kernel, half, [VMEM] * 5)(g0, g2, g3, g1, token)
     return loss.reshape(128), run, passage_grad
 
 

time: 103 us -> 103 us (level)
  transfers between devices with their start and end apart: 26 -> 26, of which waited for: 17 -> 16; matrix products, arithmetic and copies ran while one was open for 0% -> 0% of each run, Pallas kernels for 17% -> 17%
where the time goes in v8:
time: 103 us; the launch traced here: 102 us
  waiting for transfers between devices  40.2 us (39%)
  starting transfers between devices  37.4 us (36%)
  Pallas kernels  22.1 us (21%)
  local copies, waits for them, and re-layouts  2.01 us (2%)
    ppermute x26, waiting for transfers between devices, send(): return lax.ppermute(v, AXES, perm)  40.2 us
    ppermute x26, starting transfers between devices, send(): return lax.ppermute(v, AXES, perm)  37.4 us
    pallas_call x2, Pallas kernels, query(): call(lambda *r: query_kernel(half, *r), shape(640, WIDTH, kind), [VMEM] *...  5.9 us
    pallas_call x2, Pallas kernels, early(): call(lambda *r: early_kernel(which, *r), (tile, tile, shape(32, 768, F32)...  4.27 us
    pallas_call x1, Pallas kernels, local(): call(near_kernel, (shape(256, WIDTH, F32), shape(256, WIDTH, BF), shape(2...  3.5 us
    pallas_call x4, Pallas kernels, block(): call(kernel, outs, [VMEM] * (4 + len(got)))(mine, theirs, factor, lse, *got)  2.11 us
  transfers between devices with their start and end apart: 26, of which 16 were waited for; matrix products, arithmetic and copies ran while one was open for 0% of the time, Pallas kernels for 17%

profile of v8, /device:TPU:0, one launch (start us, length us, event | category | flops | bytes accessed | tf_op | source)
XLA Modules:
  0.0 102.4 jit_solution(15647299478963965617)
XLA Ops:
  0.6 1.9 %shard_map.76.a_ref = bf16[144,2048]{1,0:T(8,128)(2,1)} custom-call(bf16[128,2048]{1,0:T(8,128)(2,1)} %q_ref.1, s32[16,128]{1,0:T(8,128)} %bitcast.4, s32[16,128]{1,0:T(8,128)} %bitcast.5, s32[1,128]{1,0:T(1,128)} %bitcast.6), custom_call_target="tpu_custom_call" | custom-call | tf_op jit(solution)/shard_map/pallas_call | solution.py:361
  2.7 1.7 %collective-permute-start.5 = (bf16[144,2048]{1,0:T(8,128)(2,1)}, bf16[144,2048]{1,0:T(8,128)(2,1)S(1)}, u32[]{:S(2)}, u32[]{:S(2)}) collective-permute-start(bf16[144,2048]{1,0:T(8,128)(2,1)} %shard_map.76.a_ref), channel_id=1, source_target_pairs={{0,32},{1,97},{2,34},{3,99},{4,36},{5,101},{6,38},{7,103},{8,40},{... | collective-permute-start | bytes 1769480 | tf_op jit(solution)/shard_map/ppermute | solution.py:48
  4.4 3.0 %collective-permute-start = (bf16[64,2048]{1,0:T(8,128)(2,1)}, bf16[64,2048]{1,0:T(8,128)(2,1)S(1)}, u32[]{:S(2)}, u32[]{:S(2)}) collective-permute-start(bf16[64,2048]{1,0:T(8,128)(2,1)} %b_ref.1), channel_id=1, source_target_pairs={{0,16},{1,5},{2,18},{3,7},{4,20},{5,1},{6,22},{7,3},{8,24},{9,13},... | collective-permute-start | bytes 786440 | tf_op jit(solution)/shard_map/ppermute | solution.py:48
  12.5 2.9 %collective-permute-done.1.refs_3_ = bf16[64,2048]{1,0:T(8,128)(2,1)S(1)} collective-permute-done((bf16[64,2048]{1,0:T(8,128)(2,1)}, bf16[64,2048]{1,0:T(8,128)(2,1)S(1)}, u32[]{:S(2)}, u32[]{:S(2)}) %collective-permute-start.1) | collective-permute-done | bytes 262176 | tf_op jit(solution)/shard_map/ppermute | solution.py:48
  16.4 4.0 %collective-permute-start.4 = (bf16[256,2048]{1,0:T(8,128)(2,1)S(1)}, bf16[256,2048]{1,0:T(8,128)(2,1)S(1)}, u32[]{:S(2)}, u32[]{:S(2)}) collective-permute-start(bf16[256,2048]{1,0:T(8,128)(2,1)S(1)} %shard_map.78.r_0_.refs_0_.r_8_), channel_id=1, source_target_pairs={{0,4},{1,17},{2,6},{3,19},{4,0},{5,21},{6,2},{7,23},{8,12},{9,25},... | collective-permute-start | bytes 3145736 | tf_op jit(solution)/shard_map/ppermute | solution.py:48
  20.4 1.6 %collective-permute-start.6 = (bf16[144,2048]{1,0:T(8,128)(2,1)S(1)}, bf16[144,2048]{1,0:T(8,128)(2,1)S(1)}, u32[]{:S(2)}, u32[]{:S(2)}) collective-permute-start(bf16[144,2048]{1,0:T(8,128)(2,1)S(1)} %collective-permute-done.5.r_4_.refs_9_.refs_6_), channel_id=1, source_target_pairs={{0,32},{1,97},{2,34},{3,99},{4,36},{5,101},{6,38},{7,103},{8,40},{... | collective-permute-start | bytes 1769480 | tf_op jit(solution)/shard_map/ppermute | solution.py:48
  23.0 2.2 %collective-permute-start.10 = (bf16[256,2048]{1,0:T(8,128)(2,1)S(1)}, bf16[256,2048]{1,0:T(8,128)(2,1)S(1)}, u32[]{:S(2)}, u32[]{:S(2)}) collective-permute-start(bf16[256,2048]{1,0:T(8,128)(2,1)S(1)} %shard_map.78.r_0_.refs_0_.r_8_), channel_id=1, source_target_pairs={{0,6},{1,25},{2,0},{3,27},{4,2},{5,29},{6,4},{7,31},{8,14},{9,1},{... | collective-permute-start | bytes 3145736 | tf_op jit(solution)/shard_map/ppermute | solution.py:48
  25.2 6.3 %collective-permute-done.6.r_6_.refs_11_.refs_8_ = bf16[144,2048]{1,0:T(8,128)(2,1)S(1)} collective-permute-done((bf16[144,2048]{1,0:T(8,128)(2,1)S(1)}, bf16[144,2048]{1,0:T(8,128)(2,1)S(1)}, u32[]{:S(2)}, u32[]{:S(2)}) %collective-permute-start.6) | collective-permute-done | bytes 589856 | tf_op jit(solution)/shard_map/ppermute | solution.py:48
  31.9 1.4 %collective-permute-done.4.r_1_.refs_2_.r_10_ = bf16[256,2048]{1,0:T(8,128)(2,1)S(1)} collective-permute-done((bf16[256,2048]{1,0:T(8,128)(2,1)S(1)}, bf16[256,2048]{1,0:T(8,128)(2,1)S(1)}, u32[]{:S(2)}, u32[]{:S(2)}) %collective-permute-start.4) | collective-permute-done | bytes 1048608 | tf_op jit(solution)/shard_map/ppermute | solution.py:48
  33.3 9.3 %collective-permute-done.11.refs_4_.refs_13_.refs_10_ = bf16[144,2048]{1,0:T(8,128)(2,1)S(1)} collective-permute-done((bf16[144,2048]{1,0:T(8,128)(2,1)S(1)}, bf16[144,2048]{1,0:T(8,128)(2,1)S(1)}, u32[]{:S(2)}, u32[]{:S(2)}) %collective-permute-start.11) | collective-permute-done | bytes 589856 | tf_op jit(solution)/shard_map/ppermute | solution.py:48
  42.6 2.1 %shard_map.79 = (f32[256,256]{1,0:T(8,128)S(1)}, f32[256,256]{1,0:T(8,128)S(1)}, f32[32,768]{1,0:T(8,128)S(1)}) custom-call(bf16[256,2048]{1,0:T(8,128)(2,1)S(1)} %shard_map.78.r_0_.refs_0_.r_8_, bf16[256,2048]{1,0:T(8,128)(2,1)S(1)} %collective-permute-done.4.r_1_.refs_2_.r_10_, bf16[144,2048]{1,0:T(8,128)(2,1)S(1)} %get-tuple-element.37.r_2_.refs_7_.refs_4_, ...), custom_call_target="tpu_custom_call" | custom-call | flops 1610612736 | tf_op jit(solution)/shard_map/pallas_call | solution.py:402
  45.5 2.1 %shard_map.80 = (f32[256,256]{1,0:T(8,128)S(1)}, f32[256,256]{1,0:T(8,128)S(1)}, f32[32,768]{1,0:T(8,128)S(1)}) custom-call(bf16[256,2048]{1,0:T(8,128)(2,1)S(1)} %collective-permute-done.9.r_0_.refs_1_.r_9_, bf16[256,2048]{1,0:T(8,128)(2,1)S(1)} %collective-permute-done.10.r_1_.refs_3_.r_11_, bf16[144,2048]{1,0:T(8,128)(2,1)S(1)} %get-tuple-element.37.r_2_.refs_7_.refs_4_, ...), custom_call_target="tpu_custom_call" | custom-call | flops 1610612736 | tf_op jit(solution)/shard_map/pallas_call | solution.py:402
  47.6 1.4 %shard_map.81 = (f32[64,256]{1,0:T(8,128)S(1)}, f32[8,1024]{1,0:T(8,128)S(1)}) custom-call(bf16[256,2048]{1,0:T(8,128)(2,1)S(1)} %shard_map.78.r_0_.refs_0_.r_8_, bf16[256,2048]{1,0:T(8,128)(2,1)S(1)} %collective-permute-done.9.r_0_.refs_1_.r_9_, bf16[256,2048]{1,0:T(8,128)(2,1)S(1)} %collective-permute-done.4.r_1_.refs_2_.r_10_, ...), custom_call_target="tpu_custom_call" | custom-call | flops 1073741824 | tf_op jit(solution)/shard_map/pallas_call | solution.py:411
  49.1 1.2 %collective-permute-done.13.r_1_.other = f32[8,1024]{1,0:T(8,128)S(1)} collective-permute-done((f32[8,1024]{1,0:T(8,128)S(1)}, f32[8,1024]{1,0:T(8,128)S(1)}, u32[]{:S(2)}, u32[]{:S(2)}) %collective-permute-start.13) | collective-permute-done | bytes 32800 | tf_op jit(solution)/shard_map/ppermute | solution.py:48
  50.3 1.8 %collective-permute-start.14 = (f32[8,1024]{1,0:T(8,128)S(1)}, f32[8,1024]{1,0:T(8,128)S(1)}, u32[]{:S(2)}, u32[]{:S(2)}) collective-permute-start(f32[8,1024]{1,0:T(8,128)S(1)} %shard_map.82.r_12_.r_0_), channel_id=1, source_target_pairs={{0,32},{1,97},{2,34},{3,99},{4,36},{5,101},{6,38},{7,103},{8,40},{... | collective-permute-start | bytes 98312 | tf_op jit(solution)/shard_map/ppermute | solution.py:48
  52.1 2.9 %shard_map.83.r_2_.r_0_ = f32[640,2048]{1,0:T(8,128)S(1)} custom-call(f32[256,256]{1,0:T(8,128)S(1)} %get-tuple-element.41.r_0_.refs_0_, f32[256,256]{1,0:T(8,128)S(1)} %get-tuple-element.42.r_1_.refs_1_, f32[256,256]{1,0:T(8,128)S(1)} %get-tuple-element.43.r_2_.t_ref, f32[256,256]{1,0:T(8,128)S(1)} %get-tuple-element.44.r_3_.refs_2_, ...), custom_call_target="tpu_custom_call" | custom-call | flops 2684354560 | tf_op jit(solution)/shard_map/pallas_call | solution.py:421
  55.7 1.8 %collective-permute-start.15 = (f32[8,1024]{1,0:T(8,128)S(1)}, f32[8,1024]{1,0:T(8,128)S(1)}, u32[]{:S(2)}, u32[]{:S(2)}) collective-permute-start(f32[8,1024]{1,0:T(8,128)S(1)} %shard_map.84.r_12_.stats), channel_id=1, source_target_pairs={{0,64},{1,65},{2,66},{3,67},{4,68},{5,69},{6,70},{7,71},{8,72},{9,... | collective-permute-start | bytes 98312 | tf_op jit(solution)/shard_map/ppermute | solution.py:48
  57.5 3.0 %shard_map.85._ = bf16[640,2048]{1,0:T(8,128)(2,1)S(1)} custom-call(f32[256,256]{1,0:T(8,128)S(1)} %get-tuple-element.41.r_0_.refs_0_, f32[256,256]{1,0:T(8,128)S(1)} %get-tuple-element.42.r_1_.refs_1_, f32[256,256]{1,0:T(8,128)S(1)} %get-tuple-element.43.r_2_.t_ref, f32[256,256]{1,0:T(8,128)S(1)} %get-tuple-element.44.r_3_.refs_2_, ...), custom_call_target="tpu_custom_call" | custom-call | flops 2684354560 | tf_op jit(solution)/shard_map/pallas_call | solution.py:421
  61.5 1.3 %shard_map.92 = bf16[256,2048]{1,0:T(8,128)(2,1)S(1)} custom-call(f32[256,256]{1,0:T(8,128)S(1)} %get-tuple-element.43.r_2_.t_ref, f32[32,768]{1,0:T(8,128)S(1)} %get-tuple-element.45.refs_6_.r_4_.refs_3_.refs_0_, f32[32,768]{1,0:T(8,128)S(1)} %get-tuple-element.46.refs_7_.r_5_.refs_4_.refs_1_, f32[64,256]{1,0:T(8,128)S(1)} %get-tuple-element.47.r_6_.refs_5_.refs_2_, ...), custom_call_target="tpu_custom_call" | custom-call | flops 1073741824 | tf_op jit(solution)/shard_map/pallas_call | solution.py:439
  62.8 2.6 %collective-permute-start.21 = (bf16[256,2048]{1,0:T(8,128)(2,1)S(1)}, bf16[256,2048]{1,0:T(8,128)(2,1)S(1)}, u32[]{:S(2)}, u32[]{:S(2)}) collective-permute-start(bf16[256,2048]{1,0:T(8,128)(2,1)S(1)} %shard_map.92), channel_id=1, source_target_pairs={{0,4},{1,17},{2,6},{3,19},{4,0},{5,21},{6,2},{7,23},{8,12},{9,25},... | collective-permute-start | bytes 3145736 | tf_op jit(solution)/shard_map/ppermute | solution.py:48
  66.6 1.1 %collective-permute-start.17 = (bf16[128,2048]{1,0:T(8,128)(2,1)S(1)}, bf16[128,2048]{1,0:T(8,128)(2,1)S(1)}, u32[]{:S(2)}, u32[]{:S(2)}) collective-permute-start(bf16[128,2048]{1,0:T(8,128)(2,1)S(1)} %shard_map.87), channel_id=1, source_target_pairs={{0,96},{1,33},{2,98},{3,35},{4,100},{5,37},{6,102},{7,39},{8,104},... | collective-permute-start | bytes 1572872 | tf_op jit(solution)/shard_map/ppermute | solution.py:48
  67.8 3.5 %shard_map.91 = (f32[256,2048]{1,0:T(8,128)S(1)}, bf16[256,2048]{1,0:T(8,128)(2,1)S(1)}, bf16[256,2048]{1,0:T(8,128)(2,1)S(1)}) custom-call(f32[256,256]{1,0:T(8,128)S(1)} %get-tuple-element.41.r_0_.refs_0_, f32[256,256]{1,0:T(8,128)S(1)} %get-tuple-element.42.r_1_.refs_1_, f32[256,256]{1,0:T(8,128)S(1)} %get-tuple-element.44.r_3_.refs_2_, ...), custom_call_target="tpu_custom_call" | custom-call | flops 3221225472 | tf_op jit(solution)/shard_map/pallas_call | solution.py:444
  71.3 2.7 %collective-permute-start.20 = (bf16[256,2048]{1,0:T(8,128)(2,1)S(1)}, bf16[256,2048]{1,0:T(8,128)(2,1)S(1)}, u32[]{:S(2)}, u32[]{:S(2)}) collective-permute-start(bf16[256,2048]{1,0:T(8,128)(2,1)S(1)} %get-tuple-element.56), channel_id=1, source_target_pairs={{0,6},{1,25},{2,0},{3,27},{4,2},{5,29},{6,4},{7,31},{8,14},{9,1},{... | collective-permute-start | bytes 3145736 | tf_op jit(solution)/shard_map/ppermute | solution.py:48
  74.0 1.9 %collective-permute-done.17.r_4_ = bf16[128,2048]{1,0:T(8,128)(2,1)S(1)} collective-permute-done((bf16[128,2048]{1,0:T(8,128)(2,1)S(1)}, bf16[128,2048]{1,0:T(8,128)(2,1)S(1)}, u32[]{:S(2)}, u32[]{:S(2)}) %collective-permute-start.17) | collective-permute-done | bytes 524320 | tf_op jit(solution)/shard_map/ppermute | solution.py:48
  76.2 2.4 %collective-permute-start.18 = (bf16[128,2048]{1,0:T(8,128)(2,1)S(1)}, bf16[128,2048]{1,0:T(8,128)(2,1)S(1)}, u32[]{:S(2)}, u32[]{:S(2)}) collective-permute-start(bf16[128,2048]{1,0:T(8,128)(2,1)S(1)} %shard_map.88), channel_id=1, source_target_pairs={{0,96},{1,33},{2,98},{3,35},{4,100},{5,37},{6,102},{7,39},{8,104},... | collective-permute-start | bytes 1572872 | tf_op jit(solution)/shard_map/ppermute | solution.py:48
  78.5 6.9 %collective-permute-done.18.r_4_ = bf16[128,2048]{1,0:T(8,128)(2,1)S(1)} collective-permute-done((bf16[128,2048]{1,0:T(8,128)(2,1)S(1)}, bf16[128,2048]{1,0:T(8,128)(2,1)S(1)}, u32[]{:S(2)}, u32[]{:S(2)}) %collective-permute-start.18) | collective-permute-done | bytes 524320 | tf_op jit(solution)/shard_map/ppermute | solution.py:48
  85.7 3.6 %collective-permute-start.19 = (bf16[128,2048]{1,0:T(8,128)(2,1)S(1)}, bf16[128,2048]{1,0:T(8,128)(2,1)S(1)}, u32[]{:S(2)}, u32[]{:S(2)}) collective-permute-start(bf16[128,2048]{1,0:T(8,128)(2,1)S(1)} %shard_map.89), channel_id=1, source_target_pairs={{0,96},{1,33},{2,98},{3,35},{4,100},{5,37},{6,102},{7,39},{8,104},... | collective-permute-start | bytes 1572872 | tf_op jit(solution)/shard_map/ppermute | solution.py:48
  90.8 2.0 %collective-permute-start.23 = (bf16[64,2048]{1,0:T(8,128)(2,1)S(1)}, bf16[64,2048]{1,0:T(8,128)(2,1)S(1)}, u32[]{:S(2)}, u32[]{:S(2)}) collective-permute-start(bf16[64,2048]{1,0:T(8,128)(2,1)S(1)} %get-tuple-element.59), channel_id=1, source_target_pairs={{0,16},{1,5},{2,18},{3,7},{4,20},{5,1},{6,22},{7,3},{8,24},{9,13},... | collective-permute-start | bytes 786440 | tf_op jit(solution)/shard_map/ppermute | solution.py:48
  93.4 2.6 %collective-permute-start.25 = (bf16[64,2048]{1,0:T(8,128)(2,1)S(1)}, bf16[64,2048]{1,0:T(8,128)(2,1)S(1)}, u32[]{:S(2)}, u32[]{:S(2)}) collective-permute-start(bf16[64,2048]{1,0:T(8,128)(2,1)S(1)} %get-tuple-element.61), channel_id=1, source_target_pairs={{0,24},{1,7},{2,26},{3,1},{4,28},{5,3},{6,30},{7,5},{8,0},{9,15},{... | collective-permute-start | bytes 786440 | tf_op jit(solution)/shard_map/ppermute | solution.py:48
  96.1 1.2 %shard_map.90 = (bf16[128,2048]{1,0:T(8,128)(2,1)}, f32[8,128]{1,0:T(8,128)S(1)}, f32[1,128]{1,0:T(1,128)}) custom-call(f32[640,2048]{1,0:T(8,128)S(1)} %shard_map.83.r_2_.r_0_, bf16[640,2048]{1,0:T(8,128)(2,1)S(1)} %collective-permute-done.16.r_1_.refs_15_, f32[128,128]{1,0:T(8,128)S(1)} %get-tuple-element.51.r_2_, ...), custom_call_target="tpu_custom_call" | custom-call | tf_op jit(solution)/shard_map/pallas_call | solution.py:454
  97.3 1.5 %collective-permute-done.23.b = bf16[64,2048]{1,0:T(8,128)(2,1)S(1)} collective-permute-done((bf16[64,2048]{1,0:T(8,128)(2,1)S(1)}, bf16[64,2048]{1,0:T(8,128)(2,1)S(1)}, u32[]{:S(2)}, u32[]{:S(2)}) %collective-permute-start.23) | collective-permute-done | bytes 262176 | tf_op jit(solution)/shard_map/ppermute | solution.py:48
  98.9 2.7 %collective-permute-done.24.c = bf16[64,2048]{1,0:T(8,128)(2,1)S(1)} collective-permute-done((bf16[64,2048]{1,0:T(8,128)(2,1)S(1)}, bf16[64,2048]{1,0:T(8,128)(2,1)S(1)}, u32[]{:S(2)}, u32[]{:S(2)}) %collective-permute-start.24) | collective-permute-done | bytes 262176 | tf_op jit(solution)/shard_map/ppermute | solution.py:48
  (43 shorter events, 14.8 us)
Async XLA Ops:
  2.6 13.8 %collective-permute-start.3 = (bf16[144,2048]{1,0:T(8,128)(2,1)}, bf16[144,2048]{1,0:T(8,128)(2,1)S(1)}, u32[]{:S(2)}, u32[]{:S(2)}) collective-permute-start(bf16[144,2048]{1,0:T(8,128)(2,1)} %shard_map.76.a_ref), channel_id=1, source_target_pairs={{0,1},{1,0},{2,3},{3,2},{4,5},{5,4},{6,7},{7,6},{8,9},{9,8},{10,11... | collective-permute-start | bytes 1769480 | tf_op jit(solution)/shard_map/ppermute | solution.py:48
  2.7 17.7 %collective-permute-start.5 = (bf16[144,2048]{1,0:T(8,128)(2,1)}, bf16[144,2048]{1,0:T(8,128)(2,1)S(1)}, u32[]{:S(2)}, u32[]{:S(2)}) collective-permute-start(bf16[144,2048]{1,0:T(8,128)(2,1)} %shard_map.76.a_ref), channel_id=1, source_target_pairs={{0,32},{1,97},{2,34},{3,99},{4,36},{5,101},{6,38},{7,103},{8,40},{... | collective-permute-start | bytes 1769480 | tf_op jit(solution)/shard_map/ppermute | solution.py:48
  4.4 8.1 %collective-permute-start = (bf16[64,2048]{1,0:T(8,128)(2,1)}, bf16[64,2048]{1,0:T(8,128)(2,1)S(1)}, u32[]{:S(2)}, u32[]{:S(2)}) collective-permute-start(bf16[64,2048]{1,0:T(8,128)(2,1)} %b_ref.1), channel_id=1, source_target_pairs={{0,16},{1,5},{2,18},{3,7},{4,20},{5,1},{6,22},{7,3},{8,24},{9,13},... | collective-permute-start | bytes 786440 | tf_op jit(solution)/shard_map/ppermute | solution.py:48
  7.4 8.0 %collective-permute-start.1 = (bf16[64,2048]{1,0:T(8,128)(2,1)}, bf16[64,2048]{1,0:T(8,128)(2,1)S(1)}, u32[]{:S(2)}, u32[]{:S(2)}) collective-permute-start(bf16[64,2048]{1,0:T(8,128)(2,1)} %b_ref.1), channel_id=1, source_target_pairs={{0,24},{1,7},{2,26},{3,1},{4,28},{5,3},{6,30},{7,5},{8,0},{9,15},{... | collective-permute-start | bytes 786440 | tf_op jit(solution)/shard_map/ppermute | solution.py:48
  8.6 7.8 %collective-permute-start.2 = (bf16[64,2048]{1,0:T(8,128)(2,1)}, bf16[64,2048]{1,0:T(8,128)(2,1)S(1)}, u32[]{:S(2)}, u32[]{:S(2)}) collective-permute-start(bf16[64,2048]{1,0:T(8,128)(2,1)} %b_ref.1), channel_id=1, source_target_pairs={{0,8},{1,3},{2,10},{3,5},{4,12},{5,7},{6,14},{7,1},{8,16},{9,11},{... | collective-permute-start | bytes 786440 | tf_op jit(solution)/shard_map/ppermute | solution.py:48
  9.4 1.1 %copy-start = (bf16[144,2048]{1,0:T(8,128)(2,1)S(1)}, bf16[144,2048]{1,0:T(8,128)(2,1)}, u32[]{:S(2)}) copy-start(bf16[144,2048]{1,0:T(8,128)(2,1)} %shard_map.76.a_ref) | copy-start | bytes 1769476
  10.5 0.9 copy-start.1
  16.4 16.8 %collective-permute-start.4 = (bf16[256,2048]{1,0:T(8,128)(2,1)S(1)}, bf16[256,2048]{1,0:T(8,128)(2,1)S(1)}, u32[]{:S(2)}, u32[]{:S(2)}) collective-permute-start(bf16[256,2048]{1,0:T(8,128)(2,1)S(1)} %shard_map.78.r_0_.refs_0_.r_8_), channel_id=1, source_target_pairs={{0,4},{1,17},{2,6},{3,19},{4,0},{5,21},{6,2},{7,23},{8,12},{9,25},... | collective-permute-start | bytes 3145736 | tf_op jit(solution)/shard_map/ppermute | solution.py:48
  20.4 11.1 %collective-permute-start.6 = (bf16[144,2048]{1,0:T(8,128)(2,1)S(1)}, bf16[144,2048]{1,0:T(8,128)(2,1)S(1)}, u32[]{:S(2)}, u32[]{:S(2)}) collective-permute-start(bf16[144,2048]{1,0:T(8,128)(2,1)S(1)} %collective-permute-done.5.r_4_.refs_9_.refs_6_), channel_id=1, source_target_pairs={{0,32},{1,97},{2,34},{3,99},{4,36},{5,101},{6,38},{7,103},{8,40},{... | collective-permute-start | bytes 1769480 | tf_op jit(solution)/shard_map/ppermute | solution.py:48
  22.0 22.8 %collective-permute-start.9 = (bf16[256,2048]{1,0:T(8,128)(2,1)S(1)}, bf16[256,2048]{1,0:T(8,128)(2,1)S(1)}, u32[]{:S(2)}, u32[]{:S(2)}) collective-permute-start(bf16[256,2048]{1,0:T(8,128)(2,1)S(1)} %shard_map.78.r_0_.refs_0_.r_8_), channel_id=1, source_target_pairs={{0,2},{1,9},{2,4},{3,11},{4,6},{5,13},{6,0},{7,15},{8,10},{9,17},{... | collective-permute-start | bytes 3145736 | tf_op jit(solution)/shard_map/ppermute | solution.py:48
  23.0 22.5 %collective-permute-start.10 = (bf16[256,2048]{1,0:T(8,128)(2,1)S(1)}, bf16[256,2048]{1,0:T(8,128)(2,1)S(1)}, u32[]{:S(2)}, u32[]{:S(2)}) collective-permute-start(bf16[256,2048]{1,0:T(8,128)(2,1)S(1)} %shard_map.78.r_0_.refs_0_.r_8_), channel_id=1, source_target_pairs={{0,6},{1,25},{2,0},{3,27},{4,2},{5,29},{6,4},{7,31},{8,14},{9,1},{... | collective-permute-start | bytes 3145736 | tf_op jit(solution)/shard_map/ppermute | solution.py:48
  31.5 11.1 %collective-permute-start.11 = (bf16[144,2048]{1,0:T(8,128)(2,1)S(1)}, bf16[144,2048]{1,0:T(8,128)(2,1)S(1)}, u32[]{:S(2)}, u32[]{:S(2)}) collective-permute-start(bf16[144,2048]{1,0:T(8,128)(2,1)S(1)} %collective-permute-done.6.r_6_.refs_11_.refs_8_), channel_id=1, source_target_pairs={{0,32},{1,97},{2,34},{3,99},{4,36},{5,101},{6,38},{7,103},{8,40},{... | collective-permute-start | bytes 1769480 | tf_op jit(solution)/shard_map/ppermute | solution.py:48
  31.9 10.7 %collective-permute-start.7 = (bf16[144,2048]{1,0:T(8,128)(2,1)S(1)}, bf16[144,2048]{1,0:T(8,128)(2,1)S(1)}, u32[]{:S(2)}, u32[]{:S(2)}) collective-permute-start(bf16[144,2048]{1,0:T(8,128)(2,1)S(1)} %collective-permute-done.5.r_4_.refs_9_.refs_6_), channel_id=1, source_target_pairs={{0,1},{1,0},{2,3},{3,2},{4,5},{5,4},{6,7},{7,6},{8,9},{9,8},{10,11... | collective-permute-start | bytes 1769480 | tf_op jit(solution)/shard_map/ppermute | solution.py:48
  33.3 9.3 %collective-permute-start.8 = (bf16[144,2048]{1,0:T(8,128)(2,1)S(1)}, bf16[144,2048]{1,0:T(8,128)(2,1)S(1)}, u32[]{:S(2)}, u32[]{:S(2)}) collective-permute-start(bf16[144,2048]{1,0:T(8,128)(2,1)S(1)} %collective-permute-done.6.r_6_.refs_11_.refs_8_), channel_id=1, source_target_pairs={{0,1},{1,0},{2,3},{3,2},{4,5},{5,4},{6,7},{7,6},{8,9},{9,8},{10,11... | collective-permute-start | bytes 1769480 | tf_op jit(solution)/shard_map/ppermute | solution.py:48
  42.6 5.0 %collective-permute-start.12 = (bf16[144,2048]{1,0:T(8,128)(2,1)S(1)}, bf16[144,2048]{1,0:T(8,128)(2,1)S(1)}, u32[]{:S(2)}, u32[]{:S(2)}) collective-permute-start(bf16[144,2048]{1,0:T(8,128)(2,1)S(1)} %collective-permute-done.11.refs_4_.refs_13_.refs_10_), channel_id=1, source_target_pairs={{0,1},{1,0},{2,3},{3,2},{4,5},{5,4},{6,7},{7,6},{8,9},{9,8},{10,11... | collective-permute-start | bytes 1769480 | tf_op jit(solution)/shard_map/ppermute | solution.py:48
  49.0 1.3 %collective-permute-start.13 = (f32[8,1024]{1,0:T(8,128)S(1)}, f32[8,1024]{1,0:T(8,128)S(1)}, u32[]{:S(2)}, u32[]{:S(2)}) collective-permute-start(f32[8,1024]{1,0:T(8,128)S(1)} %get-tuple-element.48.r_0_.r_7_.raw), channel_id=1, source_target_pairs={{0,1},{1,0},{2,3},{3,2},{4,5},{5,4},{6,7},{7,6},{8,9},{9,8},{10,11... | collective-permute-start | bytes 98312 | tf_op jit(solution)/shard_map/ppermute | solution.py:48
  50.3 5.4 %collective-permute-start.14 = (f32[8,1024]{1,0:T(8,128)S(1)}, f32[8,1024]{1,0:T(8,128)S(1)}, u32[]{:S(2)}, u32[]{:S(2)}) collective-permute-start(f32[8,1024]{1,0:T(8,128)S(1)} %shard_map.82.r_12_.r_0_), channel_id=1, source_target_pairs={{0,32},{1,97},{2,34},{3,99},{4,36},{5,101},{6,38},{7,103},{8,40},{... | collective-permute-start | bytes 98312 | tf_op jit(solution)/shard_map/ppermute | solution.py:48
  55.7 5.5 %collective-permute-start.15 = (f32[8,1024]{1,0:T(8,128)S(1)}, f32[8,1024]{1,0:T(8,128)S(1)}, u32[]{:S(2)}, u32[]{:S(2)}) collective-permute-start(f32[8,1024]{1,0:T(8,128)S(1)} %shard_map.84.r_12_.stats), channel_id=1, source_target_pairs={{0,64},{1,65},{2,66},{3,67},{4,68},{5,69},{6,70},{7,71},{8,72},{9,... | collective-permute-start | bytes 98312 | tf_op jit(solution)/shard_map/ppermute | solution.py:48
  61.4 5.0 %collective-permute-start.16 = (bf16[640,2048]{1,0:T(8,128)(2,1)S(1)}, bf16[640,2048]{1,0:T(8,128)(2,1)S(1)}, u32[]{:S(2)}, u32[]{:S(2)}) collective-permute-start(bf16[640,2048]{1,0:T(8,128)(2,1)S(1)} %shard_map.85._), channel_id=1, source_target_pairs={{0,1},{1,0},{2,3},{3,2},{4,5},{5,4},{6,7},{7,6},{8,9},{9,8},{10,11... | collective-permute-start | bytes 7864328 | tf_op jit(solution)/shard_map/ppermute | solution.py:48
  62.8 26.5 %collective-permute-start.21 = (bf16[256,2048]{1,0:T(8,128)(2,1)S(1)}, bf16[256,2048]{1,0:T(8,128)(2,1)S(1)}, u32[]{:S(2)}, u32[]{:S(2)}) collective-permute-start(bf16[256,2048]{1,0:T(8,128)(2,1)S(1)} %shard_map.92), channel_id=1, source_target_pairs={{0,4},{1,17},{2,6},{3,19},{4,0},{5,21},{6,2},{7,23},{8,12},{9,25},... | collective-permute-start | bytes 3145736 | tf_op jit(solution)/shard_map/ppermute | solution.py:48
  66.6 9.2 %collective-permute-start.17 = (bf16[128,2048]{1,0:T(8,128)(2,1)S(1)}, bf16[128,2048]{1,0:T(8,128)(2,1)S(1)}, u32[]{:S(2)}, u32[]{:S(2)}) collective-permute-start(bf16[128,2048]{1,0:T(8,128)(2,1)S(1)} %shard_map.87), channel_id=1, source_target_pairs={{0,96},{1,33},{2,98},{3,35},{4,100},{5,37},{6,102},{7,39},{8,104},... | collective-permute-start | bytes 1572872 | tf_op jit(solution)/shard_map/ppermute | solution.py:48
  71.3 19.1 %collective-permute-start.20 = (bf16[256,2048]{1,0:T(8,128)(2,1)S(1)}, bf16[256,2048]{1,0:T(8,128)(2,1)S(1)}, u32[]{:S(2)}, u32[]{:S(2)}) collective-permute-start(bf16[256,2048]{1,0:T(8,128)(2,1)S(1)} %get-tuple-element.56), channel_id=1, source_target_pairs={{0,6},{1,25},{2,0},{3,27},{4,2},{5,29},{6,4},{7,31},{8,14},{9,1},{... | collective-permute-start | bytes 3145736 | tf_op jit(solution)/shard_map/ppermute | solution.py:48
  74.0 16.4 %collective-permute-start.22 = (bf16[256,2048]{1,0:T(8,128)(2,1)S(1)}, bf16[256,2048]{1,0:T(8,128)(2,1)S(1)}, u32[]{:S(2)}, u32[]{:S(2)}) collective-permute-start(bf16[256,2048]{1,0:T(8,128)(2,1)S(1)} %get-tuple-element.57), channel_id=1, source_target_pairs={{0,2},{1,9},{2,4},{3,11},{4,6},{5,13},{6,0},{7,15},{8,10},{9,17},{... | collective-permute-start | bytes 3145736 | tf_op jit(solution)/shard_map/ppermute | solution.py:48
  76.2 9.2 %collective-permute-start.18 = (bf16[128,2048]{1,0:T(8,128)(2,1)S(1)}, bf16[128,2048]{1,0:T(8,128)(2,1)S(1)}, u32[]{:S(2)}, u32[]{:S(2)}) collective-permute-start(bf16[128,2048]{1,0:T(8,128)(2,1)S(1)} %shard_map.88), channel_id=1, source_target_pairs={{0,96},{1,33},{2,98},{3,35},{4,100},{5,37},{6,102},{7,39},{8,104},... | collective-permute-start | bytes 1572872 | tf_op jit(solution)/shard_map/ppermute | solution.py:48
  85.7 10.4 %collective-permute-start.19 = (bf16[128,2048]{1,0:T(8,128)(2,1)S(1)}, bf16[128,2048]{1,0:T(8,128)(2,1)S(1)}, u32[]{:S(2)}, u32[]{:S(2)}) collective-permute-start(bf16[128,2048]{1,0:T(8,128)(2,1)S(1)} %shard_map.89), channel_id=1, source_target_pairs={{0,96},{1,33},{2,98},{3,35},{4,100},{5,37},{6,102},{7,39},{8,104},... | collective-permute-start | bytes 1572872 | tf_op jit(solution)/shard_map/ppermute | solution.py:48
  90.8 8.1 %collective-permute-start.23 = (bf16[64,2048]{1,0:T(8,128)(2,1)S(1)}, bf16[64,2048]{1,0:T(8,128)(2,1)S(1)}, u32[]{:S(2)}, u32[]{:S(2)}) collective-permute-start(bf16[64,2048]{1,0:T(8,128)(2,1)S(1)} %get-tuple-element.59), channel_id=1, source_target_pairs={{0,16},{1,5},{2,18},{3,7},{4,20},{5,1},{6,22},{7,3},{8,24},{9,13},... | collective-permute-start | bytes 786440 | tf_op jit(solution)/shard_map/ppermute | solution.py:48
  92.9 8.7 %collective-permute-start.24 = (bf16[64,2048]{1,0:T(8,128)(2,1)S(1)}, bf16[64,2048]{1,0:T(8,128)(2,1)S(1)}, u32[]{:S(2)}, u32[]{:S(2)}) collective-permute-start(bf16[64,2048]{1,0:T(8,128)(2,1)S(1)} %get-tuple-element.60), channel_id=1, source_target_pairs={{0,8},{1,3},{2,10},{3,5},{4,12},{5,7},{6,14},{7,1},{8,16},{9,11},{... | collective-permute-start | bytes 786440 | tf_op jit(solution)/shard_map/ppermute | solution.py:48
  93.4 8.1 %collective-permute-start.25 = (bf16[64,2048]{1,0:T(8,128)(2,1)S(1)}, bf16[64,2048]{1,0:T(8,128)(2,1)S(1)}, u32[]{:S(2)}, u32[]{:S(2)}) collective-permute-start(bf16[64,2048]{1,0:T(8,128)(2,1)S(1)} %get-tuple-element.61), channel_id=1, source_target_pairs={{0,24},{1,7},{2,26},{3,1},{4,28},{5,3},{6,30},{7,5},{8,0},{9,15},{... | collective-permute-start | bytes 786440 | tf_op jit(solution)/shard_map/ppermute | solution.py:48
